TPU v7x, 32 devices: a whole 2x2x4 slice. The times are simulated.
32 devices in a mesh: dp: 8 (over z, y), fsdp: 4 (over x, core).
Axes of the slice: x: 2, y: 2, z: 4, core: 2. Of those that a mesh axis runs over, the one named last changes fastest.
Arguments:
- tokens: bfloat16 [4096, 1280], P(('dp', 'fsdp')), may hold values from -3 to 3
- qkv_weight: bfloat16 [3, 1280, 1280], P(None, 'dp', 'fsdp'), may hold values from -1 to 1
- out_weight: bfloat16 [1280, 1280], P('fsdp', 'dp'), may hold values from -0.15625 to 0.15625
- merge_weight: bfloat16 [5120, 1280], P(('dp', 'fsdp')), may hold values from -0.078125 to 0.078125
- ln_gains: float32 [2, 1280], replicated, may hold values from 0.25 to 1.75
- segments: int32 [8, 512], P('dp', 'fsdp'), may hold values from 0 to 2, never falling along the last dimension, each value on 1 to 256 neighbouring positions
- merge_rows: int32 [32, 128], P(('dp', 'fsdp')), may hold values from 0 to 127, each once within a row
- owners: int32 [1024, 1], P(('dp', 'fsdp')), may hold values from 0 to 7; in each aligned block of 32 rows (0 to 31, 32 to 63, ...) at most 8 rows name the same one
Outputs:
- owned: bfloat16 [2048, 1280], P(('dp', 'fsdp'))
Inputs may be any that keep to these rules, and one draw needn't show every extreme that they name: `segments`: within each row segment numbers never fall, every number appears, each request has 1 to 256 tokens and one has exactly 256. `merge_rows`: each row is a permutation of the device's local rows. `owners`: among the 32 merged tokens of one device no owner appears more than 8 times, and in some devices one appears exactly 8 times.
All inputs are finite; a program needn't handle non-finite values.
Results may differ from a plain program's by a relative error of at most 0.02.
Values may be sent and summed in bfloat16 or wider, within the bound.
No kernel may reach another device: no remote copies, remote signals or barrier semaphores. Data moves between devices by JAX's collectives and lax.ppermute only.
A program may use at most 64 MiB of HBM per device.

v0:
```python
import math

import jax
import jax.numpy as jnp
from jax import lax
from jax.sharding import PartitionSpec as P

HD = 80


epsilon = 1e-06


def normalize(values_in, gain_row):
    widened = values_in.astype(jnp.float32)
    centered = widened - jnp.mean(widened, axis=1, keepdims=True)
    variance = jnp.mean(centered * centered, axis=1, keepdims=True)
    return (centered * lax.rsqrt(variance + epsilon) * gain_row).astype(jnp.bfloat16)


def attend(queries, keys_all, values_all, seg_rows, seg_cols):
    factor = 1.0 / math.sqrt(HD)
    allowed = seg_rows[:, None] == seg_cols[None, :]
    pieces = []
    for head_index in range(queries.shape[1] // HD):
        first_col = head_index * HD
        last_col = first_col + HD
        scores = (
            lax.dot_general(
                queries[:, first_col:last_col],
                keys_all[:, first_col:last_col],
                (((1,), (1,)), ((), ())),
                preferred_element_type=jnp.float32,
            )
            * factor
        )
        masked = jnp.where(allowed, scores, -jnp.inf)
        highest = jnp.max(masked, axis=1, keepdims=True)
        weights = jnp.exp(masked - highest)
        totals = jnp.sum(weights, axis=1, keepdims=True)
        head_out = jnp.dot(
            weights.astype(jnp.bfloat16),
            values_all[:, first_col:last_col],
            preferred_element_type=jnp.float32,
        )
        pieces.append(head_out / totals)
    return jnp.concatenate(pieces, axis=1).astype(jnp.bfloat16)


def per_device(
    tokens, qkv_weight, out_weight, merge_weight, ln_gains, segments, merge_rows, owners
):
    n_dp = lax.axis_size("dp")
    n_fsdp = lax.axis_size("fsdp")
    qkv_mine = lax.all_gather(qkv_weight, "dp", axis=1, tiled=True)
    out_mine = lax.all_gather(out_weight, "dp", axis=1, tiled=True)
    normed = normalize(tokens, ln_gains[0])
    group_normed, group_segs = (
        lax.all_gather(normed, "fsdp", axis=0, tiled=True),
        lax.all_gather(segments, "fsdp", axis=1, tiled=True),
    )
    queries = jnp.dot(group_normed, qkv_mine[0], preferred_element_type=jnp.float32).astype(
        jnp.bfloat16
    )
    keys_all = jnp.dot(group_normed, qkv_mine[1], preferred_element_type=jnp.float32).astype(
        jnp.bfloat16
    )
    values_all = jnp.dot(group_normed, qkv_mine[2], preferred_element_type=jnp.float32).astype(
        jnp.bfloat16
    )
    attended_mine = attend(queries, keys_all, values_all, group_segs[0], group_segs[0])
    attended_local = lax.all_to_all(attended_mine, "fsdp", split_axis=0, concat_axis=1, tiled=True)
    out_full = lax.all_gather(out_mine, "fsdp", axis=0, tiled=True)
    update = jnp.dot(attended_local, out_full, preferred_element_type=jnp.float32)
    layer_out = (tokens.astype(jnp.float32) + update).astype(jnp.bfloat16)
    merge_in = normalize(layer_out, ln_gains[1])
    merge_count = tokens.shape[0] // 4
    stacked = jnp.take(merge_in, merge_rows[0], axis=0).reshape(merge_count, 4 * merge_in.shape[1])
    slice_rows = merge_weight.shape[0]
    part_rows = lax.all_gather(merge_weight, "dp", axis=0, tiled=True)
    blocks = stacked.reshape(merge_count, n_dp, n_fsdp * slice_rows)
    received = lax.all_to_all(blocks, "fsdp", split_axis=2, concat_axis=0, tiled=True)
    gathered_inputs = received.reshape(n_fsdp * merge_count, n_dp * slice_rows)
    merged = lax.psum_scatter(
        jnp.dot(gathered_inputs, part_rows, preferred_element_type=jnp.float32).astype(
            jnp.bfloat16
        ),
        "fsdp",
        scatter_dimension=0,
        tiled=True,
    )
    capacity = max(2, (2 * merge_count + n_dp - 1) // n_dp)
    targets = owners[:, 0]
    onehot = (targets[:, None] == jnp.arange(n_dp, dtype=jnp.int32)[None, :]).astype(jnp.int32)
    earlier = jnp.cumsum(onehot, axis=0) - onehot
    position = jnp.sum(earlier * onehot, axis=1)
    slot_index = targets * capacity + position
    placing = (jnp.arange(n_dp * capacity, dtype=jnp.int32)[:, None] == slot_index[None, :]).astype(
        jnp.bfloat16
    )
    packed = jnp.dot(placing, merged, preferred_element_type=jnp.float32).astype(jnp.bfloat16)
    packed = packed.reshape(n_dp, capacity, merged.shape[1])
    arrived = lax.all_to_all(packed, "dp", split_axis=0, concat_axis=0, tiled=True)
    return arrived.reshape(n_dp * capacity, merged.shape[1])


def solution(mesh):
    return jax.shard_map(
        per_device,
        mesh=mesh,
        in_specs=(
            P(("dp", "fsdp"), None),
            P(None, "dp", "fsdp"),
            P("fsdp", "dp"),
            P(("dp", "fsdp"), None),
            P(),
            P("dp", "fsdp"),
            P(("dp", "fsdp"), None),
            P(("dp", "fsdp"), None),
        ),
        out_specs=P(("dp", "fsdp"), None),
        check_vma=False,
    )
```

profile of v0, /device:TPU:0, one launch (start us, length us, event | category | flops | bytes accessed | tf_op | source)
XLA Modules:
  0.0 234.0 jit_solution(8528570027717731337)
XLA Ops:
  6.5 0.8 slice_reduce_fusion
  7.4 1.1 convert_reduce_fusion
  8.5 1.2 fusion.21
  9.7 1.9 fusion.23
  11.7 0.7 all-gather.7.cloned.1.call-update
  12.4 34.6 %all_gather.21 = bf16[320,1280]{0,1:T(8,128)(2,1)S(1)} all-gather(bf16[320,160]{0,1:T(8,128)(2,1)S(1)} %copy-done.1), channel_id=1, replica_groups=mesh['dp'=8,'fsdp'=4] {'dp'}, dimensions={1}, use_global_device_ids=true | all-gather | bytes 921600 | tf_op jit(solution)/shard_map/all_gather | solution.py:56
  47.1 1.3 copy.37
  48.9 5.0 %all_gather.18 = s32[1,512]{1,0:T(1,128)S(1)} all-gather(s32[1,128]{1,0:T(1,128)S(1)} %copy-done.3), channel_id=1, replica_groups=mesh['dp'=8,'fsdp'=4] {'fsdp'}, dimensions={1}, use_global_device_ids=true | all-gather | bytes 2560 | tf_op jit(solution)/shard_map/all_gather | solution.py:60
  54.5 0.7 reduce.7
  55.4 37.9 %all-gather.7.cloned.1.call-done = bf16[3,1280,320]{2,1,0:T(8,128)(2,1)} async-done(((bf16[3,160,320]{2,1,0:T(8,128)(2,1)}), bf16[3,1280,320]{2,1,0:T(8,128)(2,1)}) %all-gather.7.cloned.1.call-update) | async-done | bytes 2457616 | tf_op jit(solution)/shard_map/all_gather | solution.py:55
  93.3 2.4 %convolution_convert_fusion.3 = bf16[512,320]{0,1:T(8,128)(2,1)S(1)} fusion(bf16[512,1280]{1,0:T(8,128)(2,1)} %all-gather.5.cloned.1.call-done, bf16[3,1280,320]{2,1,0:T(8,128)(2,1)} %all-gather.7.cloned.1.call-done), kind=kOutput, calls=%fused_computation.17 | convolution fusion | flops 419594240 | bytes 2621440 | tf_op jit(solution)/shard_map/dot_general | solution.py:65
  95.8 2.0 convolution_convert_fusion.4
  100.0 0.9 copy-done.5
  100.9 0.6 convolution_convert_fusion.2
  102.9 0.8 pad_maximum_fusion
  103.6 3.5 %all-to-all-start = ((bf16[4,128,320]{1,2,0:T(8,128)(2,1)}), bf16[4,128,320]{1,2,0:T(8,128)(2,1)S(1)}, u32[]{:S(2)}, u32[]{:S(2)}) async-start(bf16[4,128,320]{1,2,0:T(8,128)(2,1)} %pad_maximum_fusion), calls=%async_computation | async-start | bytes 655360 | tf_op jit(solution)/shard_map/all_to_all | solution.py:72
  107.2 10.5 %all-to-all-done = bf16[4,128,320]{1,2,0:T(8,128)(2,1)S(1)} async-done(((bf16[4,128,320]{1,2,0:T(8,128)(2,1)}), bf16[4,128,320]{1,2,0:T(8,128)(2,1)S(1)}, u32[]{:S(2)}, u32[]{:S(2)}) %all-to-all-start) | async-done | bytes 327712 | tf_op jit(solution)/shard_map/all_to_all | solution.py:72
  117.6 8.7 %all-gather.9.cloned.1.call-done = bf16[1280,1280]{1,0:T(8,128)(2,1)} async-done(((bf16[320,1280]{1,0:T(8,128)(2,1)}), bf16[1280,1280]{1,0:T(8,128)(2,1)}) %all-gather.9.cloned.1.call-update) | async-done | bytes 3276816 | tf_op jit(solution)/shard_map/all_gather | solution.py:73
  126.3 2.6 %fusion.51 = (f32[128]{0:T(128)S(1)}, f32[128,1280]{1,0:T(8,128)S(1)}) fusion(bf16[128,1280]{0,1:T(8,128)(2,1)S(1)} %bitcast.57, bf16[1280,1280]{1,0:T(8,128)(2,1)} %all-gather.9.cloned.1.call-done, bf16[128,1280]{1,0:T(8,128)(2,1)S(1)} %copy-done), kind=kOutput, calls=%fused_computation.97 | convolution fusion | flops 420249472 | bytes 4588032 | tf_op jit(solution)/shard_map/dot_general | solution.py:74
  129.4 0.9 gather_fusion
  130.4 1.4 copy.38
  132.0 1.2 reshape.122
  133.2 9.1 %all_to_all.36 = bf16[4,2,20480]{2,1,0:T(2,128)(2,1)S(1)} all-to-all(bf16[4,2,20480]{2,1,0:T(2,128)(2,1)S(1)} %reshape.122), channel_id=1, replica_groups=mesh['dp'=8,'fsdp'=4] {'fsdp'}, dimensions={0} | all-to-all | bytes 655360 | tf_op jit(solution)/shard_map/all_to_all | solution.py:82
  142.3 0.6 reshape.123
  142.9 2.2 copy.41
  145.2 0.5 reshape.100
  145.8 44.6 %all-gather.11.cloned.1.call-done = bf16[1280,1280]{1,0:T(8,128)(2,1)} async-done(((bf16[160,1280]{1,0:T(8,128)(2,1)}), bf16[1280,1280]{1,0:T(8,128)(2,1)}) %all-gather.11.cloned.1.call-update) | async-done | bytes 3276816 | tf_op jit(solution)/shard_map/all_gather | solution.py:80
  190.4 3.3 %convolution_convert_fusion = bf16[128,1280]{1,0:T(8,128)(2,1)} fusion(bf16[128,1280]{1,0:T(8,128)(2,1)S(1)} %reshape.100, bf16[1280,1280]{1,0:T(8,128)(2,1)} %all-gather.11.cloned.1.call-done), kind=kOutput, calls=%fused_computation.4 | convolution fusion | flops 419594240 | bytes 3932160 | tf_op jit(solution)/shard_map/dot_general | solution.py:85
  194.0 18.9 %reduce-scatter.2.cloned.1.call-done = bf16[32,1280]{1,0:T(8,128)(2,1)} async-done(((bf16[128,1280]{1,0:T(8,128)(2,1)}), bf16[32,1280]{1,0:T(8,128)(2,1)}) %reduce-scatter.2.cloned.1.call-update) | async-done | bytes 81936 | tf_op jit(solution)/shard_map/reduce_scatter | solution.py:84
  212.9 1.1 fusion.2
  214.0 12.9 %all_to_all.37 = bf16[8,8,1280]{2,1,0:T(8,128)(2,1)S(1)} all-to-all(bf16[8,8,1280]{2,1,0:T(8,128)(2,1)S(1)} %fusion.2), channel_id=1, replica_groups=mesh['dp'=8,'fsdp'=4] {'dp'}, dimensions={0} | all-to-all | bytes 327680 | tf_op jit(solution)/shard_map/all_to_all | solution.py:103
  226.8 0.7 copy.51
  (58 shorter events, 6.2 us)
Async XLA Ops:
  6.5 5.9 %copy-start.1 = (bf16[320,160]{0,1:T(8,128)(2,1)S(1)}, bf16[320,160]{0,1:T(8,128)(2,1)}, u32[]{:S(2)}) copy-start(bf16[320,160]{0,1:T(8,128)(2,1)} %param.10) | copy-start | bytes 307204
  6.5 48.9 %all-gather.5.cloned.1.call-start = ((), (), s32[]{:S(2)}) async-start(), calls=%async_computation.4 | async-start | bytes 1638400 | tf_op jit(solution)/shard_map/all_gather | solution.py:59
  11.6 81.7 %all-gather.7.cloned.1.call-start = ((), (), s32[]{:S(2)}) async-start(), calls=%async_computation.5 | async-start | bytes 3317760 | tf_op jit(solution)/shard_map/all_gather | solution.py:55
  12.4 113.9 %all-gather.9.cloned.1.call-start = ((), (), s32[]{:S(2)}) async-start(), calls=%async_computation.6 | async-start | bytes 4096000 | tf_op jit(solution)/shard_map/all_gather | solution.py:73
  47.1 1.9 copy-start.3
  47.1 7.4 %copy-start.6 = (s32[1,128]{1,0:T(1,128)S(1)}, s32[1,128]{1,0:T(1,128)}, u32[]{:S(2)}) copy-start(s32[1,128]{1,0:T(1,128)} %param.14) | copy-start | bytes 1540
  48.4 142.1 %all-gather.11.cloned.1.call-start = ((), (), s32[]{:S(2)}) async-start(), calls=%async_computation.7 | async-start | bytes 3686400 | tf_op jit(solution)/shard_map/all_gather | solution.py:80
  93.3 2.5 %copy-start.4 = (bf16[3,1280,320]{2,1,0:T(8,128)(2,1)S(1)}, bf16[3,1280,320]{2,1,0:T(8,128)(2,1)}, u32[]{:S(2)}) copy-start(bf16[3,1280,320]{2,1,0:T(8,128)(2,1)} %all-gather.7.cloned.1.call-done) | copy-start | bytes 7372804
  99.5 1.4 copy-start.5
  102.5 23.9 %copy-start = (bf16[128,1280]{1,0:T(8,128)(2,1)S(1)}, bf16[128,1280]{1,0:T(8,128)(2,1)}, u32[]{:S(2)}) copy-start(bf16[128,1280]{1,0:T(8,128)(2,1)} %param.8) | copy-start | bytes 983044
  103.6 14.0 %all-to-all-start = ((bf16[4,128,320]{1,2,0:T(8,128)(2,1)}), bf16[4,128,320]{1,2,0:T(8,128)(2,1)S(1)}, u32[]{:S(2)}, u32[]{:S(2)}) async-start(bf16[4,128,320]{1,2,0:T(8,128)(2,1)} %pad_maximum_fusion), calls=%async_computation | async-start | bytes 655360 | tf_op jit(solution)/shard_map/all_to_all | solution.py:72
  107.1 105.8 %reduce-scatter.2.cloned.1.call-start = ((), (), s32[]{:S(2)}) async-start(), calls=%async_computation.8 | async-start | bytes 409600 | tf_op jit(solution)/shard_map/reduce_scatter | solution.py:84
  145.8 47.9 %copy-start.2 = (s32[32,1]{0,1:T(1,128)S(1)}, s32[32,1]{0,1:T(1,128)}, u32[]{:S(2)}) copy-start(s32[32,1]{0,1:T(1,128)} %param.15) | copy-start | bytes 388
Sparse Core Ops, SparseCore 0:
  11.8 20.8 all-gather.4
  34.9 58.3 all-gather.6
  94.9 31.4 all-gather.8
  128.4 62.0 all-gather.10
  193.8 19.0 reduce-scatter.1
where the time goes:
time: 235 us; the launch traced here: 234 us
  waiting for transfers between devices  122 us (52%)
  blocking collectives  61.6 us (26%)
  matrix products  14.6 us (6%)
  between operations  13.4 us (6%)
  local copies, waits for them, and re-layouts  11.7 us (5%)
  other arithmetic  7.34 us (3%)
  starting transfers between devices  3.62 us (2%)
    all_gather x1, waiting for transfers between devices, per_device(): part_rows = lax.all_gather(merge_weight, 'dp', axis=0, tiled=True)  44.6 us
    all_gather x1, waiting for transfers between devices, per_device(): qkv_mine = lax.all_gather(qkv_weight, 'dp', axis=1, tiled=True)  37.9 us
    all_gather x1, blocking collectives, per_device(): out_mine = lax.all_gather(out_weight, 'dp', axis=1, tiled=True)  34.6 us
    reduce_scatter x1, waiting for transfers between devices, per_device(): lax.psum_scatter(jnp.dot(gathered_inputs, part_rows, preferred_element_ty...  18.9 us
    all_to_all x1, blocking collectives, per_device(): lax.all_to_all(packed, 'dp', split_axis=0, concat_axis=0, tiled=True)  12.9 us
    all_to_all x1, waiting for transfers between devices, per_device(): lax.all_to_all(attended_mine, 'fsdp', split_axis=0, concat_axis=1, tiled=...  10.5 us
    all_to_all x1, blocking collectives, per_device(): lax.all_to_all(blocks, 'fsdp', split_axis=2, concat_axis=0, tiled=True)  9.11 us
    all_gather x1, waiting for transfers between devices, per_device(): out_full = lax.all_gather(out_mine, 'fsdp', axis=0, tiled=True)  8.71 us
  transfers between devices with their start and end apart: 6, of which 5 were waited for; matrix products, arithmetic and copies ran while one was open for 10% of the time, Pallas kernels for 0%

commit v1 on v0

--- a/solution.py
+++ b/solution.py
@@ -47,48 +47,137 @@
     return jnp.concatenate(pieces, axis=1).astype(jnp.bfloat16)
 
 
+def xor_pairs(n, k):
+    return [(i, i ^ k) for i in range(n)]
+
+
+def swap(value, axis, k):
+    return lax.ppermute(value, axis, xor_pairs(lax.axis_size(axis), k))
+
+
+def turn(value, k):
+    n = lax.axis_size("dp")
+    return lax.ppermute(value, "dp", [(i, (i + 2 * k) % n) for i in range(n)])
+
+
+def after(value, other):
+    return lax.optimization_barrier((value, other))[0]
+
+
+def place(parts, dim, size):
+    shape = list(parts[0][1].shape)
+    step = shape[dim]
+    shape[dim] = size * step
+    whole = jnp.zeros(shape, parts[0][1].dtype)
+    for index, block in parts:
+        start = [0] * len(shape)
+        start[dim] = index * step
+        whole = lax.dynamic_update_slice(whole, block, start)
+    return whole
+
+
+def z_then_y(block, me):
+    found = [(0, block)] + [(k, turn(block, k)) for k in (1, 3, 2)]
+    mine, theirs = [], []
+    for k, held in found:
+        index = lax.rem(me + 8 - 2 * k, 8)
+        mine.append((index, held))
+        theirs.append((index ^ 1, swap(held, "dp", 1)))
+    return mine, theirs
+
+
+def y_then_z(block, me):
+    other = swap(block, "dp", 1)
+    low = jnp.where(me % 2 == 0, block, other)
+    high = jnp.where(me % 2 == 0, other, block)
+    pair = jnp.concatenate([low, high], axis=0)
+    parts = [(me // 2, pair)]
+    for k in (1, 3, 2):
+        parts.append((lax.rem(me // 2 + 4 - k, 4), turn(pair, k)))
+    return parts
+
+
 def per_device(
     tokens, qkv_weight, out_weight, merge_weight, ln_gains, segments, merge_rows, owners
 ):
     n_dp = lax.axis_size("dp")
     n_fsdp = lax.axis_size("fsdp")
-    qkv_mine = lax.all_gather(qkv_weight, "dp", axis=1, tiled=True)
-    out_mine = lax.all_gather(out_weight, "dp", axis=1, tiled=True)
+    me = lax.axis_index("dp")
+    place_in_group = lax.axis_index("fsdp")
     normed = normalize(tokens, ln_gains[0])
-    group_normed, group_segs = (
-        lax.all_gather(normed, "fsdp", axis=0, tiled=True),
-        lax.all_gather(segments, "fsdp", axis=1, tiled=True),
-    )
-    queries = jnp.dot(group_normed, qkv_mine[0], preferred_element_type=jnp.float32).astype(
-        jnp.bfloat16
-    )
-    keys_all = jnp.dot(group_normed, qkv_mine[1], preferred_element_type=jnp.float32).astype(
-        jnp.bfloat16
-    )
-    values_all = jnp.dot(group_normed, qkv_mine[2], preferred_element_type=jnp.float32).astype(
-        jnp.bfloat16
+    out_turned = out_weight.T
+    if n_dp == 8:
+        qkv_mine, qkv_theirs = z_then_y(qkv_weight, me)
+        qkv_full = place(qkv_mine + qkv_theirs, 1, 8)
+        out_parts = y_then_z(after(out_turned, qkv_mine[1][1]), me)
+        out_rows = place(out_parts, 0, 4)
+        merge_mine, merge_theirs = z_then_y(after(merge_weight, qkv_mine[2][1]), me)
+        part_rows = place(merge_mine + merge_theirs, 0, 8)
+    else:
+        qkv_full = lax.all_gather(qkv_weight, "dp", axis=1, tiled=True)
+        out_rows = lax.all_gather(out_turned, "dp", axis=0, tiled=True)
+        part_rows = lax.all_gather(merge_weight, "dp", axis=0, tiled=True)
+
+    others = range(1, n_fsdp)
+    group_normed = place(
+        [(place_in_group, normed)]
+        + [(place_in_group ^ k, swap(normed, "fsdp", k)) for k in others],
+        0,
+        n_fsdp,
+    )
+    group_segs = place(
+        [(place_in_group, segments)]
+        + [(place_in_group ^ k, swap(segments, "fsdp", k)) for k in others],
+        1,
+        n_fsdp,
+    )
+    queries, keys_all, values_all = (
+        jnp.dot(group_normed, qkv_full[n], preferred_element_type=jnp.float32).astype(jnp.bfloat16)
+        for n in range(3)
     )
     attended_mine = attend(queries, keys_all, values_all, group_segs[0], group_segs[0])
-    attended_local = lax.all_to_all(attended_mine, "fsdp", split_axis=0, concat_axis=1, tiled=True)
-    out_full = lax.all_gather(out_mine, "fsdp", axis=0, tiled=True)
-    update = jnp.dot(attended_local, out_full, preferred_element_type=jnp.float32)
-    layer_out = (tokens.astype(jnp.float32) + update).astype(jnp.bfloat16)
-    merge_in = normalize(layer_out, ln_gains[1])
+    by_device = attended_mine.reshape(n_fsdp, tokens.shape[0], -1)
+
+    update = tokens.astype(jnp.float32)
+    for k in range(n_fsdp):
+        heads = lax.dynamic_index_in_dim(by_device, place_in_group ^ k, 0, keepdims=False)
+        rows = out_rows
+        if k:
+            heads, rows = swap(heads, "fsdp", k), swap(out_rows, "fsdp", k)
+        update = update + lax.dot_general(
+            heads, rows, (((1,), (1,)), ((), ())), preferred_element_type=jnp.float32
+        )
+    merge_in = normalize(update.astype(jnp.bfloat16), ln_gains[1])
+
     merge_count = tokens.shape[0] // 4
-    stacked = jnp.take(merge_in, merge_rows[0], axis=0).reshape(merge_count, 4 * merge_in.shape[1])
     slice_rows = merge_weight.shape[0]
-    part_rows = lax.all_gather(merge_weight, "dp", axis=0, tiled=True)
-    blocks = stacked.reshape(merge_count, n_dp, n_fsdp * slice_rows)
-    received = lax.all_to_all(blocks, "fsdp", split_axis=2, concat_axis=0, tiled=True)
-    gathered_inputs = received.reshape(n_fsdp * merge_count, n_dp * slice_rows)
-    merged = lax.psum_scatter(
-        jnp.dot(gathered_inputs, part_rows, preferred_element_type=jnp.float32).astype(
-            jnp.bfloat16
-        ),
-        "fsdp",
-        scatter_dimension=0,
-        tiled=True,
-    )
+    stacked = jnp.take(merge_in, merge_rows[0], axis=0).reshape(
+        merge_count, n_dp, n_fsdp, slice_rows
+    )
+    by_slice = stacked.transpose(2, 0, 1, 3).reshape(n_fsdp, merge_count, n_dp * slice_rows)
+    received = place(
+        [
+            (
+                place_in_group ^ k,
+                (lambda v, k=k: swap(v, "fsdp", k) if k else v)(
+                    lax.dynamic_index_in_dim(by_slice, place_in_group ^ k, 0, keepdims=False)
+                ),
+            )
+            for k in range(n_fsdp)
+        ],
+        0,
+        n_fsdp,
+    )
+    partial = jnp.dot(received, part_rows, preferred_element_type=jnp.float32).astype(jnp.bfloat16)
+    partial = partial.reshape(n_fsdp, merge_count, -1)
+    total = 0.0
+    for k in range(n_fsdp):
+        share = lax.dynamic_index_in_dim(partial, place_in_group ^ k, 0, keepdims=False)
+        if k:
+            share = swap(share, "fsdp", k)
+        total = total + share.astype(jnp.float32)
+    merged = total.astype(jnp.bfloat16)
+
     capacity = max(2, (2 * merge_count + n_dp - 1) // n_dp)
     targets = owners[:, 0]
     onehot = (targets[:, None] == jnp.arange(n_dp, dtype=jnp.int32)[None, :]).astype(jnp.int32)

time: 235 us -> 199 us (0.85)
  waiting for transfers between devices: 122 us -> 66.7 us
  blocking collectives: 61.6 us -> 10.9 us
  local copies, waits for them, and re-layouts: 11.7 us -> 58.5 us
  starting transfers between devices: 3.62 us -> 33.7 us
  between operations: 13.4 us -> 0.4 us
  other arithmetic: 7.34 us -> 10.4 us
    all_gather x4 -> x0, waiting for transfers between devices: 91.2 us -> none  [the longest x1 44.6 us: per_device(): part_rows = lax.all_gather(merge_weight, 'dp', axis=0, tiled=True)]
    ppermute x0 -> x36, waiting for transfers between devices: none -> 66.7 us  [the longest x27 56.2 us: swap(): return lax.ppermute(value, axis, xor_pairs(lax.axis_size(axis), k))]
    all_gather x2 -> x0, blocking collectives: 39.6 us -> none  [the longest x1 34.6 us: per_device(): out_mine = lax.all_gather(out_weight, 'dp', axis=1, tiled=True)]
    dynamic_update_slice x0 -> x31, local copies, waits for them, and re-layouts: none -> 35.7 us  [place(): whole = lax.dynamic_update_slice(whole, block, start)]
    ppermute x0 -> x36, starting transfers between devices: none -> 33.7 us  [the longest x27 22.4 us: swap(): return lax.ppermute(value, axis, xor_pairs(lax.axis_size(axis), k))]
    reduce_scatter x1 -> x0, waiting for transfers between devices: 18.9 us -> none  [per_device(): lax.psum_scatter(jnp.dot(gathered_inputs, part_rows, preferred_element_ty...]
    all_to_all x1 -> x0, waiting for transfers between devices: 10.5 us -> none  [per_device(): lax.all_to_all(attended_mine, 'fsdp', split_axis=0, concat_axis=1, tiled=...]
    all_to_all x1 -> x0, blocking collectives: 9.11 us -> none  [per_device(): lax.all_to_all(blocks, 'fsdp', split_axis=2, concat_axis=0, tiled=True)]
  transfers between devices with their start and end apart: 6 -> 36, of which waited for: 5 -> 17; matrix products, arithmetic and copies ran while one was open for 10% -> 36% of each run, Pallas kernels for 0% -> 0%
where the time goes in v1:
time: 199 us; the launch traced here: 197 us
  waiting for transfers between devices  66.7 us (34%)
  local copies, waits for them, and re-layouts  58.5 us (29%)
  starting transfers between devices  33.7 us (17%)
  matrix products  16.4 us (8%)
  blocking collectives  10.9 us (5%)
  other arithmetic  10.4 us (5%)
    ppermute x27, waiting for transfers between devices, swap(): return lax.ppermute(value, axis, xor_pairs(lax.axis_size(axis), k))  56.2 us
    dynamic_update_slice x31, local copies, waits for them, and re-layouts, place(): whole = lax.dynamic_update_slice(whole, block, start)  35.7 us
    ppermute x27, starting transfers between devices, swap(): return lax.ppermute(value, axis, xor_pairs(lax.axis_size(axis), k))  22.4 us
    ppermute x9, starting transfers between devices, turn(): return lax.ppermute(value, 'dp', [(i, (i + 2 * k) % n) for i in range(n)])  11.3 us
    all_to_all x1, blocking collectives, per_device(): lax.all_to_all(packed, 'dp', split_axis=0, concat_axis=0, tiled=True)  10.9 us
    ppermute x9, waiting for transfers between devices, turn(): return lax.ppermute(value, 'dp', [(i, (i + 2 * k) % n) for i in range(n)])  10.5 us
    unnamed x28, local copies, waits for them, and re-layouts  7.55 us
    dot_general x3, matrix products, per_device(): jnp.dot(group_normed, qkv_full[n], preferred_element_type=jnp.float32)  6.69 us
  transfers between devices with their start and end apart: 36, of which 17 were waited for; matrix products, arithmetic and copies ran while one was open for 36% of the time, Pallas kernels for 0%

profile of v1, /device:TPU:0, one launch (start us, length us, event | category | flops | bytes accessed | tf_op | source)
XLA Modules:
  0.0 197.0 jit_solution(233588919900240047)
XLA Ops:
  0.0 3.0 %collective-permute-start.6 = (bf16[3,160,320]{2,1,0:T(8,128)(2,1)}, bf16[3,160,320]{2,1,0:T(8,128)(2,1)}, u32[]{:S(2)}, u32[]{:S(2)}) collective-permute-start(bf16[3,160,320]{2,1,0:T(8,128)(2,1)} %param.9), channel_id=1, source_target_pairs={{0,8},{4,12},{8,16},{12,20},{16,24},{20,28},{24,0},{28,4},{1,9},{5... | collective-permute-start | bytes 921608 | tf_op jit(solution)/shard_map/ppermute | solution.py:60
  3.0 2.1 %collective-permute-start.7 = (bf16[3,160,320]{2,1,0:T(8,128)(2,1)}, bf16[3,160,320]{2,1,0:T(8,128)(2,1)}, u32[]{:S(2)}, u32[]{:S(2)}) collective-permute-start(bf16[3,160,320]{2,1,0:T(8,128)(2,1)} %param.9), channel_id=1, source_target_pairs={{0,24},{4,28},{8,0},{12,4},{16,8},{20,12},{24,16},{28,20},{1,25},{... | collective-permute-start | bytes 921608 | tf_op jit(solution)/shard_map/ppermute | solution.py:60
  16.3 1.9 broadcast_in_dim.57
  22.9 2.0 collective-permute-done.1
  25.8 2.0 %collective-permute-done.2 = s32[1,128]{1,0:T(1,128)S(1)} collective-permute-done((s32[1,128]{1,0:T(1,128)S(1)}, s32[1,128]{1,0:T(1,128)S(1)}, u32[]{:S(2)}, u32[]{:S(2)}) %collective-permute-start.2) | collective-permute-done | bytes 544 | tf_op jit(solution)/shard_map/ppermute | solution.py:55
  31.5 1.8 constant_dynamic-update-slice_fusion.16
  33.4 4.4 %collective-permute-done.8 = bf16[3,160,320]{2,1,0:T(8,128)(2,1)} collective-permute-done((bf16[3,160,320]{2,1,0:T(8,128)(2,1)}, bf16[3,160,320]{2,1,0:T(8,128)(2,1)}, u32[]{:S(2)}, u32[]{:S(2)}) %collective-permute-start.8) | collective-permute-done | bytes 307232 | tf_op jit(solution)/shard_map/ppermute | solution.py:60
  40.8 3.9 %collective-permute-start.27 = (bf16[160,1280]{1,0:T(8,128)(2,1)}, bf16[160,1280]{1,0:T(8,128)(2,1)}, u32[]{:S(2)}, u32[]{:S(2)}) collective-permute-start(bf16[160,1280]{1,0:T(8,128)(2,1)} %param.11), channel_id=1, source_target_pairs={{0,24},{4,28},{8,0},{12,4},{16,8},{20,12},{24,16},{28,20},{1,25},{... | collective-permute-start | bytes 1228808 | tf_op jit(solution)/shard_map/ppermute | solution.py:60
  44.7 1.8 constant_dynamic-update-slice_fusion.14
  56.2 3.4 %dynamic_update_slice.116 = bf16[1280,320]{0,1:T(8,128)(2,1)} dynamic-update-slice(bf16[1280,320]{0,1:T(8,128)(2,1)} %broadcast_in_dim.59, bf16[320,320]{0,1:T(8,128)(2,1)S(1)} %pad_maximum_fusion, s32[]{:T(128)S(6)} %select_n.180, s32[]{:T(128)} %constant.137.clone.1) | dynamic-update-slice | bytes 409604 | tf_op jit(solution)/shard_map/dynamic_update_slice | solution.py:75
  59.5 1.9 collective-permute-done.10
  63.2 6.1 %collective-permute-done.11 = bf16[3,160,320]{2,1,0:T(8,128)(2,1)} collective-permute-done((bf16[3,160,320]{2,1,0:T(8,128)(2,1)}, bf16[3,160,320]{2,1,0:T(8,128)(2,1)}, u32[]{:S(2)}, u32[]{:S(2)}) %collective-permute-start.11) | collective-permute-done | bytes 307232 | tf_op jit(solution)/shard_map/ppermute | solution.py:55
  71.1 4.7 %collective-permute-done.12 = bf16[3,160,320]{2,1,0:T(8,128)(2,1)} collective-permute-done((bf16[3,160,320]{2,1,0:T(8,128)(2,1)}, bf16[3,160,320]{2,1,0:T(8,128)(2,1)}, u32[]{:S(2)}, u32[]{:S(2)}) %collective-permute-start.12) | collective-permute-done | bytes 307232 | tf_op jit(solution)/shard_map/ppermute | solution.py:55
  76.1 1.8 constant_dynamic-update-slice_fusion.11
  77.9 2.2 %convolution_convert_fusion.4 = bf16[512,320]{0,1:T(8,128)(2,1)S(1)} fusion(bf16[512,1280]{1,0:T(8,128)(2,1)} %constant_dynamic-update-slice_fusion.19, bf16[3,1280,320]{2,1,0:T(8,128)(2,1)} %constant_dynamic-update-slice_fusion.11), kind=kOutput, calls=%fused_computation.20 | convolution fusion | flops 419594240 | bytes 2621440 | tf_op jit(solution)/shard_map/dot_general | solution.py:135
  80.1 2.2 %convolution_convert_fusion.3 = bf16[512,320]{0,1:T(8,128)(2,1)S(1)} fusion(bf16[512,1280]{1,0:T(8,128)(2,1)} %constant_dynamic-update-slice_fusion.19, bf16[3,1280,320]{2,1,0:T(8,128)(2,1)} %constant_dynamic-update-slice_fusion.11), kind=kOutput, calls=%fused_computation.19 | convolution fusion | flops 419594240 | bytes 2621440 | tf_op jit(solution)/shard_map/dot_general | solution.py:135
  82.4 2.2 %convolution_convert_fusion.2 = bf16[512,320]{0,1:T(8,128)(2,1)S(1)} fusion(bf16[512,1280]{1,0:T(8,128)(2,1)} %constant_dynamic-update-slice_fusion.19, bf16[3,1280,320]{2,1,0:T(8,128)(2,1)} %constant_dynamic-update-slice_fusion.11), kind=kOutput, calls=%fused_computation.18 | convolution fusion | flops 419594240 | bytes 2621440 | tf_op jit(solution)/shard_map/dot_general | solution.py:135
  91.8 3.2 %dynamic_update_slice.117 = bf16[1280,320]{0,1:T(8,128)(2,1)} dynamic-update-slice(bf16[1280,320]{0,1:T(8,128)(2,1)} %dynamic_update_slice.116, bf16[320,320]{0,1:T(8,128)(2,1)} %copy-done.7, s32[]{:T(128)S(6)} %select_n.181, s32[]{:T(128)} %constant.137.clone.1) | dynamic-update-slice | bytes 409604 | tf_op jit(solution)/shard_map/dynamic_update_slice | solution.py:75
  95.1 2.2 %fusion.13 = bf16[10,4,8,128]{3,2,1,0:T(8,128)(2,1)} fusion(f32[512,512]{0,1:T(8,128)} %copy-done.5, f32[512]{0:T(512)S(1)} %get-tuple-element.24, bf16[512,320]{0,1:T(8,128)(2,1)} %copy-done.10, f32[512]{0:T(512)S(1)} %fusion.14), kind=kOutput, calls=%fused_computation.32 | convolution fusion | flops 42549248 | bytes 1216512 | tf_op jit(solution)/shard_map/dot_general | solution.py:41
  98.3 3.8 %dynamic_update_slice.118 = bf16[1280,320]{0,1:T(8,128)(2,1)} dynamic-update-slice(bf16[1280,320]{0,1:T(8,128)(2,1)} %dynamic_update_slice.117, bf16[320,320]{0,1:T(8,128)(2,1)} %collective-permute-done.15, s32[]{:T(128)S(6)} %select_n.182, s32[]{:T(128)} %constant.137.clone.1) | dynamic-update-slice | bytes 409604 | tf_op jit(solution)/shard_map/dynamic_update_slice | solution.py:75
  103.6 6.1 %collective-permute-done.16 = bf16[320,320]{0,1:T(8,128)(2,1)} collective-permute-done((bf16[320,320]{0,1:T(8,128)(2,1)S(1)}, bf16[320,320]{0,1:T(8,128)(2,1)}, u32[]{:S(2)}, u32[]{:S(2)}) %collective-permute-start.16) | collective-permute-done | bytes 204832 | tf_op jit(solution)/shard_map/ppermute | solution.py:60
  109.7 3.4 %dynamic_update_slice.119 = bf16[1280,320]{0,1:T(8,128)(2,1)} dynamic-update-slice(bf16[1280,320]{0,1:T(8,128)(2,1)} %dynamic_update_slice.118, bf16[320,320]{0,1:T(8,128)(2,1)} %collective-permute-done.16, s32[]{:T(128)S(6)} %select_n.183, s32[]{:T(128)} %constant.137.clone.1) | dynamic-update-slice | bytes 409604 | tf_op jit(solution)/shard_map/dynamic_update_slice | solution.py:75
  127.0 8.3 %collective-permute-done.30 = bf16[160,1280]{1,0:T(8,128)(2,1)S(1)} collective-permute-done((bf16[160,1280]{1,0:T(8,128)(2,1)}, bf16[160,1280]{1,0:T(8,128)(2,1)S(1)}, u32[]{:S(2)}, u32[]{:S(2)}) %collective-permute-start.30) | collective-permute-done | bytes 409632 | tf_op jit(solution)/shard_map/ppermute | solution.py:55
  136.0 8.2 %collective-permute-done.31 = bf16[160,1280]{1,0:T(8,128)(2,1)S(1)} collective-permute-done((bf16[160,1280]{1,0:T(8,128)(2,1)}, bf16[160,1280]{1,0:T(8,128)(2,1)S(1)}, u32[]{:S(2)}, u32[]{:S(2)}) %collective-permute-start.31) | collective-permute-done | bytes 409632 | tf_op jit(solution)/shard_map/ppermute | solution.py:55
  144.2 8.1 %collective-permute-done.32 = bf16[160,1280]{1,0:T(8,128)(2,1)S(1)} collective-permute-done((bf16[160,1280]{1,0:T(8,128)(2,1)}, bf16[160,1280]{1,0:T(8,128)(2,1)S(1)}, u32[]{:S(2)}, u32[]{:S(2)}) %collective-permute-start.32) | collective-permute-done | bytes 409632 | tf_op jit(solution)/shard_map/ppermute | solution.py:55
  154.3 5.1 %collective-permute-done.19 = bf16[128,320]{0,1:T(8,128)(2,1)S(1)} collective-permute-done((bf16[128,320]{0,1:T(8,128)(2,1)S(1)}, bf16[128,320]{0,1:T(8,128)(2,1)S(1)}, u32[]{:S(2)}, u32[]{:S(2)}) %collective-permute-start.19) | collective-permute-done | bytes 81952 | tf_op jit(solution)/shard_map/ppermute | solution.py:55
  164.1 2.5 %gather.7 = bf16[32,8,4,160]{3,2,1,0:T(4,128)(2,1)} reshape(bf16[128,1280]{1,0:T(8,128)(2,1)} %gather_fusion) | data formatting | bytes 655360 | tf_op jit(solution)/shard_map/jit(_take)/gather | solution.py:154
  166.6 2.0 fusion.31
  168.6 2.3 %reshape.111 = bf16[4,32,1280]{2,1,0:T(8,128)(2,1)} reshape(bf16[4,32,8,160]{3,2,1,0:T(8,128)(2,1)} %fusion.31) | data formatting | bytes 655360 | tf_op jit(solution)/shard_map/reshape | solution.py:157
  174.7 2.2 %collective-permute-done.24 = bf16[32,1280]{1,0:T(8,128)(2,1)S(1)} collective-permute-done((bf16[32,1280]{1,0:T(8,128)(2,1)S(1)}, bf16[32,1280]{1,0:T(8,128)(2,1)S(1)}, u32[]{:S(2)}, u32[]{:S(2)}) %collective-permute-start.24) | collective-permute-done | bytes 81952 | tf_op jit(solution)/shard_map/ppermute | solution.py:55
  181.0 3.4 %collective-permute-done.34 = bf16[32,1280]{1,0:T(8,128)(2,1)S(1)} collective-permute-done((bf16[32,1280]{1,0:T(8,128)(2,1)S(1)}, bf16[32,1280]{1,0:T(8,128)(2,1)S(1)}, u32[]{:S(2)}, u32[]{:S(2)}) %collective-permute-start.34) | collective-permute-done | bytes 81952 | tf_op jit(solution)/shard_map/ppermute | solution.py:55
  185.5 10.9 %all_to_all.5 = bf16[8,8,1280]{2,1,0:T(8,128)(2,1)S(1)} all-to-all(bf16[8,8,1280]{2,1,0:T(8,128)(2,1)S(1)} %fusion.5), channel_id=1, replica_groups=mesh['dp'=8,'fsdp'=4] {'dp'}, dimensions={0} | all-to-all | bytes 327680 | tf_op jit(solution)/shard_map/all_to_all | solution.py:192
  (160 shorter events, 77.6 us)
Async XLA Ops:
  0.0 28.1 %collective-permute-start.6 = (bf16[3,160,320]{2,1,0:T(8,128)(2,1)}, bf16[3,160,320]{2,1,0:T(8,128)(2,1)}, u32[]{:S(2)}, u32[]{:S(2)}) collective-permute-start(bf16[3,160,320]{2,1,0:T(8,128)(2,1)} %param.9), channel_id=1, source_target_pairs={{0,8},{4,12},{8,16},{12,20},{16,24},{20,28},{24,0},{28,4},{1,9},{5... | collective-permute-start | bytes 921608 | tf_op jit(solution)/shard_map/ppermute | solution.py:60
  3.0 26.5 %collective-permute-start.7 = (bf16[3,160,320]{2,1,0:T(8,128)(2,1)}, bf16[3,160,320]{2,1,0:T(8,128)(2,1)}, u32[]{:S(2)}, u32[]{:S(2)}) collective-permute-start(bf16[3,160,320]{2,1,0:T(8,128)(2,1)} %param.9), channel_id=1, source_target_pairs={{0,24},{4,28},{8,0},{12,4},{16,8},{20,12},{24,16},{28,20},{1,25},{... | collective-permute-start | bytes 921608 | tf_op jit(solution)/shard_map/ppermute | solution.py:60
  5.1 32.6 %collective-permute-start.8 = (bf16[3,160,320]{2,1,0:T(8,128)(2,1)}, bf16[3,160,320]{2,1,0:T(8,128)(2,1)}, u32[]{:S(2)}, u32[]{:S(2)}) collective-permute-start(bf16[3,160,320]{2,1,0:T(8,128)(2,1)} %param.9), channel_id=1, source_target_pairs={{0,16},{4,20},{8,24},{12,28},{16,0},{20,4},{24,8},{28,12},{1,17},{... | collective-permute-start | bytes 921608 | tf_op jit(solution)/shard_map/ppermute | solution.py:60
  6.1 34.7 %collective-permute-start.9 = (bf16[3,160,320]{2,1,0:T(8,128)(2,1)}, bf16[3,160,320]{2,1,0:T(8,128)(2,1)}, u32[]{:S(2)}, u32[]{:S(2)}) collective-permute-start(bf16[3,160,320]{2,1,0:T(8,128)(2,1)} %param.9), channel_id=1, source_target_pairs={{0,4},{4,0},{8,12},{12,8},{16,20},{20,16},{24,28},{28,24},{1,5},{5... | collective-permute-start | bytes 921608 | tf_op jit(solution)/shard_map/ppermute | solution.py:55
  7.6 13.7 %collective-permute-start = (s32[1,128]{1,0:T(1,128)}, s32[1,128]{1,0:T(1,128)S(1)}, u32[]{:S(2)}, u32[]{:S(2)}) collective-permute-start(s32[1,128]{1,0:T(1,128)} %param.13), channel_id=1, source_target_pairs={{0,1},{1,0},{2,3},{3,2},{4,5},{5,4},{6,7},{7,6},{8,9},{9,8},{10,11... | collective-permute-start | bytes 1544 | tf_op jit(solution)/shard_map/ppermute | solution.py:55
  27.8 18.7 %collective-permute-start.3 = (bf16[128,1280]{1,0:T(8,128)(2,1)}, bf16[128,1280]{1,0:T(8,128)(2,1)S(1)}, u32[]{:S(2)}, u32[]{:S(2)}) collective-permute-start(bf16[128,1280]{1,0:T(8,128)(2,1)} %get-tuple-element.12), channel_id=1, source_target_pairs={{0,1},{1,0},{2,3},{3,2},{4,5},{5,4},{6,7},{7,6},{8,9},{9,8},{10,11... | collective-permute-start | bytes 983048 | tf_op jit(solution)/shard_map/ppermute | solution.py:55
  28.2 20.5 %collective-permute-start.4 = (bf16[128,1280]{1,0:T(8,128)(2,1)}, bf16[128,1280]{1,0:T(8,128)(2,1)S(1)}, u32[]{:S(2)}, u32[]{:S(2)}) collective-permute-start(bf16[128,1280]{1,0:T(8,128)(2,1)} %get-tuple-element.12), channel_id=1, source_target_pairs={{0,2},{1,3},{2,0},{3,1},{4,6},{5,7},{6,4},{7,5},{8,10},{9,11},{10,... | collective-permute-start | bytes 983048 | tf_op jit(solution)/shard_map/ppermute | solution.py:55
  29.6 20.4 %collective-permute-start.5 = (bf16[128,1280]{1,0:T(8,128)(2,1)}, bf16[128,1280]{1,0:T(8,128)(2,1)S(1)}, u32[]{:S(2)}, u32[]{:S(2)}) collective-permute-start(bf16[128,1280]{1,0:T(8,128)(2,1)} %get-tuple-element.12), channel_id=1, source_target_pairs={{0,3},{1,2},{2,1},{3,0},{4,7},{5,6},{6,5},{7,4},{8,11},{9,10},{10,... | collective-permute-start | bytes 983048 | tf_op jit(solution)/shard_map/ppermute | solution.py:55
  37.7 81.0 %collective-permute-start.26 = (bf16[160,1280]{1,0:T(8,128)(2,1)}, bf16[160,1280]{1,0:T(8,128)(2,1)}, u32[]{:S(2)}, u32[]{:S(2)}) collective-permute-start(bf16[160,1280]{1,0:T(8,128)(2,1)} %param.11), channel_id=1, source_target_pairs={{0,8},{4,12},{8,16},{12,20},{16,24},{20,28},{24,0},{28,4},{1,9},{5... | collective-permute-start | bytes 1228808 | tf_op jit(solution)/shard_map/ppermute | solution.py:60
  40.8 80.5 %collective-permute-start.27 = (bf16[160,1280]{1,0:T(8,128)(2,1)}, bf16[160,1280]{1,0:T(8,128)(2,1)}, u32[]{:S(2)}, u32[]{:S(2)}) collective-permute-start(bf16[160,1280]{1,0:T(8,128)(2,1)} %param.11), channel_id=1, source_target_pairs={{0,24},{4,28},{8,0},{12,4},{16,8},{20,12},{24,16},{28,20},{1,25},{... | collective-permute-start | bytes 1228808 | tf_op jit(solution)/shard_map/ppermute | solution.py:60
  46.5 7.0 %collective-permute-start.13 = (bf16[160,320]{0,1:T(8,128)(2,1)S(1)}, bf16[160,320]{0,1:T(8,128)(2,1)S(1)}, u32[]{:S(2)}, u32[]{:S(2)}) collective-permute-start(bf16[160,320]{0,1:T(8,128)(2,1)S(1)} %bitcast.96), channel_id=1, source_target_pairs={{0,4},{4,0},{8,12},{12,8},{16,20},{20,16},{24,28},{28,24},{1,5},{5... | collective-permute-start | bytes 307208 | tf_op jit(solution)/shard_map/ppermute | solution.py:55
  48.7 12.8 %collective-permute-start.10 = (bf16[3,160,320]{2,1,0:T(8,128)(2,1)}, bf16[3,160,320]{2,1,0:T(8,128)(2,1)}, u32[]{:S(2)}, u32[]{:S(2)}) collective-permute-start(bf16[3,160,320]{2,1,0:T(8,128)(2,1)} %collective-permute-done.6), channel_id=1, source_target_pairs={{0,4},{4,0},{8,12},{12,8},{16,20},{20,16},{24,28},{28,24},{1,5},{5... | collective-permute-start | bytes 921608 | tf_op jit(solution)/shard_map/ppermute | solution.py:55
  50.0 19.4 %collective-permute-start.11 = (bf16[3,160,320]{2,1,0:T(8,128)(2,1)}, bf16[3,160,320]{2,1,0:T(8,128)(2,1)}, u32[]{:S(2)}, u32[]{:S(2)}) collective-permute-start(bf16[3,160,320]{2,1,0:T(8,128)(2,1)} %collective-permute-done.7), channel_id=1, source_target_pairs={{0,4},{4,0},{8,12},{12,8},{16,20},{20,16},{24,28},{28,24},{1,5},{5... | collective-permute-start | bytes 921608 | tf_op jit(solution)/shard_map/ppermute | solution.py:55
  53.4 22.4 %collective-permute-start.12 = (bf16[3,160,320]{2,1,0:T(8,128)(2,1)}, bf16[3,160,320]{2,1,0:T(8,128)(2,1)}, u32[]{:S(2)}, u32[]{:S(2)}) collective-permute-start(bf16[3,160,320]{2,1,0:T(8,128)(2,1)} %collective-permute-done.8), channel_id=1, source_target_pairs={{0,4},{4,0},{8,12},{12,8},{16,20},{20,16},{24,28},{28,24},{1,5},{5... | collective-permute-start | bytes 921608 | tf_op jit(solution)/shard_map/ppermute | solution.py:55
  61.4 61.3 %collective-permute-start.28 = (bf16[160,1280]{1,0:T(8,128)(2,1)}, bf16[160,1280]{1,0:T(8,128)(2,1)}, u32[]{:S(2)}, u32[]{:S(2)}) collective-permute-start(bf16[160,1280]{1,0:T(8,128)(2,1)} %param.11), channel_id=1, source_target_pairs={{0,16},{4,20},{8,24},{12,28},{16,0},{20,4},{24,8},{28,12},{1,17},{... | collective-permute-start | bytes 1228808 | tf_op jit(solution)/shard_map/ppermute | solution.py:60
  69.3 20.4 %collective-permute-start.14 = (bf16[320,320]{0,1:T(8,128)(2,1)S(1)}, bf16[320,320]{0,1:T(8,128)(2,1)S(1)}, u32[]{:S(2)}, u32[]{:S(2)}) collective-permute-start(bf16[320,320]{0,1:T(8,128)(2,1)S(1)} %pad_maximum_fusion), channel_id=1, source_target_pairs={{0,8},{4,12},{8,16},{12,20},{16,24},{20,28},{24,0},{28,4},{1,9},{5... | collective-permute-start | bytes 614408 | tf_op jit(solution)/shard_map/ppermute | solution.py:60
  75.8 21.4 %collective-permute-start.15 = (bf16[320,320]{0,1:T(8,128)(2,1)S(1)}, bf16[320,320]{0,1:T(8,128)(2,1)}, u32[]{:S(2)}, u32[]{:S(2)}) collective-permute-start(bf16[320,320]{0,1:T(8,128)(2,1)S(1)} %pad_maximum_fusion), channel_id=1, source_target_pairs={{0,24},{4,28},{8,0},{12,4},{16,8},{20,12},{24,16},{28,20},{1,25},{... | collective-permute-start | bytes 614408 | tf_op jit(solution)/shard_map/ppermute | solution.py:60
  90.4 34.1 %collective-permute-start.29 = (bf16[160,1280]{1,0:T(8,128)(2,1)}, bf16[160,1280]{1,0:T(8,128)(2,1)}, u32[]{:S(2)}, u32[]{:S(2)}) collective-permute-start(bf16[160,1280]{1,0:T(8,128)(2,1)} %param.11), channel_id=1, source_target_pairs={{0,4},{4,0},{8,12},{12,8},{16,20},{20,16},{24,28},{28,24},{1,5},{5... | collective-permute-start | bytes 1228808 | tf_op jit(solution)/shard_map/ppermute | solution.py:55
  97.3 12.4 %collective-permute-start.16 = (bf16[320,320]{0,1:T(8,128)(2,1)S(1)}, bf16[320,320]{0,1:T(8,128)(2,1)}, u32[]{:S(2)}, u32[]{:S(2)}) collective-permute-start(bf16[320,320]{0,1:T(8,128)(2,1)S(1)} %pad_maximum_fusion), channel_id=1, source_target_pairs={{0,16},{4,20},{8,24},{12,28},{16,0},{20,4},{24,8},{28,12},{1,17},{... | collective-permute-start | bytes 614408 | tf_op jit(solution)/shard_map/ppermute | solution.py:60
  113.1 40.8 %collective-permute-start.18 = (bf16[1280,320]{0,1:T(8,128)(2,1)}, bf16[1280,320]{0,1:T(8,128)(2,1)S(1)}, u32[]{:S(2)}, u32[]{:S(2)}) collective-permute-start(bf16[1280,320]{0,1:T(8,128)(2,1)} %dynamic_update_slice.119), channel_id=1, source_target_pairs={{0,1},{1,0},{2,3},{3,2},{4,5},{5,4},{6,7},{7,6},{8,9},{9,8},{10,11... | collective-permute-start | bytes 2457608 | tf_op jit(solution)/shard_map/ppermute | solution.py:55
  118.7 40.6 %collective-permute-start.20 = (bf16[1280,320]{0,1:T(8,128)(2,1)}, bf16[1280,320]{0,1:T(8,128)(2,1)S(1)}, u32[]{:S(2)}, u32[]{:S(2)}) collective-permute-start(bf16[1280,320]{0,1:T(8,128)(2,1)} %dynamic_update_slice.119), channel_id=1, source_target_pairs={{0,2},{1,3},{2,0},{3,1},{4,6},{5,7},{6,4},{7,5},{8,10},{9,11},{10,... | collective-permute-start | bytes 2457608 | tf_op jit(solution)/shard_map/ppermute | solution.py:55
  121.3 39.0 %collective-permute-start.22 = (bf16[1280,320]{0,1:T(8,128)(2,1)}, bf16[1280,320]{0,1:T(8,128)(2,1)S(1)}, u32[]{:S(2)}, u32[]{:S(2)}) collective-permute-start(bf16[1280,320]{0,1:T(8,128)(2,1)} %dynamic_update_slice.119), channel_id=1, source_target_pairs={{0,3},{1,2},{2,1},{3,0},{4,7},{5,6},{6,5},{7,4},{8,11},{9,10},{10,... | collective-permute-start | bytes 2457608 | tf_op jit(solution)/shard_map/ppermute | solution.py:55
  122.8 12.6 %collective-permute-start.30 = (bf16[160,1280]{1,0:T(8,128)(2,1)}, bf16[160,1280]{1,0:T(8,128)(2,1)S(1)}, u32[]{:S(2)}, u32[]{:S(2)}) collective-permute-start(bf16[160,1280]{1,0:T(8,128)(2,1)} %collective-permute-done.26), channel_id=1, source_target_pairs={{0,4},{4,0},{8,12},{12,8},{16,20},{20,16},{24,28},{28,24},{1,5},{5... | collective-permute-start | bytes 1228808 | tf_op jit(solution)/shard_map/ppermute | solution.py:55
  124.5 19.6 %collective-permute-start.31 = (bf16[160,1280]{1,0:T(8,128)(2,1)}, bf16[160,1280]{1,0:T(8,128)(2,1)S(1)}, u32[]{:S(2)}, u32[]{:S(2)}) collective-permute-start(bf16[160,1280]{1,0:T(8,128)(2,1)} %collective-permute-done.27), channel_id=1, source_target_pairs={{0,4},{4,0},{8,12},{12,8},{16,20},{20,16},{24,28},{28,24},{1,5},{5... | collective-permute-start | bytes 1228808 | tf_op jit(solution)/shard_map/ppermute | solution.py:55
  135.4 16.9 %collective-permute-start.32 = (bf16[160,1280]{1,0:T(8,128)(2,1)}, bf16[160,1280]{1,0:T(8,128)(2,1)S(1)}, u32[]{:S(2)}, u32[]{:S(2)}) collective-permute-start(bf16[160,1280]{1,0:T(8,128)(2,1)} %collective-permute-done.28), channel_id=1, source_target_pairs={{0,4},{4,0},{8,12},{12,8},{16,20},{20,16},{24,28},{28,24},{1,5},{5... | collective-permute-start | bytes 1228808 | tf_op jit(solution)/shard_map/ppermute | solution.py:55
  144.1 9.7 %collective-permute-start.17 = (bf16[128,320]{0,1:T(8,128)(2,1)S(1)}, bf16[128,320]{0,1:T(8,128)(2,1)S(1)}, u32[]{:S(2)}, u32[]{:S(2)}) collective-permute-start(bf16[128,320]{0,1:T(8,128)(2,1)S(1)} %get-tuple-element.19), channel_id=1, source_target_pairs={{0,1},{1,0},{2,3},{3,2},{4,5},{5,4},{6,7},{7,6},{8,9},{9,8},{10,11... | collective-permute-start | bytes 245768 | tf_op jit(solution)/shard_map/ppermute | solution.py:55
  152.3 7.1 %collective-permute-start.19 = (bf16[128,320]{0,1:T(8,128)(2,1)S(1)}, bf16[128,320]{0,1:T(8,128)(2,1)S(1)}, u32[]{:S(2)}, u32[]{:S(2)}) collective-permute-start(bf16[128,320]{0,1:T(8,128)(2,1)S(1)} %get-tuple-element.21), channel_id=1, source_target_pairs={{0,2},{1,3},{2,0},{3,1},{4,6},{5,7},{6,4},{7,5},{8,10},{9,11},{10,... | collective-permute-start | bytes 245768 | tf_op jit(solution)/shard_map/ppermute | solution.py:55
  153.8 6.5 %collective-permute-start.21 = (bf16[128,320]{0,1:T(8,128)(2,1)S(1)}, bf16[128,320]{0,1:T(8,128)(2,1)S(1)}, u32[]{:S(2)}, u32[]{:S(2)}) collective-permute-start(bf16[128,320]{0,1:T(8,128)(2,1)S(1)} %get-tuple-element.20), channel_id=1, source_target_pairs={{0,3},{1,2},{2,1},{3,0},{4,7},{5,6},{6,5},{7,4},{8,11},{9,10},{10,... | collective-permute-start | bytes 245768 | tf_op jit(solution)/shard_map/ppermute | solution.py:55
  172.1 4.8 %collective-permute-start.24 = (bf16[32,1280]{1,0:T(8,128)(2,1)S(1)}, bf16[32,1280]{1,0:T(8,128)(2,1)S(1)}, u32[]{:S(2)}, u32[]{:S(2)}) collective-permute-start(bf16[32,1280]{1,0:T(8,128)(2,1)S(1)} %get-tuple-element.17), channel_id=1, source_target_pairs={{0,2},{1,3},{2,0},{3,1},{4,6},{5,7},{6,4},{7,5},{8,10},{9,11},{10,... | collective-permute-start | bytes 245768 | tf_op jit(solution)/shard_map/ppermute | solution.py:55
  173.6 4.7 %collective-permute-start.25 = (bf16[32,1280]{1,0:T(8,128)(2,1)S(1)}, bf16[32,1280]{1,0:T(8,128)(2,1)S(1)}, u32[]{:S(2)}, u32[]{:S(2)}) collective-permute-start(bf16[32,1280]{1,0:T(8,128)(2,1)S(1)} %get-tuple-element.16), channel_id=1, source_target_pairs={{0,3},{1,2},{2,1},{3,0},{4,7},{5,6},{6,5},{7,4},{8,11},{9,10},{10,... | collective-permute-start | bytes 245768 | tf_op jit(solution)/shard_map/ppermute | solution.py:55
  179.2 5.2 %collective-permute-start.34 = (bf16[32,1280]{1,0:T(8,128)(2,1)S(1)}, bf16[32,1280]{1,0:T(8,128)(2,1)S(1)}, u32[]{:S(2)}, u32[]{:S(2)}) collective-permute-start(bf16[32,1280]{1,0:T(8,128)(2,1)S(1)} %get-tuple-element.15), channel_id=1, source_target_pairs={{0,2},{1,3},{2,0},{3,1},{4,6},{5,7},{6,4},{7,5},{8,10},{9,11},{10,... | collective-permute-start | bytes 245768 | tf_op jit(solution)/shard_map/ppermute | solution.py:55
  180.6 4.7 %collective-permute-start.35 = (bf16[32,1280]{1,0:T(8,128)(2,1)S(1)}, bf16[32,1280]{1,0:T(8,128)(2,1)S(1)}, u32[]{:S(2)}, u32[]{:S(2)}) collective-permute-start(bf16[32,1280]{1,0:T(8,128)(2,1)S(1)} %get-tuple-element.14), channel_id=1, source_target_pairs={{0,3},{1,2},{2,1},{3,0},{4,7},{5,6},{6,5},{7,4},{8,11},{9,10},{10,... | collective-permute-start | bytes 245768 | tf_op jit(solution)/shard_map/ppermute | solution.py:55
  (15 other events, 132.9 us)

commit v2 on v0

--- a/solution.py
+++ b/solution.py
@@ -1,8 +1,11 @@
+import functools
 import math
 
 import jax
 import jax.numpy as jnp
 from jax import lax
+from jax.experimental import pallas as pl
+from jax.experimental.pallas import tpu as pltpu
 from jax.sharding import PartitionSpec as P
 
 HD = 80
@@ -47,26 +50,26 @@
     return jnp.concatenate(pieces, axis=1).astype(jnp.bfloat16)
 
 
-def per_device(
+def slot_numbers(targets, capacity):
+    n = targets.shape[0]
+    same = targets[:, None] == targets[None, :]
+    before = jnp.arange(n)[None, :] < jnp.arange(n)[:, None]
+    return targets * capacity, jnp.sum((same & before).astype(jnp.int32), axis=1)
+
+
+def by_gathers(
     tokens, qkv_weight, out_weight, merge_weight, ln_gains, segments, merge_rows, owners
 ):
     n_dp = lax.axis_size("dp")
-    n_fsdp = lax.axis_size("fsdp")
     qkv_mine = lax.all_gather(qkv_weight, "dp", axis=1, tiled=True)
     out_mine = lax.all_gather(out_weight, "dp", axis=1, tiled=True)
+    n_fsdp = lax.axis_size("fsdp")
     normed = normalize(tokens, ln_gains[0])
-    group_normed, group_segs = (
-        lax.all_gather(normed, "fsdp", axis=0, tiled=True),
-        lax.all_gather(segments, "fsdp", axis=1, tiled=True),
-    )
-    queries = jnp.dot(group_normed, qkv_mine[0], preferred_element_type=jnp.float32).astype(
-        jnp.bfloat16
-    )
-    keys_all = jnp.dot(group_normed, qkv_mine[1], preferred_element_type=jnp.float32).astype(
-        jnp.bfloat16
-    )
-    values_all = jnp.dot(group_normed, qkv_mine[2], preferred_element_type=jnp.float32).astype(
-        jnp.bfloat16
+    group_normed = lax.all_gather(normed, "fsdp", axis=0, tiled=True)
+    group_segs = lax.all_gather(segments, "fsdp", axis=1, tiled=True)
+    queries, keys_all, values_all = (
+        jnp.dot(group_normed, qkv_mine[n], preferred_element_type=jnp.float32).astype(jnp.bfloat16)
+        for n in range(3)
     )
     attended_mine = attend(queries, keys_all, values_all, group_segs[0], group_segs[0])
     attended_local = lax.all_to_all(attended_mine, "fsdp", split_axis=0, concat_axis=1, tiled=True)
@@ -90,23 +93,300 @@
         tiled=True,
     )
     capacity = max(2, (2 * merge_count + n_dp - 1) // n_dp)
-    targets = owners[:, 0]
-    onehot = (targets[:, None] == jnp.arange(n_dp, dtype=jnp.int32)[None, :]).astype(jnp.int32)
-    earlier = jnp.cumsum(onehot, axis=0) - onehot
-    position = jnp.sum(earlier * onehot, axis=1)
-    slot_index = targets * capacity + position
-    placing = (jnp.arange(n_dp * capacity, dtype=jnp.int32)[:, None] == slot_index[None, :]).astype(
-        jnp.bfloat16
-    )
+    first, rank = slot_numbers(owners[:, 0], capacity)
+    placing = (
+        jnp.arange(n_dp * capacity, dtype=jnp.int32)[:, None] == (first + rank)[None, :]
+    ).astype(jnp.bfloat16)
     packed = jnp.dot(placing, merged, preferred_element_type=jnp.float32).astype(jnp.bfloat16)
     packed = packed.reshape(n_dp, capacity, merged.shape[1])
     arrived = lax.all_to_all(packed, "dp", split_axis=0, concat_axis=0, tiled=True)
     return arrived.reshape(n_dp * capacity, merged.shape[1])
 
 
+def swap(value, axis, k):
+    return lax.ppermute(value, axis, [(i, i ^ k) for i in range(lax.axis_size(axis))])
+
+
+def turn(value, k):
+    n = lax.axis_size("dp")
+    return lax.ppermute(value, "dp", [(i, (i + 2 * k) % n) for i in range(n)])
+
+
+def across(value, k):
+    n_dp, n_fsdp = lax.axis_size("dp"), lax.axis_size("fsdp")
+    pairs = [
+        (i * n_fsdp + j, (i ^ 1) * n_fsdp + (j ^ k)) for i in range(n_dp) for j in range(n_fsdp)
+    ]
+    return lax.ppermute(value, ("dp", "fsdp"), pairs)
+
+
+def after(value, other):
+    return lax.optimization_barrier((value, other))[0]
+
+
+ROUNDS = (1, 3, 2)
+ORDER = (0, 1, 3, 2)
+
+
+def dot(a, b):
+    return jnp.dot(a, b, preferred_element_type=jnp.float32)
+
+
+def dot_turned(a, b):
+    return lax.dot_general(a, b, (((1,), (1,)), ((), ())), preferred_element_type=jnp.float32)
+
+
+def call(kernel, outs, operands, scratch=(), flops=0, smem=0, exps=0):
+    moved = sum(math.prod(x.shape) * x.dtype.itemsize for x in (*operands, *outs))
+    specs = [pl.BlockSpec(memory_space=pltpu.SMEM)] * smem
+    specs += [pl.BlockSpec(memory_space=pltpu.VMEM)] * (len(operands) - smem)
+    return pl.pallas_call(
+        kernel,
+        out_shape=tuple(outs),
+        in_specs=specs,
+        out_specs=tuple(pl.BlockSpec(memory_space=pltpu.VMEM) for _ in outs),
+        scratch_shapes=list(scratch),
+        compiler_params=pltpu.CompilerParams(vmem_limit_bytes=40 * 1024 * 1024),
+        cost_estimate=pl.CostEstimate(
+            flops=flops, bytes_accessed=moved, transcendentals=exps
+        ),
+    )(*operands)
+
+
+def norm_kernel(tokens_ref, gains_ref, segs_ref, out_ref):
+    rows = tokens_ref.shape[0]
+    out_ref[0:rows, :] = normalize(tokens_ref[...], gains_ref[0:1, :])
+    out_ref[rows:, :] = jnp.zeros((out_ref.shape[0] - rows, out_ref.shape[1]), out_ref.dtype)
+    out_ref[rows:, 0:rows] = jnp.broadcast_to(
+        segs_ref[...].astype(jnp.float32), (out_ref.shape[0] - rows, rows)
+    ).astype(out_ref.dtype)
+
+
+def block_index(me, number, n_dp):
+    mine = lax.rem(me + n_dp - 2 * ORDER[number % 4], n_dp)
+    return mine if number < 4 else mine ^ 1
+
+
+def lay_out(me, blocks, part, whole):
+    step = blocks[0].shape[1]
+    for number, block in enumerate(blocks):
+        start = pl.multiple_of(block_index(me, number, len(blocks)) * step, 32)
+        whole[pl.ds(start, step), :] = block[part]
+
+
+def score_kernel(me_ref, *refs):
+    tokens, blocks = refs[0:4], refs[4:12]
+    rows_ref, weights_ref, totals_ref, q_whole, k_whole = refs[12:]
+    rows = tokens[0].shape[0] - 16
+    for n in range(4):
+        rows_ref[n * rows : (n + 1) * rows, :] = tokens[n][0:rows, :]
+    lay_out(me_ref[0], blocks, 0, q_whole)
+    lay_out(me_ref[0], blocks, 1, k_whole)
+    queries = dot(rows_ref[...], q_whole[...]).astype(jnp.bfloat16)
+    keys = dot(rows_ref[...], k_whole[...]).astype(jnp.bfloat16)
+    in_row = [t[rows : rows + 16, 0:rows].astype(jnp.float32)[0:1, :] for t in tokens]
+    in_col = [jnp.broadcast_to(s, (rows, rows)).T[:, 0:1] for s in in_row]
+    allowed = jnp.concatenate(in_col, axis=0) == jnp.concatenate(in_row, axis=1)
+    factor = 1.0 / math.sqrt(HD)
+    for head in range(queries.shape[1] // HD):
+        cols = slice(head * HD, (head + 1) * HD)
+        scores = dot_turned(queries[:, cols], keys[:, cols]) * factor
+        masked = jnp.where(allowed, scores, -jnp.inf)
+        weights = jnp.exp(masked - jnp.max(masked, axis=1, keepdims=True))
+        weights_ref[head] = weights.astype(jnp.bfloat16)
+        totals_ref[head] = jnp.sum(weights, axis=1, keepdims=True)
+
+
+def value_kernel(me_ref, *refs):
+    rows_ref, weights_ref, totals_ref = refs[0:3]
+    blocks = refs[3:11]
+    keep_ref, send_ref, v_whole, out_whole = refs[11:]
+    lay_out(me_ref[0], blocks, 0, v_whole)
+    lay_out(me_ref[0], blocks, 1, out_whole)
+    values = dot(rows_ref[...], v_whole[...]).astype(jnp.bfloat16)
+    pieces = []
+    for head in range(values.shape[1] // HD):
+        found = dot(weights_ref[head], values[:, head * HD : (head + 1) * HD])
+        pieces.append(found / totals_ref[head])
+    attended = jnp.concatenate(pieces, axis=1).astype(jnp.bfloat16)
+    half = attended.shape[0] // 2
+    send_ref[...] = dot_turned(attended[half:, :], out_whole[...]).astype(jnp.bfloat16)
+    keep_ref[...] = dot_turned(attended[:half, :], out_whole[...])
+
+
+def pass_kernel(keep_ref, got_ref, out_ref):
+    rows = out_ref.shape[0]
+    out_ref[...] = (keep_ref[rows:, :] + got_ref[rows:, :].astype(jnp.float32)).astype(jnp.bfloat16)
+
+
+def layer_kernel(at_ref, tokens_ref, keep_ref, core_ref, chip_ref, gains_ref, order_ref, *refs):
+    outs, slices = refs[0:4], refs[4]
+    rows, width = tokens_ref.shape
+    summed = (
+        tokens_ref[...].astype(jnp.float32)
+        + keep_ref[0:rows, :]
+        + core_ref[0:rows, :].astype(jnp.float32)
+        + chip_ref[...].astype(jnp.float32)
+    )
+    merge_in = normalize(summed.astype(jnp.bfloat16), gains_ref[1:2, :])
+    places = lax.broadcasted_iota(jnp.int32, (rows, rows), 1)
+    picking = (order_ref[...] == places).astype(jnp.bfloat16)
+    ordered = dot(picking, merge_in).astype(jnp.bfloat16)
+    step, half = width // 8, width // 2
+    for n in range(4):
+        slices[n] = jnp.concatenate(
+            [
+                ordered[:, n * step : (n + 1) * step],
+                ordered[:, half + n * step : half + (n + 1) * step],
+            ],
+            axis=1,
+        )
+    for k in range(4):
+        outs[k][...] = slices[at_ref[0] ^ k]
+
+
+def merge_kernel(me_ref, *refs):
+    inputs, blocks = refs[0:8], refs[8:12]
+    keep_ref, sends = refs[12], refs[13:16]
+    count = inputs[0].shape[0] // 4
+    z, y = me_ref[0] // 2, lax.rem(me_ref[0], 2)
+    total = jnp.zeros((8 * count, blocks[0].shape[1]), jnp.float32)
+    for number, block in enumerate(blocks):
+        at = lax.rem(z + 4 - ORDER[number], 4) * count
+        at = pl.multiple_of(at, 32)
+        rows = jnp.concatenate([x[pl.ds(at, count), :] for x in inputs], axis=0)
+        step = block.shape[0] // 2
+        low = block[pl.ds(pl.multiple_of(y * step, 32), step), :]
+        high = block[pl.ds(pl.multiple_of((1 - y) * step, 32), step), :]
+        total = total + dot(rows, jnp.concatenate([low, high], axis=0))
+    for k in range(4):
+        share = jnp.concatenate(
+            [
+                total[k * count : (k + 1) * count, :],
+                total[(4 + k) * count : (5 + k) * count, :],
+            ],
+            axis=0,
+        )
+        if k == 0:
+            keep_ref[...] = share
+        else:
+            sends[k - 1][...] = share.astype(jnp.bfloat16)
+
+
+def pack_kernel(slots_ref, keep_ref, one_ref, two_ref, three_ref, out_ref):
+    total = keep_ref[...]
+    for got in (one_ref, two_ref, three_ref):
+        total = total + got[...].astype(jnp.float32)
+    shape = (out_ref.shape[0], total.shape[0])
+    placing = (lax.broadcasted_iota(jnp.int32, shape, 0) == slots_ref[...]).astype(jnp.bfloat16)
+    out_ref[...] = dot(placing, total.astype(jnp.bfloat16)).astype(jnp.bfloat16)
+
+
+def by_permutes(
+    tokens, qkv_weight, out_weight, merge_weight, ln_gains, segments, merge_rows, owners
+):
+    rows, width = tokens.shape
+    count = rows // 4
+    n_dp, n_fsdp = lax.axis_size("dp"), lax.axis_size("fsdp")
+    me, at = lax.axis_index("dp"), lax.axis_index("fsdp")
+    y = lax.rem(me, 2)
+    me_cell, at_cell = me.reshape(1), at.reshape(1)
+    bf16, f32 = jnp.bfloat16, jnp.float32
+    shape = jax.ShapeDtypeStruct
+    cols = qkv_weight.shape[2]
+    group = n_fsdp * rows
+
+    first = qkv_weight[0:2]
+    first_z = [turn(first, k) for k in ROUNDS]
+    first_y = [swap(first, "dp", 1)]
+    second = jnp.concatenate([qkv_weight[2:3], out_weight.T[None]], axis=0)
+    second_z = [turn(after(second, first_z[0]), k) for k in ROUNDS]
+    second_y = [swap(after(second, first_y[0]), "dp", 1)]
+    first_y += [swap(block, "dp", 1) for block in first_z]
+    second_y += [swap(block, "dp", 1) for block in second_z]
+    half = merge_weight.shape[1] // 2
+    low, high = merge_weight[:, :half], merge_weight[:, half:]
+    lower = y == 0
+    theirs = swap(after(jnp.where(lower, high, low), second_y[0]), "dp", 1)
+    pair = jnp.concatenate([jnp.where(lower, low, high), theirs], axis=0)
+    merge_blocks = [pair] + [turn(after(pair, second_z[2]), k) for k in ROUNDS]
+
+    capacity = max(2, (2 * count + n_dp - 1) // n_dp)
+    mine = owners[:, 0]
+    other = swap(owners, "dp", 1)[:, 0]
+    slots = []
+    for number, targets in enumerate((mine, other)):
+        start, rank = slot_numbers(targets, 2 * capacity)
+        slots.append(start + rank + (y ^ number) * capacity)
+    slots = jnp.concatenate(slots).reshape(1, 2 * count)
+    order = merge_rows.reshape(count, 4).T.reshape(rows, 1)
+
+    (normed,) = call(
+        norm_kernel, [shape((rows + 16, width), bf16)], [tokens, ln_gains, segments]
+    )
+    along_x = swap(normed, "fsdp", 2)
+    group_rows = [normed, along_x, swap(normed, "fsdp", 1), swap(along_x, "fsdp", 1)]
+
+    heads = cols // HD
+    group_all, weights, totals = call(
+        score_kernel,
+        [
+            shape((group, width), bf16),
+            shape((heads, group, group), bf16),
+            shape((heads, group, 1), f32),
+        ],
+        [me_cell, *group_rows, first, *first_z, *first_y],
+        [pltpu.VMEM((width, cols), bf16)] * 2,
+        flops=4 * group * width * cols + 2 * group * group * cols,
+        smem=1,
+        exps=heads * group * group,
+    )
+    keep, send = call(
+        value_kernel,
+        [shape((2 * rows, width), f32), shape((2 * rows, width), bf16)],
+        [me_cell, group_all, weights, totals, second, *second_z, *second_y],
+        [pltpu.VMEM((width, cols), bf16)] * 2,
+        flops=4 * group * width * cols + 2 * group * group * cols,
+        smem=1,
+    )
+    from_core = swap(send, "fsdp", 1)
+    (onward,) = call(pass_kernel, [shape((rows, width), bf16)], [keep, from_core])
+    from_chip = swap(onward, "fsdp", 2)
+    slices = call(
+        layer_kernel,
+        [shape((rows, width // 4), bf16)] * 4,
+        [at_cell, tokens, keep, from_core, from_chip, ln_gains, order],
+        [pltpu.VMEM((4, rows, width // 4), bf16)],
+        flops=2 * rows * rows * width,
+        smem=1,
+    )
+    inputs = [slices[0]] + [swap(slices[k], "fsdp", k) for k in range(1, 4)]
+    inputs += [across(slices[k], k) for k in range(4)]
+    shares = call(
+        merge_kernel,
+        [shape((2 * count, half), f32)] + [shape((2 * count, half), bf16)] * 3,
+        [me_cell, *inputs, *merge_blocks],
+        flops=2 * 8 * count * width * half,
+        smem=1,
+    )
+    got = [swap(shares[k], "fsdp", k) for k in range(1, 4)]
+    (packed,) = call(
+        pack_kernel,
+        [shape((n_dp * 2 * capacity, half), bf16)],
+        [slots, shares[0], *got],
+        flops=2 * n_dp * 2 * capacity * 2 * count * half,
+    )
+    arrived = lax.all_to_all(
+        packed.reshape(n_dp, 2 * capacity, half), "dp", split_axis=0, concat_axis=0, tiled=True
+    )
+    arrived = arrived.reshape(n_dp // 2, 2, 2, capacity, half).transpose(0, 2, 3, 1, 4)
+    return arrived.reshape(n_dp * capacity, 2 * half)
+
+
 def solution(mesh):
+    small = mesh.shape["dp"] == 8 and mesh.shape["fsdp"] == 4
     return jax.shard_map(
-        per_device,
+        by_permutes if small else by_gathers,
         mesh=mesh,
         in_specs=(
             P(("dp", "fsdp"), None),

time: 235 us -> 149 us (0.63)
  waiting for transfers between devices: 122 us -> 61.9 us
  blocking collectives: 61.6 us -> 10.6 us
  starting transfers between devices: 3.62 us -> 50.2 us
  matrix products: 14.6 us -> 0 us
  between operations: 13.4 us -> 0.23 us
  Pallas kernels: 0 us -> 9.38 us
  other arithmetic: 7.34 us -> 2.18 us
    all_gather x4 -> x0, waiting for transfers between devices: 91.2 us -> none  [the longest x1 44.6 us: per_device(): part_rows = lax.all_gather(merge_weight, 'dp', axis=0, tiled=True)]
    ppermute x0 -> x34, waiting for transfers between devices: none -> 61.9 us  [the longest x9 37.8 us: turn(): return lax.ppermute(value, 'dp', [(i, (i + 2 * k) % n) for i in range(n)])]
    ppermute x0 -> x34, starting transfers between devices: none -> 50.2 us  [the longest x9 25.8 us: turn(): return lax.ppermute(value, 'dp', [(i, (i + 2 * k) % n) for i in range(n)])]
    all_gather x2 -> x0, blocking collectives: 39.6 us -> none  [the longest x1 34.6 us: per_device(): out_mine = lax.all_gather(out_weight, 'dp', axis=1, tiled=True)]
    reduce_scatter x1 -> x0, waiting for transfers between devices: 18.9 us -> none  [per_device(): lax.psum_scatter(jnp.dot(gathered_inputs, part_rows, preferred_element_ty...]
    dot_general x14 -> x0, matrix products: 14.6 us -> none  [the longest x1 3.28 us: per_device(): jnp.dot(gathered_inputs, part_rows, preferred_element_type=jnp.float32)]
    all_to_all x2 -> x1, blocking collectives: 22 us -> 10.6 us  [by_permutes(): lax.all_to_all(packed.reshape(n_dp, 2 * capacity, half), 'dp', split_axis...]
    all_to_all x1 -> x0, waiting for transfers between devices: 10.5 us -> none  [per_device(): lax.all_to_all(attended_mine, 'fsdp', split_axis=0, concat_axis=1, tiled=...]
  transfers between devices with their start and end apart: 6 -> 34, of which waited for: 5 -> 13; matrix products, arithmetic and copies ran while one was open for 10% -> 3% of each run, Pallas kernels for 0% -> 3%
where the time goes in v2:
time: 149 us
  waiting for transfers between devices  61.9 us (42%)
  starting transfers between devices  50.2 us (34%)
  local copies, waits for them, and re-layouts  14 us (9%)
  blocking collectives  10.6 us (7%)
  Pallas kernels  9.38 us (6%)
  other arithmetic  2.18 us (1%)
    ppermute x9, waiting for transfers between devices, turn(): return lax.ppermute(value, 'dp', [(i, (i + 2 * k) % n) for i in range(n)])  37.8 us
    ppermute x9, starting transfers between devices, turn(): return lax.ppermute(value, 'dp', [(i, (i + 2 * k) % n) for i in range(n)])  25.8 us
    ppermute x21, waiting for transfers between devices, swap(): lax.ppermute(value, axis, [(i, i ^ k) for i in range(lax.axis_size(axis))])  19.3 us
    ppermute x21, starting transfers between devices, swap(): lax.ppermute(value, axis, [(i, i ^ k) for i in range(lax.axis_size(axis))])  18.1 us
    unnamed x41, local copies, waits for them, and re-layouts  12.1 us
    all_to_all x1, blocking collectives, by_permutes(): lax.all_to_all(packed.reshape(n_dp, 2 * capacity, half), 'dp', split_axis...  10.6 us
    pallas_call x7, Pallas kernels, call(): pl.pallas_call(kernel, out_shape=tuple(outs), in_specs=specs, out_specs=t...  9.38 us
    ppermute x4, starting transfers between devices, across(): return lax.ppermute(value, ('dp', 'fsdp'), pairs)  6.3 us
  transfers between devices with their start and end apart: 34, of which 13 were waited for; matrix products, arithmetic and copies ran while one was open for 3% of the time, Pallas kernels for 3%

profile of v2, /device:TPU:0, one launch (start us, length us, event | category | flops | bytes accessed | tf_op | source)
XLA Modules:
  0.0 148.6 jit_solution(17695162896567782483)
XLA Ops:
  2.6 3.0 %collective-permute-start.1 = (bf16[144,1280]{1,0:T(8,128)(2,1)S(1)}, bf16[144,1280]{1,0:T(8,128)(2,1)S(1)}, u32[]{:S(2)}, u32[]{:S(2)}) collective-permute-start(bf16[144,1280]{1,0:T(8,128)(2,1)S(1)} %shard_map.82.refs_0_), channel_id=1, source_target_pairs={{0,2},{1,3},{2,0},{3,1},{4,6},{5,7},{6,4},{7,5},{8,10},{9,11},{10,... | collective-permute-start | bytes 1105928 | tf_op jit(solution)/shard_map/ppermute | solution.py:107
  6.6 1.6 %collective-permute-start.4 = (bf16[2,160,320]{2,1,0:T(8,128)(2,1)S(1)}, bf16[2,160,320]{2,1,0:T(8,128)(2,1)S(1)}, u32[]{:S(2)}, u32[]{:S(2)}) collective-permute-start(bf16[2,160,320]{2,1,0:T(8,128)(2,1)S(1)} %slice.12.refs_4_), channel_id=1, source_target_pairs={{0,8},{4,12},{8,16},{12,20},{16,24},{20,28},{24,0},{28,4},{1,9},{5... | collective-permute-start | bytes 614408 | tf_op jit(solution)/shard_map/ppermute | solution.py:112
  8.2 2.6 %collective-permute-start.6 = (bf16[2,160,320]{2,1,0:T(8,128)(2,1)S(1)}, bf16[2,160,320]{2,1,0:T(8,128)(2,1)S(1)}, u32[]{:S(2)}, u32[]{:S(2)}) collective-permute-start(bf16[2,160,320]{2,1,0:T(8,128)(2,1)S(1)} %slice.12.refs_4_), channel_id=1, source_target_pairs={{0,16},{4,20},{8,24},{12,28},{16,0},{20,4},{24,8},{28,12},{1,17},{... | collective-permute-start | bytes 614408 | tf_op jit(solution)/shard_map/ppermute | solution.py:112
  10.8 1.3 collective-permute-start.5
  12.2 5.3 %collective-permute-done.4.refs_5_ = bf16[2,160,320]{2,1,0:T(8,128)(2,1)S(1)} collective-permute-done((bf16[2,160,320]{2,1,0:T(8,128)(2,1)S(1)}, bf16[2,160,320]{2,1,0:T(8,128)(2,1)S(1)}, u32[]{:S(2)}, u32[]{:S(2)}) %collective-permute-start.4) | collective-permute-done | bytes 204832 | tf_op jit(solution)/shard_map/ppermute | solution.py:112
  17.5 1.5 %collective-permute-start.7 = (bf16[2,160,320]{2,1,0:T(8,128)(2,1)S(1)}, bf16[2,160,320]{2,1,0:T(8,128)(2,1)S(1)}, u32[]{:S(2)}, u32[]{:S(2)}) collective-permute-start(bf16[2,160,320]{2,1,0:T(8,128)(2,1)S(1)} %slice.12.refs_4_), channel_id=1, source_target_pairs={{0,4},{4,0},{8,12},{12,8},{16,20},{20,16},{24,28},{28,24},{1,5},{5... | collective-permute-start | bytes 614408 | tf_op jit(solution)/shard_map/ppermute | solution.py:107
  19.0 7.6 %collective-permute-done.6.refs_7_ = bf16[2,160,320]{2,1,0:T(8,128)(2,1)S(1)} collective-permute-done((bf16[2,160,320]{2,1,0:T(8,128)(2,1)S(1)}, bf16[2,160,320]{2,1,0:T(8,128)(2,1)S(1)}, u32[]{:S(2)}, u32[]{:S(2)}) %collective-permute-start.6) | collective-permute-done | bytes 204832 | tf_op jit(solution)/shard_map/ppermute | solution.py:112
  26.6 1.5 %collective-permute-start.8 = (bf16[2,160,320]{2,1,0:T(8,128)(2,1)S(1)}, bf16[2,160,320]{2,1,0:T(8,128)(2,1)S(1)}, u32[]{:S(2)}, u32[]{:S(2)}) collective-permute-start(bf16[2,160,320]{2,1,0:T(8,128)(2,1)S(1)} %collective-permute-done.4.refs_5_), channel_id=1, source_target_pairs={{0,4},{4,0},{8,12},{12,8},{16,20},{20,16},{24,28},{28,24},{1,5},{5... | collective-permute-start | bytes 614408 | tf_op jit(solution)/shard_map/ppermute | solution.py:107
  29.4 1.5 %collective-permute-start.9 = (bf16[2,160,320]{2,1,0:T(8,128)(2,1)S(1)}, bf16[2,160,320]{2,1,0:T(8,128)(2,1)S(1)}, u32[]{:S(2)}, u32[]{:S(2)}) collective-permute-start(bf16[2,160,320]{2,1,0:T(8,128)(2,1)S(1)} %collective-permute-done.5.refs_6_), channel_id=1, source_target_pairs={{0,4},{4,0},{8,12},{12,8},{16,20},{20,16},{24,28},{28,24},{1,5},{5... | collective-permute-start | bytes 614408 | tf_op jit(solution)/shard_map/ppermute | solution.py:107
  31.7 7.0 %collective-permute-start.13 = (bf16[2,160,320]{2,1,0:T(8,128)(2,1)S(1)}, bf16[2,160,320]{2,1,0:T(8,128)(2,1)S(1)}, u32[]{:S(2)}, u32[]{:S(2)}) collective-permute-start(bf16[2,160,320]{2,1,0:T(8,128)(2,1)S(1)} %pad_maximum_fusion.1.refs_3_), channel_id=1, source_target_pairs={{0,16},{4,20},{8,24},{12,28},{16,0},{20,4},{24,8},{28,12},{1,17},{... | collective-permute-start | bytes 614408 | tf_op jit(solution)/shard_map/ppermute | solution.py:112
  41.4 6.8 %collective-permute-start.12 = (bf16[2,160,320]{2,1,0:T(8,128)(2,1)S(1)}, bf16[2,160,320]{2,1,0:T(8,128)(2,1)S(1)}, u32[]{:S(2)}, u32[]{:S(2)}) collective-permute-start(bf16[2,160,320]{2,1,0:T(8,128)(2,1)S(1)} %pad_maximum_fusion.1.refs_3_), channel_id=1, source_target_pairs={{0,24},{4,28},{8,0},{12,4},{16,8},{20,12},{24,16},{28,20},{1,25},{... | collective-permute-start | bytes 614408 | tf_op jit(solution)/shard_map/ppermute | solution.py:112
  48.9 1.5 %collective-permute-start.14 = (bf16[2,160,320]{2,1,0:T(8,128)(2,1)S(1)}, bf16[2,160,320]{2,1,0:T(8,128)(2,1)S(1)}, u32[]{:S(2)}, u32[]{:S(2)}) collective-permute-start(bf16[2,160,320]{2,1,0:T(8,128)(2,1)S(1)} %pad_maximum_fusion.1.refs_3_), channel_id=1, source_target_pairs={{0,4},{4,0},{8,12},{12,8},{16,20},{20,16},{24,28},{28,24},{1,5},{5... | collective-permute-start | bytes 614408 | tf_op jit(solution)/shard_map/ppermute | solution.py:107
  50.4 4.8 %collective-permute-done.13.refs_6_ = bf16[2,160,320]{2,1,0:T(8,128)(2,1)S(1)} collective-permute-done((bf16[2,160,320]{2,1,0:T(8,128)(2,1)S(1)}, bf16[2,160,320]{2,1,0:T(8,128)(2,1)S(1)}, u32[]{:S(2)}, u32[]{:S(2)}) %collective-permute-start.13) | collective-permute-done | bytes 204832 | tf_op jit(solution)/shard_map/ppermute | solution.py:112
  55.2 1.1 collective-permute-start.17
  64.1 4.0 %shard_map.83 = (bf16[512,1280]{1,0:T(8,128)(2,1)S(1)}, bf16[4,512,512]{2,1,0:T(8,128)(2,1)S(1)}, f32[4,512,1]{2,1,0:T(8,128)S(1)}) custom-call(s32[1]{0:T(128)} %bitcast.3.me_ref, bf16[144,1280]{1,0:T(8,128)(2,1)S(1)} %shard_map.82.refs_0_, bf16[144,1280]{1,0:T(8,128)(2,1)S(1)} %collective-permute-done.1.refs_1_, bf16[144,1280]{1,0:T(8,128)(2,1)S(1)} %copy-done.6, ...), custom_call_target="tpu_custom_call" | custom-call | flops 1006632960 | bytes 6529028 | tf_op jit(solution)/shard_map/pallas_call | solution.py:143
  69.0 3.1 %shard_map.84 = (f32[256,1280]{1,0:T(8,128)S(1)}, bf16[256,1280]{1,0:T(8,128)(2,1)}) custom-call(s32[1]{0:T(128)} %bitcast.3.me_ref, bf16[512,1280]{1,0:T(8,128)(2,1)S(1)} %get-tuple-element.22.refs_0_, bf16[4,512,512]{2,1,0:T(8,128)(2,1)S(1)} %get-tuple-element.23.refs_1_, f32[4,512,1]{2,1,0:T(8,128)S(1)} %get-tuple-element.24.refs_2_, ...), custom_call_target="tpu_custom_call" | custom-call | flops 1006632960 | bytes 7020548 | tf_op jit(solution)/shard_map/pallas_call | solution.py:143
  72.1 1.1 broadcast_select_fusion.1
  73.2 1.5 collective-permute-start.27
  76.7 4.1 %collective-permute-done.27 = bf16[160,640]{1,0:T(8,128)(2,1)S(1)} collective-permute-done((bf16[160,640]{1,0:T(8,128)(2,1)S(1)}, bf16[160,640]{1,0:T(8,128)(2,1)S(1)}, u32[]{:S(2)}, u32[]{:S(2)}) %collective-permute-start.27) | collective-permute-done | bytes 204832 | tf_op jit(solution)/shard_map/ppermute | solution.py:107
  80.8 3.0 %collective-permute-start.28 = (bf16[320,640]{1,0:T(8,128)(2,1)S(1)}, bf16[320,640]{1,0:T(8,128)(2,1)S(1)}, u32[]{:S(2)}, u32[]{:S(2)}) collective-permute-start(bf16[320,640]{1,0:T(8,128)(2,1)S(1)} %pad_maximum_fusion.refs_8_), channel_id=1, source_target_pairs={{0,8},{4,12},{8,16},{12,20},{16,24},{20,28},{24,0},{28,4},{1,9},{5... | collective-permute-start | bytes 1228808 | tf_op jit(solution)/shard_map/ppermute | solution.py:112
  84.7 1.8 %collective-permute-start.30 = (bf16[320,640]{1,0:T(8,128)(2,1)S(1)}, bf16[320,640]{1,0:T(8,128)(2,1)S(1)}, u32[]{:S(2)}, u32[]{:S(2)}) collective-permute-start(bf16[320,640]{1,0:T(8,128)(2,1)S(1)} %pad_maximum_fusion.refs_8_), channel_id=1, source_target_pairs={{0,16},{4,20},{8,24},{12,28},{16,0},{20,4},{24,8},{28,12},{1,17},{... | collective-permute-start | bytes 1228808 | tf_op jit(solution)/shard_map/ppermute | solution.py:112
  87.4 7.8 %collective-permute-done.19.chip_ref = bf16[128,1280]{1,0:T(8,128)(2,1)S(1)} collective-permute-done((bf16[128,1280]{1,0:T(8,128)(2,1)S(1)}, bf16[128,1280]{1,0:T(8,128)(2,1)S(1)}, u32[]{:S(2)}, u32[]{:S(2)}) %collective-permute-start.19) | collective-permute-done | bytes 327712 | tf_op jit(solution)/shard_map/ppermute | solution.py:107
  96.8 1.6 %collective-permute-start.24 = (bf16[128,320]{1,0:T(8,128)(2,1)S(1)}, bf16[128,320]{1,0:T(8,128)(2,1)S(1)}, u32[]{:S(2)}, u32[]{:S(2)}) collective-permute-start(bf16[128,320]{1,0:T(8,128)(2,1)S(1)} %get-tuple-element.30), channel_id=1, source_target_pairs={{0,5},{1,4},{2,7},{3,6},{4,1},{5,0},{6,3},{7,2},{8,13},{9,12},{10,... | collective-permute-start | bytes 245768 | tf_op jit(solution)/shard_map/ppermute | solution.py:120
  98.4 4.2 %collective-permute-done.29.refs_10_ = bf16[320,640]{1,0:T(8,128)(2,1)S(1)} collective-permute-done((bf16[320,640]{1,0:T(8,128)(2,1)S(1)}, bf16[320,640]{1,0:T(8,128)(2,1)S(1)}, u32[]{:S(2)}, u32[]{:S(2)}) %collective-permute-start.29) | collective-permute-done | bytes 409632 | tf_op jit(solution)/shard_map/ppermute | solution.py:112
  102.6 1.7 %collective-permute-start.25 = (bf16[128,320]{1,0:T(8,128)(2,1)S(1)}, bf16[128,320]{1,0:T(8,128)(2,1)S(1)}, u32[]{:S(2)}, u32[]{:S(2)}) collective-permute-start(bf16[128,320]{1,0:T(8,128)(2,1)S(1)} %get-tuple-element.31), channel_id=1, source_target_pairs={{0,6},{1,7},{2,4},{3,5},{4,2},{5,3},{6,0},{7,1},{8,14},{9,15},{10,... | collective-permute-start | bytes 245768 | tf_op jit(solution)/shard_map/ppermute | solution.py:120
  104.3 15.9 %collective-permute-done.30.refs_11_ = bf16[320,640]{1,0:T(8,128)(2,1)S(1)} collective-permute-done((bf16[320,640]{1,0:T(8,128)(2,1)S(1)}, bf16[320,640]{1,0:T(8,128)(2,1)S(1)}, u32[]{:S(2)}, u32[]{:S(2)}) %collective-permute-start.30) | collective-permute-done | bytes 409632 | tf_op jit(solution)/shard_map/ppermute | solution.py:112
  120.3 2.7 %collective-permute-start.26 = (bf16[128,320]{1,0:T(8,128)(2,1)S(1)}, bf16[128,320]{1,0:T(8,128)(2,1)S(1)}, u32[]{:S(2)}, u32[]{:S(2)}) collective-permute-start(bf16[128,320]{1,0:T(8,128)(2,1)S(1)} %get-tuple-element.32), channel_id=1, source_target_pairs={{0,7},{1,6},{2,5},{3,4},{4,3},{5,2},{6,1},{7,0},{8,15},{9,14},{10,... | collective-permute-start | bytes 245768 | tf_op jit(solution)/shard_map/ppermute | solution.py:120
  123.3 1.7 %collective-permute-done.22.refs_3_ = bf16[128,320]{1,0:T(8,128)(2,1)S(1)} collective-permute-done((bf16[128,320]{1,0:T(8,128)(2,1)S(1)}, bf16[128,320]{1,0:T(8,128)(2,1)S(1)}, u32[]{:S(2)}, u32[]{:S(2)}) %collective-permute-start.22) | collective-permute-done | bytes 81952 | tf_op jit(solution)/shard_map/ppermute | solution.py:107
  125.0 4.8 %collective-permute-done.23.refs_4_ = bf16[128,320]{1,0:T(8,128)(2,1)S(1)} collective-permute-done((bf16[128,320]{1,0:T(8,128)(2,1)S(1)}, bf16[128,320]{1,0:T(8,128)(2,1)S(1)}, u32[]{:S(2)}, u32[]{:S(2)}) %collective-permute-start.23) | collective-permute-done | bytes 81952 | tf_op jit(solution)/shard_map/ppermute | solution.py:120
  131.5 1.3 collective-permute-start.33
  132.8 3.4 %collective-permute-done.32.two_ref = bf16[64,640]{1,0:T(8,128)(2,1)S(1)} collective-permute-done((bf16[64,640]{1,0:T(8,128)(2,1)S(1)}, bf16[64,640]{1,0:T(8,128)(2,1)S(1)}, u32[]{:S(2)}, u32[]{:S(2)}) %collective-permute-start.32) | collective-permute-done | bytes 81952 | tf_op jit(solution)/shard_map/ppermute | solution.py:107
  137.2 10.6 %all_to_all.5 = bf16[8,16,640]{2,1,0:T(8,128)(2,1)S(1)} all-to-all(bf16[8,16,640]{2,1,0:T(8,128)(2,1)S(1)} %bitcast.17), channel_id=1, replica_groups=mesh['dp'=8,'fsdp'=4] {'dp'}, dimensions={0} | all-to-all | bytes 327680 | tf_op jit(solution)/shard_map/all_to_all | solution.py:379
  (101 shorter events, 27.0 us)
Async XLA Ops:
  2.6 26.0 %collective-permute-start.1 = (bf16[144,1280]{1,0:T(8,128)(2,1)S(1)}, bf16[144,1280]{1,0:T(8,128)(2,1)S(1)}, u32[]{:S(2)}, u32[]{:S(2)}) collective-permute-start(bf16[144,1280]{1,0:T(8,128)(2,1)S(1)} %shard_map.82.refs_0_), channel_id=1, source_target_pairs={{0,2},{1,3},{2,0},{3,1},{4,6},{5,7},{6,4},{7,5},{8,10},{9,11},{10,... | collective-permute-start | bytes 1105928 | tf_op jit(solution)/shard_map/ppermute | solution.py:107
  6.6 10.9 %collective-permute-start.4 = (bf16[2,160,320]{2,1,0:T(8,128)(2,1)S(1)}, bf16[2,160,320]{2,1,0:T(8,128)(2,1)S(1)}, u32[]{:S(2)}, u32[]{:S(2)}) collective-permute-start(bf16[2,160,320]{2,1,0:T(8,128)(2,1)S(1)} %slice.12.refs_4_), channel_id=1, source_target_pairs={{0,8},{4,12},{8,16},{12,20},{16,24},{20,28},{24,0},{28,4},{1,9},{5... | collective-permute-start | bytes 614408 | tf_op jit(solution)/shard_map/ppermute | solution.py:112
  8.2 18.4 %collective-permute-start.6 = (bf16[2,160,320]{2,1,0:T(8,128)(2,1)S(1)}, bf16[2,160,320]{2,1,0:T(8,128)(2,1)S(1)}, u32[]{:S(2)}, u32[]{:S(2)}) collective-permute-start(bf16[2,160,320]{2,1,0:T(8,128)(2,1)S(1)} %slice.12.refs_4_), channel_id=1, source_target_pairs={{0,16},{4,20},{8,24},{12,28},{16,0},{20,4},{24,8},{28,12},{1,17},{... | collective-permute-start | bytes 614408 | tf_op jit(solution)/shard_map/ppermute | solution.py:112
  10.8 17.3 %collective-permute-start.5 = (bf16[2,160,320]{2,1,0:T(8,128)(2,1)S(1)}, bf16[2,160,320]{2,1,0:T(8,128)(2,1)S(1)}, u32[]{:S(2)}, u32[]{:S(2)}) collective-permute-start(bf16[2,160,320]{2,1,0:T(8,128)(2,1)S(1)} %slice.12.refs_4_), channel_id=1, source_target_pairs={{0,24},{4,28},{8,0},{12,4},{16,8},{20,12},{24,16},{28,20},{1,25},{... | collective-permute-start | bytes 614408 | tf_op jit(solution)/shard_map/ppermute | solution.py:112
  12.2 18.8 %collective-permute-start.2 = (bf16[144,1280]{1,0:T(8,128)(2,1)S(1)}, bf16[144,1280]{1,0:T(8,128)(2,1)S(1)}, u32[]{:S(2)}, u32[]{:S(2)}) collective-permute-start(bf16[144,1280]{1,0:T(8,128)(2,1)S(1)} %shard_map.82.refs_0_), channel_id=1, source_target_pairs={{0,1},{1,0},{2,3},{3,2},{4,5},{5,4},{6,7},{7,6},{8,9},{9,8},{10,11... | collective-permute-start | bytes 1105928 | tf_op jit(solution)/shard_map/ppermute | solution.py:107
  17.5 11.2 %collective-permute-start.7 = (bf16[2,160,320]{2,1,0:T(8,128)(2,1)S(1)}, bf16[2,160,320]{2,1,0:T(8,128)(2,1)S(1)}, u32[]{:S(2)}, u32[]{:S(2)}) collective-permute-start(bf16[2,160,320]{2,1,0:T(8,128)(2,1)S(1)} %slice.12.refs_4_), channel_id=1, source_target_pairs={{0,4},{4,0},{8,12},{12,8},{16,20},{20,16},{24,28},{28,24},{1,5},{5... | collective-permute-start | bytes 614408 | tf_op jit(solution)/shard_map/ppermute | solution.py:107
  26.6 12.1 %collective-permute-start.8 = (bf16[2,160,320]{2,1,0:T(8,128)(2,1)S(1)}, bf16[2,160,320]{2,1,0:T(8,128)(2,1)S(1)}, u32[]{:S(2)}, u32[]{:S(2)}) collective-permute-start(bf16[2,160,320]{2,1,0:T(8,128)(2,1)S(1)} %collective-permute-done.4.refs_5_), channel_id=1, source_target_pairs={{0,4},{4,0},{8,12},{12,8},{16,20},{20,16},{24,28},{28,24},{1,5},{5... | collective-permute-start | bytes 614408 | tf_op jit(solution)/shard_map/ppermute | solution.py:107
  28.1 12.6 %collective-permute-start.10 = (bf16[2,160,320]{2,1,0:T(8,128)(2,1)S(1)}, bf16[2,160,320]{2,1,0:T(8,128)(2,1)S(1)}, u32[]{:S(2)}, u32[]{:S(2)}) collective-permute-start(bf16[2,160,320]{2,1,0:T(8,128)(2,1)S(1)} %collective-permute-done.6.refs_7_), channel_id=1, source_target_pairs={{0,4},{4,0},{8,12},{12,8},{16,20},{20,16},{24,28},{28,24},{1,5},{5... | collective-permute-start | bytes 614408 | tf_op jit(solution)/shard_map/ppermute | solution.py:107
  28.6 29.7 %collective-permute-start.3 = (bf16[144,1280]{1,0:T(8,128)(2,1)S(1)}, bf16[144,1280]{1,0:T(8,128)(2,1)}, u32[]{:S(2)}, u32[]{:S(2)}) collective-permute-start(bf16[144,1280]{1,0:T(8,128)(2,1)S(1)} %collective-permute-done.1.refs_1_), channel_id=1, source_target_pairs={{0,1},{1,0},{2,3},{3,2},{4,5},{5,4},{6,7},{7,6},{8,9},{9,8},{10,11... | collective-permute-start | bytes 1105928 | tf_op jit(solution)/shard_map/ppermute | solution.py:107
  29.4 18.8 %collective-permute-start.9 = (bf16[2,160,320]{2,1,0:T(8,128)(2,1)S(1)}, bf16[2,160,320]{2,1,0:T(8,128)(2,1)S(1)}, u32[]{:S(2)}, u32[]{:S(2)}) collective-permute-start(bf16[2,160,320]{2,1,0:T(8,128)(2,1)S(1)} %collective-permute-done.5.refs_6_), channel_id=1, source_target_pairs={{0,4},{4,0},{8,12},{12,8},{16,20},{20,16},{24,28},{28,24},{1,5},{5... | collective-permute-start | bytes 614408 | tf_op jit(solution)/shard_map/ppermute | solution.py:107
  31.7 23.6 %collective-permute-start.13 = (bf16[2,160,320]{2,1,0:T(8,128)(2,1)S(1)}, bf16[2,160,320]{2,1,0:T(8,128)(2,1)S(1)}, u32[]{:S(2)}, u32[]{:S(2)}) collective-permute-start(bf16[2,160,320]{2,1,0:T(8,128)(2,1)S(1)} %pad_maximum_fusion.1.refs_3_), channel_id=1, source_target_pairs={{0,16},{4,20},{8,24},{12,28},{16,0},{20,4},{24,8},{28,12},{1,17},{... | collective-permute-start | bytes 614408 | tf_op jit(solution)/shard_map/ppermute | solution.py:112
  39.3 17.0 %collective-permute-start.11 = (bf16[2,160,320]{2,1,0:T(8,128)(2,1)S(1)}, bf16[2,160,320]{2,1,0:T(8,128)(2,1)S(1)}, u32[]{:S(2)}, u32[]{:S(2)}) collective-permute-start(bf16[2,160,320]{2,1,0:T(8,128)(2,1)S(1)} %pad_maximum_fusion.1.refs_3_), channel_id=1, source_target_pairs={{0,8},{4,12},{8,16},{12,20},{16,24},{20,28},{24,0},{28,4},{1,9},{5... | collective-permute-start | bytes 614408 | tf_op jit(solution)/shard_map/ppermute | solution.py:112
  41.4 15.9 %collective-permute-start.12 = (bf16[2,160,320]{2,1,0:T(8,128)(2,1)S(1)}, bf16[2,160,320]{2,1,0:T(8,128)(2,1)S(1)}, u32[]{:S(2)}, u32[]{:S(2)}) collective-permute-start(bf16[2,160,320]{2,1,0:T(8,128)(2,1)S(1)} %pad_maximum_fusion.1.refs_3_), channel_id=1, source_target_pairs={{0,24},{4,28},{8,0},{12,4},{16,8},{20,12},{24,16},{28,20},{1,25},{... | collective-permute-start | bytes 614408 | tf_op jit(solution)/shard_map/ppermute | solution.py:112
  48.9 19.2 %collective-permute-start.14 = (bf16[2,160,320]{2,1,0:T(8,128)(2,1)S(1)}, bf16[2,160,320]{2,1,0:T(8,128)(2,1)S(1)}, u32[]{:S(2)}, u32[]{:S(2)}) collective-permute-start(bf16[2,160,320]{2,1,0:T(8,128)(2,1)S(1)} %pad_maximum_fusion.1.refs_3_), channel_id=1, source_target_pairs={{0,4},{4,0},{8,12},{12,8},{16,20},{20,16},{24,28},{28,24},{1,5},{5... | collective-permute-start | bytes 614408 | tf_op jit(solution)/shard_map/ppermute | solution.py:107
  55.2 12.9 %collective-permute-start.17 = (bf16[2,160,320]{2,1,0:T(8,128)(2,1)S(1)}, bf16[2,160,320]{2,1,0:T(8,128)(2,1)S(1)}, u32[]{:S(2)}, u32[]{:S(2)}) collective-permute-start(bf16[2,160,320]{2,1,0:T(8,128)(2,1)S(1)} %collective-permute-done.13.refs_6_), channel_id=1, source_target_pairs={{0,4},{4,0},{8,12},{12,8},{16,20},{20,16},{24,28},{28,24},{1,5},{5... | collective-permute-start | bytes 614408 | tf_op jit(solution)/shard_map/ppermute | solution.py:107
  56.3 11.8 %collective-permute-start.15 = (bf16[2,160,320]{2,1,0:T(8,128)(2,1)S(1)}, bf16[2,160,320]{2,1,0:T(8,128)(2,1)S(1)}, u32[]{:S(2)}, u32[]{:S(2)}) collective-permute-start(bf16[2,160,320]{2,1,0:T(8,128)(2,1)S(1)} %collective-permute-done.11.refs_4_), channel_id=1, source_target_pairs={{0,4},{4,0},{8,12},{12,8},{16,20},{20,16},{24,28},{28,24},{1,5},{5... | collective-permute-start | bytes 614408 | tf_op jit(solution)/shard_map/ppermute | solution.py:107
  57.3 11.7 %collective-permute-start.16 = (bf16[2,160,320]{2,1,0:T(8,128)(2,1)S(1)}, bf16[2,160,320]{2,1,0:T(8,128)(2,1)S(1)}, u32[]{:S(2)}, u32[]{:S(2)}) collective-permute-start(bf16[2,160,320]{2,1,0:T(8,128)(2,1)S(1)} %collective-permute-done.12.refs_5_), channel_id=1, source_target_pairs={{0,4},{4,0},{8,12},{12,8},{16,20},{20,16},{24,28},{28,24},{1,5},{5... | collective-permute-start | bytes 614408 | tf_op jit(solution)/shard_map/ppermute | solution.py:107
  72.1 14.4 %collective-permute-start.18 = (bf16[256,1280]{1,0:T(8,128)(2,1)}, bf16[256,1280]{1,0:T(8,128)(2,1)S(1)}, u32[]{:S(2)}, u32[]{:S(2)}) collective-permute-start(bf16[256,1280]{1,0:T(8,128)(2,1)} %get-tuple-element.28), channel_id=1, source_target_pairs={{0,1},{1,0},{2,3},{3,2},{4,5},{5,4},{6,7},{7,6},{8,9},{9,8},{10,11... | collective-permute-start | bytes 1966088 | tf_op jit(solution)/shard_map/ppermute | solution.py:107
  73.2 7.6 %collective-permute-start.27 = (bf16[160,640]{1,0:T(8,128)(2,1)S(1)}, bf16[160,640]{1,0:T(8,128)(2,1)S(1)}, u32[]{:S(2)}, u32[]{:S(2)}) collective-permute-start(bf16[160,640]{1,0:T(8,128)(2,1)S(1)} %get-tuple-element.33), channel_id=1, source_target_pairs={{0,4},{4,0},{8,12},{12,8},{16,20},{20,16},{24,28},{28,24},{1,5},{5... | collective-permute-start | bytes 614408 | tf_op jit(solution)/shard_map/ppermute | solution.py:107
  74.7 21.3 %collective-permute-start = (s32[32,1]{0,1:T(1,128)S(1)}, s32[32,1]{0,1:T(1,128)S(1)}, u32[]{:S(2)}, u32[]{:S(2)}) collective-permute-start(s32[32,1]{0,1:T(1,128)S(1)} %copy-done.18), channel_id=1, source_target_pairs={{0,4},{4,0},{8,12},{12,8},{16,20},{20,16},{24,28},{28,24},{1,5},{5... | collective-permute-start | bytes 392 | tf_op jit(solution)/shard_map/ppermute | solution.py:107
  80.8 15.9 %collective-permute-start.28 = (bf16[320,640]{1,0:T(8,128)(2,1)S(1)}, bf16[320,640]{1,0:T(8,128)(2,1)S(1)}, u32[]{:S(2)}, u32[]{:S(2)}) collective-permute-start(bf16[320,640]{1,0:T(8,128)(2,1)S(1)} %pad_maximum_fusion.refs_8_), channel_id=1, source_target_pairs={{0,8},{4,12},{8,16},{12,20},{16,24},{20,28},{24,0},{28,4},{1,9},{5... | collective-permute-start | bytes 1228808 | tf_op jit(solution)/shard_map/ppermute | solution.py:112
  83.8 18.7 %collective-permute-start.29 = (bf16[320,640]{1,0:T(8,128)(2,1)S(1)}, bf16[320,640]{1,0:T(8,128)(2,1)S(1)}, u32[]{:S(2)}, u32[]{:S(2)}) collective-permute-start(bf16[320,640]{1,0:T(8,128)(2,1)S(1)} %pad_maximum_fusion.refs_8_), channel_id=1, source_target_pairs={{0,24},{4,28},{8,0},{12,4},{16,8},{20,12},{24,16},{28,20},{1,25},{... | collective-permute-start | bytes 1228808 | tf_op jit(solution)/shard_map/ppermute | solution.py:112
  84.7 35.4 %collective-permute-start.30 = (bf16[320,640]{1,0:T(8,128)(2,1)S(1)}, bf16[320,640]{1,0:T(8,128)(2,1)S(1)}, u32[]{:S(2)}, u32[]{:S(2)}) collective-permute-start(bf16[320,640]{1,0:T(8,128)(2,1)S(1)} %pad_maximum_fusion.refs_8_), channel_id=1, source_target_pairs={{0,16},{4,20},{8,24},{12,28},{16,0},{20,4},{24,8},{28,12},{1,17},{... | collective-permute-start | bytes 1228808 | tf_op jit(solution)/shard_map/ppermute | solution.py:112
  86.6 8.6 %collective-permute-start.19 = (bf16[128,1280]{1,0:T(8,128)(2,1)S(1)}, bf16[128,1280]{1,0:T(8,128)(2,1)S(1)}, u32[]{:S(2)}, u32[]{:S(2)}) collective-permute-start(bf16[128,1280]{1,0:T(8,128)(2,1)S(1)} %shard_map.85), channel_id=1, source_target_pairs={{0,2},{1,3},{2,0},{3,1},{4,6},{5,7},{6,4},{7,5},{8,10},{9,11},{10,... | collective-permute-start | bytes 983048 | tf_op jit(solution)/shard_map/ppermute | solution.py:107
  95.9 24.4 %collective-permute-start.20 = (bf16[128,320]{1,0:T(8,128)(2,1)S(1)}, bf16[128,320]{1,0:T(8,128)(2,1)S(1)}, u32[]{:S(2)}, u32[]{:S(2)}) collective-permute-start(bf16[128,320]{1,0:T(8,128)(2,1)S(1)} %get-tuple-element.30), channel_id=1, source_target_pairs={{0,1},{1,0},{2,3},{3,2},{4,5},{5,4},{6,7},{7,6},{8,9},{9,8},{10,11... | collective-permute-start | bytes 245768 | tf_op jit(solution)/shard_map/ppermute | solution.py:107
  96.0 27.0 %collective-permute-start.21 = (bf16[128,320]{1,0:T(8,128)(2,1)S(1)}, bf16[128,320]{1,0:T(8,128)(2,1)S(1)}, u32[]{:S(2)}, u32[]{:S(2)}) collective-permute-start(bf16[128,320]{1,0:T(8,128)(2,1)S(1)} %get-tuple-element.31), channel_id=1, source_target_pairs={{0,2},{1,3},{2,0},{3,1},{4,6},{5,7},{6,4},{7,5},{8,10},{9,11},{10,... | collective-permute-start | bytes 245768 | tf_op jit(solution)/shard_map/ppermute | solution.py:107
  96.8 33.1 %collective-permute-start.24 = (bf16[128,320]{1,0:T(8,128)(2,1)S(1)}, bf16[128,320]{1,0:T(8,128)(2,1)S(1)}, u32[]{:S(2)}, u32[]{:S(2)}) collective-permute-start(bf16[128,320]{1,0:T(8,128)(2,1)S(1)} %get-tuple-element.30), channel_id=1, source_target_pairs={{0,5},{1,4},{2,7},{3,6},{4,1},{5,0},{6,3},{7,2},{8,13},{9,12},{10,... | collective-permute-start | bytes 245768 | tf_op jit(solution)/shard_map/ppermute | solution.py:120
  102.6 27.3 %collective-permute-start.25 = (bf16[128,320]{1,0:T(8,128)(2,1)S(1)}, bf16[128,320]{1,0:T(8,128)(2,1)S(1)}, u32[]{:S(2)}, u32[]{:S(2)}) collective-permute-start(bf16[128,320]{1,0:T(8,128)(2,1)S(1)} %get-tuple-element.31), channel_id=1, source_target_pairs={{0,6},{1,7},{2,4},{3,5},{4,2},{5,3},{6,0},{7,1},{8,14},{9,15},{10,... | collective-permute-start | bytes 245768 | tf_op jit(solution)/shard_map/ppermute | solution.py:120
  120.3 9.6 %collective-permute-start.26 = (bf16[128,320]{1,0:T(8,128)(2,1)S(1)}, bf16[128,320]{1,0:T(8,128)(2,1)S(1)}, u32[]{:S(2)}, u32[]{:S(2)}) collective-permute-start(bf16[128,320]{1,0:T(8,128)(2,1)S(1)} %get-tuple-element.32), channel_id=1, source_target_pairs={{0,7},{1,6},{2,5},{3,4},{4,3},{5,2},{6,1},{7,0},{8,15},{9,14},{10,... | collective-permute-start | bytes 245768 | tf_op jit(solution)/shard_map/ppermute | solution.py:120
  123.0 6.8 %collective-permute-start.23 = (bf16[128,320]{1,0:T(8,128)(2,1)S(1)}, bf16[128,320]{1,0:T(8,128)(2,1)S(1)}, u32[]{:S(2)}, u32[]{:S(2)}) collective-permute-start(bf16[128,320]{1,0:T(8,128)(2,1)S(1)} %get-tuple-element.29.refs_0_), channel_id=1, source_target_pairs={{0,4},{1,5},{2,6},{3,7},{4,0},{5,1},{6,2},{7,3},{8,12},{9,13},{10,... | collective-permute-start | bytes 245768 | tf_op jit(solution)/shard_map/ppermute | solution.py:120
  130.9 5.3 %collective-permute-start.32 = (bf16[64,640]{1,0:T(8,128)(2,1)S(1)}, bf16[64,640]{1,0:T(8,128)(2,1)S(1)}, u32[]{:S(2)}, u32[]{:S(2)}) collective-permute-start(bf16[64,640]{1,0:T(8,128)(2,1)S(1)} %get-tuple-element.37), channel_id=1, source_target_pairs={{0,2},{1,3},{2,0},{3,1},{4,6},{5,7},{6,4},{7,5},{8,10},{9,11},{10,... | collective-permute-start | bytes 245768 | tf_op jit(solution)/shard_map/ppermute | solution.py:107
  131.5 5.6 %collective-permute-start.33 = (bf16[64,640]{1,0:T(8,128)(2,1)S(1)}, bf16[64,640]{1,0:T(8,128)(2,1)S(1)}, u32[]{:S(2)}, u32[]{:S(2)}) collective-permute-start(bf16[64,640]{1,0:T(8,128)(2,1)S(1)} %get-tuple-element.38), channel_id=1, source_target_pairs={{0,3},{1,2},{2,1},{3,0},{4,7},{5,6},{6,5},{7,4},{8,11},{9,10},{10,... | collective-permute-start | bytes 245768 | tf_op jit(solution)/shard_map/ppermute | solution.py:107
  (23 other events, 132.3 us)

commit v3 on v2

--- a/solution.py
+++ b/solution.py
@@ -107,25 +107,11 @@
     return lax.ppermute(value, axis, [(i, i ^ k) for i in range(lax.axis_size(axis))])
 
 
-def turn(value, k):
-    n = lax.axis_size("dp")
-    return lax.ppermute(value, "dp", [(i, (i + 2 * k) % n) for i in range(n)])
-
-
-def across(value, k):
-    n_dp, n_fsdp = lax.axis_size("dp"), lax.axis_size("fsdp")
-    pairs = [
-        (i * n_fsdp + j, (i ^ 1) * n_fsdp + (j ^ k)) for i in range(n_dp) for j in range(n_fsdp)
-    ]
-    return lax.ppermute(value, ("dp", "fsdp"), pairs)
-
-
 def after(value, other):
     return lax.optimization_barrier((value, other))[0]
 
 
-ROUNDS = (1, 3, 2)
-ORDER = (0, 1, 3, 2)
+ORDER = (0, 2, 4, 6, 1, 3, 5, 7)
 
 
 def dot(a, b):
@@ -136,24 +122,33 @@
     return lax.dot_general(a, b, (((1,), (1,)), ((), ())), preferred_element_type=jnp.float32)
 
 
-def call(kernel, outs, operands, scratch=(), flops=0, smem=0, exps=0):
+def call(kernel, outs, operands, scratch=(), flops=0, smem=0, exps=0, space=pltpu.VMEM):
     moved = sum(math.prod(x.shape) * x.dtype.itemsize for x in (*operands, *outs))
     specs = [pl.BlockSpec(memory_space=pltpu.SMEM)] * smem
-    specs += [pl.BlockSpec(memory_space=pltpu.VMEM)] * (len(operands) - smem)
+    specs += [pl.BlockSpec(memory_space=space)] * (len(operands) - smem)
     return pl.pallas_call(
         kernel,
         out_shape=tuple(outs),
         in_specs=specs,
         out_specs=tuple(pl.BlockSpec(memory_space=pltpu.VMEM) for _ in outs),
         scratch_shapes=list(scratch),
-        compiler_params=pltpu.CompilerParams(vmem_limit_bytes=40 * 1024 * 1024),
+        compiler_params=pltpu.CompilerParams(vmem_limit_bytes=16 * 1024 * 1024),
         cost_estimate=pl.CostEstimate(
             flops=flops, bytes_accessed=moved, transcendentals=exps
         ),
     )(*operands)
 
 
-def norm_kernel(tokens_ref, gains_ref, segs_ref, out_ref):
+def norm_kernel(tokens_in, gains_in, segs_in, out_ref, tokens_ref, gains_ref, segs_ref, sems):
+    copies = [
+        pltpu.make_async_copy(tokens_in, tokens_ref, sems.at[0]),
+        pltpu.make_async_copy(gains_in, gains_ref, sems.at[1]),
+        pltpu.make_async_copy(segs_in, segs_ref, sems.at[2]),
+    ]
+    for copy in copies:
+        copy.start()
+    for copy in copies:
+        copy.wait()
     rows = tokens_ref.shape[0]
     out_ref[0:rows, :] = normalize(tokens_ref[...], gains_ref[0:1, :])
     out_ref[rows:, :] = jnp.zeros((out_ref.shape[0] - rows, out_ref.shape[1]), out_ref.dtype)
@@ -162,15 +157,10 @@
     ).astype(out_ref.dtype)
 
 
-def block_index(me, number, n_dp):
-    mine = lax.rem(me + n_dp - 2 * ORDER[number % 4], n_dp)
-    return mine if number < 4 else mine ^ 1
-
-
 def lay_out(me, blocks, part, whole):
     step = blocks[0].shape[1]
-    for number, block in enumerate(blocks):
-        start = pl.multiple_of(block_index(me, number, len(blocks)) * step, 32)
+    for number, block in zip(ORDER, blocks):
+        start = pl.multiple_of((me ^ number) * step, 32)
         whole[pl.ds(start, step), :] = block[part]
 
 
@@ -219,8 +209,8 @@
     out_ref[...] = (keep_ref[rows:, :] + got_ref[rows:, :].astype(jnp.float32)).astype(jnp.bfloat16)
 
 
-def layer_kernel(at_ref, tokens_ref, keep_ref, core_ref, chip_ref, gains_ref, order_ref, *refs):
-    outs, slices = refs[0:4], refs[4]
+def layer_kernel(tokens_ref, keep_ref, core_ref, chip_ref, gains_ref, order_ref, *refs):
+    (slices,) = refs
     rows, width = tokens_ref.shape
     summed = (
         tokens_ref[...].astype(jnp.float32)
@@ -234,39 +224,35 @@
     ordered = dot(picking, merge_in).astype(jnp.bfloat16)
     step, half = width // 8, width // 2
     for n in range(4):
-        slices[n] = jnp.concatenate(
+        part = jnp.concatenate(
             [
                 ordered[:, n * step : (n + 1) * step],
                 ordered[:, half + n * step : half + (n + 1) * step],
             ],
             axis=1,
         )
-    for k in range(4):
-        outs[k][...] = slices[at_ref[0] ^ k]
-
-
-def merge_kernel(me_ref, *refs):
-    inputs, blocks = refs[0:8], refs[8:12]
-    keep_ref, sends = refs[12], refs[13:16]
-    count = inputs[0].shape[0] // 4
+        part = jnp.concatenate([part[: rows // 2, :], part[rows // 2 :, :]], axis=1)
+        slices[n] = part
+        slices[4 + n] = part
+
+
+def merge_kernel(me_ref, at_ref, inputs, *refs):
+    blocks, (keep_ref, *sends), total = refs[0:4], refs[4:8], refs[8]
+    count, width = inputs.shape[1] // 2, inputs.shape[2] // 2
     z, y = me_ref[0] // 2, lax.rem(me_ref[0], 2)
-    total = jnp.zeros((8 * count, blocks[0].shape[1]), jnp.float32)
     for number, block in enumerate(blocks):
-        at = lax.rem(z + 4 - ORDER[number], 4) * count
-        at = pl.multiple_of(at, 32)
-        rows = jnp.concatenate([x[pl.ds(at, count), :] for x in inputs], axis=0)
+        position = z ^ number
+        at = pl.multiple_of(lax.rem(position, 2) * count, 32)
+        rows = inputs[:, pl.ds(at, count), :].reshape(8 * count, 2 * width)
+        rows = jnp.where(position < 2, rows[:, :width], rows[:, width:])
         step = block.shape[0] // 2
         low = block[pl.ds(pl.multiple_of(y * step, 32), step), :]
         high = block[pl.ds(pl.multiple_of((1 - y) * step, 32), step), :]
-        total = total + dot(rows, jnp.concatenate([low, high], axis=0))
+        found = dot(rows, jnp.concatenate([low, high], axis=0)).reshape(total.shape)
+        total[...] = found if number == 0 else total[...] + found
     for k in range(4):
-        share = jnp.concatenate(
-            [
-                total[k * count : (k + 1) * count, :],
-                total[(4 + k) * count : (5 + k) * count, :],
-            ],
-            axis=0,
-        )
+        to = at_ref[0] ^ k
+        share = jnp.concatenate([total[4 * y + to], total[4 * (1 - y) + to]], axis=0)
         if k == 0:
             keep_ref[...] = share
         else:
@@ -297,19 +283,24 @@
     group = n_fsdp * rows
 
     first = qkv_weight[0:2]
-    first_z = [turn(first, k) for k in ROUNDS]
+    first_z = [swap(first, "dp", 2), swap(first, "dp", 4)]
     first_y = [swap(first, "dp", 1)]
+    first_z += [swap(first_z[1], "dp", 2)]
     second = jnp.concatenate([qkv_weight[2:3], out_weight.T[None]], axis=0)
-    second_z = [turn(after(second, first_z[0]), k) for k in ROUNDS]
-    second_y = [swap(after(second, first_y[0]), "dp", 1)]
-    first_y += [swap(block, "dp", 1) for block in first_z]
-    second_y += [swap(block, "dp", 1) for block in second_z]
     half = merge_weight.shape[1] // 2
     low, high = merge_weight[:, :half], merge_weight[:, half:]
     lower = y == 0
-    theirs = swap(after(jnp.where(lower, high, low), second_y[0]), "dp", 1)
+    theirs = swap(after(jnp.where(lower, high, low), first_y[0]), "dp", 1)
+    held = after(second, first_z[0])
+    second_z = [swap(held, "dp", 2), swap(held, "dp", 4)]
+    second_y = [swap(held, "dp", 1)]
+    second_z += [swap(second_z[1], "dp", 2)]
+    first_y += [swap(block, "dp", 1) for block in first_z]
+    second_y += [swap(block, "dp", 1) for block in second_z]
     pair = jnp.concatenate([jnp.where(lower, low, high), theirs], axis=0)
-    merge_blocks = [pair] + [turn(after(pair, second_z[2]), k) for k in ROUNDS]
+    held = after(pair, second_z[1])
+    merge_blocks = [pair, swap(held, "dp", 2), swap(held, "dp", 4)]
+    merge_blocks += [swap(merge_blocks[2], "dp", 2)]
 
     capacity = max(2, (2 * count + n_dp - 1) // n_dp)
     mine = owners[:, 0]
@@ -322,7 +313,14 @@
     order = merge_rows.reshape(count, 4).T.reshape(rows, 1)
 
     (normed,) = call(
-        norm_kernel, [shape((rows + 16, width), bf16)], [tokens, ln_gains, segments]
+        norm_kernel, [shape((rows + 16, width), bf16)], [after(tokens, first), ln_gains, segments],
+        [
+            pltpu.VMEM(tokens.shape, bf16),
+            pltpu.VMEM(ln_gains.shape, f32),
+            pltpu.VMEM(segments.shape, jnp.int32),
+            pltpu.SemaphoreType.DMA((3,)),
+        ],
+        space=pl.ANY,
     )
     along_x = swap(normed, "fsdp", 2)
     group_rows = [normed, along_x, swap(normed, "fsdp", 1), swap(along_x, "fsdp", 1)]
@@ -335,7 +333,7 @@
             shape((heads, group, group), bf16),
             shape((heads, group, 1), f32),
         ],
-        [me_cell, *group_rows, first, *first_z, *first_y],
+        [after(me_cell, theirs), *group_rows, first, *first_z, *first_y],
         [pltpu.VMEM((width, cols), bf16)] * 2,
         flops=4 * group * width * cols + 2 * group * group * cols,
         smem=1,
@@ -344,7 +342,7 @@
     keep, send = call(
         value_kernel,
         [shape((2 * rows, width), f32), shape((2 * rows, width), bf16)],
-        [me_cell, group_all, weights, totals, second, *second_z, *second_y],
+        [after(me_cell, merge_blocks[1]), group_all, weights, totals, second, *second_z, *second_y],
         [pltpu.VMEM((width, cols), bf16)] * 2,
         flops=4 * group * width * cols + 2 * group * group * cols,
         smem=1,
@@ -352,22 +350,30 @@
     from_core = swap(send, "fsdp", 1)
     (onward,) = call(pass_kernel, [shape((rows, width), bf16)], [keep, from_core])
     from_chip = swap(onward, "fsdp", 2)
-    slices = call(
+    (slices,) = call(
         layer_kernel,
-        [shape((rows, width // 4), bf16)] * 4,
-        [at_cell, tokens, keep, from_core, from_chip, ln_gains, order],
-        [pltpu.VMEM((4, rows, width // 4), bf16)],
+        [shape((8, rows // 2, width // 2), bf16)],
+        [tokens, keep, from_core, after(from_chip, merge_blocks[2]), ln_gains, order],
         flops=2 * rows * rows * width,
-        smem=1,
-    )
-    inputs = [slices[0]] + [swap(slices[k], "fsdp", k) for k in range(1, 4)]
-    inputs += [across(slices[k], k) for k in range(4)]
+    )
+    both = 2 * n_fsdp
+    inputs = lax.all_to_all(
+        slices,
+        ("dp", "fsdp"),
+        split_axis=0,
+        concat_axis=0,
+        tiled=True,
+        axis_index_groups=[
+            list(range(i, i + both)) for i in range(0, n_dp * n_fsdp, both)
+        ],
+    )
     shares = call(
         merge_kernel,
         [shape((2 * count, half), f32)] + [shape((2 * count, half), bf16)] * 3,
-        [me_cell, *inputs, *merge_blocks],
+        [me_cell, at_cell, inputs, *merge_blocks],
+        [pltpu.VMEM((8, count, half), f32)],
         flops=2 * 8 * count * width * half,
-        smem=1,
+        smem=2,
     )
     got = [swap(shares[k], "fsdp", k) for k in range(1, 4)]
     (packed,) = call(

time: 149 us -> 137 us (0.919)
  starting transfers between devices: 50.2 us -> 28.3 us
  waiting for transfers between devices: 61.9 us -> 74.4 us
  local copies, waits for them, and re-layouts: 14 us -> 6.32 us
  other arithmetic: 2.18 us -> 4.99 us
    ppermute x21 -> x27, waiting for transfers between devices: 19.3 us -> 74.4 us  [swap(): lax.ppermute(value, axis, [(i, i ^ k) for i in range(lax.axis_size(axis))])]
    ppermute x13 -> x0, waiting for transfers between devices: 42.6 us -> none  [the longest x9 37.8 us: turn(): return lax.ppermute(value, 'dp', [(i, (i + 2 * k) % n) for i in range(n)])]
    ppermute x13 -> x0, starting transfers between devices: 32.1 us -> none  [the longest x9 25.8 us: turn(): return lax.ppermute(value, 'dp', [(i, (i + 2 * k) % n) for i in range(n)])]
    unnamed x41 -> x17, local copies, waits for them, and re-layouts: 12.1 us -> 3.7 us
    ppermute x21 -> x27, starting transfers between devices: 18.1 us -> 24.8 us  [swap(): lax.ppermute(value, axis, [(i, i ^ k) for i in range(lax.axis_size(axis))])]
    all_to_all x0 -> x1, starting transfers between devices: none -> 3.54 us  [by_permutes(): lax.all_to_all(slices, ('dp', 'fsdp'), split_axis=0, concat_axis=0, tiled...]
  transfers between devices with their start and end apart: 34 -> 28, of which waited for: 13 -> 12; matrix products, arithmetic and copies ran while one was open for 3% -> 5% of each run, Pallas kernels for 3% -> 5%
where the time goes in v3:
time: 137 us; the launch traced here: 136 us
  waiting for transfers between devices  74.4 us (54%)
  starting transfers between devices  28.3 us (21%)
  blocking collectives  11.4 us (8%)
  Pallas kernels  10.6 us (8%)
  local copies, waits for them, and re-layouts  6.32 us (5%)
  other arithmetic  4.99 us (4%)
    ppermute x27, waiting for transfers between devices, swap(): lax.ppermute(value, axis, [(i, i ^ k) for i in range(lax.axis_size(axis))])  74.4 us
    ppermute x27, starting transfers between devices, swap(): lax.ppermute(value, axis, [(i, i ^ k) for i in range(lax.axis_size(axis))])  24.8 us
    all_to_all x1, blocking collectives, by_permutes(): lax.all_to_all(packed.reshape(n_dp, 2 * capacity, half), 'dp', split_axis...  11.4 us
    pallas_call x7, Pallas kernels, call(): pl.pallas_call(kernel, out_shape=tuple(outs), in_specs=specs, out_specs=t...  10.6 us
    unnamed x17, local copies, waits for them, and re-layouts  3.7 us
    all_to_all x1, starting transfers between devices, by_permutes(): lax.all_to_all(slices, ('dp', 'fsdp'), split_axis=0, concat_axis=0, tiled...  3.54 us
  transfers between devices with their start and end apart: 28, of which 12 were waited for; matrix products, arithmetic and copies ran while one was open for 5% of the time, Pallas kernels for 5%

profile of v3, /device:TPU:0, one launch (start us, length us, event | category | flops | bytes accessed | tf_op | source)
XLA Modules:
  0.0 136.2 jit_solution(9302163511705386442)
XLA Ops:
  0.0 1.0 slice.14.refs_4_
  1.0 3.0 %collective-permute-start.1 = (bf16[2,160,320]{2,1,0:T(8,128)(2,1)S(1)}, bf16[2,160,320]{2,1,0:T(8,128)(2,1)S(1)}, u32[]{:S(2)}, u32[]{:S(2)}) collective-permute-start(bf16[2,160,320]{2,1,0:T(8,128)(2,1)S(1)} %slice.14.refs_4_), channel_id=1, source_target_pairs={{0,4},{4,0},{8,12},{12,8},{16,20},{20,16},{24,28},{28,24},{1,5},{5... | collective-permute-start | bytes 614408 | tf_op jit(solution)/shard_map/ppermute | solution.py:107
  4.1 2.6 %collective-permute-start.9 = (bf16[2,160,320]{2,1,0:T(8,128)(2,1)S(1)}, bf16[2,160,320]{2,1,0:T(8,128)(2,1)S(1)}, u32[]{:S(2)}, u32[]{:S(2)}) collective-permute-start(bf16[2,160,320]{2,1,0:T(8,128)(2,1)S(1)} %slice.14.refs_4_), channel_id=1, source_target_pairs={{0,16},{4,20},{8,24},{12,28},{16,0},{20,4},{24,8},{28,12},{1,17},{... | collective-permute-start | bytes 614408 | tf_op jit(solution)/shard_map/ppermute | solution.py:107
  6.6 1.0 copy-done
  9.4 1.6 %collective-permute-start.6 = (bf16[144,1280]{1,0:T(8,128)(2,1)S(1)}, bf16[144,1280]{1,0:T(8,128)(2,1)S(1)}, u32[]{:S(2)}, u32[]{:S(2)}) collective-permute-start(bf16[144,1280]{1,0:T(8,128)(2,1)S(1)} %shard_map.82.refs_0_), channel_id=1, source_target_pairs={{0,2},{1,3},{2,0},{3,1},{4,6},{5,7},{6,4},{7,5},{8,10},{9,11},{10,... | collective-permute-start | bytes 1105928 | tf_op jit(solution)/shard_map/ppermute | solution.py:107
  10.9 1.6 %collective-permute-start.3 = (bf16[2,160,320]{2,1,0:T(8,128)(2,1)S(1)}, bf16[2,160,320]{2,1,0:T(8,128)(2,1)S(1)}, u32[]{:S(2)}, u32[]{:S(2)}) collective-permute-start(bf16[2,160,320]{2,1,0:T(8,128)(2,1)S(1)} %slice.14.refs_4_), channel_id=1, source_target_pairs={{0,8},{4,12},{8,0},{12,4},{16,24},{20,28},{24,16},{28,20},{1,9},{5... | collective-permute-start | bytes 614408 | tf_op jit(solution)/shard_map/ppermute | solution.py:107
  12.5 1.1 broadcast_select_fusion.1
  14.2 8.7 %collective-permute-done.3.refs_5_ = bf16[2,160,320]{2,1,0:T(8,128)(2,1)S(1)} collective-permute-done((bf16[2,160,320]{2,1,0:T(8,128)(2,1)S(1)}, bf16[2,160,320]{2,1,0:T(8,128)(2,1)S(1)}, u32[]{:S(2)}, u32[]{:S(2)}) %collective-permute-start.3) | collective-permute-done | bytes 204832 | tf_op jit(solution)/shard_map/ppermute | solution.py:107
  22.9 1.0 collective-permute-start.4
  23.9 2.5 %collective-permute-start.10 = (bf16[2,160,320]{2,1,0:T(8,128)(2,1)S(1)}, bf16[2,160,320]{2,1,0:T(8,128)(2,1)S(1)}, u32[]{:S(2)}, u32[]{:S(2)}) collective-permute-start(bf16[2,160,320]{2,1,0:T(8,128)(2,1)S(1)} %collective-permute-done.9.refs_6_), channel_id=1, source_target_pairs={{0,8},{4,12},{8,0},{12,4},{16,24},{20,28},{24,16},{28,20},{1,9},{5... | collective-permute-start | bytes 614408 | tf_op jit(solution)/shard_map/ppermute | solution.py:107
  26.9 1.5 %collective-permute-start.12 = (bf16[2,160,320]{2,1,0:T(8,128)(2,1)S(1)}, bf16[2,160,320]{2,1,0:T(8,128)(2,1)S(1)}, u32[]{:S(2)}, u32[]{:S(2)}) collective-permute-start(bf16[2,160,320]{2,1,0:T(8,128)(2,1)S(1)} %collective-permute-done.9.refs_6_), channel_id=1, source_target_pairs={{0,4},{4,0},{8,12},{12,8},{16,20},{20,16},{24,28},{28,24},{1,5},{5... | collective-permute-start | bytes 614408 | tf_op jit(solution)/shard_map/ppermute | solution.py:107
  28.4 8.6 %collective-permute-done.4.refs_5_ = bf16[2,160,320]{2,1,0:T(8,128)(2,1)S(1)} collective-permute-done((bf16[2,160,320]{2,1,0:T(8,128)(2,1)S(1)}, bf16[2,160,320]{2,1,0:T(8,128)(2,1)S(1)}, u32[]{:S(2)}, u32[]{:S(2)}) %collective-permute-start.4) | collective-permute-done | bytes 204832 | tf_op jit(solution)/shard_map/ppermute | solution.py:107
  37.2 2.0 %collective-permute-start.5 = (bf16[320,640]{1,0:T(8,128)(2,1)S(1)}, bf16[320,640]{1,0:T(8,128)(2,1)S(1)}, u32[]{:S(2)}, u32[]{:S(2)}) collective-permute-start(bf16[320,640]{1,0:T(8,128)(2,1)S(1)} %pad_maximum_fusion.refs_0_), channel_id=1, source_target_pairs={{0,8},{4,12},{8,0},{12,4},{16,24},{20,28},{24,16},{28,20},{1,9},{5... | collective-permute-start | bytes 1228808 | tf_op jit(solution)/shard_map/ppermute | solution.py:107
  39.8 6.1 %collective-permute-done.14.refs_4_ = bf16[2,160,320]{2,1,0:T(8,128)(2,1)S(1)} collective-permute-done((bf16[2,160,320]{2,1,0:T(8,128)(2,1)S(1)}, bf16[2,160,320]{2,1,0:T(8,128)(2,1)S(1)}, u32[]{:S(2)}, u32[]{:S(2)}) %collective-permute-start.14) | collective-permute-done | bytes 204832 | tf_op jit(solution)/shard_map/ppermute | solution.py:107
  47.0 0.9 collective-permute-start.18
  47.9 11.6 %collective-permute-done.15.refs_6_ = bf16[2,160,320]{2,1,0:T(8,128)(2,1)S(1)} collective-permute-done((bf16[2,160,320]{2,1,0:T(8,128)(2,1)S(1)}, bf16[2,160,320]{2,1,0:T(8,128)(2,1)S(1)}, u32[]{:S(2)}, u32[]{:S(2)}) %collective-permute-start.15) | collective-permute-done | bytes 204832 | tf_op jit(solution)/shard_map/ppermute | solution.py:107
  60.1 1.5 %collective-permute-start.19 = (bf16[2,160,320]{2,1,0:T(8,128)(2,1)S(1)}, bf16[2,160,320]{2,1,0:T(8,128)(2,1)S(1)}, u32[]{:S(2)}, u32[]{:S(2)}) collective-permute-start(bf16[2,160,320]{2,1,0:T(8,128)(2,1)S(1)} %collective-permute-done.15.refs_6_), channel_id=1, source_target_pairs={{0,4},{4,0},{8,12},{12,8},{16,20},{20,16},{24,28},{28,24},{1,5},{5... | collective-permute-start | bytes 614408 | tf_op jit(solution)/shard_map/ppermute | solution.py:107
  61.6 3.0 %shard_map.83 = (bf16[512,1280]{1,0:T(8,128)(2,1)S(1)}, bf16[4,512,512]{2,1,0:T(8,128)(2,1)S(1)}, f32[4,512,1]{2,1,0:T(8,128)S(1)}) custom-call(s32[1]{0:T(128)} %bitcast.3.me_ref, bf16[144,1280]{1,0:T(8,128)(2,1)S(1)} %shard_map.82.refs_0_, bf16[144,1280]{1,0:T(8,128)(2,1)S(1)} %collective-permute-done.6.refs_1_, ...), custom_call_target="tpu_custom_call" | custom-call | flops 1006632960 | bytes 6529028 | tf_op jit(solution)/shard_map/pallas_call | solution.py:129
  64.7 3.7 %collective-permute-done.17.refs_8_ = bf16[2,160,320]{2,1,0:T(8,128)(2,1)S(1)} collective-permute-done((bf16[2,160,320]{2,1,0:T(8,128)(2,1)S(1)}, bf16[2,160,320]{2,1,0:T(8,128)(2,1)S(1)}, u32[]{:S(2)}, u32[]{:S(2)}) %collective-permute-start.17) | collective-permute-done | bytes 204832 | tf_op jit(solution)/shard_map/ppermute | solution.py:107
  68.4 4.0 %collective-permute-done.19.refs_10_ = bf16[2,160,320]{2,1,0:T(8,128)(2,1)S(1)} collective-permute-done((bf16[2,160,320]{2,1,0:T(8,128)(2,1)S(1)}, bf16[2,160,320]{2,1,0:T(8,128)(2,1)S(1)}, u32[]{:S(2)}, u32[]{:S(2)}) %collective-permute-start.19) | collective-permute-done | bytes 204832 | tf_op jit(solution)/shard_map/ppermute | solution.py:107
  72.5 2.5 %shard_map.84 = (f32[256,1280]{1,0:T(8,128)S(1)}, bf16[256,1280]{1,0:T(8,128)(2,1)S(1)}) custom-call(s32[1]{0:T(128)} %bitcast.3.me_ref, bf16[512,1280]{1,0:T(8,128)(2,1)S(1)} %get-tuple-element.27.refs_0_, bf16[4,512,512]{2,1,0:T(8,128)(2,1)S(1)} %get-tuple-element.28.refs_1_, f32[4,512,1]{2,1,0:T(8,128)S(1)} %get-tuple-element.29.refs_2_, ...), custom_call_target="tpu_custom_call" | custom-call | flops 1006632960 | bytes 7020548 | tf_op jit(solution)/shard_map/pallas_call | solution.py:129
  75.8 1.4 %collective-permute-done.20.got_ref.core_ref = bf16[256,1280]{1,0:T(8,128)(2,1)S(1)} collective-permute-done((bf16[256,1280]{1,0:T(8,128)(2,1)S(1)}, bf16[256,1280]{1,0:T(8,128)(2,1)S(1)}, u32[]{:S(2)}, u32[]{:S(2)}) %collective-permute-start.20) | collective-permute-done | bytes 655392 | tf_op jit(solution)/shard_map/ppermute | solution.py:107
  81.1 15.4 %collective-permute-done.22.refs_2_ = bf16[320,640]{1,0:T(8,128)(2,1)S(1)} collective-permute-done((bf16[320,640]{1,0:T(8,128)(2,1)S(1)}, bf16[320,640]{1,0:T(8,128)(2,1)S(1)}, u32[]{:S(2)}, u32[]{:S(2)}) %collective-permute-start.22) | collective-permute-done | bytes 409632 | tf_op jit(solution)/shard_map/ppermute | solution.py:107
  97.4 2.6 %shard_map.86 = bf16[8,64,640]{2,1,0:T(8,128)(2,1)} custom-call(bf16[128,1280]{1,0:T(8,128)(2,1)S(1)} %copy-done.1, f32[256,1280]{1,0:T(8,128)S(1)} %get-tuple-element.30.keep_ref, bf16[256,1280]{1,0:T(8,128)(2,1)S(1)} %collective-permute-done.20.got_ref.core_ref, bf16[128,1280]{1,0:T(8,128)(2,1)} %collective-permute-done.21.chip_ref, ...), custom_call_target="tpu_custom_call" | custom-call | flops 41943040 | bytes 3287552 | tf_op jit(solution)/shard_map/pallas_call | solution.py:129
  100.0 3.5 %all-to-all-start = ((bf16[8,64,640]{2,1,0:T(8,128)(2,1)}), bf16[8,64,640]{2,1,0:T(8,128)(2,1)S(1)}, u32[]{:S(2)}, u32[]{:S(2)}) async-start(bf16[8,64,640]{2,1,0:T(8,128)(2,1)} %shard_map.86), calls=%async_computation | async-start | bytes 1310720 | tf_op jit(solution)/shard_map/all_to_all | solution.py:360
  103.6 0.9 convert_reduce_fusion.1
  106.8 9.6 %collective-permute-done.23.refs_3_ = bf16[320,640]{1,0:T(8,128)(2,1)S(1)} collective-permute-done((bf16[320,640]{1,0:T(8,128)(2,1)S(1)}, bf16[320,640]{1,0:T(8,128)(2,1)S(1)}, u32[]{:S(2)}, u32[]{:S(2)}) %collective-permute-start.23) | collective-permute-done | bytes 409632 | tf_op jit(solution)/shard_map/ppermute | solution.py:107
  116.4 1.0 shard_map.87
  117.5 1.7 %collective-permute-start.25 = (bf16[64,640]{1,0:T(8,128)(2,1)S(1)}, bf16[64,640]{1,0:T(8,128)(2,1)S(1)}, u32[]{:S(2)}, u32[]{:S(2)}) collective-permute-start(bf16[64,640]{1,0:T(8,128)(2,1)S(1)} %get-tuple-element.35), channel_id=1, source_target_pairs={{0,2},{1,3},{2,0},{3,1},{4,6},{5,7},{6,4},{7,5},{8,10},{9,11},{10,... | collective-permute-start | bytes 245768 | tf_op jit(solution)/shard_map/ppermute | solution.py:107
  119.4 3.1 %collective-permute-done.25.two_ref = bf16[64,640]{1,0:T(8,128)(2,1)S(1)} collective-permute-done((bf16[64,640]{1,0:T(8,128)(2,1)S(1)}, bf16[64,640]{1,0:T(8,128)(2,1)S(1)}, u32[]{:S(2)}, u32[]{:S(2)}) %collective-permute-start.25) | collective-permute-done | bytes 81952 | tf_op jit(solution)/shard_map/ppermute | solution.py:107
  122.5 1.4 %collective-permute-done.26.three_ref = bf16[64,640]{1,0:T(8,128)(2,1)S(1)} collective-permute-done((bf16[64,640]{1,0:T(8,128)(2,1)S(1)}, bf16[64,640]{1,0:T(8,128)(2,1)S(1)}, u32[]{:S(2)}, u32[]{:S(2)}) %collective-permute-start.26) | collective-permute-done | bytes 81952 | tf_op jit(solution)/shard_map/ppermute | solution.py:107
  124.1 11.4 %all_to_all.10 = bf16[8,16,640]{2,1,0:T(8,128)(2,1)S(1)} all-to-all(bf16[8,16,640]{2,1,0:T(8,128)(2,1)S(1)} %bitcast.17), channel_id=1, replica_groups=mesh['dp'=8,'fsdp'=4] {'dp'}, dimensions={0} | all-to-all | bytes 327680 | tf_op jit(solution)/shard_map/all_to_all | solution.py:385
  (65 shorter events, 14.3 us)
Async XLA Ops:
  0.0 14.2 %slice-start = ((bf16[3,160,320]{2,1,0:T(8,128)(2,1)}), bf16[1,160,320]{2,1,0:T(8,128)(2,1)S(1)}, s32[]{:S(2)}) async-start(bf16[3,160,320]{2,1,0:T(8,128)(2,1)} %param.9), calls=%async_computation.2 | async-start | bytes 245760 | tf_op jit(solution)/shard_map/slice | solution.py:289
  0.0 14.2 %copy-start.6 = (bf16[320,160]{0,1:T(8,128)(2,1)S(1)}, bf16[320,160]{0,1:T(8,128)(2,1)}, u32[]{:S(2)}) copy-start(bf16[320,160]{0,1:T(8,128)(2,1)} %param.10) | copy-start | bytes 307204
  1.0 12.6 %collective-permute-start.1 = (bf16[2,160,320]{2,1,0:T(8,128)(2,1)S(1)}, bf16[2,160,320]{2,1,0:T(8,128)(2,1)S(1)}, u32[]{:S(2)}, u32[]{:S(2)}) collective-permute-start(bf16[2,160,320]{2,1,0:T(8,128)(2,1)S(1)} %slice.14.refs_4_), channel_id=1, source_target_pairs={{0,4},{4,0},{8,12},{12,8},{16,20},{20,16},{24,28},{28,24},{1,5},{5... | collective-permute-start | bytes 614408 | tf_op jit(solution)/shard_map/ppermute | solution.py:107
  4.1 19.9 %collective-permute-start.9 = (bf16[2,160,320]{2,1,0:T(8,128)(2,1)S(1)}, bf16[2,160,320]{2,1,0:T(8,128)(2,1)S(1)}, u32[]{:S(2)}, u32[]{:S(2)}) collective-permute-start(bf16[2,160,320]{2,1,0:T(8,128)(2,1)S(1)} %slice.14.refs_4_), channel_id=1, source_target_pairs={{0,16},{4,20},{8,24},{12,28},{16,0},{20,4},{24,8},{28,12},{1,17},{... | collective-permute-start | bytes 614408 | tf_op jit(solution)/shard_map/ppermute | solution.py:107
  9.4 17.0 %collective-permute-start.6 = (bf16[144,1280]{1,0:T(8,128)(2,1)S(1)}, bf16[144,1280]{1,0:T(8,128)(2,1)S(1)}, u32[]{:S(2)}, u32[]{:S(2)}) collective-permute-start(bf16[144,1280]{1,0:T(8,128)(2,1)S(1)} %shard_map.82.refs_0_), channel_id=1, source_target_pairs={{0,2},{1,3},{2,0},{3,1},{4,6},{5,7},{6,4},{7,5},{8,10},{9,11},{10,... | collective-permute-start | bytes 1105928 | tf_op jit(solution)/shard_map/ppermute | solution.py:107
  10.9 26.1 %collective-permute-start.7 = (bf16[144,1280]{1,0:T(8,128)(2,1)S(1)}, bf16[144,1280]{1,0:T(8,128)(2,1)S(1)}, u32[]{:S(2)}, u32[]{:S(2)}) collective-permute-start(bf16[144,1280]{1,0:T(8,128)(2,1)S(1)} %shard_map.82.refs_0_), channel_id=1, source_target_pairs={{0,1},{1,0},{2,3},{3,2},{4,5},{5,4},{6,7},{7,6},{8,9},{9,8},{10,11... | collective-permute-start | bytes 1105928 | tf_op jit(solution)/shard_map/ppermute | solution.py:107
  10.9 12.0 %collective-permute-start.3 = (bf16[2,160,320]{2,1,0:T(8,128)(2,1)S(1)}, bf16[2,160,320]{2,1,0:T(8,128)(2,1)S(1)}, u32[]{:S(2)}, u32[]{:S(2)}) collective-permute-start(bf16[2,160,320]{2,1,0:T(8,128)(2,1)S(1)} %slice.14.refs_4_), channel_id=1, source_target_pairs={{0,8},{4,12},{8,0},{12,4},{16,24},{20,28},{24,16},{28,20},{1,9},{5... | collective-permute-start | bytes 614408 | tf_op jit(solution)/shard_map/ppermute | solution.py:107
  13.6 13.3 %collective-permute-start.2 = (bf16[160,640]{1,0:T(8,128)(2,1)S(1)}, bf16[160,640]{1,0:T(8,128)(2,1)S(1)}, u32[]{:S(2)}, u32[]{:S(2)}) collective-permute-start(bf16[160,640]{1,0:T(8,128)(2,1)S(1)} %get-tuple-element.21), channel_id=1, source_target_pairs={{0,4},{4,0},{8,12},{12,8},{16,20},{20,16},{24,28},{28,24},{1,5},{5... | collective-permute-start | bytes 614408 | tf_op jit(solution)/shard_map/ppermute | solution.py:107
  22.9 14.1 %collective-permute-start.4 = (bf16[2,160,320]{2,1,0:T(8,128)(2,1)S(1)}, bf16[2,160,320]{2,1,0:T(8,128)(2,1)S(1)}, u32[]{:S(2)}, u32[]{:S(2)}) collective-permute-start(bf16[2,160,320]{2,1,0:T(8,128)(2,1)S(1)} %pad_maximum_fusion.1.refs_3_), channel_id=1, source_target_pairs={{0,16},{4,20},{8,24},{12,28},{16,0},{20,4},{24,8},{28,12},{1,17},{... | collective-permute-start | bytes 614408 | tf_op jit(solution)/shard_map/ppermute | solution.py:107
  23.9 13.3 %collective-permute-start.10 = (bf16[2,160,320]{2,1,0:T(8,128)(2,1)S(1)}, bf16[2,160,320]{2,1,0:T(8,128)(2,1)S(1)}, u32[]{:S(2)}, u32[]{:S(2)}) collective-permute-start(bf16[2,160,320]{2,1,0:T(8,128)(2,1)S(1)} %collective-permute-done.9.refs_6_), channel_id=1, source_target_pairs={{0,8},{4,12},{8,0},{12,4},{16,24},{20,28},{24,16},{28,20},{1,9},{5... | collective-permute-start | bytes 614408 | tf_op jit(solution)/shard_map/ppermute | solution.py:107
  26.4 12.8 %collective-permute-start.11 = (bf16[2,160,320]{2,1,0:T(8,128)(2,1)S(1)}, bf16[2,160,320]{2,1,0:T(8,128)(2,1)S(1)}, u32[]{:S(2)}, u32[]{:S(2)}) collective-permute-start(bf16[2,160,320]{2,1,0:T(8,128)(2,1)S(1)} %collective-permute-done.3.refs_5_), channel_id=1, source_target_pairs={{0,4},{4,0},{8,12},{12,8},{16,20},{20,16},{24,28},{28,24},{1,5},{5... | collective-permute-start | bytes 614408 | tf_op jit(solution)/shard_map/ppermute | solution.py:107
  26.9 12.8 %collective-permute-start.12 = (bf16[2,160,320]{2,1,0:T(8,128)(2,1)S(1)}, bf16[2,160,320]{2,1,0:T(8,128)(2,1)S(1)}, u32[]{:S(2)}, u32[]{:S(2)}) collective-permute-start(bf16[2,160,320]{2,1,0:T(8,128)(2,1)S(1)} %collective-permute-done.9.refs_6_), channel_id=1, source_target_pairs={{0,4},{4,0},{8,12},{12,8},{16,20},{20,16},{24,28},{28,24},{1,5},{5... | collective-permute-start | bytes 614408 | tf_op jit(solution)/shard_map/ppermute | solution.py:107
  37.0 23.1 %collective-permute-start.8 = (bf16[144,1280]{1,0:T(8,128)(2,1)S(1)}, bf16[144,1280]{1,0:T(8,128)(2,1)S(1)}, u32[]{:S(2)}, u32[]{:S(2)}) collective-permute-start(bf16[144,1280]{1,0:T(8,128)(2,1)S(1)} %collective-permute-done.6.refs_1_), channel_id=1, source_target_pairs={{0,1},{1,0},{2,3},{3,2},{4,5},{5,4},{6,7},{7,6},{8,9},{9,8},{10,11... | collective-permute-start | bytes 1105928 | tf_op jit(solution)/shard_map/ppermute | solution.py:107
  37.1 8.8 %collective-permute-start.14 = (bf16[2,160,320]{2,1,0:T(8,128)(2,1)S(1)}, bf16[2,160,320]{2,1,0:T(8,128)(2,1)S(1)}, u32[]{:S(2)}, u32[]{:S(2)}) collective-permute-start(bf16[2,160,320]{2,1,0:T(8,128)(2,1)S(1)} %pad_maximum_fusion.1.refs_3_), channel_id=1, source_target_pairs={{0,8},{4,12},{8,0},{12,4},{16,24},{20,28},{24,16},{28,20},{1,9},{5... | collective-permute-start | bytes 614408 | tf_op jit(solution)/shard_map/ppermute | solution.py:107
  37.2 27.5 %collective-permute-start.5 = (bf16[320,640]{1,0:T(8,128)(2,1)S(1)}, bf16[320,640]{1,0:T(8,128)(2,1)S(1)}, u32[]{:S(2)}, u32[]{:S(2)}) collective-permute-start(bf16[320,640]{1,0:T(8,128)(2,1)S(1)} %pad_maximum_fusion.refs_0_), channel_id=1, source_target_pairs={{0,8},{4,12},{8,0},{12,4},{16,24},{20,28},{24,16},{28,20},{1,9},{5... | collective-permute-start | bytes 1228808 | tf_op jit(solution)/shard_map/ppermute | solution.py:107
  39.2 7.8 %collective-permute-start.13 = (bf16[2,160,320]{2,1,0:T(8,128)(2,1)S(1)}, bf16[2,160,320]{2,1,0:T(8,128)(2,1)S(1)}, u32[]{:S(2)}, u32[]{:S(2)}) collective-permute-start(bf16[2,160,320]{2,1,0:T(8,128)(2,1)S(1)} %collective-permute-done.10.refs_7_), channel_id=1, source_target_pairs={{0,4},{4,0},{8,12},{12,8},{16,20},{20,16},{24,28},{28,24},{1,5},{5... | collective-permute-start | bytes 614408 | tf_op jit(solution)/shard_map/ppermute | solution.py:107
  39.7 19.9 %collective-permute-start.15 = (bf16[2,160,320]{2,1,0:T(8,128)(2,1)S(1)}, bf16[2,160,320]{2,1,0:T(8,128)(2,1)S(1)}, u32[]{:S(2)}, u32[]{:S(2)}) collective-permute-start(bf16[2,160,320]{2,1,0:T(8,128)(2,1)S(1)} %collective-permute-done.4.refs_5_), channel_id=1, source_target_pairs={{0,8},{4,12},{8,0},{12,4},{16,24},{20,28},{24,16},{28,20},{1,9},{5... | collective-permute-start | bytes 614408 | tf_op jit(solution)/shard_map/ppermute | solution.py:107
  45.9 18.8 %collective-permute-start.16 = (bf16[2,160,320]{2,1,0:T(8,128)(2,1)S(1)}, bf16[2,160,320]{2,1,0:T(8,128)(2,1)S(1)}, u32[]{:S(2)}, u32[]{:S(2)}) collective-permute-start(bf16[2,160,320]{2,1,0:T(8,128)(2,1)S(1)} %pad_maximum_fusion.1.refs_3_), channel_id=1, source_target_pairs={{0,4},{4,0},{8,12},{12,8},{16,20},{20,16},{24,28},{28,24},{1,5},{5... | collective-permute-start | bytes 614408 | tf_op jit(solution)/shard_map/ppermute | solution.py:107
  47.0 17.7 %collective-permute-start.18 = (bf16[2,160,320]{2,1,0:T(8,128)(2,1)S(1)}, bf16[2,160,320]{2,1,0:T(8,128)(2,1)S(1)}, u32[]{:S(2)}, u32[]{:S(2)}) collective-permute-start(bf16[2,160,320]{2,1,0:T(8,128)(2,1)S(1)} %collective-permute-done.4.refs_5_), channel_id=1, source_target_pairs={{0,4},{4,0},{8,12},{12,8},{16,20},{20,16},{24,28},{28,24},{1,5},{5... | collective-permute-start | bytes 614408 | tf_op jit(solution)/shard_map/ppermute | solution.py:107
  59.6 8.9 %collective-permute-start.17 = (bf16[2,160,320]{2,1,0:T(8,128)(2,1)S(1)}, bf16[2,160,320]{2,1,0:T(8,128)(2,1)S(1)}, u32[]{:S(2)}, u32[]{:S(2)}) collective-permute-start(bf16[2,160,320]{2,1,0:T(8,128)(2,1)S(1)} %collective-permute-done.14.refs_4_), channel_id=1, source_target_pairs={{0,4},{4,0},{8,12},{12,8},{16,20},{20,16},{24,28},{28,24},{1,5},{5... | collective-permute-start | bytes 614408 | tf_op jit(solution)/shard_map/ppermute | solution.py:107
  60.1 12.4 %collective-permute-start.19 = (bf16[2,160,320]{2,1,0:T(8,128)(2,1)S(1)}, bf16[2,160,320]{2,1,0:T(8,128)(2,1)S(1)}, u32[]{:S(2)}, u32[]{:S(2)}) collective-permute-start(bf16[2,160,320]{2,1,0:T(8,128)(2,1)S(1)} %collective-permute-done.15.refs_6_), channel_id=1, source_target_pairs={{0,4},{4,0},{8,12},{12,8},{16,20},{20,16},{24,28},{28,24},{1,5},{5... | collective-permute-start | bytes 614408 | tf_op jit(solution)/shard_map/ppermute | solution.py:107
  75.0 21.6 %copy-start.1 = (bf16[128,1280]{1,0:T(8,128)(2,1)S(1)}, bf16[128,1280]{1,0:T(8,128)(2,1)}, u32[]{:S(2)}) copy-start(bf16[128,1280]{1,0:T(8,128)(2,1)} %tokens_ref.1) | copy-start | bytes 983044
  75.0 21.6 %copy-start.4 = (f32[2,1280]{1,0:T(2,128)S(1)}, f32[2,1280]{1,0:T(2,128)}, u32[]{:S(2)}) copy-start(f32[2,1280]{1,0:T(2,128)} %gains_ref.1) | copy-start | bytes 30724
  75.0 2.2 %collective-permute-start.20 = (bf16[256,1280]{1,0:T(8,128)(2,1)S(1)}, bf16[256,1280]{1,0:T(8,128)(2,1)S(1)}, u32[]{:S(2)}, u32[]{:S(2)}) collective-permute-start(bf16[256,1280]{1,0:T(8,128)(2,1)S(1)} %get-tuple-element.31), channel_id=1, source_target_pairs={{0,1},{1,0},{2,3},{3,2},{4,5},{5,4},{6,7},{7,6},{8,9},{9,8},{10,11... | collective-permute-start | bytes 1966088 | tf_op jit(solution)/shard_map/ppermute | solution.py:107
  75.1 21.5 %collective-permute-start.22 = (bf16[320,640]{1,0:T(8,128)(2,1)S(1)}, bf16[320,640]{1,0:T(8,128)(2,1)S(1)}, u32[]{:S(2)}, u32[]{:S(2)}) collective-permute-start(bf16[320,640]{1,0:T(8,128)(2,1)S(1)} %pad_maximum_fusion.refs_0_), channel_id=1, source_target_pairs={{0,16},{4,20},{8,24},{12,28},{16,0},{20,4},{24,8},{28,12},{1,17},{... | collective-permute-start | bytes 1228808 | tf_op jit(solution)/shard_map/ppermute | solution.py:107
  78.0 18.6 %collective-permute-start.21 = (bf16[128,1280]{1,0:T(8,128)(2,1)}, bf16[128,1280]{1,0:T(8,128)(2,1)}, u32[]{:S(2)}, u32[]{:S(2)}) collective-permute-start(bf16[128,1280]{1,0:T(8,128)(2,1)} %shard_map.85), channel_id=1, source_target_pairs={{0,2},{1,3},{2,0},{3,1},{4,6},{5,7},{6,4},{7,5},{8,10},{9,11},{10,... | collective-permute-start | bytes 983048 | tf_op jit(solution)/shard_map/ppermute | solution.py:107
  78.5 26.7 %collective-permute-start = (s32[32,1]{0,1:T(1,128)}, s32[32,1]{0,1:T(1,128)}, u32[]{:S(2)}, u32[]{:S(2)}) collective-permute-start(s32[32,1]{0,1:T(1,128)} %param.15), channel_id=1, source_target_pairs={{0,4},{4,0},{8,12},{12,8},{16,20},{20,16},{24,28},{28,24},{1,5},{5... | collective-permute-start | bytes 392 | tf_op jit(solution)/shard_map/ppermute | solution.py:107
  100.0 16.3 %all-to-all-start = ((bf16[8,64,640]{2,1,0:T(8,128)(2,1)}), bf16[8,64,640]{2,1,0:T(8,128)(2,1)S(1)}, u32[]{:S(2)}, u32[]{:S(2)}) async-start(bf16[8,64,640]{2,1,0:T(8,128)(2,1)} %shard_map.86), calls=%async_computation | async-start | bytes 1310720 | tf_op jit(solution)/shard_map/all_to_all | solution.py:360
  104.5 11.9 %collective-permute-start.23 = (bf16[320,640]{1,0:T(8,128)(2,1)S(1)}, bf16[320,640]{1,0:T(8,128)(2,1)S(1)}, u32[]{:S(2)}, u32[]{:S(2)}) collective-permute-start(bf16[320,640]{1,0:T(8,128)(2,1)S(1)} %collective-permute-done.22.refs_2_), channel_id=1, source_target_pairs={{0,8},{4,12},{8,0},{12,4},{16,24},{20,28},{24,16},{28,20},{1,9},{5... | collective-permute-start | bytes 1228808 | tf_op jit(solution)/shard_map/ppermute | solution.py:107
  117.4 2.0 %collective-permute-start.24 = (bf16[64,640]{1,0:T(8,128)(2,1)S(1)}, bf16[64,640]{1,0:T(8,128)(2,1)S(1)}, u32[]{:S(2)}, u32[]{:S(2)}) collective-permute-start(bf16[64,640]{1,0:T(8,128)(2,1)S(1)} %get-tuple-element.34), channel_id=1, source_target_pairs={{0,1},{1,0},{2,3},{3,2},{4,5},{5,4},{6,7},{7,6},{8,9},{9,8},{10,11... | collective-permute-start | bytes 245768 | tf_op jit(solution)/shard_map/ppermute | solution.py:107
  117.5 5.0 %collective-permute-start.25 = (bf16[64,640]{1,0:T(8,128)(2,1)S(1)}, bf16[64,640]{1,0:T(8,128)(2,1)S(1)}, u32[]{:S(2)}, u32[]{:S(2)}) collective-permute-start(bf16[64,640]{1,0:T(8,128)(2,1)S(1)} %get-tuple-element.35), channel_id=1, source_target_pairs={{0,2},{1,3},{2,0},{3,1},{4,6},{5,7},{6,4},{7,5},{8,10},{9,11},{10,... | collective-permute-start | bytes 245768 | tf_op jit(solution)/shard_map/ppermute | solution.py:107
  119.2 4.7 %collective-permute-start.26 = (bf16[64,640]{1,0:T(8,128)(2,1)S(1)}, bf16[64,640]{1,0:T(8,128)(2,1)S(1)}, u32[]{:S(2)}, u32[]{:S(2)}) collective-permute-start(bf16[64,640]{1,0:T(8,128)(2,1)S(1)} %get-tuple-element.36), channel_id=1, source_target_pairs={{0,3},{1,2},{2,1},{3,0},{4,7},{5,6},{6,5},{7,4},{8,11},{9,10},{10,... | collective-permute-start | bytes 245768 | tf_op jit(solution)/shard_map/ppermute | solution.py:107
  (5 other events, 7.7 us)

commit v4 on v3

--- a/solution.py
+++ b/solution.py
@@ -284,21 +284,36 @@
 
     first = qkv_weight[0:2]
     first_z = [swap(first, "dp", 2), swap(first, "dp", 4)]
+    (normed,) = call(
+        norm_kernel,
+        [shape((rows + 16, width), bf16)],
+        [after(tokens, first_z[0]), ln_gains, segments],
+        [
+            pltpu.VMEM(tokens.shape, bf16),
+            pltpu.VMEM(ln_gains.shape, f32),
+            pltpu.VMEM(segments.shape, jnp.int32),
+            pltpu.SemaphoreType.DMA((3,)),
+        ],
+        space=pltpu.HBM,
+    )
+    along_x = swap(normed, "fsdp", 2)
+    group_rows = [normed, along_x, swap(normed, "fsdp", 1), swap(along_x, "fsdp", 1)]
+
     first_y = [swap(first, "dp", 1)]
     first_z += [swap(first_z[1], "dp", 2)]
     second = jnp.concatenate([qkv_weight[2:3], out_weight.T[None]], axis=0)
     half = merge_weight.shape[1] // 2
     low, high = merge_weight[:, :half], merge_weight[:, half:]
     lower = y == 0
-    theirs = swap(after(jnp.where(lower, high, low), first_y[0]), "dp", 1)
-    held = after(second, first_z[0])
+    theirs = swap(after(jnp.where(lower, high, low), first_z[0]), "dp", 1)
+    held = after(second, first_z[1])
     second_z = [swap(held, "dp", 2), swap(held, "dp", 4)]
     second_y = [swap(held, "dp", 1)]
     second_z += [swap(second_z[1], "dp", 2)]
     first_y += [swap(block, "dp", 1) for block in first_z]
     second_y += [swap(block, "dp", 1) for block in second_z]
     pair = jnp.concatenate([jnp.where(lower, low, high), theirs], axis=0)
-    held = after(pair, second_z[1])
+    held = after(pair, (second_z[2], *first_y[:3], *group_rows[2:]))
     merge_blocks = [pair, swap(held, "dp", 2), swap(held, "dp", 4)]
     merge_blocks += [swap(merge_blocks[2], "dp", 2)]
 
@@ -311,19 +326,6 @@
         slots.append(start + rank + (y ^ number) * capacity)
     slots = jnp.concatenate(slots).reshape(1, 2 * count)
     order = merge_rows.reshape(count, 4).T.reshape(rows, 1)
-
-    (normed,) = call(
-        norm_kernel, [shape((rows + 16, width), bf16)], [after(tokens, first), ln_gains, segments],
-        [
-            pltpu.VMEM(tokens.shape, bf16),
-            pltpu.VMEM(ln_gains.shape, f32),
-            pltpu.VMEM(segments.shape, jnp.int32),
-            pltpu.SemaphoreType.DMA((3,)),
-        ],
-        space=pl.ANY,
-    )
-    along_x = swap(normed, "fsdp", 2)
-    group_rows = [normed, along_x, swap(normed, "fsdp", 1), swap(along_x, "fsdp", 1)]
 
     heads = cols // HD
     group_all, weights, totals = call(
@@ -342,7 +344,7 @@
     keep, send = call(
         value_kernel,
         [shape((2 * rows, width), f32), shape((2 * rows, width), bf16)],
-        [after(me_cell, merge_blocks[1]), group_all, weights, totals, second, *second_z, *second_y],
+        [me_cell, group_all, weights, totals, second, *second_z, *second_y],
         [pltpu.VMEM((width, cols), bf16)] * 2,
         flops=4 * group * width * cols + 2 * group * group * cols,
         smem=1,

time: 137 us -> 136 us (level)
  waiting for transfers between devices: 74.4 us -> 77.2 us
  other arithmetic: 4.99 us -> 2.23 us
  local copies, waits for them, and re-layouts: 6.32 us -> 4.89 us
    ppermute x27, waiting for transfers between devices: 74.4 us -> 77.2 us  [swap(): lax.ppermute(value, axis, [(i, i ^ k) for i in range(lax.axis_size(axis))])]
    reduce_sum x2, other arithmetic: 1.79 us -> 0.36 us  [slot_numbers(): jnp.sum((same & before).astype(jnp.int32), axis=1)]
  transfers between devices with their start and end apart: 28 -> 28, of which waited for: 12 -> 16; matrix products, arithmetic and copies ran while one was open for 5% -> 2% of each run, Pallas kernels for 5% -> 5%
where the time goes in v4:
time: 136 us; the launch traced here: 135 us
  waiting for transfers between devices  77.2 us (57%)
  starting transfers between devices  29.5 us (22%)
  blocking collectives  11.5 us (8%)
  Pallas kernels  9.88 us (7%)
  local copies, waits for them, and re-layouts  4.89 us (4%)
  other arithmetic  2.23 us (2%)
    ppermute x27, waiting for transfers between devices, swap(): lax.ppermute(value, axis, [(i, i ^ k) for i in range(lax.axis_size(axis))])  77.2 us
    ppermute x27, starting transfers between devices, swap(): lax.ppermute(value, axis, [(i, i ^ k) for i in range(lax.axis_size(axis))])  25.9 us
    all_to_all x1, blocking collectives, by_permutes(): lax.all_to_all(packed.reshape(n_dp, 2 * capacity, half), 'dp', split_axis...  11.5 us
    pallas_call x7, Pallas kernels, call(): pl.pallas_call(kernel, out_shape=tuple(outs), in_specs=specs, out_specs=t...  9.88 us
    all_to_all x1, starting transfers between devices, by_permutes(): lax.all_to_all(slices, ('dp', 'fsdp'), split_axis=0, concat_axis=0, tiled...  3.54 us
    unnamed x17, local copies, waits for them, and re-layouts  2.9 us
  transfers between devices with their start and end apart: 28, of which 16 were waited for; matrix products, arithmetic and copies ran while one was open for 2% of the time, Pallas kernels for 5%

profile of v4, /device:TPU:0, one launch (start us, length us, event | category | flops | bytes accessed | tf_op | source)
XLA Modules:
  0.0 135.4 jit_solution(10444474277722409674)
XLA Ops:
  1.0 3.1 %collective-permute-start.1 = (bf16[2,160,320]{2,1,0:T(8,128)(2,1)S(1)}, bf16[2,160,320]{2,1,0:T(8,128)(2,1)S(1)}, u32[]{:S(2)}, u32[]{:S(2)}) collective-permute-start(bf16[2,160,320]{2,1,0:T(8,128)(2,1)S(1)} %slice.14.refs_4_), channel_id=1, source_target_pairs={{0,8},{4,12},{8,0},{12,4},{16,24},{20,28},{24,16},{28,20},{1,9},{5... | collective-permute-start | bytes 614408 | tf_op jit(solution)/shard_map/ppermute | solution.py:107
  4.1 2.6 %collective-permute-start.6 = (bf16[2,160,320]{2,1,0:T(8,128)(2,1)S(1)}, bf16[2,160,320]{2,1,0:T(8,128)(2,1)S(1)}, u32[]{:S(2)}, u32[]{:S(2)}) collective-permute-start(bf16[2,160,320]{2,1,0:T(8,128)(2,1)S(1)} %slice.14.refs_4_), channel_id=1, source_target_pairs={{0,16},{4,20},{8,24},{12,28},{16,0},{20,4},{24,8},{28,12},{1,17},{... | collective-permute-start | bytes 614408 | tf_op jit(solution)/shard_map/ppermute | solution.py:107
  6.7 1.5 %collective-permute-start.8 = (bf16[2,160,320]{2,1,0:T(8,128)(2,1)S(1)}, bf16[2,160,320]{2,1,0:T(8,128)(2,1)S(1)}, u32[]{:S(2)}, u32[]{:S(2)}) collective-permute-start(bf16[2,160,320]{2,1,0:T(8,128)(2,1)S(1)} %slice.14.refs_4_), channel_id=1, source_target_pairs={{0,4},{4,0},{8,12},{12,8},{16,20},{20,16},{24,28},{28,24},{1,5},{5... | collective-permute-start | bytes 614408 | tf_op jit(solution)/shard_map/ppermute | solution.py:107
  8.2 7.0 %collective-permute-done.1.refs_5_ = bf16[2,160,320]{2,1,0:T(8,128)(2,1)S(1)} collective-permute-done((bf16[2,160,320]{2,1,0:T(8,128)(2,1)S(1)}, bf16[2,160,320]{2,1,0:T(8,128)(2,1)S(1)}, u32[]{:S(2)}, u32[]{:S(2)}) %collective-permute-start.1) | collective-permute-done | bytes 204832 | tf_op jit(solution)/shard_map/ppermute | solution.py:107
  18.0 1.7 %collective-permute-start.3 = (bf16[144,1280]{1,0:T(8,128)(2,1)S(1)}, bf16[144,1280]{1,0:T(8,128)(2,1)S(1)}, u32[]{:S(2)}, u32[]{:S(2)}) collective-permute-start(bf16[144,1280]{1,0:T(8,128)(2,1)S(1)} %shard_map.82.refs_0_), channel_id=1, source_target_pairs={{0,2},{1,3},{2,0},{3,1},{4,6},{5,7},{6,4},{7,5},{8,10},{9,11},{10,... | collective-permute-start | bytes 1105928 | tf_op jit(solution)/shard_map/ppermute | solution.py:107
  20.8 1.6 %collective-permute-start.2 = (bf16[160,640]{1,0:T(8,128)(2,1)S(1)}, bf16[160,640]{1,0:T(8,128)(2,1)S(1)}, u32[]{:S(2)}, u32[]{:S(2)}) collective-permute-start(bf16[160,640]{1,0:T(8,128)(2,1)S(1)} %get-tuple-element.20), channel_id=1, source_target_pairs={{0,4},{4,0},{8,12},{12,8},{16,20},{20,16},{24,28},{28,24},{1,5},{5... | collective-permute-start | bytes 614408 | tf_op jit(solution)/shard_map/ppermute | solution.py:107
  23.0 1.5 %collective-permute-start.9 = (bf16[2,160,320]{2,1,0:T(8,128)(2,1)S(1)}, bf16[2,160,320]{2,1,0:T(8,128)(2,1)S(1)}, u32[]{:S(2)}, u32[]{:S(2)}) collective-permute-start(bf16[2,160,320]{2,1,0:T(8,128)(2,1)S(1)} %collective-permute-done.1.refs_5_), channel_id=1, source_target_pairs={{0,4},{4,0},{8,12},{12,8},{16,20},{20,16},{24,28},{28,24},{1,5},{5... | collective-permute-start | bytes 614408 | tf_op jit(solution)/shard_map/ppermute | solution.py:107
  24.5 4.3 %collective-permute-done.2 = bf16[160,640]{1,0:T(8,128)(2,1)S(1)} collective-permute-done((bf16[160,640]{1,0:T(8,128)(2,1)S(1)}, bf16[160,640]{1,0:T(8,128)(2,1)S(1)}, u32[]{:S(2)}, u32[]{:S(2)}) %collective-permute-start.2) | collective-permute-done | bytes 204832 | tf_op jit(solution)/shard_map/ppermute | solution.py:107
  29.8 4.3 %collective-permute-done.10.refs_10_ = bf16[2,160,320]{2,1,0:T(8,128)(2,1)S(1)} collective-permute-done((bf16[2,160,320]{2,1,0:T(8,128)(2,1)S(1)}, bf16[2,160,320]{2,1,0:T(8,128)(2,1)S(1)}, u32[]{:S(2)}, u32[]{:S(2)}) %collective-permute-start.10) | collective-permute-done | bytes 204832 | tf_op jit(solution)/shard_map/ppermute | solution.py:107
  34.1 2.9 %collective-permute-done.9.refs_9_ = bf16[2,160,320]{2,1,0:T(8,128)(2,1)S(1)} collective-permute-done((bf16[2,160,320]{2,1,0:T(8,128)(2,1)S(1)}, bf16[2,160,320]{2,1,0:T(8,128)(2,1)S(1)}, u32[]{:S(2)}, u32[]{:S(2)}) %collective-permute-start.9) | collective-permute-done | bytes 204832 | tf_op jit(solution)/shard_map/ppermute | solution.py:107
  37.0 1.5 %collective-permute-start.11 = (bf16[2,160,320]{2,1,0:T(8,128)(2,1)S(1)}, bf16[2,160,320]{2,1,0:T(8,128)(2,1)S(1)}, u32[]{:S(2)}, u32[]{:S(2)}) collective-permute-start(bf16[2,160,320]{2,1,0:T(8,128)(2,1)S(1)} %collective-permute-done.7.refs_7_), channel_id=1, source_target_pairs={{0,4},{4,0},{8,12},{12,8},{16,20},{20,16},{24,28},{28,24},{1,5},{5... | collective-permute-start | bytes 614408 | tf_op jit(solution)/shard_map/ppermute | solution.py:107
  38.5 5.3 %collective-permute-done.12.refs_4_ = bf16[2,160,320]{2,1,0:T(8,128)(2,1)S(1)} collective-permute-done((bf16[2,160,320]{2,1,0:T(8,128)(2,1)S(1)}, bf16[2,160,320]{2,1,0:T(8,128)(2,1)S(1)}, u32[]{:S(2)}, u32[]{:S(2)}) %collective-permute-start.12) | collective-permute-done | bytes 204832 | tf_op jit(solution)/shard_map/ppermute | solution.py:107
  43.8 1.5 %collective-permute-start.15 = (bf16[2,160,320]{2,1,0:T(8,128)(2,1)S(1)}, bf16[2,160,320]{2,1,0:T(8,128)(2,1)S(1)}, u32[]{:S(2)}, u32[]{:S(2)}) collective-permute-start(bf16[2,160,320]{2,1,0:T(8,128)(2,1)S(1)} %pad_maximum_fusion.1.refs_3_), channel_id=1, source_target_pairs={{0,4},{4,0},{8,12},{12,8},{16,20},{20,16},{24,28},{28,24},{1,5},{5... | collective-permute-start | bytes 614408 | tf_op jit(solution)/shard_map/ppermute | solution.py:107
  45.8 1.5 %collective-permute-start.16 = (bf16[2,160,320]{2,1,0:T(8,128)(2,1)S(1)}, bf16[2,160,320]{2,1,0:T(8,128)(2,1)S(1)}, u32[]{:S(2)}, u32[]{:S(2)}) collective-permute-start(bf16[2,160,320]{2,1,0:T(8,128)(2,1)S(1)} %collective-permute-done.12.refs_4_), channel_id=1, source_target_pairs={{0,4},{4,0},{8,12},{12,8},{16,20},{20,16},{24,28},{28,24},{1,5},{5... | collective-permute-start | bytes 614408 | tf_op jit(solution)/shard_map/ppermute | solution.py:107
  48.2 3.1 %shard_map.83 = (bf16[512,1280]{1,0:T(8,128)(2,1)S(1)}, bf16[4,512,512]{2,1,0:T(8,128)(2,1)S(1)}, f32[4,512,1]{2,1,0:T(8,128)S(1)}) custom-call(s32[1]{0:T(128)} %bitcast.3.me_ref, bf16[144,1280]{1,0:T(8,128)(2,1)S(1)} %shard_map.82.refs_0_, bf16[144,1280]{1,0:T(8,128)(2,1)S(1)} %collective-permute-done.3.refs_1_, ...), custom_call_target="tpu_custom_call" | custom-call | flops 1006632960 | bytes 6529028 | tf_op jit(solution)/shard_map/pallas_call | solution.py:129
  51.2 1.5 %collective-permute-done.15.refs_7_ = bf16[2,160,320]{2,1,0:T(8,128)(2,1)S(1)} collective-permute-done((bf16[2,160,320]{2,1,0:T(8,128)(2,1)S(1)}, bf16[2,160,320]{2,1,0:T(8,128)(2,1)S(1)}, u32[]{:S(2)}, u32[]{:S(2)}) %collective-permute-start.15) | collective-permute-done | bytes 204832 | tf_op jit(solution)/shard_map/ppermute | solution.py:107
  52.7 5.3 %collective-permute-done.17.refs_9_ = bf16[2,160,320]{2,1,0:T(8,128)(2,1)S(1)} collective-permute-done((bf16[2,160,320]{2,1,0:T(8,128)(2,1)S(1)}, bf16[2,160,320]{2,1,0:T(8,128)(2,1)S(1)}, u32[]{:S(2)}, u32[]{:S(2)}) %collective-permute-start.17) | collective-permute-done | bytes 204832 | tf_op jit(solution)/shard_map/ppermute | solution.py:107
  58.0 3.7 %collective-permute-done.16.refs_8_ = bf16[2,160,320]{2,1,0:T(8,128)(2,1)S(1)} collective-permute-done((bf16[2,160,320]{2,1,0:T(8,128)(2,1)S(1)}, bf16[2,160,320]{2,1,0:T(8,128)(2,1)S(1)}, u32[]{:S(2)}, u32[]{:S(2)}) %collective-permute-start.16) | collective-permute-done | bytes 204832 | tf_op jit(solution)/shard_map/ppermute | solution.py:107
  61.6 2.6 %collective-permute-done.18.refs_10_ = bf16[2,160,320]{2,1,0:T(8,128)(2,1)S(1)} collective-permute-done((bf16[2,160,320]{2,1,0:T(8,128)(2,1)S(1)}, bf16[2,160,320]{2,1,0:T(8,128)(2,1)S(1)}, u32[]{:S(2)}, u32[]{:S(2)}) %collective-permute-start.18) | collective-permute-done | bytes 204832 | tf_op jit(solution)/shard_map/ppermute | solution.py:107
  64.3 2.5 %shard_map.84 = (f32[256,1280]{1,0:T(8,128)S(1)}, bf16[256,1280]{1,0:T(8,128)(2,1)S(1)}) custom-call(s32[1]{0:T(128)} %bitcast.3.me_ref, bf16[512,1280]{1,0:T(8,128)(2,1)S(1)} %get-tuple-element.23.refs_0_, bf16[4,512,512]{2,1,0:T(8,128)(2,1)S(1)} %get-tuple-element.24.refs_1_, f32[4,512,1]{2,1,0:T(8,128)S(1)} %get-tuple-element.25.refs_2_, ...), custom_call_target="tpu_custom_call" | custom-call | flops 1006632960 | bytes 7020548 | tf_op jit(solution)/shard_map/pallas_call | solution.py:129
  67.7 1.3 collective-permute-done.19.got_ref.core_ref
  69.8 1.4 %collective-permute-start = (s32[32,1]{0,1:T(1,128)S(1)}, s32[32,1]{0,1:T(1,128)S(1)}, u32[]{:S(2)}, u32[]{:S(2)}) collective-permute-start(s32[32,1]{0,1:T(1,128)S(1)} %copy-done.6), channel_id=1, source_target_pairs={{0,4},{4,0},{8,12},{12,8},{16,20},{20,16},{24,28},{28,24},{1,5},{5... | collective-permute-start | bytes 392 | tf_op jit(solution)/shard_map/ppermute | solution.py:107
  72.6 15.8 %collective-permute-done.21.refs_2_ = bf16[320,640]{1,0:T(8,128)(2,1)S(1)} collective-permute-done((bf16[320,640]{1,0:T(8,128)(2,1)S(1)}, bf16[320,640]{1,0:T(8,128)(2,1)S(1)}, u32[]{:S(2)}, u32[]{:S(2)}) %collective-permute-start.21) | collective-permute-done | bytes 409632 | tf_op jit(solution)/shard_map/ppermute | solution.py:107
  88.4 2.6 %shard_map.86 = bf16[8,64,640]{2,1,0:T(8,128)(2,1)} custom-call(bf16[128,1280]{1,0:T(8,128)(2,1)S(1)} %copy-done.1, f32[256,1280]{1,0:T(8,128)S(1)} %get-tuple-element.27.keep_ref, bf16[256,1280]{1,0:T(8,128)(2,1)S(1)} %collective-permute-done.19.got_ref.core_ref, bf16[128,1280]{1,0:T(8,128)(2,1)} %collective-permute-done.20.chip_ref, ...), custom_call_target="tpu_custom_call" | custom-call | flops 41943040 | bytes 3287552 | tf_op jit(solution)/shard_map/pallas_call | solution.py:129
  91.1 3.5 %all-to-all-start = ((bf16[8,64,640]{2,1,0:T(8,128)(2,1)}), bf16[8,64,640]{2,1,0:T(8,128)(2,1)S(1)}, u32[]{:S(2)}, u32[]{:S(2)}) async-start(bf16[8,64,640]{2,1,0:T(8,128)(2,1)} %shard_map.86), calls=%async_computation | async-start | bytes 1310720 | tf_op jit(solution)/shard_map/all_to_all | solution.py:362
  94.9 2.0 %collective-permute-start.23 = (bf16[320,640]{1,0:T(8,128)(2,1)S(1)}, bf16[320,640]{1,0:T(8,128)(2,1)S(1)}, u32[]{:S(2)}, u32[]{:S(2)}) collective-permute-start(bf16[320,640]{1,0:T(8,128)(2,1)S(1)} %collective-permute-done.21.refs_2_), channel_id=1, source_target_pairs={{0,8},{4,12},{8,0},{12,4},{16,24},{20,28},{24,16},{28,20},{1,9},{5... | collective-permute-start | bytes 1228808 | tf_op jit(solution)/shard_map/ppermute | solution.py:107
  97.1 10.0 %collective-permute-done.22.refs_1_ = bf16[320,640]{1,0:T(8,128)(2,1)S(1)} collective-permute-done((bf16[320,640]{1,0:T(8,128)(2,1)S(1)}, bf16[320,640]{1,0:T(8,128)(2,1)S(1)}, u32[]{:S(2)}, u32[]{:S(2)}) %collective-permute-start.22) | collective-permute-done | bytes 409632 | tf_op jit(solution)/shard_map/ppermute | solution.py:107
  107.1 8.3 %collective-permute-done.23.refs_3_ = bf16[320,640]{1,0:T(8,128)(2,1)S(1)} collective-permute-done((bf16[320,640]{1,0:T(8,128)(2,1)S(1)}, bf16[320,640]{1,0:T(8,128)(2,1)S(1)}, u32[]{:S(2)}, u32[]{:S(2)}) %collective-permute-start.23) | collective-permute-done | bytes 409632 | tf_op jit(solution)/shard_map/ppermute | solution.py:107
  116.6 1.7 %collective-permute-start.25 = (bf16[64,640]{1,0:T(8,128)(2,1)S(1)}, bf16[64,640]{1,0:T(8,128)(2,1)S(1)}, u32[]{:S(2)}, u32[]{:S(2)}) collective-permute-start(bf16[64,640]{1,0:T(8,128)(2,1)S(1)} %get-tuple-element.33), channel_id=1, source_target_pairs={{0,2},{1,3},{2,0},{3,1},{4,6},{5,7},{6,4},{7,5},{8,10},{9,11},{10,... | collective-permute-start | bytes 245768 | tf_op jit(solution)/shard_map/ppermute | solution.py:107
  118.5 3.1 %collective-permute-done.25.two_ref = bf16[64,640]{1,0:T(8,128)(2,1)S(1)} collective-permute-done((bf16[64,640]{1,0:T(8,128)(2,1)S(1)}, bf16[64,640]{1,0:T(8,128)(2,1)S(1)}, u32[]{:S(2)}, u32[]{:S(2)}) %collective-permute-start.25) | collective-permute-done | bytes 81952 | tf_op jit(solution)/shard_map/ppermute | solution.py:107
  121.6 1.4 %collective-permute-done.26.three_ref = bf16[64,640]{1,0:T(8,128)(2,1)S(1)} collective-permute-done((bf16[64,640]{1,0:T(8,128)(2,1)S(1)}, bf16[64,640]{1,0:T(8,128)(2,1)S(1)}, u32[]{:S(2)}, u32[]{:S(2)}) %collective-permute-start.26) | collective-permute-done | bytes 81952 | tf_op jit(solution)/shard_map/ppermute | solution.py:107
  123.2 11.5 %all_to_all.10 = bf16[8,16,640]{2,1,0:T(8,128)(2,1)S(1)} all-to-all(bf16[8,16,640]{2,1,0:T(8,128)(2,1)S(1)} %bitcast.17), channel_id=1, replica_groups=mesh['dp'=8,'fsdp'=4] {'dp'}, dimensions={0} | all-to-all | bytes 327680 | tf_op jit(solution)/shard_map/all_to_all | solution.py:387
  (65 shorter events, 13.5 us)
Async XLA Ops:
  0.0 22.3 %slice-start = ((bf16[3,160,320]{2,1,0:T(8,128)(2,1)}), bf16[1,160,320]{2,1,0:T(8,128)(2,1)S(1)}, s32[]{:S(2)}) async-start(bf16[3,160,320]{2,1,0:T(8,128)(2,1)} %param.9), calls=%async_computation.2 | async-start | bytes 245760 | tf_op jit(solution)/shard_map/slice | solution.py:304
  0.0 22.3 %copy-start.5 = (bf16[320,160]{0,1:T(8,128)(2,1)S(1)}, bf16[320,160]{0,1:T(8,128)(2,1)}, u32[]{:S(2)}) copy-start(bf16[320,160]{0,1:T(8,128)(2,1)} %param.10) | copy-start | bytes 307204
  1.0 14.2 %collective-permute-start.1 = (bf16[2,160,320]{2,1,0:T(8,128)(2,1)S(1)}, bf16[2,160,320]{2,1,0:T(8,128)(2,1)S(1)}, u32[]{:S(2)}, u32[]{:S(2)}) collective-permute-start(bf16[2,160,320]{2,1,0:T(8,128)(2,1)S(1)} %slice.14.refs_4_), channel_id=1, source_target_pairs={{0,8},{4,12},{8,0},{12,4},{16,24},{20,28},{24,16},{28,20},{1,9},{5... | collective-permute-start | bytes 614408 | tf_op jit(solution)/shard_map/ppermute | solution.py:107
  4.1 18.2 %collective-permute-start.6 = (bf16[2,160,320]{2,1,0:T(8,128)(2,1)S(1)}, bf16[2,160,320]{2,1,0:T(8,128)(2,1)S(1)}, u32[]{:S(2)}, u32[]{:S(2)}) collective-permute-start(bf16[2,160,320]{2,1,0:T(8,128)(2,1)S(1)} %slice.14.refs_4_), channel_id=1, source_target_pairs={{0,16},{4,20},{8,24},{12,28},{16,0},{20,4},{24,8},{28,12},{1,17},{... | collective-permute-start | bytes 614408 | tf_op jit(solution)/shard_map/ppermute | solution.py:107
  6.7 16.3 %collective-permute-start.8 = (bf16[2,160,320]{2,1,0:T(8,128)(2,1)S(1)}, bf16[2,160,320]{2,1,0:T(8,128)(2,1)S(1)}, u32[]{:S(2)}, u32[]{:S(2)}) collective-permute-start(bf16[2,160,320]{2,1,0:T(8,128)(2,1)S(1)} %slice.14.refs_4_), channel_id=1, source_target_pairs={{0,4},{4,0},{8,12},{12,8},{16,20},{20,16},{24,28},{28,24},{1,5},{5... | collective-permute-start | bytes 614408 | tf_op jit(solution)/shard_map/ppermute | solution.py:107
  18.0 11.4 %collective-permute-start.3 = (bf16[144,1280]{1,0:T(8,128)(2,1)S(1)}, bf16[144,1280]{1,0:T(8,128)(2,1)S(1)}, u32[]{:S(2)}, u32[]{:S(2)}) collective-permute-start(bf16[144,1280]{1,0:T(8,128)(2,1)S(1)} %shard_map.82.refs_0_), channel_id=1, source_target_pairs={{0,2},{1,3},{2,0},{3,1},{4,6},{5,7},{6,4},{7,5},{8,10},{9,11},{10,... | collective-permute-start | bytes 1105928 | tf_op jit(solution)/shard_map/ppermute | solution.py:107
  20.8 8.1 %collective-permute-start.2 = (bf16[160,640]{1,0:T(8,128)(2,1)S(1)}, bf16[160,640]{1,0:T(8,128)(2,1)S(1)}, u32[]{:S(2)}, u32[]{:S(2)}) collective-permute-start(bf16[160,640]{1,0:T(8,128)(2,1)S(1)} %get-tuple-element.20), channel_id=1, source_target_pairs={{0,4},{4,0},{8,12},{12,8},{16,20},{20,16},{24,28},{28,24},{1,5},{5... | collective-permute-start | bytes 614408 | tf_op jit(solution)/shard_map/ppermute | solution.py:107
  22.3 7.0 %collective-permute-start.7 = (bf16[2,160,320]{2,1,0:T(8,128)(2,1)S(1)}, bf16[2,160,320]{2,1,0:T(8,128)(2,1)S(1)}, u32[]{:S(2)}, u32[]{:S(2)}) collective-permute-start(bf16[2,160,320]{2,1,0:T(8,128)(2,1)S(1)} %collective-permute-done.6.refs_6_), channel_id=1, source_target_pairs={{0,8},{4,12},{8,0},{12,4},{16,24},{20,28},{24,16},{28,20},{1,9},{5... | collective-permute-start | bytes 614408 | tf_op jit(solution)/shard_map/ppermute | solution.py:107
  22.4 11.7 %collective-permute-start.10 = (bf16[2,160,320]{2,1,0:T(8,128)(2,1)S(1)}, bf16[2,160,320]{2,1,0:T(8,128)(2,1)S(1)}, u32[]{:S(2)}, u32[]{:S(2)}) collective-permute-start(bf16[2,160,320]{2,1,0:T(8,128)(2,1)S(1)} %collective-permute-done.6.refs_6_), channel_id=1, source_target_pairs={{0,4},{4,0},{8,12},{12,8},{16,20},{20,16},{24,28},{28,24},{1,5},{5... | collective-permute-start | bytes 614408 | tf_op jit(solution)/shard_map/ppermute | solution.py:107
  23.0 14.0 %collective-permute-start.9 = (bf16[2,160,320]{2,1,0:T(8,128)(2,1)S(1)}, bf16[2,160,320]{2,1,0:T(8,128)(2,1)S(1)}, u32[]{:S(2)}, u32[]{:S(2)}) collective-permute-start(bf16[2,160,320]{2,1,0:T(8,128)(2,1)S(1)} %collective-permute-done.1.refs_5_), channel_id=1, source_target_pairs={{0,4},{4,0},{8,12},{12,8},{16,20},{20,16},{24,28},{28,24},{1,5},{5... | collective-permute-start | bytes 614408 | tf_op jit(solution)/shard_map/ppermute | solution.py:107
  28.8 9.7 %collective-permute-start.13 = (bf16[2,160,320]{2,1,0:T(8,128)(2,1)S(1)}, bf16[2,160,320]{2,1,0:T(8,128)(2,1)S(1)}, u32[]{:S(2)}, u32[]{:S(2)}) collective-permute-start(bf16[2,160,320]{2,1,0:T(8,128)(2,1)S(1)} %pad_maximum_fusion.1.refs_3_), channel_id=1, source_target_pairs={{0,16},{4,20},{8,24},{12,28},{16,0},{20,4},{24,8},{28,12},{1,17},{... | collective-permute-start | bytes 614408 | tf_op jit(solution)/shard_map/ppermute | solution.py:107
  29.3 16.0 %collective-permute-start.4 = (bf16[144,1280]{1,0:T(8,128)(2,1)S(1)}, bf16[144,1280]{1,0:T(8,128)(2,1)S(1)}, u32[]{:S(2)}, u32[]{:S(2)}) collective-permute-start(bf16[144,1280]{1,0:T(8,128)(2,1)S(1)} %shard_map.82.refs_0_), channel_id=1, source_target_pairs={{0,1},{1,0},{2,3},{3,2},{4,5},{5,4},{6,7},{7,6},{8,9},{9,8},{10,11... | collective-permute-start | bytes 1105928 | tf_op jit(solution)/shard_map/ppermute | solution.py:107
  29.3 18.9 %collective-permute-start.5 = (bf16[144,1280]{1,0:T(8,128)(2,1)S(1)}, bf16[144,1280]{1,0:T(8,128)(2,1)S(1)}, u32[]{:S(2)}, u32[]{:S(2)}) collective-permute-start(bf16[144,1280]{1,0:T(8,128)(2,1)S(1)} %collective-permute-done.3.refs_1_), channel_id=1, source_target_pairs={{0,1},{1,0},{2,3},{3,2},{4,5},{5,4},{6,7},{7,6},{8,9},{9,8},{10,11... | collective-permute-start | bytes 1105928 | tf_op jit(solution)/shard_map/ppermute | solution.py:107
  34.1 9.7 %collective-permute-start.12 = (bf16[2,160,320]{2,1,0:T(8,128)(2,1)S(1)}, bf16[2,160,320]{2,1,0:T(8,128)(2,1)S(1)}, u32[]{:S(2)}, u32[]{:S(2)}) collective-permute-start(bf16[2,160,320]{2,1,0:T(8,128)(2,1)S(1)} %pad_maximum_fusion.1.refs_3_), channel_id=1, source_target_pairs={{0,8},{4,12},{8,0},{12,4},{16,24},{20,28},{24,16},{28,20},{1,9},{5... | collective-permute-start | bytes 614408 | tf_op jit(solution)/shard_map/ppermute | solution.py:107
  37.0 8.8 %collective-permute-start.11 = (bf16[2,160,320]{2,1,0:T(8,128)(2,1)S(1)}, bf16[2,160,320]{2,1,0:T(8,128)(2,1)S(1)}, u32[]{:S(2)}, u32[]{:S(2)}) collective-permute-start(bf16[2,160,320]{2,1,0:T(8,128)(2,1)S(1)} %collective-permute-done.7.refs_7_), channel_id=1, source_target_pairs={{0,4},{4,0},{8,12},{12,8},{16,20},{20,16},{24,28},{28,24},{1,5},{5... | collective-permute-start | bytes 614408 | tf_op jit(solution)/shard_map/ppermute | solution.py:107
  38.5 8.8 %collective-permute-start.14 = (bf16[2,160,320]{2,1,0:T(8,128)(2,1)S(1)}, bf16[2,160,320]{2,1,0:T(8,128)(2,1)S(1)}, u32[]{:S(2)}, u32[]{:S(2)}) collective-permute-start(bf16[2,160,320]{2,1,0:T(8,128)(2,1)S(1)} %collective-permute-done.13.refs_5_), channel_id=1, source_target_pairs={{0,8},{4,12},{8,0},{12,4},{16,24},{20,28},{24,16},{28,20},{1,9},{5... | collective-permute-start | bytes 614408 | tf_op jit(solution)/shard_map/ppermute | solution.py:107
  43.8 8.9 %collective-permute-start.15 = (bf16[2,160,320]{2,1,0:T(8,128)(2,1)S(1)}, bf16[2,160,320]{2,1,0:T(8,128)(2,1)S(1)}, u32[]{:S(2)}, u32[]{:S(2)}) collective-permute-start(bf16[2,160,320]{2,1,0:T(8,128)(2,1)S(1)} %pad_maximum_fusion.1.refs_3_), channel_id=1, source_target_pairs={{0,4},{4,0},{8,12},{12,8},{16,20},{20,16},{24,28},{28,24},{1,5},{5... | collective-permute-start | bytes 614408 | tf_op jit(solution)/shard_map/ppermute | solution.py:107
  45.3 12.6 %collective-permute-start.17 = (bf16[2,160,320]{2,1,0:T(8,128)(2,1)S(1)}, bf16[2,160,320]{2,1,0:T(8,128)(2,1)S(1)}, u32[]{:S(2)}, u32[]{:S(2)}) collective-permute-start(bf16[2,160,320]{2,1,0:T(8,128)(2,1)S(1)} %collective-permute-done.13.refs_5_), channel_id=1, source_target_pairs={{0,4},{4,0},{8,12},{12,8},{16,20},{20,16},{24,28},{28,24},{1,5},{5... | collective-permute-start | bytes 614408 | tf_op jit(solution)/shard_map/ppermute | solution.py:107
  45.8 15.8 %collective-permute-start.16 = (bf16[2,160,320]{2,1,0:T(8,128)(2,1)S(1)}, bf16[2,160,320]{2,1,0:T(8,128)(2,1)S(1)}, u32[]{:S(2)}, u32[]{:S(2)}) collective-permute-start(bf16[2,160,320]{2,1,0:T(8,128)(2,1)S(1)} %collective-permute-done.12.refs_4_), channel_id=1, source_target_pairs={{0,4},{4,0},{8,12},{12,8},{16,20},{20,16},{24,28},{28,24},{1,5},{5... | collective-permute-start | bytes 614408 | tf_op jit(solution)/shard_map/ppermute | solution.py:107
  47.4 16.9 %collective-permute-start.18 = (bf16[2,160,320]{2,1,0:T(8,128)(2,1)S(1)}, bf16[2,160,320]{2,1,0:T(8,128)(2,1)S(1)}, u32[]{:S(2)}, u32[]{:S(2)}) collective-permute-start(bf16[2,160,320]{2,1,0:T(8,128)(2,1)S(1)} %collective-permute-done.14.refs_6_), channel_id=1, source_target_pairs={{0,4},{4,0},{8,12},{12,8},{16,20},{20,16},{24,28},{28,24},{1,5},{5... | collective-permute-start | bytes 614408 | tf_op jit(solution)/shard_map/ppermute | solution.py:107
  66.8 2.2 %collective-permute-start.19 = (bf16[256,1280]{1,0:T(8,128)(2,1)S(1)}, bf16[256,1280]{1,0:T(8,128)(2,1)S(1)}, u32[]{:S(2)}, u32[]{:S(2)}) collective-permute-start(bf16[256,1280]{1,0:T(8,128)(2,1)S(1)} %get-tuple-element.28), channel_id=1, source_target_pairs={{0,1},{1,0},{2,3},{3,2},{4,5},{5,4},{6,7},{7,6},{8,9},{9,8},{10,11... | collective-permute-start | bytes 1966088 | tf_op jit(solution)/shard_map/ppermute | solution.py:107
  67.0 21.5 %copy-start.1 = (bf16[128,1280]{1,0:T(8,128)(2,1)S(1)}, bf16[128,1280]{1,0:T(8,128)(2,1)}, u32[]{:S(2)}) copy-start(bf16[128,1280]{1,0:T(8,128)(2,1)} %tokens_ref.1) | copy-start | bytes 983044
  67.0 21.5 %copy-start.3 = (f32[2,1280]{1,0:T(2,128)S(1)}, f32[2,1280]{1,0:T(2,128)}, u32[]{:S(2)}) copy-start(f32[2,1280]{1,0:T(2,128)} %gains_ref.1) | copy-start | bytes 30724
  67.0 21.5 %collective-permute-start.21 = (bf16[320,640]{1,0:T(8,128)(2,1)S(1)}, bf16[320,640]{1,0:T(8,128)(2,1)S(1)}, u32[]{:S(2)}, u32[]{:S(2)}) collective-permute-start(bf16[320,640]{1,0:T(8,128)(2,1)S(1)} %pad_maximum_fusion.refs_0_), channel_id=1, source_target_pairs={{0,16},{4,20},{8,24},{12,28},{16,0},{20,4},{24,8},{28,12},{1,17},{... | collective-permute-start | bytes 1228808 | tf_op jit(solution)/shard_map/ppermute | solution.py:107
  69.0 19.4 %collective-permute-start.20 = (bf16[128,1280]{1,0:T(8,128)(2,1)S(1)}, bf16[128,1280]{1,0:T(8,128)(2,1)}, u32[]{:S(2)}, u32[]{:S(2)}) collective-permute-start(bf16[128,1280]{1,0:T(8,128)(2,1)S(1)} %shard_map.85), channel_id=1, source_target_pairs={{0,2},{1,3},{2,0},{3,1},{4,6},{5,7},{6,4},{7,5},{8,10},{9,11},{10,... | collective-permute-start | bytes 983048 | tf_op jit(solution)/shard_map/ppermute | solution.py:107
  69.8 27.1 %collective-permute-start = (s32[32,1]{0,1:T(1,128)S(1)}, s32[32,1]{0,1:T(1,128)S(1)}, u32[]{:S(2)}, u32[]{:S(2)}) collective-permute-start(s32[32,1]{0,1:T(1,128)S(1)} %copy-done.6), channel_id=1, source_target_pairs={{0,4},{4,0},{8,12},{12,8},{16,20},{20,16},{24,28},{28,24},{1,5},{5... | collective-permute-start | bytes 392 | tf_op jit(solution)/shard_map/ppermute | solution.py:107
  91.1 24.4 %all-to-all-start = ((bf16[8,64,640]{2,1,0:T(8,128)(2,1)}), bf16[8,64,640]{2,1,0:T(8,128)(2,1)S(1)}, u32[]{:S(2)}, u32[]{:S(2)}) async-start(bf16[8,64,640]{2,1,0:T(8,128)(2,1)} %shard_map.86), calls=%async_computation | async-start | bytes 1310720 | tf_op jit(solution)/shard_map/all_to_all | solution.py:362
  94.8 12.3 %collective-permute-start.22 = (bf16[320,640]{1,0:T(8,128)(2,1)S(1)}, bf16[320,640]{1,0:T(8,128)(2,1)S(1)}, u32[]{:S(2)}, u32[]{:S(2)}) collective-permute-start(bf16[320,640]{1,0:T(8,128)(2,1)S(1)} %pad_maximum_fusion.refs_0_), channel_id=1, source_target_pairs={{0,8},{4,12},{8,0},{12,4},{16,24},{20,28},{24,16},{28,20},{1,9},{5... | collective-permute-start | bytes 1228808 | tf_op jit(solution)/shard_map/ppermute | solution.py:107
  94.9 20.6 %collective-permute-start.23 = (bf16[320,640]{1,0:T(8,128)(2,1)S(1)}, bf16[320,640]{1,0:T(8,128)(2,1)S(1)}, u32[]{:S(2)}, u32[]{:S(2)}) collective-permute-start(bf16[320,640]{1,0:T(8,128)(2,1)S(1)} %collective-permute-done.21.refs_2_), channel_id=1, source_target_pairs={{0,8},{4,12},{8,0},{12,4},{16,24},{20,28},{24,16},{28,20},{1,9},{5... | collective-permute-start | bytes 1228808 | tf_op jit(solution)/shard_map/ppermute | solution.py:107
  116.5 2.0 %collective-permute-start.24 = (bf16[64,640]{1,0:T(8,128)(2,1)S(1)}, bf16[64,640]{1,0:T(8,128)(2,1)S(1)}, u32[]{:S(2)}, u32[]{:S(2)}) collective-permute-start(bf16[64,640]{1,0:T(8,128)(2,1)S(1)} %get-tuple-element.32), channel_id=1, source_target_pairs={{0,1},{1,0},{2,3},{3,2},{4,5},{5,4},{6,7},{7,6},{8,9},{9,8},{10,11... | collective-permute-start | bytes 245768 | tf_op jit(solution)/shard_map/ppermute | solution.py:107
  116.6 5.0 %collective-permute-start.25 = (bf16[64,640]{1,0:T(8,128)(2,1)S(1)}, bf16[64,640]{1,0:T(8,128)(2,1)S(1)}, u32[]{:S(2)}, u32[]{:S(2)}) collective-permute-start(bf16[64,640]{1,0:T(8,128)(2,1)S(1)} %get-tuple-element.33), channel_id=1, source_target_pairs={{0,2},{1,3},{2,0},{3,1},{4,6},{5,7},{6,4},{7,5},{8,10},{9,11},{10,... | collective-permute-start | bytes 245768 | tf_op jit(solution)/shard_map/ppermute | solution.py:107
  118.3 4.7 %collective-permute-start.26 = (bf16[64,640]{1,0:T(8,128)(2,1)S(1)}, bf16[64,640]{1,0:T(8,128)(2,1)S(1)}, u32[]{:S(2)}, u32[]{:S(2)}) collective-permute-start(bf16[64,640]{1,0:T(8,128)(2,1)S(1)} %get-tuple-element.34), channel_id=1, source_target_pairs={{0,3},{1,2},{2,1},{3,0},{4,7},{5,6},{6,5},{7,4},{8,11},{9,10},{10,... | collective-permute-start | bytes 245768 | tf_op jit(solution)/shard_map/ppermute | solution.py:107
  (5 other events, 9.9 us)

commit v5 on v3

--- a/solution.py
+++ b/solution.py
@@ -122,10 +122,10 @@
     return lax.dot_general(a, b, (((1,), (1,)), ((), ())), preferred_element_type=jnp.float32)
 
 
-def call(kernel, outs, operands, scratch=(), flops=0, smem=0, exps=0, space=pltpu.VMEM):
+def call(kernel, outs, operands, scratch=(), flops=0, smem=0, exps=0):
     moved = sum(math.prod(x.shape) * x.dtype.itemsize for x in (*operands, *outs))
     specs = [pl.BlockSpec(memory_space=pltpu.SMEM)] * smem
-    specs += [pl.BlockSpec(memory_space=space)] * (len(operands) - smem)
+    specs += [pl.BlockSpec(memory_space=pltpu.VMEM)] * (len(operands) - smem)
     return pl.pallas_call(
         kernel,
         out_shape=tuple(outs),
@@ -139,22 +139,11 @@
     )(*operands)
 
 
-def norm_kernel(tokens_in, gains_in, segs_in, out_ref, tokens_ref, gains_ref, segs_ref, sems):
-    copies = [
-        pltpu.make_async_copy(tokens_in, tokens_ref, sems.at[0]),
-        pltpu.make_async_copy(gains_in, gains_ref, sems.at[1]),
-        pltpu.make_async_copy(segs_in, segs_ref, sems.at[2]),
-    ]
-    for copy in copies:
-        copy.start()
-    for copy in copies:
-        copy.wait()
-    rows = tokens_ref.shape[0]
-    out_ref[0:rows, :] = normalize(tokens_ref[...], gains_ref[0:1, :])
-    out_ref[rows:, :] = jnp.zeros((out_ref.shape[0] - rows, out_ref.shape[1]), out_ref.dtype)
-    out_ref[rows:, 0:rows] = jnp.broadcast_to(
-        segs_ref[...].astype(jnp.float32), (out_ref.shape[0] - rows, rows)
-    ).astype(out_ref.dtype)
+def norm_kernel(gains_ref, *refs):
+    tokens, out_ref = refs[0:4], refs[4]
+    rows = tokens[0].shape[0] - 16
+    for n in range(4):
+        out_ref[n * rows : (n + 1) * rows, :] = normalize(tokens[n][0:rows, :], gains_ref[0:1, :])
 
 
 def lay_out(me, blocks, part, whole):
@@ -164,40 +153,29 @@
         whole[pl.ds(start, step), :] = block[part]
 
 
-def score_kernel(me_ref, *refs):
-    tokens, blocks = refs[0:4], refs[4:12]
-    rows_ref, weights_ref, totals_ref, q_whole, k_whole = refs[12:]
-    rows = tokens[0].shape[0] - 16
-    for n in range(4):
-        rows_ref[n * rows : (n + 1) * rows, :] = tokens[n][0:rows, :]
+def attention_kernel(me_ref, rows_ref, *refs):
+    marks, blocks = refs[0:4], refs[4:12]
+    keep_ref, send_ref, q_whole, k_whole, v_whole, out_whole = refs[12:]
     lay_out(me_ref[0], blocks, 0, q_whole)
     lay_out(me_ref[0], blocks, 1, k_whole)
+    lay_out(me_ref[0], blocks, 2, v_whole)
+    lay_out(me_ref[0], blocks, 3, out_whole)
     queries = dot(rows_ref[...], q_whole[...]).astype(jnp.bfloat16)
     keys = dot(rows_ref[...], k_whole[...]).astype(jnp.bfloat16)
-    in_row = [t[rows : rows + 16, 0:rows].astype(jnp.float32)[0:1, :] for t in tokens]
+    values = dot(rows_ref[...], v_whole[...]).astype(jnp.bfloat16)
+    rows = marks[0].shape[0] - 16
+    in_row = [t[rows : rows + 16, 0:rows].astype(jnp.float32)[0:1, :] for t in marks]
     in_col = [jnp.broadcast_to(s, (rows, rows)).T[:, 0:1] for s in in_row]
     allowed = jnp.concatenate(in_col, axis=0) == jnp.concatenate(in_row, axis=1)
     factor = 1.0 / math.sqrt(HD)
+    pieces = []
     for head in range(queries.shape[1] // HD):
         cols = slice(head * HD, (head + 1) * HD)
         scores = dot_turned(queries[:, cols], keys[:, cols]) * factor
         masked = jnp.where(allowed, scores, -jnp.inf)
         weights = jnp.exp(masked - jnp.max(masked, axis=1, keepdims=True))
-        weights_ref[head] = weights.astype(jnp.bfloat16)
-        totals_ref[head] = jnp.sum(weights, axis=1, keepdims=True)
-
-
-def value_kernel(me_ref, *refs):
-    rows_ref, weights_ref, totals_ref = refs[0:3]
-    blocks = refs[3:11]
-    keep_ref, send_ref, v_whole, out_whole = refs[11:]
-    lay_out(me_ref[0], blocks, 0, v_whole)
-    lay_out(me_ref[0], blocks, 1, out_whole)
-    values = dot(rows_ref[...], v_whole[...]).astype(jnp.bfloat16)
-    pieces = []
-    for head in range(values.shape[1] // HD):
-        found = dot(weights_ref[head], values[:, head * HD : (head + 1) * HD])
-        pieces.append(found / totals_ref[head])
+        totals = jnp.sum(weights, axis=1, keepdims=True)
+        pieces.append(dot(weights.astype(jnp.bfloat16), values[:, cols]) / totals)
     attended = jnp.concatenate(pieces, axis=1).astype(jnp.bfloat16)
     half = attended.shape[0] // 2
     send_ref[...] = dot_turned(attended[half:, :], out_whole[...]).astype(jnp.bfloat16)
@@ -237,18 +215,19 @@
 
 
 def merge_kernel(me_ref, at_ref, inputs, *refs):
-    blocks, (keep_ref, *sends), total = refs[0:4], refs[4:8], refs[8]
+    pieces, (keep_ref, *sends), total = refs[0:8], refs[8:12], refs[12]
     count, width = inputs.shape[1] // 2, inputs.shape[2] // 2
     z, y = me_ref[0] // 2, lax.rem(me_ref[0], 2)
-    for number, block in enumerate(blocks):
+    for number in range(4):
         position = z ^ number
         at = pl.multiple_of(lax.rem(position, 2) * count, 32)
         rows = inputs[:, pl.ds(at, count), :].reshape(8 * count, 2 * width)
         rows = jnp.where(position < 2, rows[:, :width], rows[:, width:])
-        step = block.shape[0] // 2
-        low = block[pl.ds(pl.multiple_of(y * step, 32), step), :]
-        high = block[pl.ds(pl.multiple_of((1 - y) * step, 32), step), :]
-        found = dot(rows, jnp.concatenate([low, high], axis=0)).reshape(total.shape)
+        own, other = pieces[2 * number][...], pieces[2 * number + 1][...]
+        block = jnp.concatenate(
+            [jnp.where(y == 0, own, other), jnp.where(y == 0, other, own)], axis=0
+        )
+        found = dot(rows, block).reshape(total.shape)
         total[...] = found if number == 0 else total[...] + found
     for k in range(4):
         to = at_ref[0] ^ k
@@ -282,25 +261,28 @@
     cols = qkv_weight.shape[2]
     group = n_fsdp * rows
 
-    first = qkv_weight[0:2]
-    first_z = [swap(first, "dp", 2), swap(first, "dp", 4)]
-    first_y = [swap(first, "dp", 1)]
-    first_z += [swap(first_z[1], "dp", 2)]
-    second = jnp.concatenate([qkv_weight[2:3], out_weight.T[None]], axis=0)
+    heads = jnp.concatenate([qkv_weight, out_weight.T[None]], axis=0)
+    along_z = [swap(heads, "dp", 2), swap(heads, "dp", 4)]
+    along_y = [swap(heads, "dp", 1)]
+    along_z += [swap(along_z[1], "dp", 2)]
+    along_y += [swap(block, "dp", 1) for block in along_z]
+
+    marks = jnp.pad(segments.astype(bf16), ((0, 15), (0, width - rows)))
+    marked = after(jnp.concatenate([tokens, marks], axis=0), along_z[0])
+    along_x = swap(marked, "fsdp", 2)
+    group_rows = [marked, along_x, swap(marked, "fsdp", 1), swap(along_x, "fsdp", 1)]
+    (normed,) = call(norm_kernel, [shape((group, width), bf16)], [ln_gains, *group_rows])
+
     half = merge_weight.shape[1] // 2
     low, high = merge_weight[:, :half], merge_weight[:, half:]
     lower = y == 0
-    theirs = swap(after(jnp.where(lower, high, low), first_y[0]), "dp", 1)
-    held = after(second, first_z[0])
-    second_z = [swap(held, "dp", 2), swap(held, "dp", 4)]
-    second_y = [swap(held, "dp", 1)]
-    second_z += [swap(second_z[1], "dp", 2)]
-    first_y += [swap(block, "dp", 1) for block in first_z]
-    second_y += [swap(block, "dp", 1) for block in second_z]
-    pair = jnp.concatenate([jnp.where(lower, low, high), theirs], axis=0)
-    held = after(pair, second_z[1])
-    merge_blocks = [pair, swap(held, "dp", 2), swap(held, "dp", 4)]
-    merge_blocks += [swap(merge_blocks[2], "dp", 2)]
+    mine = jnp.where(lower, low, high)
+    theirs = swap(after(jnp.where(lower, high, low), along_z[0]), "dp", 1)
+    held, held_other = after((mine, theirs), (along_z[2], *along_y[:3], *group_rows[2:]))
+    merge_pieces = [mine, theirs, swap(held, "dp", 2), swap(held_other, "dp", 2)]
+    merge_pieces += [swap(held, "dp", 4)]
+    merge_pieces += [swap(after(held_other, merge_pieces[4]), "dp", 4)]
+    merge_pieces += [swap(piece, "dp", 2) for piece in merge_pieces[4:6]]
 
     capacity = max(2, (2 * count + n_dp - 1) // n_dp)
     mine = owners[:, 0]
@@ -312,40 +294,21 @@
     slots = jnp.concatenate(slots).reshape(1, 2 * count)
     order = merge_rows.reshape(count, 4).T.reshape(rows, 1)
 
-    (normed,) = call(
-        norm_kernel, [shape((rows + 16, width), bf16)], [after(tokens, first), ln_gains, segments],
+    keep, send = call(
+        attention_kernel,
+        [shape((2 * rows, width), f32), shape((2 * rows, width), bf16)],
         [
-            pltpu.VMEM(tokens.shape, bf16),
-            pltpu.VMEM(ln_gains.shape, f32),
-            pltpu.VMEM(segments.shape, jnp.int32),
-            pltpu.SemaphoreType.DMA((3,)),
+            after(me_cell, merge_pieces[2:5]),
+            normed,
+            *group_rows,
+            heads,
+            *along_z,
+            *along_y,
         ],
-        space=pl.ANY,
-    )
-    along_x = swap(normed, "fsdp", 2)
-    group_rows = [normed, along_x, swap(normed, "fsdp", 1), swap(along_x, "fsdp", 1)]
-
-    heads = cols // HD
-    group_all, weights, totals = call(
-        score_kernel,
-        [
-            shape((group, width), bf16),
-            shape((heads, group, group), bf16),
-            shape((heads, group, 1), f32),
-        ],
-        [after(me_cell, theirs), *group_rows, first, *first_z, *first_y],
-        [pltpu.VMEM((width, cols), bf16)] * 2,
-        flops=4 * group * width * cols + 2 * group * group * cols,
+        [pltpu.VMEM((width, cols), bf16)] * 4,
+        flops=8 * group * width * cols + 4 * group * group * cols,
         smem=1,
-        exps=heads * group * group,
-    )
-    keep, send = call(
-        value_kernel,
-        [shape((2 * rows, width), f32), shape((2 * rows, width), bf16)],
-        [after(me_cell, merge_blocks[1]), group_all, weights, totals, second, *second_z, *second_y],
-        [pltpu.VMEM((width, cols), bf16)] * 2,
-        flops=4 * group * width * cols + 2 * group * group * cols,
-        smem=1,
+        exps=cols // HD * group * group,
     )
     from_core = swap(send, "fsdp", 1)
     (onward,) = call(pass_kernel, [shape((rows, width), bf16)], [keep, from_core])
@@ -353,7 +316,7 @@
     (slices,) = call(
         layer_kernel,
         [shape((8, rows // 2, width // 2), bf16)],
-        [tokens, keep, from_core, after(from_chip, merge_blocks[2]), ln_gains, order],
+        [tokens, keep, from_core, after(from_chip, merge_pieces[5:7]), ln_gains, order],
         flops=2 * rows * rows * width,
     )
     both = 2 * n_fsdp
@@ -370,7 +333,7 @@
     shares = call(
         merge_kernel,
         [shape((2 * count, half), f32)] + [shape((2 * count, half), bf16)] * 3,
-        [me_cell, at_cell, inputs, *merge_blocks],
+        [me_cell, at_cell, inputs, *merge_pieces],
         [pltpu.VMEM((8, count, half), f32)],
         flops=2 * 8 * count * width * half,
         smem=2,

time: 137 us -> 130 us (0.949)
  waiting for transfers between devices: 74.4 us -> 69.7 us
  local copies, waits for them, and re-layouts: 6.32 us -> 3.75 us
  starting transfers between devices: 28.3 us -> 30.7 us
    ppermute x27 -> x23, waiting for transfers between devices: 74.4 us -> 66.7 us  [swap(): lax.ppermute(value, axis, [(i, i ^ k) for i in range(lax.axis_size(axis))])]
    all_to_all x1, waiting for transfers between devices: 0.01 us -> 3.01 us  [by_permutes(): lax.all_to_all(slices, ('dp', 'fsdp'), split_axis=0, concat_axis=0, tiled...]
    ppermute x27 -> x23, starting transfers between devices: 24.8 us -> 27.1 us  [swap(): lax.ppermute(value, axis, [(i, i ^ k) for i in range(lax.axis_size(axis))])]
    concatenate x2, other arithmetic: 0.09 us -> 2.18 us  [the longest x1 1.19 us: by_permutes(): heads = jnp.concatenate([qkv_weight, out_weight.T[None]], axis=0)]
    reduce_sum x2, other arithmetic: 1.79 us -> 0.36 us  [slot_numbers(): jnp.sum((same & before).astype(jnp.int32), axis=1)]
    unnamed x17 -> x31, local copies, waits for them, and re-layouts: 3.7 us -> 2.78 us
    pallas_call x7 -> x6, Pallas kernels: 10.6 us -> 10.2 us  [call(): pl.pallas_call(kernel, out_shape=tuple(outs), in_specs=specs, out_specs=t...]
  transfers between devices with their start and end apart: 28 -> 24, of which waited for: 12 -> 14; matrix products, arithmetic and copies ran while one was open for 5% -> 3% of each run, Pallas kernels for 5% -> 2%
where the time goes in v5:
time: 130 us; the launch traced here: 129 us
  waiting for transfers between devices  69.7 us (54%)
  starting transfers between devices  30.7 us (24%)
  blocking collectives  10.8 us (8%)
  Pallas kernels  10.2 us (8%)
  other arithmetic  4.03 us (3%)
  local copies, waits for them, and re-layouts  3.75 us (3%)
    ppermute x23, waiting for transfers between devices, swap(): lax.ppermute(value, axis, [(i, i ^ k) for i in range(lax.axis_size(axis))])  66.7 us
    ppermute x23, starting transfers between devices, swap(): lax.ppermute(value, axis, [(i, i ^ k) for i in range(lax.axis_size(axis))])  27.1 us
    all_to_all x1, blocking collectives, by_permutes(): lax.all_to_all(packed.reshape(n_dp, 2 * capacity, half), 'dp', split_axis...  10.8 us
    pallas_call x6, Pallas kernels, call(): pl.pallas_call(kernel, out_shape=tuple(outs), in_specs=specs, out_specs=t...  10.2 us
    all_to_all x1, starting transfers between devices, by_permutes(): lax.all_to_all(slices, ('dp', 'fsdp'), split_axis=0, concat_axis=0, tiled...  3.67 us
    all_to_all x1, waiting for transfers between devices, by_permutes(): lax.all_to_all(slices, ('dp', 'fsdp'), split_axis=0, concat_axis=0, tiled...  3.01 us
    unnamed x31, local copies, waits for them, and re-layouts  2.78 us
  transfers between devices with their start and end apart: 24, of which 14 were waited for; matrix products, arithmetic and copies ran while one was open for 3% of the time, Pallas kernels for 2%

profile of v5, /device:TPU:0, one launch (start us, length us, event | category | flops | bytes accessed | tf_op | source)
XLA Modules:
  0.0 129.5 jit_solution(3224208366980772215)
XLA Ops:
  0.0 1.2 pad_maximum_fusion.refs_4_
  1.2 3.1 %collective-permute-start.1 = (bf16[4,160,320]{2,1,0:T(8,128)(2,1)S(1)}, bf16[4,160,320]{2,1,0:T(8,128)(2,1)S(1)}, u32[]{:S(2)}, u32[]{:S(2)}) collective-permute-start(bf16[4,160,320]{2,1,0:T(8,128)(2,1)S(1)} %pad_maximum_fusion.refs_4_), channel_id=1, source_target_pairs={{0,8},{4,12},{8,0},{12,4},{16,24},{20,28},{24,16},{28,20},{1,9},{5... | collective-permute-start | bytes 1228808 | tf_op jit(solution)/shard_map/ppermute | solution.py:107
  4.3 2.6 %collective-permute-start.3 = (bf16[4,160,320]{2,1,0:T(8,128)(2,1)S(1)}, bf16[4,160,320]{2,1,0:T(8,128)(2,1)S(1)}, u32[]{:S(2)}, u32[]{:S(2)}) collective-permute-start(bf16[4,160,320]{2,1,0:T(8,128)(2,1)S(1)} %pad_maximum_fusion.refs_4_), channel_id=1, source_target_pairs={{0,16},{4,20},{8,24},{12,28},{16,0},{20,4},{24,8},{28,12},{1,17},{... | collective-permute-start | bytes 1228808 | tf_op jit(solution)/shard_map/ppermute | solution.py:107
  6.9 1.5 %collective-permute-start.5 = (bf16[4,160,320]{2,1,0:T(8,128)(2,1)S(1)}, bf16[4,160,320]{2,1,0:T(8,128)(2,1)S(1)}, u32[]{:S(2)}, u32[]{:S(2)}) collective-permute-start(bf16[4,160,320]{2,1,0:T(8,128)(2,1)S(1)} %pad_maximum_fusion.refs_4_), channel_id=1, source_target_pairs={{0,4},{4,0},{8,12},{12,8},{16,20},{20,16},{24,28},{28,24},{1,5},{5... | collective-permute-start | bytes 1228808 | tf_op jit(solution)/shard_map/ppermute | solution.py:107
  10.1 15.9 %collective-permute-done.1.refs_5_ = bf16[4,160,320]{2,1,0:T(8,128)(2,1)S(1)} collective-permute-done((bf16[4,160,320]{2,1,0:T(8,128)(2,1)S(1)}, bf16[4,160,320]{2,1,0:T(8,128)(2,1)S(1)}, u32[]{:S(2)}, u32[]{:S(2)}) %collective-permute-start.1) | collective-permute-done | bytes 409632 | tf_op jit(solution)/shard_map/ppermute | solution.py:107
  25.9 1.7 %collective-permute-start.9 = (bf16[144,1280]{1,0:T(8,128)(2,1)S(1)}, bf16[144,1280]{1,0:T(8,128)(2,1)S(1)}, u32[]{:S(2)}, u32[]{:S(2)}) collective-permute-start(bf16[144,1280]{1,0:T(8,128)(2,1)S(1)} %fusion.1.refs_0_), channel_id=1, source_target_pairs={{0,2},{1,3},{2,0},{3,1},{4,6},{5,7},{6,4},{7,5},{8,10},{9,11},{10,... | collective-permute-start | bytes 1105928 | tf_op jit(solution)/shard_map/ppermute | solution.py:107
  28.9 1.6 %collective-permute-start.2 = (bf16[160,640]{1,0:T(8,128)(2,1)S(1)}, bf16[160,640]{1,0:T(8,128)(2,1)S(1)}, u32[]{:S(2)}, u32[]{:S(2)}) collective-permute-start(bf16[160,640]{1,0:T(8,128)(2,1)S(1)} %get-tuple-element.18), channel_id=1, source_target_pairs={{0,4},{4,0},{8,12},{12,8},{16,20},{20,16},{24,28},{28,24},{1,5},{5... | collective-permute-start | bytes 614408 | tf_op jit(solution)/shard_map/ppermute | solution.py:107
  31.0 1.5 %collective-permute-start.7 = (bf16[4,160,320]{2,1,0:T(8,128)(2,1)S(1)}, bf16[4,160,320]{2,1,0:T(8,128)(2,1)S(1)}, u32[]{:S(2)}, u32[]{:S(2)}) collective-permute-start(bf16[4,160,320]{2,1,0:T(8,128)(2,1)S(1)} %collective-permute-done.3.refs_6_), channel_id=1, source_target_pairs={{0,4},{4,0},{8,12},{12,8},{16,20},{20,16},{24,28},{28,24},{1,5},{5... | collective-permute-start | bytes 1228808 | tf_op jit(solution)/shard_map/ppermute | solution.py:107
  32.6 4.5 %collective-permute-done.2.refs_1_ = bf16[160,640]{1,0:T(8,128)(2,1)S(1)} collective-permute-done((bf16[160,640]{1,0:T(8,128)(2,1)S(1)}, bf16[160,640]{1,0:T(8,128)(2,1)S(1)}, u32[]{:S(2)}, u32[]{:S(2)}) %collective-permute-start.2) | collective-permute-done | bytes 204832 | tf_op jit(solution)/shard_map/ppermute | solution.py:107
  37.5 1.9 %collective-permute-done.4.refs_7_ = bf16[4,160,320]{2,1,0:T(8,128)(2,1)S(1)} collective-permute-done((bf16[4,160,320]{2,1,0:T(8,128)(2,1)S(1)}, bf16[4,160,320]{2,1,0:T(8,128)(2,1)S(1)}, u32[]{:S(2)}, u32[]{:S(2)}) %collective-permute-start.4) | collective-permute-done | bytes 409632 | tf_op jit(solution)/shard_map/ppermute | solution.py:107
  39.4 1.5 %collective-permute-start.14 = (bf16[4,160,320]{2,1,0:T(8,128)(2,1)S(1)}, bf16[4,160,320]{2,1,0:T(8,128)(2,1)S(1)}, u32[]{:S(2)}, u32[]{:S(2)}) collective-permute-start(bf16[4,160,320]{2,1,0:T(8,128)(2,1)S(1)} %collective-permute-done.4.refs_7_), channel_id=1, source_target_pairs={{0,4},{4,0},{8,12},{12,8},{16,20},{20,16},{24,28},{28,24},{1,5},{5... | collective-permute-start | bytes 1228808 | tf_op jit(solution)/shard_map/ppermute | solution.py:107
  40.9 6.6 %collective-permute-done.6.refs_9_ = bf16[4,160,320]{2,1,0:T(8,128)(2,1)S(1)} collective-permute-done((bf16[4,160,320]{2,1,0:T(8,128)(2,1)S(1)}, bf16[4,160,320]{2,1,0:T(8,128)(2,1)S(1)}, u32[]{:S(2)}, u32[]{:S(2)}) %collective-permute-start.6) | collective-permute-done | bytes 409632 | tf_op jit(solution)/shard_map/ppermute | solution.py:107
  47.6 10.5 %collective-permute-done.7.refs_10_ = bf16[4,160,320]{2,1,0:T(8,128)(2,1)S(1)} collective-permute-done((bf16[4,160,320]{2,1,0:T(8,128)(2,1)S(1)}, bf16[4,160,320]{2,1,0:T(8,128)(2,1)S(1)}, u32[]{:S(2)}, u32[]{:S(2)}) %collective-permute-start.7) | collective-permute-done | bytes 409632 | tf_op jit(solution)/shard_map/ppermute | solution.py:107
  58.1 1.6 %collective-permute-start.11 = (bf16[160,640]{1,0:T(8,128)(2,1)S(1)}, bf16[160,640]{1,0:T(8,128)(2,1)S(1)}, u32[]{:S(2)}, u32[]{:S(2)}) collective-permute-start(bf16[160,640]{1,0:T(8,128)(2,1)S(1)} %get-tuple-element.20.refs_0_), channel_id=1, source_target_pairs={{0,8},{4,12},{8,0},{12,4},{16,24},{20,28},{24,16},{28,20},{1,9},{5... | collective-permute-start | bytes 614408 | tf_op jit(solution)/shard_map/ppermute | solution.py:107
  60.2 2.6 %collective-permute-start.13 = (bf16[160,640]{1,0:T(8,128)(2,1)S(1)}, bf16[160,640]{1,0:T(8,128)(2,1)}, u32[]{:S(2)}, u32[]{:S(2)}) collective-permute-start(bf16[160,640]{1,0:T(8,128)(2,1)S(1)} %get-tuple-element.20.refs_0_), channel_id=1, source_target_pairs={{0,16},{4,20},{8,24},{12,28},{16,0},{20,4},{24,8},{28,12},{1,17},{... | collective-permute-start | bytes 614408 | tf_op jit(solution)/shard_map/ppermute | solution.py:107
  63.7 3.4 %collective-permute-done.11.refs_2_ = bf16[160,640]{1,0:T(8,128)(2,1)S(1)} collective-permute-done((bf16[160,640]{1,0:T(8,128)(2,1)S(1)}, bf16[160,640]{1,0:T(8,128)(2,1)S(1)}, u32[]{:S(2)}, u32[]{:S(2)}) %collective-permute-start.11) | collective-permute-done | bytes 204832 | tf_op jit(solution)/shard_map/ppermute | solution.py:107
  67.0 2.2 %collective-permute-done.12.refs_3_ = bf16[160,640]{1,0:T(8,128)(2,1)S(1)} collective-permute-done((bf16[160,640]{1,0:T(8,128)(2,1)S(1)}, bf16[160,640]{1,0:T(8,128)(2,1)S(1)}, u32[]{:S(2)}, u32[]{:S(2)}) %collective-permute-start.12) | collective-permute-done | bytes 204832 | tf_op jit(solution)/shard_map/ppermute | solution.py:107
  69.3 1.1 copy-done.9
  71.4 5.3 %shard_map.83 = (f32[256,1280]{1,0:T(8,128)S(1)}, bf16[256,1280]{1,0:T(8,128)(2,1)S(1)}) custom-call(s32[1]{0:T(128)} %bitcast.3.me_ref, bf16[512,1280]{1,0:T(8,128)(2,1)S(1)} %shard_map.82.rows_ref, bf16[144,1280]{1,0:T(8,128)(2,1)S(1)} %fusion.1.refs_0_, bf16[144,1280]{1,0:T(8,128)(2,1)S(1)} %collective-permute-done.9.refs_1_, ...), custom_call_target="tpu_custom_call" | custom-call | flops 2013265920 | bytes 8028164 | tf_op jit(solution)/shard_map/pallas_call | solution.py:129
  76.8 2.1 %collective-permute-done.15.got_ref.core_ref = bf16[256,1280]{1,0:T(8,128)(2,1)S(1)} collective-permute-done((bf16[256,1280]{1,0:T(8,128)(2,1)S(1)}, bf16[256,1280]{1,0:T(8,128)(2,1)S(1)}, u32[]{:S(2)}, u32[]{:S(2)}) %collective-permute-start.15) | collective-permute-done | bytes 655392 | tf_op jit(solution)/shard_map/ppermute | solution.py:107
  78.9 1.7 %collective-permute-start.16 = (bf16[128,1280]{1,0:T(8,128)(2,1)S(1)}, bf16[128,1280]{1,0:T(8,128)(2,1)S(1)}, u32[]{:S(2)}, u32[]{:S(2)}) collective-permute-start(bf16[128,1280]{1,0:T(8,128)(2,1)S(1)} %shard_map.84), channel_id=1, source_target_pairs={{0,2},{1,3},{2,0},{3,1},{4,6},{5,7},{6,4},{7,5},{8,10},{9,11},{10,... | collective-permute-start | bytes 983048 | tf_op jit(solution)/shard_map/ppermute | solution.py:107
  80.7 1.4 %collective-permute-start.17 = (bf16[160,640]{1,0:T(8,128)(2,1)S(1)}, bf16[160,640]{1,0:T(8,128)(2,1)}, u32[]{:S(2)}, u32[]{:S(2)}) collective-permute-start(bf16[160,640]{1,0:T(8,128)(2,1)S(1)} %collective-permute-done.2.refs_1_), channel_id=1, source_target_pairs={{0,16},{4,20},{8,24},{12,28},{16,0},{20,4},{24,8},{28,12},{1,17},{... | collective-permute-start | bytes 614408 | tf_op jit(solution)/shard_map/ppermute | solution.py:107
  82.2 1.5 %collective-permute-start = (s32[32,1]{0,1:T(1,128)S(1)}, s32[32,1]{0,1:T(1,128)S(1)}, u32[]{:S(2)}, u32[]{:S(2)}) collective-permute-start(s32[32,1]{0,1:T(1,128)S(1)} %copy-done.13), channel_id=1, source_target_pairs={{0,4},{4,0},{8,12},{12,8},{16,20},{20,16},{24,28},{28,24},{1,5},{5... | collective-permute-start | bytes 392 | tf_op jit(solution)/shard_map/ppermute | solution.py:107
  85.4 7.5 %collective-permute-done.17.refs_5_ = bf16[160,640]{1,0:T(8,128)(2,1)} collective-permute-done((bf16[160,640]{1,0:T(8,128)(2,1)S(1)}, bf16[160,640]{1,0:T(8,128)(2,1)}, u32[]{:S(2)}, u32[]{:S(2)}) %collective-permute-start.17) | collective-permute-done | bytes 204832 | tf_op jit(solution)/shard_map/ppermute | solution.py:107
  92.9 1.6 %shard_map.85 = bf16[8,64,640]{2,1,0:T(8,128)(2,1)} custom-call(bf16[128,1280]{1,0:T(8,128)(2,1)S(1)} %copy-done, f32[256,1280]{1,0:T(8,128)S(1)} %get-tuple-element.23.keep_ref, bf16[256,1280]{1,0:T(8,128)(2,1)S(1)} %collective-permute-done.15.got_ref.core_ref, bf16[128,1280]{1,0:T(8,128)(2,1)S(1)} %collective-permute-done.16.chip_ref, ...), custom_call_target="tpu_custom_call" | custom-call | flops 41943040 | bytes 3287552 | tf_op jit(solution)/shard_map/pallas_call | solution.py:129
  94.6 3.7 %all-to-all-start = ((bf16[8,64,640]{2,1,0:T(8,128)(2,1)}), bf16[8,64,640]{2,1,0:T(8,128)(2,1)S(1)}, u32[]{:S(2)}, u32[]{:S(2)}) async-start(bf16[8,64,640]{2,1,0:T(8,128)(2,1)} %shard_map.85), calls=%async_computation | async-start | bytes 1310720 | tf_op jit(solution)/shard_map/all_to_all | solution.py:323
  99.2 7.1 %collective-permute-done.19.refs_7_ = bf16[160,640]{1,0:T(8,128)(2,1)S(1)} collective-permute-done((bf16[160,640]{1,0:T(8,128)(2,1)}, bf16[160,640]{1,0:T(8,128)(2,1)S(1)}, u32[]{:S(2)}, u32[]{:S(2)}) %collective-permute-start.19) | collective-permute-done | bytes 204832 | tf_op jit(solution)/shard_map/ppermute | solution.py:107
  106.3 3.0 %all-to-all-done.inputs = bf16[8,64,640]{2,1,0:T(8,128)(2,1)S(1)} async-done(((bf16[8,64,640]{2,1,0:T(8,128)(2,1)}), bf16[8,64,640]{2,1,0:T(8,128)(2,1)S(1)}, u32[]{:S(2)}, u32[]{:S(2)}) %all-to-all-start) | async-done | bytes 655392 | tf_op jit(solution)/shard_map/all_to_all | solution.py:323
  109.3 2.2 %shard_map.86 = (f32[64,640]{1,0:T(8,128)S(1)}, bf16[64,640]{1,0:T(8,128)(2,1)S(1)}, bf16[64,640]{1,0:T(8,128)(2,1)S(1)}, bf16[64,640]{1,0:T(8,128)(2,1)S(1)}) custom-call(s32[1]{0:T(128)} %bitcast.3.me_ref, s32[1]{0:T(128)} %bitcast.4.at_ref, bf16[8,64,640]{2,1,0:T(8,128)(2,1)S(1)} %all-to-all-done.inputs, bf16[160,640]{1,0:T(8,128)(2,1)S(1)} %get-tuple-element.20.refs_0_, ...), custom_call_target="tpu_custom_call" | custom-call | flops 419430400 | bytes 2703368 | tf_op jit(solution)/shard_map/pallas_call | solution.py:129
  112.2 1.2 collective-permute-start.22
  113.5 3.4 %collective-permute-done.21.two_ref = bf16[64,640]{1,0:T(8,128)(2,1)S(1)} collective-permute-done((bf16[64,640]{1,0:T(8,128)(2,1)S(1)}, bf16[64,640]{1,0:T(8,128)(2,1)S(1)}, u32[]{:S(2)}, u32[]{:S(2)}) %collective-permute-start.21) | collective-permute-done | bytes 81952 | tf_op jit(solution)/shard_map/ppermute | solution.py:107
  118.0 10.8 %all_to_all.10 = bf16[8,16,640]{2,1,0:T(8,128)(2,1)S(1)} all-to-all(bf16[8,16,640]{2,1,0:T(8,128)(2,1)S(1)} %bitcast.17), channel_id=1, replica_groups=mesh['dp'=8,'fsdp'=4] {'dp'}, dimensions={0} | all-to-all | bytes 327680 | tf_op jit(solution)/shard_map/all_to_all | solution.py:348
  (68 shorter events, 11.8 us)
Async XLA Ops:
  0.0 28.9 %copy-start.12 = (bf16[160,1280]{1,0:T(8,128)(2,1)S(1)}, bf16[160,1280]{1,0:T(8,128)(2,1)}, u32[]{:S(2)}) copy-start(bf16[160,1280]{1,0:T(8,128)(2,1)} %param.11) | copy-start | bytes 1228804
  0.0 62.8 %copy-start.5 = (f32[2,1280]{1,0:T(2,128)S(1)}, f32[2,1280]{1,0:T(2,128)}, u32[]{:S(2)}) copy-start(f32[2,1280]{1,0:T(2,128)} %gains_ref.3) | copy-start | bytes 30724
  1.2 24.7 %collective-permute-start.1 = (bf16[4,160,320]{2,1,0:T(8,128)(2,1)S(1)}, bf16[4,160,320]{2,1,0:T(8,128)(2,1)S(1)}, u32[]{:S(2)}, u32[]{:S(2)}) collective-permute-start(bf16[4,160,320]{2,1,0:T(8,128)(2,1)S(1)} %pad_maximum_fusion.refs_4_), channel_id=1, source_target_pairs={{0,8},{4,12},{8,0},{12,4},{16,24},{20,28},{24,16},{28,20},{1,9},{5... | collective-permute-start | bytes 1228808 | tf_op jit(solution)/shard_map/ppermute | solution.py:107
  4.3 24.2 %collective-permute-start.3 = (bf16[4,160,320]{2,1,0:T(8,128)(2,1)S(1)}, bf16[4,160,320]{2,1,0:T(8,128)(2,1)S(1)}, u32[]{:S(2)}, u32[]{:S(2)}) collective-permute-start(bf16[4,160,320]{2,1,0:T(8,128)(2,1)S(1)} %pad_maximum_fusion.refs_4_), channel_id=1, source_target_pairs={{0,16},{4,20},{8,24},{12,28},{16,0},{20,4},{24,8},{28,12},{1,17},{... | collective-permute-start | bytes 1228808 | tf_op jit(solution)/shard_map/ppermute | solution.py:107
  6.9 24.2 %collective-permute-start.5 = (bf16[4,160,320]{2,1,0:T(8,128)(2,1)S(1)}, bf16[4,160,320]{2,1,0:T(8,128)(2,1)S(1)}, u32[]{:S(2)}, u32[]{:S(2)}) collective-permute-start(bf16[4,160,320]{2,1,0:T(8,128)(2,1)S(1)} %pad_maximum_fusion.refs_4_), channel_id=1, source_target_pairs={{0,4},{4,0},{8,12},{12,8},{16,20},{20,16},{24,28},{28,24},{1,5},{5... | collective-permute-start | bytes 1228808 | tf_op jit(solution)/shard_map/ppermute | solution.py:107
  25.9 32.2 %copy-start.6 = (bf16[4,160,320]{2,1,0:T(8,128)(2,1)}, bf16[4,160,320]{2,1,0:T(8,128)(2,1)S(1)}, u32[]{:S(2)}) copy-start(bf16[4,160,320]{2,1,0:T(8,128)(2,1)S(1)} %collective-permute-done.1.refs_5_) | copy-start | bytes 1228804
  25.9 11.1 %collective-permute-start.9 = (bf16[144,1280]{1,0:T(8,128)(2,1)S(1)}, bf16[144,1280]{1,0:T(8,128)(2,1)S(1)}, u32[]{:S(2)}, u32[]{:S(2)}) collective-permute-start(bf16[144,1280]{1,0:T(8,128)(2,1)S(1)} %fusion.1.refs_0_), channel_id=1, source_target_pairs={{0,2},{1,3},{2,0},{3,1},{4,6},{5,7},{6,4},{7,5},{8,10},{9,11},{10,... | collective-permute-start | bytes 1105928 | tf_op jit(solution)/shard_map/ppermute | solution.py:107
  28.4 35.2 %copy-start.8 = (bf16[4,160,320]{2,1,0:T(8,128)(2,1)}, bf16[4,160,320]{2,1,0:T(8,128)(2,1)S(1)}, u32[]{:S(2)}) copy-start(bf16[4,160,320]{2,1,0:T(8,128)(2,1)S(1)} %collective-permute-done.3.refs_6_) | copy-start | bytes 1228804
  28.4 10.9 %collective-permute-start.4 = (bf16[4,160,320]{2,1,0:T(8,128)(2,1)S(1)}, bf16[4,160,320]{2,1,0:T(8,128)(2,1)S(1)}, u32[]{:S(2)}, u32[]{:S(2)}) collective-permute-start(bf16[4,160,320]{2,1,0:T(8,128)(2,1)S(1)} %collective-permute-done.3.refs_6_), channel_id=1, source_target_pairs={{0,8},{4,12},{8,0},{12,4},{16,24},{20,28},{24,16},{28,20},{1,9},{5... | collective-permute-start | bytes 1228808 | tf_op jit(solution)/shard_map/ppermute | solution.py:107
  28.9 8.1 %collective-permute-start.2 = (bf16[160,640]{1,0:T(8,128)(2,1)S(1)}, bf16[160,640]{1,0:T(8,128)(2,1)S(1)}, u32[]{:S(2)}, u32[]{:S(2)}) collective-permute-start(bf16[160,640]{1,0:T(8,128)(2,1)S(1)} %get-tuple-element.18), channel_id=1, source_target_pairs={{0,4},{4,0},{8,12},{12,8},{16,20},{20,16},{24,28},{28,24},{1,5},{5... | collective-permute-start | bytes 614408 | tf_op jit(solution)/shard_map/ppermute | solution.py:107
  30.5 17.0 %collective-permute-start.6 = (bf16[4,160,320]{2,1,0:T(8,128)(2,1)S(1)}, bf16[4,160,320]{2,1,0:T(8,128)(2,1)S(1)}, u32[]{:S(2)}, u32[]{:S(2)}) collective-permute-start(bf16[4,160,320]{2,1,0:T(8,128)(2,1)S(1)} %collective-permute-done.1.refs_5_), channel_id=1, source_target_pairs={{0,4},{4,0},{8,12},{12,8},{16,20},{20,16},{24,28},{28,24},{1,5},{5... | collective-permute-start | bytes 1228808 | tf_op jit(solution)/shard_map/ppermute | solution.py:107
  31.0 32.6 %copy-start.10 = (bf16[4,160,320]{2,1,0:T(8,128)(2,1)}, bf16[4,160,320]{2,1,0:T(8,128)(2,1)S(1)}, u32[]{:S(2)}) copy-start(bf16[4,160,320]{2,1,0:T(8,128)(2,1)S(1)} %collective-permute-done.5.refs_8_) | copy-start | bytes 1228804
  31.0 27.0 %collective-permute-start.7 = (bf16[4,160,320]{2,1,0:T(8,128)(2,1)S(1)}, bf16[4,160,320]{2,1,0:T(8,128)(2,1)S(1)}, u32[]{:S(2)}, u32[]{:S(2)}) collective-permute-start(bf16[4,160,320]{2,1,0:T(8,128)(2,1)S(1)} %collective-permute-done.3.refs_6_), channel_id=1, source_target_pairs={{0,4},{4,0},{8,12},{12,8},{16,20},{20,16},{24,28},{28,24},{1,5},{5... | collective-permute-start | bytes 1228808 | tf_op jit(solution)/shard_map/ppermute | solution.py:107
  37.0 3.9 %collective-permute-start.8 = (bf16[144,1280]{1,0:T(8,128)(2,1)S(1)}, bf16[144,1280]{1,0:T(8,128)(2,1)S(1)}, u32[]{:S(2)}, u32[]{:S(2)}) collective-permute-start(bf16[144,1280]{1,0:T(8,128)(2,1)S(1)} %fusion.1.refs_0_), channel_id=1, source_target_pairs={{0,1},{1,0},{2,3},{3,2},{4,5},{5,4},{6,7},{7,6},{8,9},{9,8},{10,11... | collective-permute-start | bytes 1105928 | tf_op jit(solution)/shard_map/ppermute | solution.py:107
  37.0 21.1 %collective-permute-start.10 = (bf16[144,1280]{1,0:T(8,128)(2,1)S(1)}, bf16[144,1280]{1,0:T(8,128)(2,1)S(1)}, u32[]{:S(2)}, u32[]{:S(2)}) collective-permute-start(bf16[144,1280]{1,0:T(8,128)(2,1)S(1)} %collective-permute-done.9.refs_1_), channel_id=1, source_target_pairs={{0,1},{1,0},{2,3},{3,2},{4,5},{5,4},{6,7},{7,6},{8,9},{9,8},{10,11... | collective-permute-start | bytes 1105928 | tf_op jit(solution)/shard_map/ppermute | solution.py:107
  39.4 29.8 %collective-permute-start.14 = (bf16[4,160,320]{2,1,0:T(8,128)(2,1)S(1)}, bf16[4,160,320]{2,1,0:T(8,128)(2,1)S(1)}, u32[]{:S(2)}, u32[]{:S(2)}) collective-permute-start(bf16[4,160,320]{2,1,0:T(8,128)(2,1)S(1)} %collective-permute-done.4.refs_7_), channel_id=1, source_target_pairs={{0,4},{4,0},{8,12},{12,8},{16,20},{20,16},{24,28},{28,24},{1,5},{5... | collective-permute-start | bytes 1228808 | tf_op jit(solution)/shard_map/ppermute | solution.py:107
  58.1 8.9 %collective-permute-start.11 = (bf16[160,640]{1,0:T(8,128)(2,1)S(1)}, bf16[160,640]{1,0:T(8,128)(2,1)S(1)}, u32[]{:S(2)}, u32[]{:S(2)}) collective-permute-start(bf16[160,640]{1,0:T(8,128)(2,1)S(1)} %get-tuple-element.20.refs_0_), channel_id=1, source_target_pairs={{0,8},{4,12},{8,0},{12,4},{16,24},{20,28},{24,16},{28,20},{1,9},{5... | collective-permute-start | bytes 614408 | tf_op jit(solution)/shard_map/ppermute | solution.py:107
  59.7 9.5 %collective-permute-start.12 = (bf16[160,640]{1,0:T(8,128)(2,1)S(1)}, bf16[160,640]{1,0:T(8,128)(2,1)S(1)}, u32[]{:S(2)}, u32[]{:S(2)}) collective-permute-start(bf16[160,640]{1,0:T(8,128)(2,1)S(1)} %collective-permute-done.2.refs_1_), channel_id=1, source_target_pairs={{0,8},{4,12},{8,0},{12,4},{16,24},{20,28},{24,16},{28,20},{1,9},{5... | collective-permute-start | bytes 614408 | tf_op jit(solution)/shard_map/ppermute | solution.py:107
  60.2 9.0 %collective-permute-start.13 = (bf16[160,640]{1,0:T(8,128)(2,1)S(1)}, bf16[160,640]{1,0:T(8,128)(2,1)}, u32[]{:S(2)}, u32[]{:S(2)}) collective-permute-start(bf16[160,640]{1,0:T(8,128)(2,1)S(1)} %get-tuple-element.20.refs_0_), channel_id=1, source_target_pairs={{0,16},{4,20},{8,24},{12,28},{16,0},{20,4},{24,8},{28,12},{1,17},{... | collective-permute-start | bytes 614408 | tf_op jit(solution)/shard_map/ppermute | solution.py:107
  76.7 16.2 %copy-start = (bf16[128,1280]{1,0:T(8,128)(2,1)S(1)}, bf16[128,1280]{1,0:T(8,128)(2,1)}, u32[]{:S(2)}) copy-start(bf16[128,1280]{1,0:T(8,128)(2,1)} %tokens_ref.1) | copy-start | bytes 983044
  76.7 2.2 %collective-permute-start.15 = (bf16[256,1280]{1,0:T(8,128)(2,1)S(1)}, bf16[256,1280]{1,0:T(8,128)(2,1)S(1)}, u32[]{:S(2)}, u32[]{:S(2)}) collective-permute-start(bf16[256,1280]{1,0:T(8,128)(2,1)S(1)} %get-tuple-element.24), channel_id=1, source_target_pairs={{0,1},{1,0},{2,3},{3,2},{4,5},{5,4},{6,7},{7,6},{8,9},{9,8},{10,11... | collective-permute-start | bytes 1966088 | tf_op jit(solution)/shard_map/ppermute | solution.py:107
  78.9 14.0 %collective-permute-start.16 = (bf16[128,1280]{1,0:T(8,128)(2,1)S(1)}, bf16[128,1280]{1,0:T(8,128)(2,1)S(1)}, u32[]{:S(2)}, u32[]{:S(2)}) collective-permute-start(bf16[128,1280]{1,0:T(8,128)(2,1)S(1)} %shard_map.84), channel_id=1, source_target_pairs={{0,2},{1,3},{2,0},{3,1},{4,6},{5,7},{6,4},{7,5},{8,10},{9,11},{10,... | collective-permute-start | bytes 983048 | tf_op jit(solution)/shard_map/ppermute | solution.py:107
  80.7 12.2 %collective-permute-start.17 = (bf16[160,640]{1,0:T(8,128)(2,1)S(1)}, bf16[160,640]{1,0:T(8,128)(2,1)}, u32[]{:S(2)}, u32[]{:S(2)}) collective-permute-start(bf16[160,640]{1,0:T(8,128)(2,1)S(1)} %collective-permute-done.2.refs_1_), channel_id=1, source_target_pairs={{0,16},{4,20},{8,24},{12,28},{16,0},{20,4},{24,8},{28,12},{1,17},{... | collective-permute-start | bytes 614408 | tf_op jit(solution)/shard_map/ppermute | solution.py:107
  82.1 10.8 %collective-permute-start.18 = (bf16[160,640]{1,0:T(8,128)(2,1)}, bf16[160,640]{1,0:T(8,128)(2,1)}, u32[]{:S(2)}, u32[]{:S(2)}) collective-permute-start(bf16[160,640]{1,0:T(8,128)(2,1)} %collective-permute-done.13.refs_4_), channel_id=1, source_target_pairs={{0,8},{4,12},{8,0},{12,4},{16,24},{20,28},{24,16},{28,20},{1,9},{5... | collective-permute-start | bytes 614408 | tf_op jit(solution)/shard_map/ppermute | solution.py:107
  82.2 16.2 %collective-permute-start = (s32[32,1]{0,1:T(1,128)S(1)}, s32[32,1]{0,1:T(1,128)S(1)}, u32[]{:S(2)}, u32[]{:S(2)}) collective-permute-start(s32[32,1]{0,1:T(1,128)S(1)} %copy-done.13), channel_id=1, source_target_pairs={{0,4},{4,0},{8,12},{12,8},{16,20},{20,16},{24,28},{28,24},{1,5},{5... | collective-permute-start | bytes 392 | tf_op jit(solution)/shard_map/ppermute | solution.py:107
  94.5 14.8 %copy-start.2 = (bf16[160,640]{1,0:T(8,128)(2,1)S(1)}, bf16[160,640]{1,0:T(8,128)(2,1)}, u32[]{:S(2)}) copy-start(bf16[160,640]{1,0:T(8,128)(2,1)} %copy-done.1) | copy-start | bytes 614404
  94.5 14.8 %copy-start.4 = (bf16[160,640]{1,0:T(8,128)(2,1)S(1)}, bf16[160,640]{1,0:T(8,128)(2,1)}, u32[]{:S(2)}) copy-start(bf16[160,640]{1,0:T(8,128)(2,1)} %copy-done.3) | copy-start | bytes 614404
  94.6 14.8 %all-to-all-start = ((bf16[8,64,640]{2,1,0:T(8,128)(2,1)}), bf16[8,64,640]{2,1,0:T(8,128)(2,1)S(1)}, u32[]{:S(2)}, u32[]{:S(2)}) async-start(bf16[8,64,640]{2,1,0:T(8,128)(2,1)} %shard_map.85), calls=%async_computation | async-start | bytes 1310720 | tf_op jit(solution)/shard_map/all_to_all | solution.py:323
  98.6 7.7 %collective-permute-start.19 = (bf16[160,640]{1,0:T(8,128)(2,1)}, bf16[160,640]{1,0:T(8,128)(2,1)S(1)}, u32[]{:S(2)}, u32[]{:S(2)}) collective-permute-start(bf16[160,640]{1,0:T(8,128)(2,1)} %collective-permute-done.17.refs_5_), channel_id=1, source_target_pairs={{0,8},{4,12},{8,0},{12,4},{16,24},{20,28},{24,16},{28,20},{1,9},{5... | collective-permute-start | bytes 614408 | tf_op jit(solution)/shard_map/ppermute | solution.py:107
  111.5 2.0 %collective-permute-start.20 = (bf16[64,640]{1,0:T(8,128)(2,1)S(1)}, bf16[64,640]{1,0:T(8,128)(2,1)S(1)}, u32[]{:S(2)}, u32[]{:S(2)}) collective-permute-start(bf16[64,640]{1,0:T(8,128)(2,1)S(1)} %get-tuple-element.28), channel_id=1, source_target_pairs={{0,1},{1,0},{2,3},{3,2},{4,5},{5,4},{6,7},{7,6},{8,9},{9,8},{10,11... | collective-permute-start | bytes 245768 | tf_op jit(solution)/shard_map/ppermute | solution.py:107
  111.6 5.3 %collective-permute-start.21 = (bf16[64,640]{1,0:T(8,128)(2,1)S(1)}, bf16[64,640]{1,0:T(8,128)(2,1)S(1)}, u32[]{:S(2)}, u32[]{:S(2)}) collective-permute-start(bf16[64,640]{1,0:T(8,128)(2,1)S(1)} %get-tuple-element.29), channel_id=1, source_target_pairs={{0,2},{1,3},{2,0},{3,1},{4,6},{5,7},{6,4},{7,5},{8,10},{9,11},{10,... | collective-permute-start | bytes 245768 | tf_op jit(solution)/shard_map/ppermute | solution.py:107
  112.2 5.5 %collective-permute-start.22 = (bf16[64,640]{1,0:T(8,128)(2,1)S(1)}, bf16[64,640]{1,0:T(8,128)(2,1)S(1)}, u32[]{:S(2)}, u32[]{:S(2)}) collective-permute-start(bf16[64,640]{1,0:T(8,128)(2,1)S(1)} %get-tuple-element.30), channel_id=1, source_target_pairs={{0,3},{1,2},{2,1},{3,0},{4,7},{5,6},{6,5},{7,4},{8,11},{9,10},{10,... | collective-permute-start | bytes 245768 | tf_op jit(solution)/shard_map/ppermute | solution.py:107
  (7 other events, 43.6 us)

commit v6 on v5

--- a/solution.py
+++ b/solution.py
@@ -262,10 +262,16 @@
     group = n_fsdp * rows
 
     heads = jnp.concatenate([qkv_weight, out_weight.T[None]], axis=0)
-    along_z = [swap(heads, "dp", 2), swap(heads, "dp", 4)]
-    along_y = [swap(heads, "dp", 1)]
-    along_z += [swap(along_z[1], "dp", 2)]
-    along_y += [swap(block, "dp", 1) for block in along_z]
+    along_z, along_y = [swap(heads, "dp", 2)], [swap(heads, "dp", 1)]
+    along_z += [swap(after(heads, (along_z[0], along_y[0])), "dp", 4)]
+    along_y += [swap(along_z[0], "dp", 1)]
+    half = merge_weight.shape[1] // 2
+    low, high = merge_weight[:, :half], merge_weight[:, half:]
+    lower = y == 0
+    mine = jnp.where(lower, low, high)
+    theirs = swap(after(jnp.where(lower, high, low), along_z[0]), "dp", 1)
+    along_z += [swap(after(along_z[1], (along_y[1], theirs)), "dp", 2)]
+    along_y += [swap(block, "dp", 1) for block in along_z[1:]]
 
     marks = jnp.pad(segments.astype(bf16), ((0, 15), (0, width - rows)))
     marked = after(jnp.concatenate([tokens, marks], axis=0), along_z[0])
@@ -273,15 +279,10 @@
     group_rows = [marked, along_x, swap(marked, "fsdp", 1), swap(along_x, "fsdp", 1)]
     (normed,) = call(norm_kernel, [shape((group, width), bf16)], [ln_gains, *group_rows])
 
-    half = merge_weight.shape[1] // 2
-    low, high = merge_weight[:, :half], merge_weight[:, half:]
-    lower = y == 0
-    mine = jnp.where(lower, low, high)
-    theirs = swap(after(jnp.where(lower, high, low), along_z[0]), "dp", 1)
-    held, held_other = after((mine, theirs), (along_z[2], *along_y[:3], *group_rows[2:]))
+    far = swap(after(mine, (along_z[2], *group_rows[2:])), "dp", 4)
+    held, held_other = after((mine, theirs), far)
     merge_pieces = [mine, theirs, swap(held, "dp", 2), swap(held_other, "dp", 2)]
-    merge_pieces += [swap(held, "dp", 4)]
-    merge_pieces += [swap(after(held_other, merge_pieces[4]), "dp", 4)]
+    merge_pieces += [far, swap(held_other, "dp", 4)]
     merge_pieces += [swap(piece, "dp", 2) for piece in merge_pieces[4:6]]
 
     capacity = max(2, (2 * count + n_dp - 1) // n_dp)
@@ -298,7 +299,7 @@
         attention_kernel,
         [shape((2 * rows, width), f32), shape((2 * rows, width), bf16)],
         [
-            after(me_cell, merge_pieces[2:5]),
+            after(me_cell, far),
             normed,
             *group_rows,
             heads,

time: 130 us -> 132 us (1.015)
  waiting for transfers between devices: 69.7 us -> 76.3 us
  starting transfers between devices: 30.7 us -> 27.8 us
    ppermute x23, waiting for transfers between devices: 66.7 us -> 76.3 us  [swap(): lax.ppermute(value, axis, [(i, i ^ k) for i in range(lax.axis_size(axis))])]
    all_to_all x1, waiting for transfers between devices: 3.01 us -> 0.01 us  [by_permutes(): lax.all_to_all(slices, ('dp', 'fsdp'), split_axis=0, concat_axis=0, tiled...]
    ppermute x23, starting transfers between devices: 27.1 us -> 24.3 us  [swap(): lax.ppermute(value, axis, [(i, i ^ k) for i in range(lax.axis_size(axis))])]
    unnamed x31 -> x19, local copies, waits for them, and re-layouts: 2.78 us -> 2.57 us
  transfers between devices with their start and end apart: 24 -> 24, of which waited for: 14 -> 13; matrix products, arithmetic and copies ran while one was open for 3% -> 2% of each run, Pallas kernels for 2% -> 2%
where the time goes in v6:
time: 132 us
  waiting for transfers between devices  76.3 us (58%)
  starting transfers between devices  27.8 us (21%)
  blocking collectives  10.4 us (8%)
  Pallas kernels  10.2 us (8%)
  local copies, waits for them, and re-layouts  3.55 us (3%)
  other arithmetic  3.31 us (3%)
    ppermute x23, waiting for transfers between devices, swap(): lax.ppermute(value, axis, [(i, i ^ k) for i in range(lax.axis_size(axis))])  76.3 us
    ppermute x23, starting transfers between devices, swap(): lax.ppermute(value, axis, [(i, i ^ k) for i in range(lax.axis_size(axis))])  24.3 us
    all_to_all x1, blocking collectives, by_permutes(): lax.all_to_all(packed.reshape(n_dp, 2 * capacity, half), 'dp', split_axis...  10.4 us
    pallas_call x6, Pallas kernels, call(): pl.pallas_call(kernel, out_shape=tuple(outs), in_specs=specs, out_specs=t...  10.2 us
    all_to_all x1, starting transfers between devices, by_permutes(): lax.all_to_all(slices, ('dp', 'fsdp'), split_axis=0, concat_axis=0, tiled...  3.54 us
  transfers between devices with their start and end apart: 24, of which 13 were waited for; matrix products, arithmetic and copies ran while one was open for 2% of the time, Pallas kernels for 2%

profile of v6, /device:TPU:0, one launch (start us, length us, event | category | flops | bytes accessed | tf_op | source)
XLA Modules:
  0.0 131.8 jit_solution(2793404048680693120)
XLA Ops:
  0.0 1.2 pad_maximum_fusion.refs_4_
  1.2 3.1 %collective-permute-start.1 = (bf16[4,160,320]{2,1,0:T(8,128)(2,1)S(1)}, bf16[4,160,320]{2,1,0:T(8,128)(2,1)S(1)}, u32[]{:S(2)}, u32[]{:S(2)}) collective-permute-start(bf16[4,160,320]{2,1,0:T(8,128)(2,1)S(1)} %pad_maximum_fusion.refs_4_), channel_id=1, source_target_pairs={{0,8},{4,12},{8,0},{12,4},{16,24},{20,28},{24,16},{28,20},{1,9},{5... | collective-permute-start | bytes 1228808 | tf_op jit(solution)/shard_map/ppermute | solution.py:107
  4.3 1.5 %collective-permute-start.2 = (bf16[4,160,320]{2,1,0:T(8,128)(2,1)S(1)}, bf16[4,160,320]{2,1,0:T(8,128)(2,1)S(1)}, u32[]{:S(2)}, u32[]{:S(2)}) collective-permute-start(bf16[4,160,320]{2,1,0:T(8,128)(2,1)S(1)} %pad_maximum_fusion.refs_4_), channel_id=1, source_target_pairs={{0,4},{4,0},{8,12},{12,8},{16,20},{20,16},{24,28},{28,24},{1,5},{5... | collective-permute-start | bytes 1228808 | tf_op jit(solution)/shard_map/ppermute | solution.py:107
  5.8 9.7 %collective-permute-done.1.refs_5_ = bf16[4,160,320]{2,1,0:T(8,128)(2,1)S(1)} collective-permute-done((bf16[4,160,320]{2,1,0:T(8,128)(2,1)S(1)}, bf16[4,160,320]{2,1,0:T(8,128)(2,1)S(1)}, u32[]{:S(2)}, u32[]{:S(2)}) %collective-permute-start.1) | collective-permute-done | bytes 409632 | tf_op jit(solution)/shard_map/ppermute | solution.py:107
  15.5 1.5 %collective-permute-done.2.refs_8_ = bf16[4,160,320]{2,1,0:T(8,128)(2,1)S(1)} collective-permute-done((bf16[4,160,320]{2,1,0:T(8,128)(2,1)S(1)}, bf16[4,160,320]{2,1,0:T(8,128)(2,1)S(1)}, u32[]{:S(2)}, u32[]{:S(2)}) %collective-permute-start.2) | collective-permute-done | bytes 409632 | tf_op jit(solution)/shard_map/ppermute | solution.py:107
  17.0 2.6 %collective-permute-start.3 = (bf16[4,160,320]{2,1,0:T(8,128)(2,1)S(1)}, bf16[4,160,320]{2,1,0:T(8,128)(2,1)S(1)}, u32[]{:S(2)}, u32[]{:S(2)}) collective-permute-start(bf16[4,160,320]{2,1,0:T(8,128)(2,1)S(1)} %pad_maximum_fusion.refs_4_), channel_id=1, source_target_pairs={{0,16},{4,20},{8,24},{12,28},{16,0},{20,4},{24,8},{28,12},{1,17},{... | collective-permute-start | bytes 1228808 | tf_op jit(solution)/shard_map/ppermute | solution.py:107
  19.6 1.5 %collective-permute-start.4 = (bf16[4,160,320]{2,1,0:T(8,128)(2,1)S(1)}, bf16[4,160,320]{2,1,0:T(8,128)(2,1)S(1)}, u32[]{:S(2)}, u32[]{:S(2)}) collective-permute-start(bf16[4,160,320]{2,1,0:T(8,128)(2,1)S(1)} %collective-permute-done.1.refs_5_), channel_id=1, source_target_pairs={{0,4},{4,0},{8,12},{12,8},{16,20},{20,16},{24,28},{28,24},{1,5},{5... | collective-permute-start | bytes 1228808 | tf_op jit(solution)/shard_map/ppermute | solution.py:107
  21.1 1.1 broadcast_select_fusion
  22.8 1.6 %collective-permute-start.8 = (bf16[144,1280]{1,0:T(8,128)(2,1)S(1)}, bf16[144,1280]{1,0:T(8,128)(2,1)S(1)}, u32[]{:S(2)}, u32[]{:S(2)}) collective-permute-start(bf16[144,1280]{1,0:T(8,128)(2,1)S(1)} %fusion.1.refs_0_), channel_id=1, source_target_pairs={{0,2},{1,3},{2,0},{3,1},{4,6},{5,7},{6,4},{7,5},{8,10},{9,11},{10,... | collective-permute-start | bytes 1105928 | tf_op jit(solution)/shard_map/ppermute | solution.py:107
  24.3 11.1 %collective-permute-done.5.refs_1_ = bf16[160,640]{1,0:T(8,128)(2,1)S(1)} collective-permute-done((bf16[160,640]{1,0:T(8,128)(2,1)S(1)}, bf16[160,640]{1,0:T(8,128)(2,1)S(1)}, u32[]{:S(2)}, u32[]{:S(2)}) %collective-permute-start.5) | collective-permute-done | bytes 204832 | tf_op jit(solution)/shard_map/ppermute | solution.py:107
  35.4 4.7 %collective-permute-done.3.refs_6_ = bf16[4,160,320]{2,1,0:T(8,128)(2,1)S(1)} collective-permute-done((bf16[4,160,320]{2,1,0:T(8,128)(2,1)S(1)}, bf16[4,160,320]{2,1,0:T(8,128)(2,1)S(1)}, u32[]{:S(2)}, u32[]{:S(2)}) %collective-permute-start.3) | collective-permute-done | bytes 409632 | tf_op jit(solution)/shard_map/ppermute | solution.py:107
  40.7 1.5 %collective-permute-start.11 = (bf16[4,160,320]{2,1,0:T(8,128)(2,1)S(1)}, bf16[4,160,320]{2,1,0:T(8,128)(2,1)S(1)}, u32[]{:S(2)}, u32[]{:S(2)}) collective-permute-start(bf16[4,160,320]{2,1,0:T(8,128)(2,1)S(1)} %collective-permute-done.3.refs_6_), channel_id=1, source_target_pairs={{0,4},{4,0},{8,12},{12,8},{16,20},{20,16},{24,28},{28,24},{1,5},{5... | collective-permute-start | bytes 1228808 | tf_op jit(solution)/shard_map/ppermute | solution.py:107
  42.2 11.0 %collective-permute-done.6.refs_7_ = bf16[4,160,320]{2,1,0:T(8,128)(2,1)S(1)} collective-permute-done((bf16[4,160,320]{2,1,0:T(8,128)(2,1)S(1)}, bf16[4,160,320]{2,1,0:T(8,128)(2,1)S(1)}, u32[]{:S(2)}, u32[]{:S(2)}) %collective-permute-start.6) | collective-permute-done | bytes 409632 | tf_op jit(solution)/shard_map/ppermute | solution.py:107
  53.2 1.5 %collective-permute-start.12 = (bf16[4,160,320]{2,1,0:T(8,128)(2,1)S(1)}, bf16[4,160,320]{2,1,0:T(8,128)(2,1)S(1)}, u32[]{:S(2)}, u32[]{:S(2)}) collective-permute-start(bf16[4,160,320]{2,1,0:T(8,128)(2,1)S(1)} %collective-permute-done.6.refs_7_), channel_id=1, source_target_pairs={{0,4},{4,0},{8,12},{12,8},{16,20},{20,16},{24,28},{28,24},{1,5},{5... | collective-permute-start | bytes 1228808 | tf_op jit(solution)/shard_map/ppermute | solution.py:107
  56.4 9.5 %collective-permute-done.10.refs_4_ = bf16[160,640]{1,0:T(8,128)(2,1)} collective-permute-done((bf16[160,640]{1,0:T(8,128)(2,1)S(1)}, bf16[160,640]{1,0:T(8,128)(2,1)}, u32[]{:S(2)}, u32[]{:S(2)}) %collective-permute-start.10) | collective-permute-done | bytes 204832 | tf_op jit(solution)/shard_map/ppermute | solution.py:107
  65.9 1.0 copy-done.3
  68.0 5.2 %shard_map.83 = (f32[256,1280]{1,0:T(8,128)S(1)}, bf16[256,1280]{1,0:T(8,128)(2,1)S(1)}) custom-call(s32[1]{0:T(128)} %bitcast.3.me_ref, bf16[512,1280]{1,0:T(8,128)(2,1)S(1)} %shard_map.82.rows_ref, bf16[144,1280]{1,0:T(8,128)(2,1)S(1)} %fusion.1.refs_0_, bf16[144,1280]{1,0:T(8,128)(2,1)S(1)} %collective-permute-done.8.refs_1_, ...), custom_call_target="tpu_custom_call" | custom-call | flops 2013265920 | bytes 8028164 | tf_op jit(solution)/shard_map/pallas_call | solution.py:129
  73.3 2.1 %collective-permute-done.13.got_ref.core_ref = bf16[256,1280]{1,0:T(8,128)(2,1)S(1)} collective-permute-done((bf16[256,1280]{1,0:T(8,128)(2,1)S(1)}, bf16[256,1280]{1,0:T(8,128)(2,1)S(1)}, u32[]{:S(2)}, u32[]{:S(2)}) %collective-permute-start.13) | collective-permute-done | bytes 655392 | tf_op jit(solution)/shard_map/ppermute | solution.py:107
  75.5 1.6 %collective-permute-start.14 = (bf16[128,1280]{1,0:T(8,128)(2,1)S(1)}, bf16[128,1280]{1,0:T(8,128)(2,1)S(1)}, u32[]{:S(2)}, u32[]{:S(2)}) collective-permute-start(bf16[128,1280]{1,0:T(8,128)(2,1)S(1)} %shard_map.84), channel_id=1, source_target_pairs={{0,2},{1,3},{2,0},{3,1},{4,6},{5,7},{6,4},{7,5},{8,10},{9,11},{10,... | collective-permute-start | bytes 983048 | tf_op jit(solution)/shard_map/ppermute | solution.py:107
  77.0 1.7 %collective-permute-start.15 = (bf16[160,640]{1,0:T(8,128)(2,1)S(1)}, bf16[160,640]{1,0:T(8,128)(2,1)}, u32[]{:S(2)}, u32[]{:S(2)}) collective-permute-start(bf16[160,640]{1,0:T(8,128)(2,1)S(1)} %collective-permute-done.5.refs_1_), channel_id=1, source_target_pairs={{0,16},{4,20},{8,24},{12,28},{16,0},{20,4},{24,8},{28,12},{1,17},{... | collective-permute-start | bytes 614408 | tf_op jit(solution)/shard_map/ppermute | solution.py:107
  78.8 1.5 %collective-permute-start = (s32[32,1]{0,1:T(1,128)S(1)}, s32[32,1]{0,1:T(1,128)S(1)}, u32[]{:S(2)}, u32[]{:S(2)}) collective-permute-start(s32[32,1]{0,1:T(1,128)S(1)} %copy-done.6), channel_id=1, source_target_pairs={{0,4},{4,0},{8,12},{12,8},{16,20},{20,16},{24,28},{28,24},{1,5},{5... | collective-permute-start | bytes 392 | tf_op jit(solution)/shard_map/ppermute | solution.py:107
  81.7 7.6 %collective-permute-done.15.refs_5_ = bf16[160,640]{1,0:T(8,128)(2,1)} collective-permute-done((bf16[160,640]{1,0:T(8,128)(2,1)S(1)}, bf16[160,640]{1,0:T(8,128)(2,1)}, u32[]{:S(2)}, u32[]{:S(2)}) %collective-permute-start.15) | collective-permute-done | bytes 204832 | tf_op jit(solution)/shard_map/ppermute | solution.py:107
  89.9 1.7 %shard_map.85 = bf16[8,64,640]{2,1,0:T(8,128)(2,1)} custom-call(bf16[128,1280]{1,0:T(8,128)(2,1)S(1)} %copy-done, f32[256,1280]{1,0:T(8,128)S(1)} %get-tuple-element.26.keep_ref, bf16[256,1280]{1,0:T(8,128)(2,1)S(1)} %collective-permute-done.13.got_ref.core_ref, bf16[128,1280]{1,0:T(8,128)(2,1)S(1)} %collective-permute-done.14.chip_ref, ...), custom_call_target="tpu_custom_call" | custom-call | flops 41943040 | bytes 3287552 | tf_op jit(solution)/shard_map/pallas_call | solution.py:129
  91.6 3.5 %all-to-all-start = ((bf16[8,64,640]{2,1,0:T(8,128)(2,1)}), bf16[8,64,640]{2,1,0:T(8,128)(2,1)S(1)}, u32[]{:S(2)}, u32[]{:S(2)}) async-start(bf16[8,64,640]{2,1,0:T(8,128)(2,1)} %shard_map.85), calls=%async_computation | async-start | bytes 1310720 | tf_op jit(solution)/shard_map/all_to_all | solution.py:324
  95.8 1.8 %collective-permute-start.17 = (bf16[160,640]{1,0:T(8,128)(2,1)S(1)}, bf16[160,640]{1,0:T(8,128)(2,1)S(1)}, u32[]{:S(2)}, u32[]{:S(2)}) collective-permute-start(bf16[160,640]{1,0:T(8,128)(2,1)S(1)} %get-tuple-element.30.refs_0_), channel_id=1, source_target_pairs={{0,8},{4,12},{8,0},{12,4},{16,24},{20,28},{24,16},{28,20},{1,9},{5... | collective-permute-start | bytes 614408 | tf_op jit(solution)/shard_map/ppermute | solution.py:107
  97.8 10.1 %collective-permute-done.17.refs_2_ = bf16[160,640]{1,0:T(8,128)(2,1)S(1)} collective-permute-done((bf16[160,640]{1,0:T(8,128)(2,1)S(1)}, bf16[160,640]{1,0:T(8,128)(2,1)S(1)}, u32[]{:S(2)}, u32[]{:S(2)}) %collective-permute-start.17) | collective-permute-done | bytes 204832 | tf_op jit(solution)/shard_map/ppermute | solution.py:107
  107.9 3.9 %collective-permute-done.19.refs_7_ = bf16[160,640]{1,0:T(8,128)(2,1)S(1)} collective-permute-done((bf16[160,640]{1,0:T(8,128)(2,1)}, bf16[160,640]{1,0:T(8,128)(2,1)S(1)}, u32[]{:S(2)}, u32[]{:S(2)}) %collective-permute-start.19) | collective-permute-done | bytes 204832 | tf_op jit(solution)/shard_map/ppermute | solution.py:107
  111.8 2.2 %shard_map.86 = (f32[64,640]{1,0:T(8,128)S(1)}, bf16[64,640]{1,0:T(8,128)(2,1)S(1)}, bf16[64,640]{1,0:T(8,128)(2,1)S(1)}, bf16[64,640]{1,0:T(8,128)(2,1)S(1)}) custom-call(s32[1]{0:T(128)} %bitcast.3.me_ref, s32[1]{0:T(128)} %bitcast.4.at_ref, bf16[8,64,640]{2,1,0:T(8,128)(2,1)S(1)} %all-to-all-done.inputs, bf16[160,640]{1,0:T(8,128)(2,1)S(1)} %get-tuple-element.30.refs_0_, ...), custom_call_target="tpu_custom_call" | custom-call | flops 419430400 | bytes 2703368 | tf_op jit(solution)/shard_map/pallas_call | solution.py:129
  114.1 1.7 %collective-permute-start.21 = (bf16[64,640]{1,0:T(8,128)(2,1)S(1)}, bf16[64,640]{1,0:T(8,128)(2,1)S(1)}, u32[]{:S(2)}, u32[]{:S(2)}) collective-permute-start(bf16[64,640]{1,0:T(8,128)(2,1)S(1)} %get-tuple-element.33), channel_id=1, source_target_pairs={{0,2},{1,3},{2,0},{3,1},{4,6},{5,7},{6,4},{7,5},{8,10},{9,11},{10,... | collective-permute-start | bytes 245768 | tf_op jit(solution)/shard_map/ppermute | solution.py:107
  116.0 3.1 %collective-permute-done.21.two_ref = bf16[64,640]{1,0:T(8,128)(2,1)S(1)} collective-permute-done((bf16[64,640]{1,0:T(8,128)(2,1)S(1)}, bf16[64,640]{1,0:T(8,128)(2,1)S(1)}, u32[]{:S(2)}, u32[]{:S(2)}) %collective-permute-start.21) | collective-permute-done | bytes 81952 | tf_op jit(solution)/shard_map/ppermute | solution.py:107
  119.1 1.4 %collective-permute-done.22.three_ref = bf16[64,640]{1,0:T(8,128)(2,1)S(1)} collective-permute-done((bf16[64,640]{1,0:T(8,128)(2,1)S(1)}, bf16[64,640]{1,0:T(8,128)(2,1)S(1)}, u32[]{:S(2)}, u32[]{:S(2)}) %collective-permute-start.22) | collective-permute-done | bytes 81952 | tf_op jit(solution)/shard_map/ppermute | solution.py:107
  120.7 10.4 %all_to_all.10 = bf16[8,16,640]{2,1,0:T(8,128)(2,1)S(1)} all-to-all(bf16[8,16,640]{2,1,0:T(8,128)(2,1)S(1)} %bitcast.17), channel_id=1, replica_groups=mesh['dp'=8,'fsdp'=4] {'dp'}, dimensions={0} | all-to-all | bytes 327680 | tf_op jit(solution)/shard_map/all_to_all | solution.py:349
  (56 shorter events, 8.0 us)
Async XLA Ops:
  0.0 22.2 %copy-start.7 = (s32[1,128]{1,0:T(1,128)S(1)}, s32[1,128]{1,0:T(1,128)}, u32[]{:S(2)}) copy-start(s32[1,128]{1,0:T(1,128)} %param.13) | copy-start | bytes 1540
  0.0 22.7 %copy-start = (bf16[128,1280]{1,0:T(8,128)(2,1)S(1)}, bf16[128,1280]{1,0:T(8,128)(2,1)}, u32[]{:S(2)}) copy-start(bf16[128,1280]{1,0:T(8,128)(2,1)} %tokens_ref.1) | copy-start | bytes 983044
  0.0 55.5 %copy-start.1 = (f32[2,1280]{1,0:T(2,128)S(1)}, f32[2,1280]{1,0:T(2,128)}, u32[]{:S(2)}) copy-start(f32[2,1280]{1,0:T(2,128)} %gains_ref.3) | copy-start | bytes 30724
  1.2 14.3 %collective-permute-start.1 = (bf16[4,160,320]{2,1,0:T(8,128)(2,1)S(1)}, bf16[4,160,320]{2,1,0:T(8,128)(2,1)S(1)}, u32[]{:S(2)}, u32[]{:S(2)}) collective-permute-start(bf16[4,160,320]{2,1,0:T(8,128)(2,1)S(1)} %pad_maximum_fusion.refs_4_), channel_id=1, source_target_pairs={{0,8},{4,12},{8,0},{12,4},{16,24},{20,28},{24,16},{28,20},{1,9},{5... | collective-permute-start | bytes 1228808 | tf_op jit(solution)/shard_map/ppermute | solution.py:107
  4.3 12.7 %collective-permute-start.2 = (bf16[4,160,320]{2,1,0:T(8,128)(2,1)S(1)}, bf16[4,160,320]{2,1,0:T(8,128)(2,1)S(1)}, u32[]{:S(2)}, u32[]{:S(2)}) collective-permute-start(bf16[4,160,320]{2,1,0:T(8,128)(2,1)S(1)} %pad_maximum_fusion.refs_4_), channel_id=1, source_target_pairs={{0,4},{4,0},{8,12},{12,8},{16,20},{20,16},{24,28},{28,24},{1,5},{5... | collective-permute-start | bytes 1228808 | tf_op jit(solution)/shard_map/ppermute | solution.py:107
  15.5 40.8 %copy-start.2 = (bf16[4,160,320]{2,1,0:T(8,128)(2,1)}, bf16[4,160,320]{2,1,0:T(8,128)(2,1)S(1)}, u32[]{:S(2)}) copy-start(bf16[4,160,320]{2,1,0:T(8,128)(2,1)S(1)} %collective-permute-done.1.refs_5_) | copy-start | bytes 1228804
  17.0 39.4 %copy-start.4 = (bf16[4,160,320]{2,1,0:T(8,128)(2,1)}, bf16[4,160,320]{2,1,0:T(8,128)(2,1)S(1)}, u32[]{:S(2)}) copy-start(bf16[4,160,320]{2,1,0:T(8,128)(2,1)S(1)} %collective-permute-done.2.refs_8_) | copy-start | bytes 1228804
  17.0 23.2 %collective-permute-start.3 = (bf16[4,160,320]{2,1,0:T(8,128)(2,1)S(1)}, bf16[4,160,320]{2,1,0:T(8,128)(2,1)S(1)}, u32[]{:S(2)}, u32[]{:S(2)}) collective-permute-start(bf16[4,160,320]{2,1,0:T(8,128)(2,1)S(1)} %pad_maximum_fusion.refs_4_), channel_id=1, source_target_pairs={{0,16},{4,20},{8,24},{12,28},{16,0},{20,4},{24,8},{28,12},{1,17},{... | collective-permute-start | bytes 1228808 | tf_op jit(solution)/shard_map/ppermute | solution.py:107
  19.6 20.6 %collective-permute-start.4 = (bf16[4,160,320]{2,1,0:T(8,128)(2,1)S(1)}, bf16[4,160,320]{2,1,0:T(8,128)(2,1)S(1)}, u32[]{:S(2)}, u32[]{:S(2)}) collective-permute-start(bf16[4,160,320]{2,1,0:T(8,128)(2,1)S(1)} %collective-permute-done.1.refs_5_), channel_id=1, source_target_pairs={{0,4},{4,0},{8,12},{12,8},{16,20},{20,16},{24,28},{28,24},{1,5},{5... | collective-permute-start | bytes 1228808 | tf_op jit(solution)/shard_map/ppermute | solution.py:107
  22.2 13.3 %collective-permute-start.5 = (bf16[160,640]{1,0:T(8,128)(2,1)S(1)}, bf16[160,640]{1,0:T(8,128)(2,1)S(1)}, u32[]{:S(2)}, u32[]{:S(2)}) collective-permute-start(bf16[160,640]{1,0:T(8,128)(2,1)S(1)} %get-tuple-element.21), channel_id=1, source_target_pairs={{0,4},{4,0},{8,12},{12,8},{16,20},{20,16},{24,28},{28,24},{1,5},{5... | collective-permute-start | bytes 614408 | tf_op jit(solution)/shard_map/ppermute | solution.py:107
  22.8 17.4 %collective-permute-start.8 = (bf16[144,1280]{1,0:T(8,128)(2,1)S(1)}, bf16[144,1280]{1,0:T(8,128)(2,1)S(1)}, u32[]{:S(2)}, u32[]{:S(2)}) collective-permute-start(bf16[144,1280]{1,0:T(8,128)(2,1)S(1)} %fusion.1.refs_0_), channel_id=1, source_target_pairs={{0,2},{1,3},{2,0},{3,1},{4,6},{5,7},{6,4},{7,5},{8,10},{9,11},{10,... | collective-permute-start | bytes 1105928 | tf_op jit(solution)/shard_map/ppermute | solution.py:107
  40.2 13.0 %collective-permute-start.6 = (bf16[4,160,320]{2,1,0:T(8,128)(2,1)S(1)}, bf16[4,160,320]{2,1,0:T(8,128)(2,1)S(1)}, u32[]{:S(2)}, u32[]{:S(2)}) collective-permute-start(bf16[4,160,320]{2,1,0:T(8,128)(2,1)S(1)} %collective-permute-done.3.refs_6_), channel_id=1, source_target_pairs={{0,8},{4,12},{8,0},{12,4},{16,24},{20,28},{24,16},{28,20},{1,9},{5... | collective-permute-start | bytes 1228808 | tf_op jit(solution)/shard_map/ppermute | solution.py:107
  40.2 14.6 %collective-permute-start.7 = (bf16[144,1280]{1,0:T(8,128)(2,1)S(1)}, bf16[144,1280]{1,0:T(8,128)(2,1)S(1)}, u32[]{:S(2)}, u32[]{:S(2)}) collective-permute-start(bf16[144,1280]{1,0:T(8,128)(2,1)S(1)} %fusion.1.refs_0_), channel_id=1, source_target_pairs={{0,1},{1,0},{2,3},{3,2},{4,5},{5,4},{6,7},{7,6},{8,9},{9,8},{10,11... | collective-permute-start | bytes 1105928 | tf_op jit(solution)/shard_map/ppermute | solution.py:107
  40.2 14.5 %collective-permute-start.9 = (bf16[144,1280]{1,0:T(8,128)(2,1)S(1)}, bf16[144,1280]{1,0:T(8,128)(2,1)S(1)}, u32[]{:S(2)}, u32[]{:S(2)}) collective-permute-start(bf16[144,1280]{1,0:T(8,128)(2,1)S(1)} %collective-permute-done.8.refs_1_), channel_id=1, source_target_pairs={{0,1},{1,0},{2,3},{3,2},{4,5},{5,4},{6,7},{7,6},{8,9},{9,8},{10,11... | collective-permute-start | bytes 1105928 | tf_op jit(solution)/shard_map/ppermute | solution.py:107
  40.7 25.2 %collective-permute-start.11 = (bf16[4,160,320]{2,1,0:T(8,128)(2,1)S(1)}, bf16[4,160,320]{2,1,0:T(8,128)(2,1)S(1)}, u32[]{:S(2)}, u32[]{:S(2)}) collective-permute-start(bf16[4,160,320]{2,1,0:T(8,128)(2,1)S(1)} %collective-permute-done.3.refs_6_), channel_id=1, source_target_pairs={{0,4},{4,0},{8,12},{12,8},{16,20},{20,16},{24,28},{28,24},{1,5},{5... | collective-permute-start | bytes 1228808 | tf_op jit(solution)/shard_map/ppermute | solution.py:107
  53.2 12.7 %collective-permute-start.12 = (bf16[4,160,320]{2,1,0:T(8,128)(2,1)S(1)}, bf16[4,160,320]{2,1,0:T(8,128)(2,1)S(1)}, u32[]{:S(2)}, u32[]{:S(2)}) collective-permute-start(bf16[4,160,320]{2,1,0:T(8,128)(2,1)S(1)} %collective-permute-done.6.refs_7_), channel_id=1, source_target_pairs={{0,4},{4,0},{8,12},{12,8},{16,20},{20,16},{24,28},{28,24},{1,5},{5... | collective-permute-start | bytes 1228808 | tf_op jit(solution)/shard_map/ppermute | solution.py:107
  54.7 11.1 %collective-permute-start.10 = (bf16[160,640]{1,0:T(8,128)(2,1)S(1)}, bf16[160,640]{1,0:T(8,128)(2,1)}, u32[]{:S(2)}, u32[]{:S(2)}) collective-permute-start(bf16[160,640]{1,0:T(8,128)(2,1)S(1)} %get-tuple-element.30.refs_0_), channel_id=1, source_target_pairs={{0,16},{4,20},{8,24},{12,28},{16,0},{20,4},{24,8},{28,12},{1,17},{... | collective-permute-start | bytes 614408 | tf_op jit(solution)/shard_map/ppermute | solution.py:107
  65.9 1.0 copy-start.3
  73.2 5.6 %copy-start.6 = (s32[32,1]{0,1:T(1,128)S(1)}, s32[32,1]{0,1:T(1,128)}, u32[]{:S(2)}) copy-start(s32[32,1]{0,1:T(1,128)} %param.15) | copy-start | bytes 388
  73.2 7.6 %copy-start.8 = (s32[1,128]{1,0:T(1,128)S(1)}, s32[1,128]{1,0:T(1,128)}, u32[]{:S(2)}) copy-start(s32[1,128]{1,0:T(1,128)} %param.14) | copy-start | bytes 1540
  73.2 2.2 %collective-permute-start.13 = (bf16[256,1280]{1,0:T(8,128)(2,1)S(1)}, bf16[256,1280]{1,0:T(8,128)(2,1)S(1)}, u32[]{:S(2)}, u32[]{:S(2)}) collective-permute-start(bf16[256,1280]{1,0:T(8,128)(2,1)S(1)} %get-tuple-element.27), channel_id=1, source_target_pairs={{0,1},{1,0},{2,3},{3,2},{4,5},{5,4},{6,7},{7,6},{8,9},{9,8},{10,11... | collective-permute-start | bytes 1966088 | tf_op jit(solution)/shard_map/ppermute | solution.py:107
  75.5 14.4 %collective-permute-start.14 = (bf16[128,1280]{1,0:T(8,128)(2,1)S(1)}, bf16[128,1280]{1,0:T(8,128)(2,1)S(1)}, u32[]{:S(2)}, u32[]{:S(2)}) collective-permute-start(bf16[128,1280]{1,0:T(8,128)(2,1)S(1)} %shard_map.84), channel_id=1, source_target_pairs={{0,2},{1,3},{2,0},{3,1},{4,6},{5,7},{6,4},{7,5},{8,10},{9,11},{10,... | collective-permute-start | bytes 983048 | tf_op jit(solution)/shard_map/ppermute | solution.py:107
  77.0 12.3 %collective-permute-start.15 = (bf16[160,640]{1,0:T(8,128)(2,1)S(1)}, bf16[160,640]{1,0:T(8,128)(2,1)}, u32[]{:S(2)}, u32[]{:S(2)}) collective-permute-start(bf16[160,640]{1,0:T(8,128)(2,1)S(1)} %collective-permute-done.5.refs_1_), channel_id=1, source_target_pairs={{0,16},{4,20},{8,24},{12,28},{16,0},{20,4},{24,8},{28,12},{1,17},{... | collective-permute-start | bytes 614408 | tf_op jit(solution)/shard_map/ppermute | solution.py:107
  78.7 11.2 %collective-permute-start.16 = (bf16[160,640]{1,0:T(8,128)(2,1)}, bf16[160,640]{1,0:T(8,128)(2,1)}, u32[]{:S(2)}, u32[]{:S(2)}) collective-permute-start(bf16[160,640]{1,0:T(8,128)(2,1)} %collective-permute-done.10.refs_4_), channel_id=1, source_target_pairs={{0,8},{4,12},{8,0},{12,4},{16,24},{20,28},{24,16},{28,20},{1,9},{5... | collective-permute-start | bytes 614408 | tf_op jit(solution)/shard_map/ppermute | solution.py:107
  78.8 16.5 %collective-permute-start = (s32[32,1]{0,1:T(1,128)S(1)}, s32[32,1]{0,1:T(1,128)S(1)}, u32[]{:S(2)}, u32[]{:S(2)}) collective-permute-start(s32[32,1]{0,1:T(1,128)S(1)} %copy-done.6), channel_id=1, source_target_pairs={{0,4},{4,0},{8,12},{12,8},{16,20},{20,16},{24,28},{28,24},{1,5},{5... | collective-permute-start | bytes 392 | tf_op jit(solution)/shard_map/ppermute | solution.py:107
  91.6 20.2 %all-to-all-start = ((bf16[8,64,640]{2,1,0:T(8,128)(2,1)}), bf16[8,64,640]{2,1,0:T(8,128)(2,1)S(1)}, u32[]{:S(2)}, u32[]{:S(2)}) async-start(bf16[8,64,640]{2,1,0:T(8,128)(2,1)} %shard_map.85), calls=%async_computation | async-start | bytes 1310720 | tf_op jit(solution)/shard_map/all_to_all | solution.py:324
  95.5 12.3 %collective-permute-start.18 = (bf16[160,640]{1,0:T(8,128)(2,1)S(1)}, bf16[160,640]{1,0:T(8,128)(2,1)S(1)}, u32[]{:S(2)}, u32[]{:S(2)}) collective-permute-start(bf16[160,640]{1,0:T(8,128)(2,1)S(1)} %collective-permute-done.5.refs_1_), channel_id=1, source_target_pairs={{0,8},{4,12},{8,0},{12,4},{16,24},{20,28},{24,16},{28,20},{1,9},{5... | collective-permute-start | bytes 614408 | tf_op jit(solution)/shard_map/ppermute | solution.py:107
  95.8 12.1 %collective-permute-start.17 = (bf16[160,640]{1,0:T(8,128)(2,1)S(1)}, bf16[160,640]{1,0:T(8,128)(2,1)S(1)}, u32[]{:S(2)}, u32[]{:S(2)}) collective-permute-start(bf16[160,640]{1,0:T(8,128)(2,1)S(1)} %get-tuple-element.30.refs_0_), channel_id=1, source_target_pairs={{0,8},{4,12},{8,0},{12,4},{16,24},{20,28},{24,16},{28,20},{1,9},{5... | collective-permute-start | bytes 614408 | tf_op jit(solution)/shard_map/ppermute | solution.py:107
  97.6 14.2 %collective-permute-start.19 = (bf16[160,640]{1,0:T(8,128)(2,1)}, bf16[160,640]{1,0:T(8,128)(2,1)S(1)}, u32[]{:S(2)}, u32[]{:S(2)}) collective-permute-start(bf16[160,640]{1,0:T(8,128)(2,1)} %collective-permute-done.15.refs_5_), channel_id=1, source_target_pairs={{0,8},{4,12},{8,0},{12,4},{16,24},{20,28},{24,16},{28,20},{1,9},{5... | collective-permute-start | bytes 614408 | tf_op jit(solution)/shard_map/ppermute | solution.py:107
  114.0 2.0 %collective-permute-start.20 = (bf16[64,640]{1,0:T(8,128)(2,1)S(1)}, bf16[64,640]{1,0:T(8,128)(2,1)S(1)}, u32[]{:S(2)}, u32[]{:S(2)}) collective-permute-start(bf16[64,640]{1,0:T(8,128)(2,1)S(1)} %get-tuple-element.32), channel_id=1, source_target_pairs={{0,1},{1,0},{2,3},{3,2},{4,5},{5,4},{6,7},{7,6},{8,9},{9,8},{10,11... | collective-permute-start | bytes 245768 | tf_op jit(solution)/shard_map/ppermute | solution.py:107
  114.1 5.0 %collective-permute-start.21 = (bf16[64,640]{1,0:T(8,128)(2,1)S(1)}, bf16[64,640]{1,0:T(8,128)(2,1)S(1)}, u32[]{:S(2)}, u32[]{:S(2)}) collective-permute-start(bf16[64,640]{1,0:T(8,128)(2,1)S(1)} %get-tuple-element.33), channel_id=1, source_target_pairs={{0,2},{1,3},{2,0},{3,1},{4,6},{5,7},{6,4},{7,5},{8,10},{9,11},{10,... | collective-permute-start | bytes 245768 | tf_op jit(solution)/shard_map/ppermute | solution.py:107
  115.8 4.7 %collective-permute-start.22 = (bf16[64,640]{1,0:T(8,128)(2,1)S(1)}, bf16[64,640]{1,0:T(8,128)(2,1)S(1)}, u32[]{:S(2)}, u32[]{:S(2)}) collective-permute-start(bf16[64,640]{1,0:T(8,128)(2,1)S(1)} %get-tuple-element.34), channel_id=1, source_target_pairs={{0,3},{1,2},{2,1},{3,0},{4,7},{5,6},{6,5},{7,4},{8,11},{9,10},{10,... | collective-permute-start | bytes 245768 | tf_op jit(solution)/shard_map/ppermute | solution.py:107
  (1 other events, 1.0 us)

commit v7 on v5

--- a/solution.py
+++ b/solution.py
@@ -150,32 +150,40 @@
     step = blocks[0].shape[1]
     for number, block in zip(ORDER, blocks):
         start = pl.multiple_of((me ^ number) * step, 32)
-        whole[pl.ds(start, step), :] = block[part]
-
-
-def attention_kernel(me_ref, rows_ref, *refs):
+        whole[pl.ds(start, step), :] = block[part if block.shape[0] == 4 else part % 2]
+
+
+def score_kernel(me_ref, rows_ref, *refs):
     marks, blocks = refs[0:4], refs[4:12]
-    keep_ref, send_ref, q_whole, k_whole, v_whole, out_whole = refs[12:]
+    weights_ref, totals_ref, q_whole, k_whole = refs[12:]
     lay_out(me_ref[0], blocks, 0, q_whole)
     lay_out(me_ref[0], blocks, 1, k_whole)
-    lay_out(me_ref[0], blocks, 2, v_whole)
-    lay_out(me_ref[0], blocks, 3, out_whole)
     queries = dot(rows_ref[...], q_whole[...]).astype(jnp.bfloat16)
     keys = dot(rows_ref[...], k_whole[...]).astype(jnp.bfloat16)
-    values = dot(rows_ref[...], v_whole[...]).astype(jnp.bfloat16)
     rows = marks[0].shape[0] - 16
     in_row = [t[rows : rows + 16, 0:rows].astype(jnp.float32)[0:1, :] for t in marks]
     in_col = [jnp.broadcast_to(s, (rows, rows)).T[:, 0:1] for s in in_row]
     allowed = jnp.concatenate(in_col, axis=0) == jnp.concatenate(in_row, axis=1)
     factor = 1.0 / math.sqrt(HD)
-    pieces = []
     for head in range(queries.shape[1] // HD):
         cols = slice(head * HD, (head + 1) * HD)
         scores = dot_turned(queries[:, cols], keys[:, cols]) * factor
         masked = jnp.where(allowed, scores, -jnp.inf)
         weights = jnp.exp(masked - jnp.max(masked, axis=1, keepdims=True))
-        totals = jnp.sum(weights, axis=1, keepdims=True)
-        pieces.append(dot(weights.astype(jnp.bfloat16), values[:, cols]) / totals)
+        weights_ref[head] = weights.astype(jnp.bfloat16)
+        totals_ref[head] = jnp.sum(weights, axis=1, keepdims=True)
+
+
+def value_kernel(me_ref, rows_ref, weights_ref, totals_ref, *refs):
+    blocks = refs[0:8]
+    keep_ref, send_ref, v_whole, out_whole = refs[8:]
+    lay_out(me_ref[0], blocks, 2, v_whole)
+    lay_out(me_ref[0], blocks, 3, out_whole)
+    values = dot(rows_ref[...], v_whole[...]).astype(jnp.bfloat16)
+    pieces = []
+    for head in range(values.shape[1] // HD):
+        found = dot(weights_ref[head], values[:, head * HD : (head + 1) * HD])
+        pieces.append(found / totals_ref[head])
     attended = jnp.concatenate(pieces, axis=1).astype(jnp.bfloat16)
     half = attended.shape[0] // 2
     send_ref[...] = dot_turned(attended[half:, :], out_whole[...]).astype(jnp.bfloat16)
@@ -262,13 +270,20 @@
     group = n_fsdp * rows
 
     heads = jnp.concatenate([qkv_weight, out_weight.T[None]], axis=0)
-    along_z = [swap(heads, "dp", 2), swap(heads, "dp", 4)]
-    along_y = [swap(heads, "dp", 1)]
-    along_z += [swap(along_z[1], "dp", 2)]
-    along_y += [swap(block, "dp", 1) for block in along_z]
+    near, beside = swap(heads, "dp", 2), swap(heads, "dp", 1)
+    first, second = heads[0:2], heads[2:4]
+    first_far = swap(first, "dp", 4)
+    second_far = swap(after(second, first_far), "dp", 4)
+    first_last = swap(first_far, "dp", 2)
+    second_last = swap(second_far, "dp", 2)
+    near_y = swap(near, "dp", 1)
+    blocks = [
+        [heads, near, far, last, beside, near_y, swap(far, "dp", 1), swap(last, "dp", 1)]
+        for far, last in ((first_far, first_last), (second_far, second_last))
+    ]
 
     marks = jnp.pad(segments.astype(bf16), ((0, 15), (0, width - rows)))
-    marked = after(jnp.concatenate([tokens, marks], axis=0), along_z[0])
+    marked = after(jnp.concatenate([tokens, marks], axis=0), (near, beside))
     along_x = swap(marked, "fsdp", 2)
     group_rows = [marked, along_x, swap(marked, "fsdp", 1), swap(along_x, "fsdp", 1)]
     (normed,) = call(norm_kernel, [shape((group, width), bf16)], [ln_gains, *group_rows])
@@ -277,12 +292,12 @@
     low, high = merge_weight[:, :half], merge_weight[:, half:]
     lower = y == 0
     mine = jnp.where(lower, low, high)
-    theirs = swap(after(jnp.where(lower, high, low), along_z[0]), "dp", 1)
-    held, held_other = after((mine, theirs), (along_z[2], *along_y[:3], *group_rows[2:]))
-    merge_pieces = [mine, theirs, swap(held, "dp", 2), swap(held_other, "dp", 2)]
-    merge_pieces += [swap(held, "dp", 4)]
-    merge_pieces += [swap(after(held_other, merge_pieces[4]), "dp", 4)]
-    merge_pieces += [swap(piece, "dp", 2) for piece in merge_pieces[4:6]]
+    held = after(mine, (second_last, blocks[1][6], *blocks[0][5:8], *group_rows[2:]))
+    merge_near, merge_far = swap(held, "dp", 2), swap(held, "dp", 4)
+    theirs = swap(after(jnp.where(lower, high, low), blocks[0][7]), "dp", 1)
+    theirs_far = swap(after(theirs, merge_far), "dp", 4)
+    merge_pieces = [mine, theirs, merge_near, swap(after(theirs, merge_far), "dp", 2)]
+    merge_pieces += [merge_far, theirs_far, swap(merge_far, "dp", 2), swap(theirs_far, "dp", 2)]
 
     capacity = max(2, (2 * count + n_dp - 1) // n_dp)
     mine = owners[:, 0]
@@ -294,21 +309,23 @@
     slots = jnp.concatenate(slots).reshape(1, 2 * count)
     order = merge_rows.reshape(count, 4).T.reshape(rows, 1)
 
+    found = cols // HD
+    weights, totals = call(
+        score_kernel,
+        [shape((found, group, group), bf16), shape((found, group, 1), f32)],
+        [me_cell, normed, *group_rows, *blocks[0]],
+        [pltpu.VMEM((width, cols), bf16)] * 2,
+        flops=4 * group * width * cols + 2 * group * group * cols,
+        smem=1,
+        exps=found * group * group,
+    )
     keep, send = call(
-        attention_kernel,
+        value_kernel,
         [shape((2 * rows, width), f32), shape((2 * rows, width), bf16)],
-        [
-            after(me_cell, merge_pieces[2:5]),
-            normed,
-            *group_rows,
-            heads,
-            *along_z,
-            *along_y,
-        ],
-        [pltpu.VMEM((width, cols), bf16)] * 4,
-        flops=8 * group * width * cols + 4 * group * group * cols,
+        [after(me_cell, merge_near), normed, weights, totals, *blocks[1]],
+        [pltpu.VMEM((width, cols), bf16)] * 2,
+        flops=4 * group * width * cols + 2 * group * group * cols,
         smem=1,
-        exps=cols // HD * group * group,
     )
     from_core = swap(send, "fsdp", 1)
     (onward,) = call(pass_kernel, [shape((rows, width), bf16)], [keep, from_core])

time: 130 us -> 131 us (level)
  waiting for transfers between devices: 69.7 us -> 53.4 us
  starting transfers between devices: 30.7 us -> 42.8 us
  Pallas kernels: 10.2 us -> 13.5 us
    ppermute x23 -> x27, waiting for transfers between devices: 66.7 us -> 53.4 us  [swap(): lax.ppermute(value, axis, [(i, i ^ k) for i in range(lax.axis_size(axis))])]
    ppermute x23 -> x27, starting transfers between devices: 27.1 us -> 38.8 us  [swap(): lax.ppermute(value, axis, [(i, i ^ k) for i in range(lax.axis_size(axis))])]
    pallas_call x6 -> x7, Pallas kernels: 10.2 us -> 13.5 us  [call(): pl.pallas_call(kernel, out_shape=tuple(outs), in_specs=specs, out_specs=t...]
    all_to_all x1, waiting for transfers between devices: 3.01 us -> 0.01 us  [by_permutes(): lax.all_to_all(slices, ('dp', 'fsdp'), split_axis=0, concat_axis=0, tiled...]
    slice x0 -> x1, other arithmetic: none -> 1.65 us  [by_permutes(): first, second = (heads[0:2], heads[2:4])]
  transfers between devices with their start and end apart: 24 -> 28, of which waited for: 14 -> 14; matrix products, arithmetic and copies ran while one was open for 3% -> 4% of each run, Pallas kernels for 2% -> 6%
where the time goes in v7:
time: 131 us
  waiting for transfers between devices  53.4 us (41%)
  starting transfers between devices  42.8 us (33%)
  Pallas kernels  13.5 us (10%)
  blocking collectives  11.7 us (9%)
  other arithmetic  5.04 us (4%)
  local copies, waits for them, and re-layouts  4.38 us (3%)
    ppermute x27, waiting for transfers between devices, swap(): lax.ppermute(value, axis, [(i, i ^ k) for i in range(lax.axis_size(axis))])  53.4 us
    ppermute x27, starting transfers between devices, swap(): lax.ppermute(value, axis, [(i, i ^ k) for i in range(lax.axis_size(axis))])  38.8 us
    pallas_call x7, Pallas kernels, call(): pl.pallas_call(kernel, out_shape=tuple(outs), in_specs=specs, out_specs=t...  13.5 us
    all_to_all x1, blocking collectives, by_permutes(): lax.all_to_all(packed.reshape(n_dp, 2 * capacity, half), 'dp', split_axis...  11.7 us
    all_to_all x1, starting transfers between devices, by_permutes(): lax.all_to_all(slices, ('dp', 'fsdp'), split_axis=0, concat_axis=0, tiled...  3.99 us
    unnamed x31, local copies, waits for them, and re-layouts  3.41 us
  transfers between devices with their start and end apart: 28, of which 14 were waited for; matrix products, arithmetic and copies ran while one was open for 4% of the time, Pallas kernels for 6%

profile of v7, /device:TPU:0, one launch (start us, length us, event | category | flops | bytes accessed | tf_op | source)
XLA Modules:
  0.0 131.0 jit_solution(14040247557622679395)
XLA Ops:
  1.2 3.1 %collective-permute-start.5 = (bf16[4,160,320]{2,1,0:T(8,128)(2,1)S(1)}, bf16[4,160,320]{2,1,0:T(8,128)(2,1)S(1)}, u32[]{:S(2)}, u32[]{:S(2)}) collective-permute-start(bf16[4,160,320]{2,1,0:T(8,128)(2,1)S(1)} %pad_maximum_fusion.refs_4_.refs_0_), channel_id=1, source_target_pairs={{0,8},{4,12},{8,0},{12,4},{16,24},{20,28},{24,16},{28,20},{1,9},{5... | collective-permute-start | bytes 1228808 | tf_op jit(solution)/shard_map/ppermute | solution.py:107
  5.8 1.7 %fusion.5 = (bf16[2,160,320]{2,1,0:T(8,128)(2,1)S(1)}, bf16[2,160,320]{2,1,0:T(8,128)(2,1)}) fusion(bf16[3,160,320]{2,1,0:T(8,128)(2,1)S(1)} %copy-done.11, bf16[1,160,320]{2,1,0:T(8,128)(2,1)} %bitcast.20), kind=kLoop, calls=%fused_computation.17 | loop fusion | flops 102400 | bytes 1126400 | tf_op jit(solution)/shard_map/slice | solution.py:274
  7.5 2.6 %collective-permute-start.1 = (bf16[2,160,320]{2,1,0:T(8,128)(2,1)S(1)}, bf16[2,160,320]{2,1,0:T(8,128)(2,1)S(1)}, u32[]{:S(2)}, u32[]{:S(2)}) collective-permute-start(bf16[2,160,320]{2,1,0:T(8,128)(2,1)S(1)} %get-tuple-element.37), channel_id=1, source_target_pairs={{0,16},{4,20},{8,24},{12,28},{16,0},{20,4},{24,8},{28,12},{1,17},{... | collective-permute-start | bytes 614408 | tf_op jit(solution)/shard_map/ppermute | solution.py:107
  10.1 10.7 %collective-permute-done.5.refs_5_.refs_1_ = bf16[4,160,320]{2,1,0:T(8,128)(2,1)S(1)} collective-permute-done((bf16[4,160,320]{2,1,0:T(8,128)(2,1)S(1)}, bf16[4,160,320]{2,1,0:T(8,128)(2,1)S(1)}, u32[]{:S(2)}, u32[]{:S(2)}) %collective-permute-start.5) | collective-permute-done | bytes 409632 | tf_op jit(solution)/shard_map/ppermute | solution.py:107
  20.8 1.7 %collective-permute-start.12 = (bf16[144,1280]{1,0:T(8,128)(2,1)S(1)}, bf16[144,1280]{1,0:T(8,128)(2,1)S(1)}, u32[]{:S(2)}, u32[]{:S(2)}) collective-permute-start(bf16[144,1280]{1,0:T(8,128)(2,1)S(1)} %fusion.1.refs_0_), channel_id=1, source_target_pairs={{0,2},{1,3},{2,0},{3,1},{4,6},{5,7},{6,4},{7,5},{8,10},{9,11},{10,... | collective-permute-start | bytes 1105928 | tf_op jit(solution)/shard_map/ppermute | solution.py:107
  25.8 3.1 %collective-permute-start.2 = (bf16[2,160,320]{2,1,0:T(8,128)(2,1)}, bf16[2,160,320]{2,1,0:T(8,128)(2,1)}, u32[]{:S(2)}, u32[]{:S(2)}) collective-permute-start(bf16[2,160,320]{2,1,0:T(8,128)(2,1)} %get-tuple-element.20), channel_id=1, source_target_pairs={{0,16},{4,20},{8,24},{12,28},{16,0},{20,4},{24,8},{28,12},{1,17},{... | collective-permute-start | bytes 614408 | tf_op jit(solution)/shard_map/ppermute | solution.py:107
  28.9 1.9 %collective-permute-done.8.refs_7_ = bf16[2,160,320]{2,1,0:T(8,128)(2,1)S(1)} collective-permute-done((bf16[2,160,320]{2,1,0:T(8,128)(2,1)S(1)}, bf16[2,160,320]{2,1,0:T(8,128)(2,1)S(1)}, u32[]{:S(2)}, u32[]{:S(2)}) %collective-permute-start.8) | collective-permute-done | bytes 204832 | tf_op jit(solution)/shard_map/ppermute | solution.py:107
  30.7 3.5 %collective-permute-start.9 = (bf16[2,160,320]{2,1,0:T(8,128)(2,1)S(1)}, bf16[2,160,320]{2,1,0:T(8,128)(2,1)}, u32[]{:S(2)}, u32[]{:S(2)}) collective-permute-start(bf16[2,160,320]{2,1,0:T(8,128)(2,1)S(1)} %collective-permute-done.8.refs_7_), channel_id=1, source_target_pairs={{0,4},{4,0},{8,12},{12,8},{16,20},{20,16},{24,28},{28,24},{1,5},{5... | collective-permute-start | bytes 614408 | tf_op jit(solution)/shard_map/ppermute | solution.py:107
  36.1 2.5 %collective-permute-done.2.refs_2_ = bf16[2,160,320]{2,1,0:T(8,128)(2,1)} collective-permute-done((bf16[2,160,320]{2,1,0:T(8,128)(2,1)}, bf16[2,160,320]{2,1,0:T(8,128)(2,1)}, u32[]{:S(2)}, u32[]{:S(2)}) %collective-permute-start.2) | collective-permute-done | bytes 204832 | tf_op jit(solution)/shard_map/ppermute | solution.py:107
  38.7 2.5 %collective-permute-done.9.refs_11_ = bf16[2,160,320]{2,1,0:T(8,128)(2,1)} collective-permute-done((bf16[2,160,320]{2,1,0:T(8,128)(2,1)S(1)}, bf16[2,160,320]{2,1,0:T(8,128)(2,1)}, u32[]{:S(2)}, u32[]{:S(2)}) %collective-permute-start.9) | collective-permute-done | bytes 204832 | tf_op jit(solution)/shard_map/ppermute | solution.py:107
  41.2 2.0 %collective-permute-start.4 = (bf16[2,160,320]{2,1,0:T(8,128)(2,1)}, bf16[2,160,320]{2,1,0:T(8,128)(2,1)S(1)}, u32[]{:S(2)}, u32[]{:S(2)}) collective-permute-start(bf16[2,160,320]{2,1,0:T(8,128)(2,1)} %collective-permute-done.2.refs_2_), channel_id=1, source_target_pairs={{0,4},{4,0},{8,12},{12,8},{16,20},{20,16},{24,28},{28,24},{1,5},{5... | collective-permute-start | bytes 614408 | tf_op jit(solution)/shard_map/ppermute | solution.py:107
  45.1 6.7 %collective-permute-done.4.refs_6_ = bf16[2,160,320]{2,1,0:T(8,128)(2,1)S(1)} collective-permute-done((bf16[2,160,320]{2,1,0:T(8,128)(2,1)}, bf16[2,160,320]{2,1,0:T(8,128)(2,1)S(1)}, u32[]{:S(2)}, u32[]{:S(2)}) %collective-permute-start.4) | collective-permute-done | bytes 204832 | tf_op jit(solution)/shard_map/ppermute | solution.py:107
  53.4 2.0 %collective-permute-start.15 = (bf16[2,160,320]{2,1,0:T(8,128)(2,1)S(1)}, bf16[2,160,320]{2,1,0:T(8,128)(2,1)S(1)}, u32[]{:S(2)}, u32[]{:S(2)}) collective-permute-start(bf16[2,160,320]{2,1,0:T(8,128)(2,1)S(1)} %collective-permute-done.3.refs_3_), channel_id=1, source_target_pairs={{0,4},{4,0},{8,12},{12,8},{16,20},{20,16},{24,28},{28,24},{1,5},{5... | collective-permute-start | bytes 614408 | tf_op jit(solution)/shard_map/ppermute | solution.py:107
  55.5 1.8 %shard_map.82.rows_ref = bf16[512,1280]{1,0:T(8,128)(2,1)S(1)} custom-call(f32[2,1280]{1,0:T(2,128)S(1)} %copy-done.10, bf16[144,1280]{1,0:T(8,128)(2,1)S(1)} %fusion.1.refs_0_, bf16[144,1280]{1,0:T(8,128)(2,1)S(1)} %collective-permute-done.12.refs_1_, bf16[144,1280]{1,0:T(8,128)(2,1)S(1)} %collective-permute-done.11.refs_2_, ...), custom_call_target="tpu_custom_call" | custom-call | bytes 2795520 | tf_op jit(solution)/shard_map/pallas_call | solution.py:129
  57.3 4.1 %shard_map.83 = (bf16[4,512,512]{2,1,0:T(8,128)(2,1)S(1)}, f32[4,512,1]{2,1,0:T(8,128)S(1)}) custom-call(s32[1]{0:T(128)} %bitcast.3.me_ref, bf16[512,1280]{1,0:T(8,128)(2,1)S(1)} %shard_map.82.rows_ref, bf16[144,1280]{1,0:T(8,128)(2,1)S(1)} %fusion.1.refs_0_, bf16[144,1280]{1,0:T(8,128)(2,1)S(1)} %collective-permute-done.12.refs_1_, ...), custom_call_target="tpu_custom_call" | custom-call | flops 1006632960 | bytes 7348228 | tf_op jit(solution)/shard_map/pallas_call | solution.py:129
  62.1 3.5 %shard_map.84 = (f32[256,1280]{1,0:T(8,128)S(1)}, bf16[256,1280]{1,0:T(8,128)(2,1)S(1)}) custom-call(s32[1]{0:T(128)} %bitcast.3.me_ref, bf16[512,1280]{1,0:T(8,128)(2,1)S(1)} %shard_map.82.rows_ref, bf16[4,512,512]{2,1,0:T(8,128)(2,1)S(1)} %get-tuple-element.24.weights_ref, f32[4,512,1]{2,1,0:T(8,128)S(1)} %get-tuple-element.25.totals_ref, ...), custom_call_target="tpu_custom_call" | custom-call | flops 1006632960 | bytes 7839748 | tf_op jit(solution)/shard_map/pallas_call | solution.py:129
  65.8 4.0 %collective-permute-start.19 = (bf16[160,640]{1,0:T(8,128)(2,1)S(1)}, bf16[160,640]{1,0:T(8,128)(2,1)}, u32[]{:S(2)}, u32[]{:S(2)}) collective-permute-start(bf16[160,640]{1,0:T(8,128)(2,1)S(1)} %get-tuple-element.22.refs_0_), channel_id=1, source_target_pairs={{0,16},{4,20},{8,24},{12,28},{16,0},{20,4},{24,8},{28,12},{1,17},{... | collective-permute-start | bytes 614408 | tf_op jit(solution)/shard_map/ppermute | solution.py:107
  69.9 1.6 %collective-permute-start.17 = (bf16[128,1280]{1,0:T(8,128)(2,1)S(1)}, bf16[128,1280]{1,0:T(8,128)(2,1)S(1)}, u32[]{:S(2)}, u32[]{:S(2)}) collective-permute-start(bf16[128,1280]{1,0:T(8,128)(2,1)S(1)} %shard_map.85), channel_id=1, source_target_pairs={{0,2},{1,3},{2,0},{3,1},{4,6},{5,7},{6,4},{7,5},{8,10},{9,11},{10,... | collective-permute-start | bytes 983048 | tf_op jit(solution)/shard_map/ppermute | solution.py:107
  71.4 1.8 %collective-permute-done.18.refs_1_ = bf16[160,640]{1,0:T(8,128)(2,1)S(1)} collective-permute-done((bf16[160,640]{1,0:T(8,128)(2,1)S(1)}, bf16[160,640]{1,0:T(8,128)(2,1)S(1)}, u32[]{:S(2)}, u32[]{:S(2)}) %collective-permute-start.18) | collective-permute-done | bytes 204832 | tf_op jit(solution)/shard_map/ppermute | solution.py:107
  73.2 6.2 %collective-permute-done.19.refs_4_ = bf16[160,640]{1,0:T(8,128)(2,1)} collective-permute-done((bf16[160,640]{1,0:T(8,128)(2,1)S(1)}, bf16[160,640]{1,0:T(8,128)(2,1)}, u32[]{:S(2)}, u32[]{:S(2)}) %collective-permute-start.19) | collective-permute-done | bytes 204832 | tf_op jit(solution)/shard_map/ppermute | solution.py:107
  79.4 3.2 %collective-permute-start.21 = (bf16[160,640]{1,0:T(8,128)(2,1)}, bf16[160,640]{1,0:T(8,128)(2,1)}, u32[]{:S(2)}, u32[]{:S(2)}) collective-permute-start(bf16[160,640]{1,0:T(8,128)(2,1)} %collective-permute-done.19.refs_4_), channel_id=1, source_target_pairs={{0,8},{4,12},{8,0},{12,4},{16,24},{20,28},{24,16},{28,20},{1,9},{5... | collective-permute-start | bytes 614408 | tf_op jit(solution)/shard_map/ppermute | solution.py:107
  82.6 1.8 %collective-permute-start = (s32[32,1]{0,1:T(1,128)S(1)}, s32[32,1]{0,1:T(1,128)S(1)}, u32[]{:S(2)}, u32[]{:S(2)}) collective-permute-start(s32[32,1]{0,1:T(1,128)S(1)} %copy-done.12), channel_id=1, source_target_pairs={{0,4},{4,0},{8,12},{12,8},{16,20},{20,16},{24,28},{28,24},{1,5},{5... | collective-permute-start | bytes 392 | tf_op jit(solution)/shard_map/ppermute | solution.py:107
  85.9 5.4 %collective-permute-done.20.refs_5_ = bf16[160,640]{1,0:T(8,128)(2,1)} collective-permute-done((bf16[160,640]{1,0:T(8,128)(2,1)S(1)}, bf16[160,640]{1,0:T(8,128)(2,1)}, u32[]{:S(2)}, u32[]{:S(2)}) %collective-permute-start.20) | collective-permute-done | bytes 204832 | tf_op jit(solution)/shard_map/ppermute | solution.py:107
  91.7 1.7 %shard_map.86 = bf16[8,64,640]{2,1,0:T(8,128)(2,1)} custom-call(bf16[128,1280]{1,0:T(8,128)(2,1)S(1)} %copy-done.1, f32[256,1280]{1,0:T(8,128)S(1)} %get-tuple-element.26.keep_ref, bf16[256,1280]{1,0:T(8,128)(2,1)S(1)} %collective-permute-done.16.got_ref.core_ref, bf16[128,1280]{1,0:T(8,128)(2,1)S(1)} %collective-permute-done.17.chip_ref, ...), custom_call_target="tpu_custom_call" | custom-call | flops 41943040 | bytes 3287552 | tf_op jit(solution)/shard_map/pallas_call | solution.py:129
  93.4 4.0 %all-to-all-start = ((bf16[8,64,640]{2,1,0:T(8,128)(2,1)}), bf16[8,64,640]{2,1,0:T(8,128)(2,1)S(1)}, u32[]{:S(2)}, u32[]{:S(2)}) async-start(bf16[8,64,640]{2,1,0:T(8,128)(2,1)} %shard_map.86), calls=%async_computation | async-start | bytes 1310720 | tf_op jit(solution)/shard_map/all_to_all | solution.py:340
  97.9 2.0 %collective-permute-start.23 = (bf16[160,640]{1,0:T(8,128)(2,1)}, bf16[160,640]{1,0:T(8,128)(2,1)S(1)}, u32[]{:S(2)}, u32[]{:S(2)}) collective-permute-start(bf16[160,640]{1,0:T(8,128)(2,1)} %collective-permute-done.20.refs_5_), channel_id=1, source_target_pairs={{0,8},{4,12},{8,0},{12,4},{16,24},{20,28},{24,16},{28,20},{1,9},{5... | collective-permute-start | bytes 614408 | tf_op jit(solution)/shard_map/ppermute | solution.py:107
  99.9 5.8 %collective-permute-done.22.refs_3_ = bf16[160,640]{1,0:T(8,128)(2,1)S(1)} collective-permute-done((bf16[160,640]{1,0:T(8,128)(2,1)S(1)}, bf16[160,640]{1,0:T(8,128)(2,1)S(1)}, u32[]{:S(2)}, u32[]{:S(2)}) %collective-permute-start.22) | collective-permute-done | bytes 204832 | tf_op jit(solution)/shard_map/ppermute | solution.py:107
  105.7 4.0 %collective-permute-done.23.refs_7_ = bf16[160,640]{1,0:T(8,128)(2,1)S(1)} collective-permute-done((bf16[160,640]{1,0:T(8,128)(2,1)}, bf16[160,640]{1,0:T(8,128)(2,1)S(1)}, u32[]{:S(2)}, u32[]{:S(2)}) %collective-permute-start.23) | collective-permute-done | bytes 204832 | tf_op jit(solution)/shard_map/ppermute | solution.py:107
  109.7 2.2 %shard_map.87 = (f32[64,640]{1,0:T(8,128)S(1)}, bf16[64,640]{1,0:T(8,128)(2,1)S(1)}, bf16[64,640]{1,0:T(8,128)(2,1)S(1)}, bf16[64,640]{1,0:T(8,128)(2,1)S(1)}) custom-call(s32[1]{0:T(128)} %bitcast.3.me_ref, s32[1]{0:T(128)} %bitcast.4.at_ref, bf16[8,64,640]{2,1,0:T(8,128)(2,1)S(1)} %all-to-all-done.inputs, bf16[160,640]{1,0:T(8,128)(2,1)S(1)} %get-tuple-element.22.refs_0_, ...), custom_call_target="tpu_custom_call" | custom-call | flops 419430400 | bytes 2703368 | tf_op jit(solution)/shard_map/pallas_call | solution.py:129
  112.0 1.7 %collective-permute-start.25 = (bf16[64,640]{1,0:T(8,128)(2,1)S(1)}, bf16[64,640]{1,0:T(8,128)(2,1)S(1)}, u32[]{:S(2)}, u32[]{:S(2)}) collective-permute-start(bf16[64,640]{1,0:T(8,128)(2,1)S(1)} %get-tuple-element.33), channel_id=1, source_target_pairs={{0,2},{1,3},{2,0},{3,1},{4,6},{5,7},{6,4},{7,5},{8,10},{9,11},{10,... | collective-permute-start | bytes 245768 | tf_op jit(solution)/shard_map/ppermute | solution.py:107
  113.9 3.1 %collective-permute-done.25.two_ref = bf16[64,640]{1,0:T(8,128)(2,1)S(1)} collective-permute-done((bf16[64,640]{1,0:T(8,128)(2,1)S(1)}, bf16[64,640]{1,0:T(8,128)(2,1)S(1)}, u32[]{:S(2)}, u32[]{:S(2)}) %collective-permute-start.25) | collective-permute-done | bytes 81952 | tf_op jit(solution)/shard_map/ppermute | solution.py:107
  118.6 11.7 %all_to_all.10 = bf16[8,16,640]{2,1,0:T(8,128)(2,1)S(1)} all-to-all(bf16[8,16,640]{2,1,0:T(8,128)(2,1)S(1)} %bitcast.17), channel_id=1, replica_groups=mesh['dp'=8,'fsdp'=4] {'dp'}, dimensions={0} | all-to-all | bytes 327680 | tf_op jit(solution)/shard_map/all_to_all | solution.py:365
  (78 shorter events, 17.3 us)
Async XLA Ops:
  1.2 54.2 %copy-start.10 = (f32[2,1280]{1,0:T(2,128)S(1)}, f32[2,1280]{1,0:T(2,128)}, u32[]{:S(2)}) copy-start(f32[2,1280]{1,0:T(2,128)} %gains_ref.3) | copy-start | bytes 30724
  1.2 19.6 %collective-permute-start.5 = (bf16[4,160,320]{2,1,0:T(8,128)(2,1)S(1)}, bf16[4,160,320]{2,1,0:T(8,128)(2,1)S(1)}, u32[]{:S(2)}, u32[]{:S(2)}) collective-permute-start(bf16[4,160,320]{2,1,0:T(8,128)(2,1)S(1)} %pad_maximum_fusion.refs_4_.refs_0_), channel_id=1, source_target_pairs={{0,8},{4,12},{8,0},{12,4},{16,24},{20,28},{24,16},{28,20},{1,9},{5... | collective-permute-start | bytes 1228808 | tf_op jit(solution)/shard_map/ppermute | solution.py:107
  4.3 16.5 %collective-permute-start.10 = (bf16[4,160,320]{2,1,0:T(8,128)(2,1)S(1)}, bf16[4,160,320]{2,1,0:T(8,128)(2,1)S(1)}, u32[]{:S(2)}, u32[]{:S(2)}) collective-permute-start(bf16[4,160,320]{2,1,0:T(8,128)(2,1)S(1)} %pad_maximum_fusion.refs_4_.refs_0_), channel_id=1, source_target_pairs={{0,4},{4,0},{8,12},{12,8},{16,20},{20,16},{24,28},{28,24},{1,5},{5... | collective-permute-start | bytes 1228808 | tf_op jit(solution)/shard_map/ppermute | solution.py:107
  7.5 15.0 %collective-permute-start.1 = (bf16[2,160,320]{2,1,0:T(8,128)(2,1)S(1)}, bf16[2,160,320]{2,1,0:T(8,128)(2,1)S(1)}, u32[]{:S(2)}, u32[]{:S(2)}) collective-permute-start(bf16[2,160,320]{2,1,0:T(8,128)(2,1)S(1)} %get-tuple-element.37), channel_id=1, source_target_pairs={{0,16},{4,20},{8,24},{12,28},{16,0},{20,4},{24,8},{28,12},{1,17},{... | collective-permute-start | bytes 614408 | tf_op jit(solution)/shard_map/ppermute | solution.py:107
  20.8 14.8 %collective-permute-start.12 = (bf16[144,1280]{1,0:T(8,128)(2,1)S(1)}, bf16[144,1280]{1,0:T(8,128)(2,1)S(1)}, u32[]{:S(2)}, u32[]{:S(2)}) collective-permute-start(bf16[144,1280]{1,0:T(8,128)(2,1)S(1)} %fusion.1.refs_0_), channel_id=1, source_target_pairs={{0,2},{1,3},{2,0},{3,1},{4,6},{5,7},{6,4},{7,5},{8,10},{9,11},{10,... | collective-permute-start | bytes 1105928 | tf_op jit(solution)/shard_map/ppermute | solution.py:107
  22.5 8.3 %collective-permute-start.8 = (bf16[2,160,320]{2,1,0:T(8,128)(2,1)S(1)}, bf16[2,160,320]{2,1,0:T(8,128)(2,1)S(1)}, u32[]{:S(2)}, u32[]{:S(2)}) collective-permute-start(bf16[2,160,320]{2,1,0:T(8,128)(2,1)S(1)} %collective-permute-done.1.refs_6_), channel_id=1, source_target_pairs={{0,8},{4,12},{8,0},{12,4},{16,24},{20,28},{24,16},{28,20},{1,9},{5... | collective-permute-start | bytes 614408 | tf_op jit(solution)/shard_map/ppermute | solution.py:107
  23.6 11.4 %collective-permute-start.7 = (bf16[2,160,320]{2,1,0:T(8,128)(2,1)S(1)}, bf16[2,160,320]{2,1,0:T(8,128)(2,1)S(1)}, u32[]{:S(2)}, u32[]{:S(2)}) collective-permute-start(bf16[2,160,320]{2,1,0:T(8,128)(2,1)S(1)} %collective-permute-done.1.refs_6_), channel_id=1, source_target_pairs={{0,4},{4,0},{8,12},{12,8},{16,20},{20,16},{24,28},{28,24},{1,5},{5... | collective-permute-start | bytes 614408 | tf_op jit(solution)/shard_map/ppermute | solution.py:107
  25.8 12.9 %collective-permute-start.2 = (bf16[2,160,320]{2,1,0:T(8,128)(2,1)}, bf16[2,160,320]{2,1,0:T(8,128)(2,1)}, u32[]{:S(2)}, u32[]{:S(2)}) collective-permute-start(bf16[2,160,320]{2,1,0:T(8,128)(2,1)} %get-tuple-element.20), channel_id=1, source_target_pairs={{0,16},{4,20},{8,24},{12,28},{16,0},{20,4},{24,8},{28,12},{1,17},{... | collective-permute-start | bytes 614408 | tf_op jit(solution)/shard_map/ppermute | solution.py:107
  30.7 10.4 %collective-permute-start.9 = (bf16[2,160,320]{2,1,0:T(8,128)(2,1)S(1)}, bf16[2,160,320]{2,1,0:T(8,128)(2,1)}, u32[]{:S(2)}, u32[]{:S(2)}) collective-permute-start(bf16[2,160,320]{2,1,0:T(8,128)(2,1)S(1)} %collective-permute-done.8.refs_7_), channel_id=1, source_target_pairs={{0,4},{4,0},{8,12},{12,8},{16,20},{20,16},{24,28},{28,24},{1,5},{5... | collective-permute-start | bytes 614408 | tf_op jit(solution)/shard_map/ppermute | solution.py:107
  34.9 16.9 %collective-permute-start.6 = (bf16[4,160,320]{2,1,0:T(8,128)(2,1)S(1)}, bf16[4,160,320]{2,1,0:T(8,128)(2,1)S(1)}, u32[]{:S(2)}, u32[]{:S(2)}) collective-permute-start(bf16[4,160,320]{2,1,0:T(8,128)(2,1)S(1)} %collective-permute-done.5.refs_5_.refs_1_), channel_id=1, source_target_pairs={{0,4},{4,0},{8,12},{12,8},{16,20},{20,16},{24,28},{28,24},{1,5},{5... | collective-permute-start | bytes 1228808 | tf_op jit(solution)/shard_map/ppermute | solution.py:107
  35.6 16.2 %collective-permute-start.11 = (bf16[144,1280]{1,0:T(8,128)(2,1)S(1)}, bf16[144,1280]{1,0:T(8,128)(2,1)S(1)}, u32[]{:S(2)}, u32[]{:S(2)}) collective-permute-start(bf16[144,1280]{1,0:T(8,128)(2,1)S(1)} %fusion.1.refs_0_), channel_id=1, source_target_pairs={{0,1},{1,0},{2,3},{3,2},{4,5},{5,4},{6,7},{7,6},{8,9},{9,8},{10,11... | collective-permute-start | bytes 1105928 | tf_op jit(solution)/shard_map/ppermute | solution.py:107
  35.6 16.2 %collective-permute-start.13 = (bf16[144,1280]{1,0:T(8,128)(2,1)S(1)}, bf16[144,1280]{1,0:T(8,128)(2,1)}, u32[]{:S(2)}, u32[]{:S(2)}) collective-permute-start(bf16[144,1280]{1,0:T(8,128)(2,1)S(1)} %collective-permute-done.12.refs_1_), channel_id=1, source_target_pairs={{0,1},{1,0},{2,3},{3,2},{4,5},{5,4},{6,7},{7,6},{8,9},{9,8},{10,11... | collective-permute-start | bytes 1105928 | tf_op jit(solution)/shard_map/ppermute | solution.py:107
  38.7 6.5 %collective-permute-start.3 = (bf16[2,160,320]{2,1,0:T(8,128)(2,1)}, bf16[2,160,320]{2,1,0:T(8,128)(2,1)S(1)}, u32[]{:S(2)}, u32[]{:S(2)}) collective-permute-start(bf16[2,160,320]{2,1,0:T(8,128)(2,1)} %collective-permute-done.2.refs_2_), channel_id=1, source_target_pairs={{0,8},{4,12},{8,0},{12,4},{16,24},{20,28},{24,16},{28,20},{1,9},{5... | collective-permute-start | bytes 614408 | tf_op jit(solution)/shard_map/ppermute | solution.py:107
  41.2 10.7 %collective-permute-start.4 = (bf16[2,160,320]{2,1,0:T(8,128)(2,1)}, bf16[2,160,320]{2,1,0:T(8,128)(2,1)S(1)}, u32[]{:S(2)}, u32[]{:S(2)}) collective-permute-start(bf16[2,160,320]{2,1,0:T(8,128)(2,1)} %collective-permute-done.2.refs_2_), channel_id=1, source_target_pairs={{0,4},{4,0},{8,12},{12,8},{16,20},{20,16},{24,28},{28,24},{1,5},{5... | collective-permute-start | bytes 614408 | tf_op jit(solution)/shard_map/ppermute | solution.py:107
  51.9 9.6 %collective-permute-start.14 = (bf16[160,640]{1,0:T(8,128)(2,1)S(1)}, bf16[160,640]{1,0:T(8,128)(2,1)S(1)}, u32[]{:S(2)}, u32[]{:S(2)}) collective-permute-start(bf16[160,640]{1,0:T(8,128)(2,1)S(1)} %get-tuple-element.22.refs_0_), channel_id=1, source_target_pairs={{0,8},{4,12},{8,0},{12,4},{16,24},{20,28},{24,16},{28,20},{1,9},{5... | collective-permute-start | bytes 614408 | tf_op jit(solution)/shard_map/ppermute | solution.py:107
  53.4 8.7 %collective-permute-start.15 = (bf16[2,160,320]{2,1,0:T(8,128)(2,1)S(1)}, bf16[2,160,320]{2,1,0:T(8,128)(2,1)S(1)}, u32[]{:S(2)}, u32[]{:S(2)}) collective-permute-start(bf16[2,160,320]{2,1,0:T(8,128)(2,1)S(1)} %collective-permute-done.3.refs_3_), channel_id=1, source_target_pairs={{0,4},{4,0},{8,12},{12,8},{16,20},{20,16},{24,28},{28,24},{1,5},{5... | collective-permute-start | bytes 614408 | tf_op jit(solution)/shard_map/ppermute | solution.py:107
  65.6 17.0 %copy-start.12 = (s32[32,1]{0,1:T(1,128)S(1)}, s32[32,1]{0,1:T(1,128)}, u32[]{:S(2)}) copy-start(s32[32,1]{0,1:T(1,128)} %param.15) | copy-start | bytes 388
  65.6 19.3 %copy-start.14 = (s32[1,128]{1,0:T(1,128)S(1)}, s32[1,128]{1,0:T(1,128)}, u32[]{:S(2)}) copy-start(s32[1,128]{1,0:T(1,128)} %param.14) | copy-start | bytes 1540
  65.6 26.1 %copy-start.1 = (bf16[128,1280]{1,0:T(8,128)(2,1)S(1)}, bf16[128,1280]{1,0:T(8,128)(2,1)}, u32[]{:S(2)}) copy-start(bf16[128,1280]{1,0:T(8,128)(2,1)} %tokens_ref.1) | copy-start | bytes 983044
  65.7 4.2 %collective-permute-start.16 = (bf16[256,1280]{1,0:T(8,128)(2,1)S(1)}, bf16[256,1280]{1,0:T(8,128)(2,1)S(1)}, u32[]{:S(2)}, u32[]{:S(2)}) collective-permute-start(bf16[256,1280]{1,0:T(8,128)(2,1)S(1)} %get-tuple-element.27), channel_id=1, source_target_pairs={{0,1},{1,0},{2,3},{3,2},{4,5},{5,4},{6,7},{7,6},{8,9},{9,8},{10,11... | collective-permute-start | bytes 1966088 | tf_op jit(solution)/shard_map/ppermute | solution.py:107
  65.7 7.5 %collective-permute-start.18 = (bf16[160,640]{1,0:T(8,128)(2,1)S(1)}, bf16[160,640]{1,0:T(8,128)(2,1)S(1)}, u32[]{:S(2)}, u32[]{:S(2)}) collective-permute-start(bf16[160,640]{1,0:T(8,128)(2,1)S(1)} %get-tuple-element.28), channel_id=1, source_target_pairs={{0,4},{4,0},{8,12},{12,8},{16,20},{20,16},{24,28},{28,24},{1,5},{5... | collective-permute-start | bytes 614408 | tf_op jit(solution)/shard_map/ppermute | solution.py:107
  65.8 13.6 %collective-permute-start.19 = (bf16[160,640]{1,0:T(8,128)(2,1)S(1)}, bf16[160,640]{1,0:T(8,128)(2,1)}, u32[]{:S(2)}, u32[]{:S(2)}) collective-permute-start(bf16[160,640]{1,0:T(8,128)(2,1)S(1)} %get-tuple-element.22.refs_0_), channel_id=1, source_target_pairs={{0,16},{4,20},{8,24},{12,28},{16,0},{20,4},{24,8},{28,12},{1,17},{... | collective-permute-start | bytes 614408 | tf_op jit(solution)/shard_map/ppermute | solution.py:107
  69.9 21.9 %collective-permute-start.17 = (bf16[128,1280]{1,0:T(8,128)(2,1)S(1)}, bf16[128,1280]{1,0:T(8,128)(2,1)S(1)}, u32[]{:S(2)}, u32[]{:S(2)}) collective-permute-start(bf16[128,1280]{1,0:T(8,128)(2,1)S(1)} %shard_map.85), channel_id=1, source_target_pairs={{0,2},{1,3},{2,0},{3,1},{4,6},{5,7},{6,4},{7,5},{8,10},{9,11},{10,... | collective-permute-start | bytes 983048 | tf_op jit(solution)/shard_map/ppermute | solution.py:107
  79.4 11.9 %collective-permute-start.20 = (bf16[160,640]{1,0:T(8,128)(2,1)S(1)}, bf16[160,640]{1,0:T(8,128)(2,1)}, u32[]{:S(2)}, u32[]{:S(2)}) collective-permute-start(bf16[160,640]{1,0:T(8,128)(2,1)S(1)} %collective-permute-done.18.refs_1_), channel_id=1, source_target_pairs={{0,16},{4,20},{8,24},{12,28},{16,0},{20,4},{24,8},{28,12},{1,17},{... | collective-permute-start | bytes 614408 | tf_op jit(solution)/shard_map/ppermute | solution.py:107
  79.4 12.3 %collective-permute-start.21 = (bf16[160,640]{1,0:T(8,128)(2,1)}, bf16[160,640]{1,0:T(8,128)(2,1)}, u32[]{:S(2)}, u32[]{:S(2)}) collective-permute-start(bf16[160,640]{1,0:T(8,128)(2,1)} %collective-permute-done.19.refs_4_), channel_id=1, source_target_pairs={{0,8},{4,12},{8,0},{12,4},{16,24},{20,28},{24,16},{28,20},{1,9},{5... | collective-permute-start | bytes 614408 | tf_op jit(solution)/shard_map/ppermute | solution.py:107
  82.6 15.0 %collective-permute-start = (s32[32,1]{0,1:T(1,128)S(1)}, s32[32,1]{0,1:T(1,128)S(1)}, u32[]{:S(2)}, u32[]{:S(2)}) collective-permute-start(s32[32,1]{0,1:T(1,128)S(1)} %copy-done.12), channel_id=1, source_target_pairs={{0,4},{4,0},{8,12},{12,8},{16,20},{20,16},{24,28},{28,24},{1,5},{5... | collective-permute-start | bytes 392 | tf_op jit(solution)/shard_map/ppermute | solution.py:107
  93.4 16.3 %all-to-all-start = ((bf16[8,64,640]{2,1,0:T(8,128)(2,1)}), bf16[8,64,640]{2,1,0:T(8,128)(2,1)S(1)}, u32[]{:S(2)}, u32[]{:S(2)}) async-start(bf16[8,64,640]{2,1,0:T(8,128)(2,1)} %shard_map.86), calls=%async_computation | async-start | bytes 1310720 | tf_op jit(solution)/shard_map/all_to_all | solution.py:340
  97.8 7.9 %collective-permute-start.22 = (bf16[160,640]{1,0:T(8,128)(2,1)S(1)}, bf16[160,640]{1,0:T(8,128)(2,1)S(1)}, u32[]{:S(2)}, u32[]{:S(2)}) collective-permute-start(bf16[160,640]{1,0:T(8,128)(2,1)S(1)} %collective-permute-done.18.refs_1_), channel_id=1, source_target_pairs={{0,8},{4,12},{8,0},{12,4},{16,24},{20,28},{24,16},{28,20},{1,9},{5... | collective-permute-start | bytes 614408 | tf_op jit(solution)/shard_map/ppermute | solution.py:107
  97.9 11.9 %collective-permute-start.23 = (bf16[160,640]{1,0:T(8,128)(2,1)}, bf16[160,640]{1,0:T(8,128)(2,1)S(1)}, u32[]{:S(2)}, u32[]{:S(2)}) collective-permute-start(bf16[160,640]{1,0:T(8,128)(2,1)} %collective-permute-done.20.refs_5_), channel_id=1, source_target_pairs={{0,8},{4,12},{8,0},{12,4},{16,24},{20,28},{24,16},{28,20},{1,9},{5... | collective-permute-start | bytes 614408 | tf_op jit(solution)/shard_map/ppermute | solution.py:107
  111.9 2.0 %collective-permute-start.24 = (bf16[64,640]{1,0:T(8,128)(2,1)S(1)}, bf16[64,640]{1,0:T(8,128)(2,1)S(1)}, u32[]{:S(2)}, u32[]{:S(2)}) collective-permute-start(bf16[64,640]{1,0:T(8,128)(2,1)S(1)} %get-tuple-element.32), channel_id=1, source_target_pairs={{0,1},{1,0},{2,3},{3,2},{4,5},{5,4},{6,7},{7,6},{8,9},{9,8},{10,11... | collective-permute-start | bytes 245768 | tf_op jit(solution)/shard_map/ppermute | solution.py:107
  112.0 5.0 %collective-permute-start.25 = (bf16[64,640]{1,0:T(8,128)(2,1)S(1)}, bf16[64,640]{1,0:T(8,128)(2,1)S(1)}, u32[]{:S(2)}, u32[]{:S(2)}) collective-permute-start(bf16[64,640]{1,0:T(8,128)(2,1)S(1)} %get-tuple-element.33), channel_id=1, source_target_pairs={{0,2},{1,3},{2,0},{3,1},{4,6},{5,7},{6,4},{7,5},{8,10},{9,11},{10,... | collective-permute-start | bytes 245768 | tf_op jit(solution)/shard_map/ppermute | solution.py:107
  113.7 4.7 %collective-permute-start.26 = (bf16[64,640]{1,0:T(8,128)(2,1)S(1)}, bf16[64,640]{1,0:T(8,128)(2,1)S(1)}, u32[]{:S(2)}, u32[]{:S(2)}) collective-permute-start(bf16[64,640]{1,0:T(8,128)(2,1)S(1)} %get-tuple-element.34), channel_id=1, source_target_pairs={{0,3},{1,2},{2,1},{3,0},{4,7},{5,6},{6,5},{7,4},{8,11},{9,10},{10,... | collective-permute-start | bytes 245768 | tf_op jit(solution)/shard_map/ppermute | solution.py:107
  (11 other events, 61.5 us)

commit v8 on v7

--- a/solution.py
+++ b/solution.py
@@ -223,7 +223,7 @@
 
 
 def merge_kernel(me_ref, at_ref, inputs, *refs):
-    pieces, (keep_ref, *sends), total = refs[0:8], refs[8:12], refs[12]
+    blocks, (keep_ref, *sends), total = refs[0:4], refs[4:8], refs[8]
     count, width = inputs.shape[1] // 2, inputs.shape[2] // 2
     z, y = me_ref[0] // 2, lax.rem(me_ref[0], 2)
     for number in range(4):
@@ -231,7 +231,8 @@
         at = pl.multiple_of(lax.rem(position, 2) * count, 32)
         rows = inputs[:, pl.ds(at, count), :].reshape(8 * count, 2 * width)
         rows = jnp.where(position < 2, rows[:, :width], rows[:, width:])
-        own, other = pieces[2 * number][...], pieces[2 * number + 1][...]
+        step = blocks[number].shape[0] // 2
+        own, other = blocks[number][:step, :], blocks[number][step:, :]
         block = jnp.concatenate(
             [jnp.where(y == 0, own, other), jnp.where(y == 0, other, own)], axis=0
         )
@@ -274,34 +275,33 @@
     first, second = heads[0:2], heads[2:4]
     first_far = swap(first, "dp", 4)
     second_far = swap(after(second, first_far), "dp", 4)
-    first_last = swap(first_far, "dp", 2)
+    first_last = swap(after(first_far, near), "dp", 2)
     second_last = swap(second_far, "dp", 2)
-    near_y = swap(near, "dp", 1)
+    half = merge_weight.shape[1] // 2
+    low, high = merge_weight[:, :half], merge_weight[:, half:]
+    lower = y == 0
+    mine = owners[:, 0]
+    note = jnp.pad(owners.astype(bf16).T, ((0, 15), (0, half - count)))
+    given = jnp.concatenate([jnp.where(lower, high, low), note], axis=0)
+    theirs = swap(after(given, heads), "dp", 1)
+    other = theirs[-16, :count].astype(jnp.int32)
+    corner = swap(beside, "dp", 2)
     blocks = [
-        [heads, near, far, last, beside, near_y, swap(far, "dp", 1), swap(last, "dp", 1)]
+        [heads, near, far, last, beside, corner, swap(far, "dp", 1), swap(last, "dp", 1)]
         for far, last in ((first_far, first_last), (second_far, second_last))
     ]
 
     marks = jnp.pad(segments.astype(bf16), ((0, 15), (0, width - rows)))
-    marked = after(jnp.concatenate([tokens, marks], axis=0), (near, beside))
+    marked = after(jnp.concatenate([tokens, marks], axis=0), first)
     along_x = swap(marked, "fsdp", 2)
     group_rows = [marked, along_x, swap(marked, "fsdp", 1), swap(along_x, "fsdp", 1)]
     (normed,) = call(norm_kernel, [shape((group, width), bf16)], [ln_gains, *group_rows])
 
-    half = merge_weight.shape[1] // 2
-    low, high = merge_weight[:, :half], merge_weight[:, half:]
-    lower = y == 0
-    mine = jnp.where(lower, low, high)
-    held = after(mine, (second_last, blocks[1][6], *blocks[0][5:8], *group_rows[2:]))
+    pair = jnp.concatenate([jnp.where(lower, low, high), theirs[:-16]], axis=0)
+    held = after(pair, (second_last, blocks[1][6], *blocks[0][5:8], *group_rows[2:]))
     merge_near, merge_far = swap(held, "dp", 2), swap(held, "dp", 4)
-    theirs = swap(after(jnp.where(lower, high, low), blocks[0][7]), "dp", 1)
-    theirs_far = swap(after(theirs, merge_far), "dp", 4)
-    merge_pieces = [mine, theirs, merge_near, swap(after(theirs, merge_far), "dp", 2)]
-    merge_pieces += [merge_far, theirs_far, swap(merge_far, "dp", 2), swap(theirs_far, "dp", 2)]
 
     capacity = max(2, (2 * count + n_dp - 1) // n_dp)
-    mine = owners[:, 0]
-    other = swap(owners, "dp", 1)[:, 0]
     slots = []
     for number, targets in enumerate((mine, other)):
         start, rank = slot_numbers(targets, 2 * capacity)
@@ -313,7 +313,7 @@
     weights, totals = call(
         score_kernel,
         [shape((found, group, group), bf16), shape((found, group, 1), f32)],
-        [me_cell, normed, *group_rows, *blocks[0]],
+        [after(me_cell, theirs), normed, *group_rows, *blocks[0]],
         [pltpu.VMEM((width, cols), bf16)] * 2,
         flops=4 * group * width * cols + 2 * group * group * cols,
         smem=1,
@@ -322,7 +322,7 @@
     keep, send = call(
         value_kernel,
         [shape((2 * rows, width), f32), shape((2 * rows, width), bf16)],
-        [after(me_cell, merge_near), normed, weights, totals, *blocks[1]],
+        [me_cell, normed, weights, totals, *blocks[1]],
         [pltpu.VMEM((width, cols), bf16)] * 2,
         flops=4 * group * width * cols + 2 * group * group * cols,
         smem=1,
@@ -333,9 +333,10 @@
     (slices,) = call(
         layer_kernel,
         [shape((8, rows // 2, width // 2), bf16)],
-        [tokens, keep, from_core, after(from_chip, merge_pieces[5:7]), ln_gains, order],
+        [tokens, keep, from_core, from_chip, ln_gains, order],
         flops=2 * rows * rows * width,
     )
+    merge_blocks = [pair, merge_near, merge_far, swap(after(merge_far, slices), "dp", 2)]
     both = 2 * n_fsdp
     inputs = lax.all_to_all(
         slices,
@@ -350,7 +351,7 @@
     shares = call(
         merge_kernel,
         [shape((2 * count, half), f32)] + [shape((2 * count, half), bf16)] * 3,
-        [me_cell, at_cell, inputs, *merge_pieces],
+        [me_cell, at_cell, inputs, *merge_blocks],
         [pltpu.VMEM((8, count, half), f32)],
         flops=2 * 8 * count * width * half,
         smem=2,

time: 131 us -> 130 us (level)
  waiting for transfers between devices: 53.4 us -> 69.3 us
  starting transfers between devices: 42.8 us -> 30.5 us
  Pallas kernels: 13.5 us -> 10.4 us
  local copies, waits for them, and re-layouts: 4.38 us -> 1.56 us
    ppermute x27 -> x23, waiting for transfers between devices: 53.4 us -> 69.3 us  [swap(): lax.ppermute(value, axis, [(i, i ^ k) for i in range(lax.axis_size(axis))])]
    ppermute x27 -> x23, starting transfers between devices: 38.8 us -> 26.8 us  [swap(): lax.ppermute(value, axis, [(i, i ^ k) for i in range(lax.axis_size(axis))])]
    pallas_call x7, Pallas kernels: 13.5 us -> 10.4 us  [call(): pl.pallas_call(kernel, out_shape=tuple(outs), in_specs=specs, out_specs=t...]
    unnamed x31 -> x17, local copies, waits for them, and re-layouts: 3.41 us -> 0.57 us
    concatenate x1 -> x2, other arithmetic: 1.2 us -> 2.87 us  [by_permutes(): heads = jnp.concatenate([qkv_weight, out_weight.T[None]], axis=0)]
    slice x1 -> x0, other arithmetic: 1.65 us -> none  [by_permutes(): first, second = (heads[0:2], heads[2:4])]
  transfers between devices with their start and end apart: 28 -> 24, of which waited for: 14 -> 12; matrix products, arithmetic and copies ran while one was open for 4% -> 4% of each run, Pallas kernels for 6% -> 5%
where the time goes in v8:
time: 130 us
  waiting for transfers between devices  69.3 us (53%)
  starting transfers between devices  30.5 us (23%)
  blocking collectives  12.5 us (10%)
  Pallas kernels  10.4 us (8%)
  other arithmetic  5.47 us (4%)
  local copies, waits for them, and re-layouts  1.56 us (1%)
    ppermute x23, waiting for transfers between devices, swap(): lax.ppermute(value, axis, [(i, i ^ k) for i in range(lax.axis_size(axis))])  69.3 us
    ppermute x23, starting transfers between devices, swap(): lax.ppermute(value, axis, [(i, i ^ k) for i in range(lax.axis_size(axis))])  26.8 us
    all_to_all x1, blocking collectives, by_permutes(): lax.all_to_all(packed.reshape(n_dp, 2 * capacity, half), 'dp', split_axis...  12.5 us
    pallas_call x7, Pallas kernels, call(): pl.pallas_call(kernel, out_shape=tuple(outs), in_specs=specs, out_specs=t...  10.4 us
    all_to_all x1, starting transfers between devices, by_permutes(): lax.all_to_all(slices, ('dp', 'fsdp'), split_axis=0, concat_axis=0, tiled...  3.72 us
    concatenate x2, other arithmetic, by_permutes(): heads = jnp.concatenate([qkv_weight, out_weight.T[None]], axis=0)  2.87 us
  transfers between devices with their start and end apart: 24, of which 12 were waited for; matrix products, arithmetic and copies ran while one was open for 4% of the time, Pallas kernels for 5%

profile of v8, /device:TPU:0, one launch (start us, length us, event | category | flops | bytes accessed | tf_op | source)
XLA Modules:
  0.0 129.9 jit_solution(4556954001426302240)
XLA Ops:
  0.0 1.2 pad_maximum_fusion.refs_4_.refs_0_
  1.3 3.1 %collective-permute-start.4 = (bf16[4,160,320]{2,1,0:T(8,128)(2,1)S(1)}, bf16[4,160,320]{2,1,0:T(8,128)(2,1)S(1)}, u32[]{:S(2)}, u32[]{:S(2)}) collective-permute-start(bf16[4,160,320]{2,1,0:T(8,128)(2,1)S(1)} %pad_maximum_fusion.refs_4_.refs_0_), channel_id=1, source_target_pairs={{0,8},{4,12},{8,0},{12,4},{16,24},{20,28},{24,16},{28,20},{1,9},{5... | collective-permute-start | bytes 1228808 | tf_op jit(solution)/shard_map/ppermute | solution.py:107
  4.4 1.5 %collective-permute-start.7 = (bf16[4,160,320]{2,1,0:T(8,128)(2,1)S(1)}, bf16[4,160,320]{2,1,0:T(8,128)(2,1)S(1)}, u32[]{:S(2)}, u32[]{:S(2)}) collective-permute-start(bf16[4,160,320]{2,1,0:T(8,128)(2,1)S(1)} %pad_maximum_fusion.refs_4_.refs_0_), channel_id=1, source_target_pairs={{0,4},{4,0},{8,12},{12,8},{16,20},{20,16},{24,28},{28,24},{1,5},{5... | collective-permute-start | bytes 1228808 | tf_op jit(solution)/shard_map/ppermute | solution.py:107
  5.9 1.6 %fusion.3 = (bf16[2,160,320]{2,1,0:T(8,128)(2,1)S(1)}, bf16[2,160,320]{2,1,0:T(8,128)(2,1)}) fusion(bf16[3,160,320]{2,1,0:T(8,128)(2,1)S(1)} %copy-done.2, bf16[1,160,320]{2,1,0:T(8,128)(2,1)} %bitcast.27), kind=kLoop, calls=%fused_computation.9 | loop fusion | flops 102400 | bytes 1126400 | tf_op jit(solution)/shard_map/concatenate | solution.py:273
  7.5 2.6 %collective-permute-start.5 = (bf16[2,160,320]{2,1,0:T(8,128)(2,1)}, bf16[2,160,320]{2,1,0:T(8,128)(2,1)S(1)}, u32[]{:S(2)}, u32[]{:S(2)}) collective-permute-start(bf16[2,160,320]{2,1,0:T(8,128)(2,1)} %get-tuple-element.38), channel_id=1, source_target_pairs={{0,16},{4,20},{8,24},{12,28},{16,0},{20,4},{24,8},{28,12},{1,17},{... | collective-permute-start | bytes 614408 | tf_op jit(solution)/shard_map/ppermute | solution.py:107
  10.2 1.6 %collective-permute-start.1 = (bf16[144,1280]{1,0:T(8,128)(2,1)S(1)}, bf16[144,1280]{1,0:T(8,128)(2,1)S(1)}, u32[]{:S(2)}, u32[]{:S(2)}) collective-permute-start(bf16[144,1280]{1,0:T(8,128)(2,1)S(1)} %fusion.2.refs_0_), channel_id=1, source_target_pairs={{0,2},{1,3},{2,0},{3,1},{4,6},{5,7},{6,4},{7,5},{8,10},{9,11},{10,... | collective-permute-start | bytes 1105928 | tf_op jit(solution)/shard_map/ppermute | solution.py:107
  12.4 7.8 %collective-permute-done.5.refs_6_ = bf16[2,160,320]{2,1,0:T(8,128)(2,1)S(1)} collective-permute-done((bf16[2,160,320]{2,1,0:T(8,128)(2,1)}, bf16[2,160,320]{2,1,0:T(8,128)(2,1)S(1)}, u32[]{:S(2)}, u32[]{:S(2)}) %collective-permute-start.5) | collective-permute-done | bytes 204832 | tf_op jit(solution)/shard_map/ppermute | solution.py:107
  20.2 3.3 %collective-permute-start.11 = (bf16[2,160,320]{2,1,0:T(8,128)(2,1)S(1)}, bf16[2,160,320]{2,1,0:T(8,128)(2,1)S(1)}, u32[]{:S(2)}, u32[]{:S(2)}) collective-permute-start(bf16[2,160,320]{2,1,0:T(8,128)(2,1)S(1)} %get-tuple-element.26), channel_id=1, source_target_pairs={{0,16},{4,20},{8,24},{12,28},{16,0},{20,4},{24,8},{28,12},{1,17},{... | collective-permute-start | bytes 614408 | tf_op jit(solution)/shard_map/ppermute | solution.py:107
  24.2 1.6 %collective-permute-start.8 = (bf16[4,160,320]{2,1,0:T(8,128)(2,1)S(1)}, bf16[4,160,320]{2,1,0:T(8,128)(2,1)S(1)}, u32[]{:S(2)}, u32[]{:S(2)}) collective-permute-start(bf16[4,160,320]{2,1,0:T(8,128)(2,1)S(1)} %collective-permute-done.7.refs_8_.refs_4_), channel_id=1, source_target_pairs={{0,8},{4,12},{8,0},{12,4},{16,24},{20,28},{24,16},{28,20},{1,9},{5... | collective-permute-start | bytes 1228808 | tf_op jit(solution)/shard_map/ppermute | solution.py:107
  25.8 9.7 %collective-permute-done.11.refs_2_ = bf16[2,160,320]{2,1,0:T(8,128)(2,1)S(1)} collective-permute-done((bf16[2,160,320]{2,1,0:T(8,128)(2,1)S(1)}, bf16[2,160,320]{2,1,0:T(8,128)(2,1)S(1)}, u32[]{:S(2)}, u32[]{:S(2)}) %collective-permute-start.11) | collective-permute-done | bytes 204832 | tf_op jit(solution)/shard_map/ppermute | solution.py:107
  35.5 1.5 %collective-permute-start.9 = (bf16[2,160,320]{2,1,0:T(8,128)(2,1)S(1)}, bf16[2,160,320]{2,1,0:T(8,128)(2,1)S(1)}, u32[]{:S(2)}, u32[]{:S(2)}) collective-permute-start(bf16[2,160,320]{2,1,0:T(8,128)(2,1)S(1)} %collective-permute-done.5.refs_6_), channel_id=1, source_target_pairs={{0,4},{4,0},{8,12},{12,8},{16,20},{20,16},{24,28},{28,24},{1,5},{5... | collective-permute-start | bytes 614408 | tf_op jit(solution)/shard_map/ppermute | solution.py:107
  37.5 13.7 %collective-permute-done.12.refs_3_ = bf16[2,160,320]{2,1,0:T(8,128)(2,1)S(1)} collective-permute-done((bf16[2,160,320]{2,1,0:T(8,128)(2,1)S(1)}, bf16[2,160,320]{2,1,0:T(8,128)(2,1)S(1)}, u32[]{:S(2)}, u32[]{:S(2)}) %collective-permute-start.12) | collective-permute-done | bytes 204832 | tf_op jit(solution)/shard_map/ppermute | solution.py:107
  51.2 1.5 %collective-permute-start.13 = (bf16[2,160,320]{2,1,0:T(8,128)(2,1)S(1)}, bf16[2,160,320]{2,1,0:T(8,128)(2,1)S(1)}, u32[]{:S(2)}, u32[]{:S(2)}) collective-permute-start(bf16[2,160,320]{2,1,0:T(8,128)(2,1)S(1)} %collective-permute-done.11.refs_2_), channel_id=1, source_target_pairs={{0,4},{4,0},{8,12},{12,8},{16,20},{20,16},{24,28},{28,24},{1,5},{5... | collective-permute-start | bytes 614408 | tf_op jit(solution)/shard_map/ppermute | solution.py:107
  53.2 0.9 shard_map.82.rows_ref
  54.1 3.0 %shard_map.83 = (bf16[4,512,512]{2,1,0:T(8,128)(2,1)S(1)}, f32[4,512,1]{2,1,0:T(8,128)S(1)}) custom-call(s32[1]{0:T(128)} %bitcast.7.me_ref, bf16[512,1280]{1,0:T(8,128)(2,1)S(1)} %shard_map.82.rows_ref, bf16[144,1280]{1,0:T(8,128)(2,1)S(1)} %fusion.2.refs_0_, bf16[144,1280]{1,0:T(8,128)(2,1)S(1)} %collective-permute-done.1.refs_1_, ...), custom_call_target="tpu_custom_call" | custom-call | flops 1006632960 | bytes 7348228 | tf_op jit(solution)/shard_map/pallas_call | solution.py:129
  57.2 2.9 %collective-permute-done.13.refs_6_ = bf16[2,160,320]{2,1,0:T(8,128)(2,1)S(1)} collective-permute-done((bf16[2,160,320]{2,1,0:T(8,128)(2,1)S(1)}, bf16[2,160,320]{2,1,0:T(8,128)(2,1)S(1)}, u32[]{:S(2)}, u32[]{:S(2)}) %collective-permute-start.13) | collective-permute-done | bytes 204832 | tf_op jit(solution)/shard_map/ppermute | solution.py:107
  60.0 4.3 %collective-permute-done.14.refs_7_ = bf16[2,160,320]{2,1,0:T(8,128)(2,1)S(1)} collective-permute-done((bf16[2,160,320]{2,1,0:T(8,128)(2,1)S(1)}, bf16[2,160,320]{2,1,0:T(8,128)(2,1)S(1)}, u32[]{:S(2)}, u32[]{:S(2)}) %collective-permute-start.14) | collective-permute-done | bytes 204832 | tf_op jit(solution)/shard_map/ppermute | solution.py:107
  64.3 2.5 %shard_map.84 = (f32[256,1280]{1,0:T(8,128)S(1)}, bf16[256,1280]{1,0:T(8,128)(2,1)S(1)}) custom-call(s32[1]{0:T(128)} %bitcast.7.me_ref, bf16[512,1280]{1,0:T(8,128)(2,1)S(1)} %shard_map.82.rows_ref, bf16[4,512,512]{2,1,0:T(8,128)(2,1)S(1)} %get-tuple-element.24.weights_ref, f32[4,512,1]{2,1,0:T(8,128)S(1)} %get-tuple-element.25.totals_ref, ...), custom_call_target="tpu_custom_call" | custom-call | flops 1006632960 | bytes 7839748 | tf_op jit(solution)/shard_map/pallas_call | solution.py:129
  66.9 2.1 %collective-permute-done.15.got_ref.core_ref = bf16[256,1280]{1,0:T(8,128)(2,1)S(1)} collective-permute-done((bf16[256,1280]{1,0:T(8,128)(2,1)S(1)}, bf16[256,1280]{1,0:T(8,128)(2,1)S(1)}, u32[]{:S(2)}, u32[]{:S(2)}) %collective-permute-start.15) | collective-permute-done | bytes 655392 | tf_op jit(solution)/shard_map/ppermute | solution.py:107
  69.0 1.6 %collective-permute-start.16 = (bf16[128,1280]{1,0:T(8,128)(2,1)S(1)}, bf16[128,1280]{1,0:T(8,128)(2,1)}, u32[]{:S(2)}, u32[]{:S(2)}) collective-permute-start(bf16[128,1280]{1,0:T(8,128)(2,1)S(1)} %shard_map.85), channel_id=1, source_target_pairs={{0,2},{1,3},{2,0},{3,1},{4,6},{5,7},{6,4},{7,5},{8,10},{9,11},{10,... | collective-permute-start | bytes 983048 | tf_op jit(solution)/shard_map/ppermute | solution.py:107
  70.7 2.6 %collective-permute-start.18 = (bf16[320,640]{1,0:T(8,128)(2,1)S(1)}, bf16[320,640]{1,0:T(8,128)(2,1)S(1)}, u32[]{:S(2)}, u32[]{:S(2)}) collective-permute-start(bf16[320,640]{1,0:T(8,128)(2,1)S(1)} %pad_maximum_fusion.1.refs_0_), channel_id=1, source_target_pairs={{0,16},{4,20},{8,24},{12,28},{16,0},{20,4},{24,8},{28,12},{1,17},{... | collective-permute-start | bytes 1228808 | tf_op jit(solution)/shard_map/ppermute | solution.py:107
  75.0 4.0 %collective-permute-done.16.chip_ref = bf16[128,1280]{1,0:T(8,128)(2,1)} collective-permute-done((bf16[128,1280]{1,0:T(8,128)(2,1)S(1)}, bf16[128,1280]{1,0:T(8,128)(2,1)}, u32[]{:S(2)}, u32[]{:S(2)}) %collective-permute-start.16) | collective-permute-done | bytes 327712 | tf_op jit(solution)/shard_map/ppermute | solution.py:107
  78.9 2.6 %shard_map.86 = bf16[8,64,640]{2,1,0:T(8,128)(2,1)} custom-call(bf16[128,1280]{1,0:T(8,128)(2,1)S(1)} %copy-done, f32[256,1280]{1,0:T(8,128)S(1)} %get-tuple-element.27.keep_ref, bf16[256,1280]{1,0:T(8,128)(2,1)S(1)} %collective-permute-done.15.got_ref.core_ref, bf16[128,1280]{1,0:T(8,128)(2,1)} %collective-permute-done.16.chip_ref, ...), custom_call_target="tpu_custom_call" | custom-call | flops 41943040 | bytes 3287552 | tf_op jit(solution)/shard_map/pallas_call | solution.py:129
  81.6 3.7 %all-to-all-start = ((bf16[8,64,640]{2,1,0:T(8,128)(2,1)}), bf16[8,64,640]{2,1,0:T(8,128)(2,1)S(1)}, u32[]{:S(2)}, u32[]{:S(2)}) async-start(bf16[8,64,640]{2,1,0:T(8,128)(2,1)} %shard_map.86), calls=%async_computation | async-start | bytes 1310720 | tf_op jit(solution)/shard_map/all_to_all | solution.py:341
  85.3 1.6 %collective-permute-start.17 = (bf16[320,640]{1,0:T(8,128)(2,1)S(1)}, bf16[320,640]{1,0:T(8,128)(2,1)S(1)}, u32[]{:S(2)}, u32[]{:S(2)}) collective-permute-start(bf16[320,640]{1,0:T(8,128)(2,1)S(1)} %pad_maximum_fusion.1.refs_0_), channel_id=1, source_target_pairs={{0,8},{4,12},{8,0},{12,4},{16,24},{20,28},{24,16},{28,20},{1,9},{5... | collective-permute-start | bytes 1228808 | tf_op jit(solution)/shard_map/ppermute | solution.py:107
  86.9 4.8 %collective-permute-done.18.refs_2_ = bf16[320,640]{1,0:T(8,128)(2,1)S(1)} collective-permute-done((bf16[320,640]{1,0:T(8,128)(2,1)S(1)}, bf16[320,640]{1,0:T(8,128)(2,1)S(1)}, u32[]{:S(2)}, u32[]{:S(2)}) %collective-permute-start.18) | collective-permute-done | bytes 409632 | tf_op jit(solution)/shard_map/ppermute | solution.py:107
  93.3 7.2 %collective-permute-done.17.refs_1_ = bf16[320,640]{1,0:T(8,128)(2,1)S(1)} collective-permute-done((bf16[320,640]{1,0:T(8,128)(2,1)S(1)}, bf16[320,640]{1,0:T(8,128)(2,1)S(1)}, u32[]{:S(2)}, u32[]{:S(2)}) %collective-permute-start.17) | collective-permute-done | bytes 409632 | tf_op jit(solution)/shard_map/ppermute | solution.py:107
  100.4 8.7 %collective-permute-done.19.refs_3_ = bf16[320,640]{1,0:T(8,128)(2,1)S(1)} collective-permute-done((bf16[320,640]{1,0:T(8,128)(2,1)S(1)}, bf16[320,640]{1,0:T(8,128)(2,1)S(1)}, u32[]{:S(2)}, u32[]{:S(2)}) %collective-permute-start.19) | collective-permute-done | bytes 409632 | tf_op jit(solution)/shard_map/ppermute | solution.py:107
  109.2 1.1 shard_map.87
  110.9 1.3 collective-permute-start.22
  112.3 3.4 %collective-permute-done.21.two_ref = bf16[64,640]{1,0:T(8,128)(2,1)S(1)} collective-permute-done((bf16[64,640]{1,0:T(8,128)(2,1)S(1)}, bf16[64,640]{1,0:T(8,128)(2,1)S(1)}, u32[]{:S(2)}, u32[]{:S(2)}) %collective-permute-start.21) | collective-permute-done | bytes 81952 | tf_op jit(solution)/shard_map/ppermute | solution.py:107
  116.7 12.5 %all_to_all.10 = bf16[8,16,640]{2,1,0:T(8,128)(2,1)S(1)} all-to-all(bf16[8,16,640]{2,1,0:T(8,128)(2,1)S(1)} %bitcast.24), channel_id=1, replica_groups=mesh['dp'=8,'fsdp'=4] {'dp'}, dimensions={0} | all-to-all | bytes 327680 | tf_op jit(solution)/shard_map/all_to_all | solution.py:366
  (61 shorter events, 8.3 us)
Async XLA Ops:
  0.0 5.9 %copy-start.2 = (bf16[3,160,320]{2,1,0:T(8,128)(2,1)S(1)}, bf16[3,160,320]{2,1,0:T(8,128)(2,1)}, u32[]{:S(2)}) copy-start(bf16[3,160,320]{2,1,0:T(8,128)(2,1)} %param.9) | copy-start | bytes 921604
  0.0 10.1 %copy-start.6 = (s32[1,128]{1,0:T(1,128)S(1)}, s32[1,128]{1,0:T(1,128)}, u32[]{:S(2)}) copy-start(s32[1,128]{1,0:T(1,128)} %param.13) | copy-start | bytes 1540
  0.0 10.1 %copy-start = (bf16[128,1280]{1,0:T(8,128)(2,1)S(1)}, bf16[128,1280]{1,0:T(8,128)(2,1)}, u32[]{:S(2)}) copy-start(bf16[128,1280]{1,0:T(8,128)(2,1)} %tokens_ref.1) | copy-start | bytes 983044
  0.0 11.7 %copy-start.3 = (bf16[160,1280]{1,0:T(8,128)(2,1)S(1)}, bf16[160,1280]{1,0:T(8,128)(2,1)}, u32[]{:S(2)}) copy-start(bf16[160,1280]{1,0:T(8,128)(2,1)} %param.11) | copy-start | bytes 1228804
  1.2 10.5 %copy-start.5 = (s32[32,1]{0,1:T(1,128)S(1)}, s32[32,1]{0,1:T(1,128)}, u32[]{:S(2)}) copy-start(s32[32,1]{0,1:T(1,128)} %param.15) | copy-start | bytes 388
  1.2 52.0 %copy-start.1 = (f32[2,1280]{1,0:T(2,128)S(1)}, f32[2,1280]{1,0:T(2,128)}, u32[]{:S(2)}) copy-start(f32[2,1280]{1,0:T(2,128)} %gains_ref.3) | copy-start | bytes 30724
  1.3 22.2 %collective-permute-start.4 = (bf16[4,160,320]{2,1,0:T(8,128)(2,1)S(1)}, bf16[4,160,320]{2,1,0:T(8,128)(2,1)S(1)}, u32[]{:S(2)}, u32[]{:S(2)}) collective-permute-start(bf16[4,160,320]{2,1,0:T(8,128)(2,1)S(1)} %pad_maximum_fusion.refs_4_.refs_0_), channel_id=1, source_target_pairs={{0,8},{4,12},{8,0},{12,4},{16,24},{20,28},{24,16},{28,20},{1,9},{5... | collective-permute-start | bytes 1228808 | tf_op jit(solution)/shard_map/ppermute | solution.py:107
  4.4 19.8 %collective-permute-start.7 = (bf16[4,160,320]{2,1,0:T(8,128)(2,1)S(1)}, bf16[4,160,320]{2,1,0:T(8,128)(2,1)S(1)}, u32[]{:S(2)}, u32[]{:S(2)}) collective-permute-start(bf16[4,160,320]{2,1,0:T(8,128)(2,1)S(1)} %pad_maximum_fusion.refs_4_.refs_0_), channel_id=1, source_target_pairs={{0,4},{4,0},{8,12},{12,8},{16,20},{20,16},{24,28},{28,24},{1,5},{5... | collective-permute-start | bytes 1228808 | tf_op jit(solution)/shard_map/ppermute | solution.py:107
  7.5 12.7 %collective-permute-start.5 = (bf16[2,160,320]{2,1,0:T(8,128)(2,1)}, bf16[2,160,320]{2,1,0:T(8,128)(2,1)S(1)}, u32[]{:S(2)}, u32[]{:S(2)}) collective-permute-start(bf16[2,160,320]{2,1,0:T(8,128)(2,1)} %get-tuple-element.38), channel_id=1, source_target_pairs={{0,16},{4,20},{8,24},{12,28},{16,0},{20,4},{24,8},{28,12},{1,17},{... | collective-permute-start | bytes 614408 | tf_op jit(solution)/shard_map/ppermute | solution.py:107
  10.2 10.1 %collective-permute-start.1 = (bf16[144,1280]{1,0:T(8,128)(2,1)S(1)}, bf16[144,1280]{1,0:T(8,128)(2,1)S(1)}, u32[]{:S(2)}, u32[]{:S(2)}) collective-permute-start(bf16[144,1280]{1,0:T(8,128)(2,1)S(1)} %fusion.2.refs_0_), channel_id=1, source_target_pairs={{0,2},{1,3},{2,0},{3,1},{4,6},{5,7},{6,4},{7,5},{8,10},{9,11},{10,... | collective-permute-start | bytes 1105928 | tf_op jit(solution)/shard_map/ppermute | solution.py:107
  11.8 11.9 %collective-permute-start = (bf16[176,640]{1,0:T(8,128)(2,1)S(1)}, bf16[176,640]{1,0:T(8,128)(2,1)S(1)}, u32[]{:S(2)}, u32[]{:S(2)}) collective-permute-start(bf16[176,640]{1,0:T(8,128)(2,1)S(1)} %fusion.4), channel_id=1, source_target_pairs={{0,4},{4,0},{8,12},{12,8},{16,20},{20,16},{24,28},{28,24},{1,5},{5... | collective-permute-start | bytes 675848 | tf_op jit(solution)/shard_map/ppermute | solution.py:107
  20.2 15.3 %collective-permute-start.2 = (bf16[144,1280]{1,0:T(8,128)(2,1)S(1)}, bf16[144,1280]{1,0:T(8,128)(2,1)S(1)}, u32[]{:S(2)}, u32[]{:S(2)}) collective-permute-start(bf16[144,1280]{1,0:T(8,128)(2,1)S(1)} %fusion.2.refs_0_), channel_id=1, source_target_pairs={{0,1},{1,0},{2,3},{3,2},{4,5},{5,4},{6,7},{7,6},{8,9},{9,8},{10,11... | collective-permute-start | bytes 1105928 | tf_op jit(solution)/shard_map/ppermute | solution.py:107
  20.2 15.3 %collective-permute-start.11 = (bf16[2,160,320]{2,1,0:T(8,128)(2,1)S(1)}, bf16[2,160,320]{2,1,0:T(8,128)(2,1)S(1)}, u32[]{:S(2)}, u32[]{:S(2)}) collective-permute-start(bf16[2,160,320]{2,1,0:T(8,128)(2,1)S(1)} %get-tuple-element.26), channel_id=1, source_target_pairs={{0,16},{4,20},{8,24},{12,28},{16,0},{20,4},{24,8},{28,12},{1,17},{... | collective-permute-start | bytes 614408 | tf_op jit(solution)/shard_map/ppermute | solution.py:107
  23.5 29.2 %collective-permute-start.3 = (bf16[144,1280]{1,0:T(8,128)(2,1)S(1)}, bf16[144,1280]{1,0:T(8,128)(2,1)S(1)}, u32[]{:S(2)}, u32[]{:S(2)}) collective-permute-start(bf16[144,1280]{1,0:T(8,128)(2,1)S(1)} %collective-permute-done.1.refs_1_), channel_id=1, source_target_pairs={{0,1},{1,0},{2,3},{3,2},{4,5},{5,4},{6,7},{7,6},{8,9},{9,8},{10,11... | collective-permute-start | bytes 1105928 | tf_op jit(solution)/shard_map/ppermute | solution.py:107
  23.7 46.9 %copy-start.4 = (bf16[176,640]{1,0:T(8,128)(2,1)}, bf16[176,640]{1,0:T(8,128)(2,1)S(1)}, u32[]{:S(2)}) copy-start(bf16[176,640]{1,0:T(8,128)(2,1)S(1)} %collective-permute-done) | copy-start | bytes 675844
  23.7 13.3 %collective-permute-start.6 = (bf16[2,160,320]{2,1,0:T(8,128)(2,1)S(1)}, bf16[2,160,320]{2,1,0:T(8,128)(2,1)S(1)}, u32[]{:S(2)}, u32[]{:S(2)}) collective-permute-start(bf16[2,160,320]{2,1,0:T(8,128)(2,1)S(1)} %collective-permute-done.5.refs_6_), channel_id=1, source_target_pairs={{0,8},{4,12},{8,0},{12,4},{16,24},{20,28},{24,16},{28,20},{1,9},{5... | collective-permute-start | bytes 614408 | tf_op jit(solution)/shard_map/ppermute | solution.py:107
  24.2 29.9 %collective-permute-start.8 = (bf16[4,160,320]{2,1,0:T(8,128)(2,1)S(1)}, bf16[4,160,320]{2,1,0:T(8,128)(2,1)S(1)}, u32[]{:S(2)}, u32[]{:S(2)}) collective-permute-start(bf16[4,160,320]{2,1,0:T(8,128)(2,1)S(1)} %collective-permute-done.7.refs_8_.refs_4_), channel_id=1, source_target_pairs={{0,8},{4,12},{8,0},{12,4},{16,24},{20,28},{24,16},{28,20},{1,9},{5... | collective-permute-start | bytes 1228808 | tf_op jit(solution)/shard_map/ppermute | solution.py:107
  35.5 15.7 %collective-permute-start.12 = (bf16[2,160,320]{2,1,0:T(8,128)(2,1)S(1)}, bf16[2,160,320]{2,1,0:T(8,128)(2,1)S(1)}, u32[]{:S(2)}, u32[]{:S(2)}) collective-permute-start(bf16[2,160,320]{2,1,0:T(8,128)(2,1)S(1)} %collective-permute-done.11.refs_2_), channel_id=1, source_target_pairs={{0,8},{4,12},{8,0},{12,4},{16,24},{20,28},{24,16},{28,20},{1,9},{5... | collective-permute-start | bytes 614408 | tf_op jit(solution)/shard_map/ppermute | solution.py:107
  35.5 18.6 %collective-permute-start.9 = (bf16[2,160,320]{2,1,0:T(8,128)(2,1)S(1)}, bf16[2,160,320]{2,1,0:T(8,128)(2,1)S(1)}, u32[]{:S(2)}, u32[]{:S(2)}) collective-permute-start(bf16[2,160,320]{2,1,0:T(8,128)(2,1)S(1)} %collective-permute-done.5.refs_6_), channel_id=1, source_target_pairs={{0,4},{4,0},{8,12},{12,8},{16,20},{20,16},{24,28},{28,24},{1,5},{5... | collective-permute-start | bytes 614408 | tf_op jit(solution)/shard_map/ppermute | solution.py:107
  37.0 17.1 %collective-permute-start.10 = (bf16[2,160,320]{2,1,0:T(8,128)(2,1)S(1)}, bf16[2,160,320]{2,1,0:T(8,128)(2,1)S(1)}, u32[]{:S(2)}, u32[]{:S(2)}) collective-permute-start(bf16[2,160,320]{2,1,0:T(8,128)(2,1)S(1)} %collective-permute-done.6.refs_7_), channel_id=1, source_target_pairs={{0,4},{4,0},{8,12},{12,8},{16,20},{20,16},{24,28},{28,24},{1,5},{5... | collective-permute-start | bytes 614408 | tf_op jit(solution)/shard_map/ppermute | solution.py:107
  51.2 8.8 %collective-permute-start.13 = (bf16[2,160,320]{2,1,0:T(8,128)(2,1)S(1)}, bf16[2,160,320]{2,1,0:T(8,128)(2,1)S(1)}, u32[]{:S(2)}, u32[]{:S(2)}) collective-permute-start(bf16[2,160,320]{2,1,0:T(8,128)(2,1)S(1)} %collective-permute-done.11.refs_2_), channel_id=1, source_target_pairs={{0,4},{4,0},{8,12},{12,8},{16,20},{20,16},{24,28},{28,24},{1,5},{5... | collective-permute-start | bytes 614408 | tf_op jit(solution)/shard_map/ppermute | solution.py:107
  52.7 11.6 %collective-permute-start.14 = (bf16[2,160,320]{2,1,0:T(8,128)(2,1)S(1)}, bf16[2,160,320]{2,1,0:T(8,128)(2,1)S(1)}, u32[]{:S(2)}, u32[]{:S(2)}) collective-permute-start(bf16[2,160,320]{2,1,0:T(8,128)(2,1)S(1)} %collective-permute-done.12.refs_3_), channel_id=1, source_target_pairs={{0,4},{4,0},{8,12},{12,8},{16,20},{20,16},{24,28},{28,24},{1,5},{5... | collective-permute-start | bytes 614408 | tf_op jit(solution)/shard_map/ppermute | solution.py:107
  66.8 2.2 %collective-permute-start.15 = (bf16[256,1280]{1,0:T(8,128)(2,1)S(1)}, bf16[256,1280]{1,0:T(8,128)(2,1)S(1)}, u32[]{:S(2)}, u32[]{:S(2)}) collective-permute-start(bf16[256,1280]{1,0:T(8,128)(2,1)S(1)} %get-tuple-element.28), channel_id=1, source_target_pairs={{0,1},{1,0},{2,3},{3,2},{4,5},{5,4},{6,7},{7,6},{8,9},{9,8},{10,11... | collective-permute-start | bytes 1966088 | tf_op jit(solution)/shard_map/ppermute | solution.py:107
  69.0 4.9 %copy-start.7 = (s32[1,128]{1,0:T(1,128)S(1)}, s32[1,128]{1,0:T(1,128)}, u32[]{:S(2)}) copy-start(s32[1,128]{1,0:T(1,128)} %param.14) | copy-start | bytes 1540
  69.0 9.9 %collective-permute-start.16 = (bf16[128,1280]{1,0:T(8,128)(2,1)S(1)}, bf16[128,1280]{1,0:T(8,128)(2,1)}, u32[]{:S(2)}, u32[]{:S(2)}) collective-permute-start(bf16[128,1280]{1,0:T(8,128)(2,1)S(1)} %shard_map.85), channel_id=1, source_target_pairs={{0,2},{1,3},{2,0},{3,1},{4,6},{5,7},{6,4},{7,5},{8,10},{9,11},{10,... | collective-permute-start | bytes 983048 | tf_op jit(solution)/shard_map/ppermute | solution.py:107
  70.7 21.1 %collective-permute-start.18 = (bf16[320,640]{1,0:T(8,128)(2,1)S(1)}, bf16[320,640]{1,0:T(8,128)(2,1)S(1)}, u32[]{:S(2)}, u32[]{:S(2)}) collective-permute-start(bf16[320,640]{1,0:T(8,128)(2,1)S(1)} %pad_maximum_fusion.1.refs_0_), channel_id=1, source_target_pairs={{0,16},{4,20},{8,24},{12,28},{16,0},{20,4},{24,8},{28,12},{1,17},{... | collective-permute-start | bytes 1228808 | tf_op jit(solution)/shard_map/ppermute | solution.py:107
  81.6 27.6 %all-to-all-start = ((bf16[8,64,640]{2,1,0:T(8,128)(2,1)}), bf16[8,64,640]{2,1,0:T(8,128)(2,1)S(1)}, u32[]{:S(2)}, u32[]{:S(2)}) async-start(bf16[8,64,640]{2,1,0:T(8,128)(2,1)} %shard_map.86), calls=%async_computation | async-start | bytes 1310720 | tf_op jit(solution)/shard_map/all_to_all | solution.py:341
  85.3 15.1 %collective-permute-start.17 = (bf16[320,640]{1,0:T(8,128)(2,1)S(1)}, bf16[320,640]{1,0:T(8,128)(2,1)S(1)}, u32[]{:S(2)}, u32[]{:S(2)}) collective-permute-start(bf16[320,640]{1,0:T(8,128)(2,1)S(1)} %pad_maximum_fusion.1.refs_0_), channel_id=1, source_target_pairs={{0,8},{4,12},{8,0},{12,4},{16,24},{20,28},{24,16},{28,20},{1,9},{5... | collective-permute-start | bytes 1228808 | tf_op jit(solution)/shard_map/ppermute | solution.py:107
  91.7 17.5 %collective-permute-start.19 = (bf16[320,640]{1,0:T(8,128)(2,1)S(1)}, bf16[320,640]{1,0:T(8,128)(2,1)S(1)}, u32[]{:S(2)}, u32[]{:S(2)}) collective-permute-start(bf16[320,640]{1,0:T(8,128)(2,1)S(1)} %collective-permute-done.18.refs_2_), channel_id=1, source_target_pairs={{0,8},{4,12},{8,0},{12,4},{16,24},{20,28},{24,16},{28,20},{1,9},{5... | collective-permute-start | bytes 1228808 | tf_op jit(solution)/shard_map/ppermute | solution.py:107
  110.2 2.0 %collective-permute-start.20 = (bf16[64,640]{1,0:T(8,128)(2,1)S(1)}, bf16[64,640]{1,0:T(8,128)(2,1)S(1)}, u32[]{:S(2)}, u32[]{:S(2)}) collective-permute-start(bf16[64,640]{1,0:T(8,128)(2,1)S(1)} %get-tuple-element.32), channel_id=1, source_target_pairs={{0,1},{1,0},{2,3},{3,2},{4,5},{5,4},{6,7},{7,6},{8,9},{9,8},{10,11... | collective-permute-start | bytes 245768 | tf_op jit(solution)/shard_map/ppermute | solution.py:107
  110.4 5.3 %collective-permute-start.21 = (bf16[64,640]{1,0:T(8,128)(2,1)S(1)}, bf16[64,640]{1,0:T(8,128)(2,1)S(1)}, u32[]{:S(2)}, u32[]{:S(2)}) collective-permute-start(bf16[64,640]{1,0:T(8,128)(2,1)S(1)} %get-tuple-element.33), channel_id=1, source_target_pairs={{0,2},{1,3},{2,0},{3,1},{4,6},{5,7},{6,4},{7,5},{8,10},{9,11},{10,... | collective-permute-start | bytes 245768 | tf_op jit(solution)/shard_map/ppermute | solution.py:107
  110.9 5.6 %collective-permute-start.22 = (bf16[64,640]{1,0:T(8,128)(2,1)S(1)}, bf16[64,640]{1,0:T(8,128)(2,1)S(1)}, u32[]{:S(2)}, u32[]{:S(2)}) collective-permute-start(bf16[64,640]{1,0:T(8,128)(2,1)S(1)} %get-tuple-element.34), channel_id=1, source_target_pairs={{0,3},{1,2},{2,1},{3,0},{4,7},{5,6},{6,5},{7,4},{8,11},{9,10},{10,... | collective-permute-start | bytes 245768 | tf_op jit(solution)/shard_map/ppermute | solution.py:107

commit v9 on v8

--- a/solution.py
+++ b/solution.py
@@ -274,31 +274,38 @@
     near, beside = swap(heads, "dp", 2), swap(heads, "dp", 1)
     first, second = heads[0:2], heads[2:4]
     first_far = swap(first, "dp", 4)
+    first_far_y = swap(after(first_far, (near, beside)), "dp", 1)
+    first_last = swap(first_far, "dp", 2)
+    corner = swap(beside, "dp", 2)
     second_far = swap(after(second, first_far), "dp", 4)
-    first_last = swap(after(first_far, near), "dp", 2)
+
+    marks = jnp.pad(segments.astype(bf16), ((0, 15), (0, width - rows)))
+    marked = after(jnp.concatenate([tokens, marks], axis=0), first)
+    along_x = swap(marked, "fsdp", 2)
+    group_rows = [marked, along_x]
+    group_rows += [swap(after(part, (first_far_y, first_last, second_far)), "fsdp", 1) for part in (marked, along_x)]
+    (normed,) = call(norm_kernel, [shape((group, width), bf16)], [ln_gains, *group_rows])
+
+    second_far_y = swap(second_far, "dp", 1)
     second_last = swap(second_far, "dp", 2)
+    blocks = [
+        [heads, near, far, last, beside, corner, far_y, swap(after(last, corner), "dp", 1)]
+        for far, last, far_y in (
+            (first_far, first_last, first_far_y),
+            (second_far, second_last, second_far_y),
+        )
+    ]
+
     half = merge_weight.shape[1] // 2
     low, high = merge_weight[:, :half], merge_weight[:, half:]
     lower = y == 0
     mine = owners[:, 0]
     note = jnp.pad(owners.astype(bf16).T, ((0, 15), (0, half - count)))
     given = jnp.concatenate([jnp.where(lower, high, low), note], axis=0)
-    theirs = swap(after(given, heads), "dp", 1)
+    theirs = swap(after(given, second_far_y), "dp", 1)
     other = theirs[-16, :count].astype(jnp.int32)
-    corner = swap(beside, "dp", 2)
-    blocks = [
-        [heads, near, far, last, beside, corner, swap(far, "dp", 1), swap(last, "dp", 1)]
-        for far, last in ((first_far, first_last), (second_far, second_last))
-    ]
-
-    marks = jnp.pad(segments.astype(bf16), ((0, 15), (0, width - rows)))
-    marked = after(jnp.concatenate([tokens, marks], axis=0), first)
-    along_x = swap(marked, "fsdp", 2)
-    group_rows = [marked, along_x, swap(marked, "fsdp", 1), swap(along_x, "fsdp", 1)]
-    (normed,) = call(norm_kernel, [shape((group, width), bf16)], [ln_gains, *group_rows])
-
     pair = jnp.concatenate([jnp.where(lower, low, high), theirs[:-16]], axis=0)
-    held = after(pair, (second_last, blocks[1][6], *blocks[0][5:8], *group_rows[2:]))
+    held = after(pair, (second_last, second_far_y, blocks[0][7]))
     merge_near, merge_far = swap(held, "dp", 2), swap(held, "dp", 4)
 
     capacity = max(2, (2 * count + n_dp - 1) // n_dp)
@@ -336,7 +343,7 @@
         [tokens, keep, from_core, from_chip, ln_gains, order],
         flops=2 * rows * rows * width,
     )
-    merge_blocks = [pair, merge_near, merge_far, swap(after(merge_far, slices), "dp", 2)]
+    merge_blocks = [pair, merge_near, merge_far, swap(after(merge_far, (slices, merge_near)), "dp", 2)]
     both = 2 * n_fsdp
     inputs = lax.all_to_all(
         slices,

time: 130 us -> 118 us (0.908)
  waiting for transfers between devices: 69.3 us -> 53.6 us
  other arithmetic: 5.47 us -> 7.19 us
  local copies, waits for them, and re-layouts: 1.56 us -> 3.01 us
  blocking collectives: 12.5 us -> 11.2 us
    ppermute x23, waiting for transfers between devices: 69.3 us -> 53.6 us  [swap(): lax.ppermute(value, axis, [(i, i ^ k) for i in range(lax.axis_size(axis))])]
    concatenate x2 -> x1, other arithmetic: 2.87 us -> 1.2 us  [by_permutes(): heads = jnp.concatenate([qkv_weight, out_weight.T[None]], axis=0)]
    slice x0 -> x1, other arithmetic: none -> 1.64 us  [by_permutes(): first, second = (heads[0:2], heads[2:4])]
  transfers between devices with their start and end apart: 24 -> 24, of which waited for: 12 -> 15; matrix products, arithmetic and copies ran while one was open for 4% -> 6% of each run, Pallas kernels for 5% -> 6%
where the time goes in v9:
time: 118 us; the launch traced here: 117 us
  waiting for transfers between devices  53.6 us (45%)
  starting transfers between devices  31.1 us (26%)
  blocking collectives  11.2 us (9%)
  Pallas kernels  11.1 us (9%)
  other arithmetic  7.19 us (6%)
  local copies, waits for them, and re-layouts  3.01 us (3%)
    ppermute x23, waiting for transfers between devices, swap(): lax.ppermute(value, axis, [(i, i ^ k) for i in range(lax.axis_size(axis))])  53.6 us
    ppermute x23, starting transfers between devices, swap(): lax.ppermute(value, axis, [(i, i ^ k) for i in range(lax.axis_size(axis))])  27.4 us
    all_to_all x1, blocking collectives, by_permutes(): lax.all_to_all(packed.reshape(n_dp, 2 * capacity, half), 'dp', split_axis...  11.2 us
    pallas_call x7, Pallas kernels, call(): pl.pallas_call(kernel, out_shape=tuple(outs), in_specs=specs, out_specs=t...  11.1 us
    all_to_all x1, starting transfers between devices, by_permutes(): lax.all_to_all(slices, ('dp', 'fsdp'), split_axis=0, concat_axis=0, tiled...  3.67 us
  transfers between devices with their start and end apart: 24, of which 15 were waited for; matrix products, arithmetic and copies ran while one was open for 6% of the time, Pallas kernels for 6%

profile of v9, /device:TPU:0, one launch (start us, length us, event | category | flops | bytes accessed | tf_op | source)
XLA Modules:
  0.0 117.4 jit_solution(17319186083310577935)
XLA Ops:
  0.0 1.2 %pad_maximum_fusion.refs_4_.refs_0_ = bf16[4,160,320]{2,1,0:T(8,128)(2,1)S(1)} fusion(bf16[1,160,320]{2,1,0:T(8,128)(2,1)} %bitcast.26, bf16[3,160,320]{2,1,0:T(8,128)(2,1)} %param.9), kind=kLoop, calls=%fused_computation.3 | loop fusion | flops 204800 | bytes 819200 | tf_op jit(solution)/shard_map/concatenate | solution.py:273
  1.2 3.0 %collective-permute-start.6 = (bf16[4,160,320]{2,1,0:T(8,128)(2,1)S(1)}, bf16[4,160,320]{2,1,0:T(8,128)(2,1)S(1)}, u32[]{:S(2)}, u32[]{:S(2)}) collective-permute-start(bf16[4,160,320]{2,1,0:T(8,128)(2,1)S(1)} %pad_maximum_fusion.refs_4_.refs_0_), channel_id=1, source_target_pairs={{0,4},{4,0},{8,12},{12,8},{16,20},{20,16},{24,28},{28,24},{1,5},{5... | collective-permute-start | bytes 1228808 | tf_op jit(solution)/shard_map/ppermute | solution.py:107
  4.3 1.6 %collective-permute-start.5 = (bf16[4,160,320]{2,1,0:T(8,128)(2,1)S(1)}, bf16[4,160,320]{2,1,0:T(8,128)(2,1)S(1)}, u32[]{:S(2)}, u32[]{:S(2)}) collective-permute-start(bf16[4,160,320]{2,1,0:T(8,128)(2,1)S(1)} %pad_maximum_fusion.refs_4_.refs_0_), channel_id=1, source_target_pairs={{0,8},{4,12},{8,0},{12,4},{16,24},{20,28},{24,16},{28,20},{1,9},{5... | collective-permute-start | bytes 1228808 | tf_op jit(solution)/shard_map/ppermute | solution.py:107
  5.9 1.6 %fusion.8 = (bf16[2,160,320]{2,1,0:T(8,128)(2,1)S(1)}, bf16[2,160,320]{2,1,0:T(8,128)(2,1)}) fusion(bf16[3,160,320]{2,1,0:T(8,128)(2,1)S(1)} %copy-done.3, bf16[1,160,320]{2,1,0:T(8,128)(2,1)} %bitcast.27), kind=kLoop, calls=%fused_computation.24 | loop fusion | flops 102400 | bytes 1126400 | tf_op jit(solution)/shard_map/slice | solution.py:275
  7.5 2.6 %collective-permute-start = (bf16[2,160,320]{2,1,0:T(8,128)(2,1)S(1)}, bf16[2,160,320]{2,1,0:T(8,128)(2,1)S(1)}, u32[]{:S(2)}, u32[]{:S(2)}) collective-permute-start(bf16[2,160,320]{2,1,0:T(8,128)(2,1)S(1)} %get-tuple-element.45), channel_id=1, source_target_pairs={{0,16},{4,20},{8,24},{12,28},{16,0},{20,4},{24,8},{28,12},{1,17},{... | collective-permute-start | bytes 614408 | tf_op jit(solution)/shard_map/ppermute | solution.py:107
  10.1 1.6 %collective-permute-start.4 = (bf16[144,1280]{1,0:T(8,128)(2,1)S(1)}, bf16[144,1280]{1,0:T(8,128)(2,1)S(1)}, u32[]{:S(2)}, u32[]{:S(2)}) collective-permute-start(bf16[144,1280]{1,0:T(8,128)(2,1)S(1)} %fusion.2.refs_0_), channel_id=1, source_target_pairs={{0,2},{1,3},{2,0},{3,1},{4,6},{5,7},{6,4},{7,5},{8,10},{9,11},{10,... | collective-permute-start | bytes 1105928 | tf_op jit(solution)/shard_map/ppermute | solution.py:107
  11.7 9.6 %collective-permute-done.refs_6_ = bf16[2,160,320]{2,1,0:T(8,128)(2,1)S(1)} collective-permute-done((bf16[2,160,320]{2,1,0:T(8,128)(2,1)S(1)}, bf16[2,160,320]{2,1,0:T(8,128)(2,1)S(1)}, u32[]{:S(2)}, u32[]{:S(2)}) %collective-permute-start) | collective-permute-done | bytes 204832 | tf_op jit(solution)/shard_map/ppermute | solution.py:107
  21.3 3.4 %collective-permute-start.1 = (bf16[2,160,320]{2,1,0:T(8,128)(2,1)}, bf16[2,160,320]{2,1,0:T(8,128)(2,1)S(1)}, u32[]{:S(2)}, u32[]{:S(2)}) collective-permute-start(bf16[2,160,320]{2,1,0:T(8,128)(2,1)} %get-tuple-element.24), channel_id=1, source_target_pairs={{0,16},{4,20},{8,24},{12,28},{16,0},{20,4},{24,8},{28,12},{1,17},{... | collective-permute-start | bytes 614408 | tf_op jit(solution)/shard_map/ppermute | solution.py:107
  25.3 1.9 %collective-permute-start.11 = (bf16[4,160,320]{2,1,0:T(8,128)(2,1)S(1)}, bf16[4,160,320]{2,1,0:T(8,128)(2,1)S(1)}, u32[]{:S(2)}, u32[]{:S(2)}) collective-permute-start(bf16[4,160,320]{2,1,0:T(8,128)(2,1)S(1)} %collective-permute-done.6.refs_8_.refs_4_), channel_id=1, source_target_pairs={{0,8},{4,12},{8,0},{12,4},{16,24},{20,28},{24,16},{28,20},{1,9},{5... | collective-permute-start | bytes 1228808 | tf_op jit(solution)/shard_map/ppermute | solution.py:107
  27.2 1.1 broadcast_select_fusion
  28.3 6.7 %collective-permute-done.1.refs_2_ = bf16[2,160,320]{2,1,0:T(8,128)(2,1)S(1)} collective-permute-done((bf16[2,160,320]{2,1,0:T(8,128)(2,1)}, bf16[2,160,320]{2,1,0:T(8,128)(2,1)S(1)}, u32[]{:S(2)}, u32[]{:S(2)}) %collective-permute-start.1) | collective-permute-done | bytes 204832 | tf_op jit(solution)/shard_map/ppermute | solution.py:107
  37.1 2.5 %collective-permute-start.13 = (bf16[2,160,320]{2,1,0:T(8,128)(2,1)S(1)}, bf16[2,160,320]{2,1,0:T(8,128)(2,1)S(1)}, u32[]{:S(2)}, u32[]{:S(2)}) collective-permute-start(bf16[2,160,320]{2,1,0:T(8,128)(2,1)S(1)} %collective-permute-done.1.refs_2_), channel_id=1, source_target_pairs={{0,8},{4,12},{8,0},{12,4},{16,24},{20,28},{24,16},{28,20},{1,9},{5... | collective-permute-start | bytes 614408 | tf_op jit(solution)/shard_map/ppermute | solution.py:107
  39.6 1.6 %collective-permute-done.2.refs_6_ = bf16[2,160,320]{2,1,0:T(8,128)(2,1)S(1)} collective-permute-done((bf16[2,160,320]{2,1,0:T(8,128)(2,1)S(1)}, bf16[2,160,320]{2,1,0:T(8,128)(2,1)S(1)}, u32[]{:S(2)}, u32[]{:S(2)}) %collective-permute-start.2) | collective-permute-done | bytes 204832 | tf_op jit(solution)/shard_map/ppermute | solution.py:107
  41.7 5.4 %collective-permute-done.11.refs_9_.refs_5_ = bf16[4,160,320]{2,1,0:T(8,128)(2,1)S(1)} collective-permute-done((bf16[4,160,320]{2,1,0:T(8,128)(2,1)S(1)}, bf16[4,160,320]{2,1,0:T(8,128)(2,1)S(1)}, u32[]{:S(2)}, u32[]{:S(2)}) %collective-permute-start.11) | collective-permute-done | bytes 409632 | tf_op jit(solution)/shard_map/ppermute | solution.py:107
  47.6 3.1 %collective-permute-done.13.refs_3_ = bf16[2,160,320]{2,1,0:T(8,128)(2,1)S(1)} collective-permute-done((bf16[2,160,320]{2,1,0:T(8,128)(2,1)S(1)}, bf16[2,160,320]{2,1,0:T(8,128)(2,1)S(1)}, u32[]{:S(2)}, u32[]{:S(2)}) %collective-permute-start.13) | collective-permute-done | bytes 204832 | tf_op jit(solution)/shard_map/ppermute | solution.py:107
  52.1 2.7 %collective-permute-done.12.refs_11_ = bf16[2,160,320]{2,1,0:T(8,128)(2,1)S(1)} collective-permute-done((bf16[2,160,320]{2,1,0:T(8,128)(2,1)S(1)}, bf16[2,160,320]{2,1,0:T(8,128)(2,1)S(1)}, u32[]{:S(2)}, u32[]{:S(2)}) %collective-permute-start.12) | collective-permute-done | bytes 204832 | tf_op jit(solution)/shard_map/ppermute | solution.py:107
  54.8 3.0 %shard_map.83 = (bf16[4,512,512]{2,1,0:T(8,128)(2,1)S(1)}, f32[4,512,1]{2,1,0:T(8,128)S(1)}) custom-call(s32[1]{0:T(128)} %bitcast.7.me_ref, bf16[512,1280]{1,0:T(8,128)(2,1)S(1)} %shard_map.82.rows_ref, bf16[144,1280]{1,0:T(8,128)(2,1)S(1)} %fusion.2.refs_0_, bf16[144,1280]{1,0:T(8,128)(2,1)S(1)} %collective-permute-done.4.refs_1_, ...), custom_call_target="tpu_custom_call" | custom-call | flops 1006632960 | bytes 7348228 | tf_op jit(solution)/shard_map/pallas_call | solution.py:129
  58.6 2.5 %shard_map.84 = (f32[256,1280]{1,0:T(8,128)S(1)}, bf16[256,1280]{1,0:T(8,128)(2,1)S(1)}) custom-call(s32[1]{0:T(128)} %bitcast.7.me_ref, bf16[512,1280]{1,0:T(8,128)(2,1)S(1)} %shard_map.82.rows_ref, bf16[4,512,512]{2,1,0:T(8,128)(2,1)S(1)} %get-tuple-element.32.weights_ref, f32[4,512,1]{2,1,0:T(8,128)S(1)} %get-tuple-element.33.totals_ref, ...), custom_call_target="tpu_custom_call" | custom-call | flops 1006632960 | bytes 7839748 | tf_op jit(solution)/shard_map/pallas_call | solution.py:129
  61.2 2.1 %collective-permute-done.15.got_ref.core_ref = bf16[256,1280]{1,0:T(8,128)(2,1)S(1)} collective-permute-done((bf16[256,1280]{1,0:T(8,128)(2,1)S(1)}, bf16[256,1280]{1,0:T(8,128)(2,1)S(1)}, u32[]{:S(2)}, u32[]{:S(2)}) %collective-permute-start.15) | collective-permute-done | bytes 655392 | tf_op jit(solution)/shard_map/ppermute | solution.py:107
  64.1 1.5 %collective-permute-start.16 = (bf16[128,1280]{1,0:T(8,128)(2,1)}, bf16[128,1280]{1,0:T(8,128)(2,1)}, u32[]{:S(2)}, u32[]{:S(2)}) collective-permute-start(bf16[128,1280]{1,0:T(8,128)(2,1)} %shard_map.85), channel_id=1, source_target_pairs={{0,2},{1,3},{2,0},{3,1},{4,6},{5,7},{6,4},{7,5},{8,10},{9,11},{10,... | collective-permute-start | bytes 983048 | tf_op jit(solution)/shard_map/ppermute | solution.py:107
  65.6 2.7 %collective-permute-start.17 = (bf16[320,640]{1,0:T(8,128)(2,1)S(1)}, bf16[320,640]{1,0:T(8,128)(2,1)S(1)}, u32[]{:S(2)}, u32[]{:S(2)}) collective-permute-start(bf16[320,640]{1,0:T(8,128)(2,1)S(1)} %pad_maximum_fusion.1.refs_0_), channel_id=1, source_target_pairs={{0,8},{4,12},{8,0},{12,4},{16,24},{20,28},{24,16},{28,20},{1,9},{5... | collective-permute-start | bytes 1228808 | tf_op jit(solution)/shard_map/ppermute | solution.py:107
  68.3 1.1 collective-permute-start.18
  72.4 1.7 %collective-permute-done.16.chip_ref = bf16[128,1280]{1,0:T(8,128)(2,1)} collective-permute-done((bf16[128,1280]{1,0:T(8,128)(2,1)}, bf16[128,1280]{1,0:T(8,128)(2,1)}, u32[]{:S(2)}, u32[]{:S(2)}) %collective-permute-start.16) | collective-permute-done | bytes 327712 | tf_op jit(solution)/shard_map/ppermute | solution.py:107
  75.0 2.6 %shard_map.86 = bf16[8,64,640]{2,1,0:T(8,128)(2,1)} custom-call(bf16[128,1280]{1,0:T(8,128)(2,1)S(1)} %copy-done, f32[256,1280]{1,0:T(8,128)S(1)} %get-tuple-element.35.keep_ref, bf16[256,1280]{1,0:T(8,128)(2,1)S(1)} %collective-permute-done.15.got_ref.core_ref, bf16[128,1280]{1,0:T(8,128)(2,1)} %collective-permute-done.16.chip_ref, ...), custom_call_target="tpu_custom_call" | custom-call | flops 41943040 | bytes 3287552 | tf_op jit(solution)/shard_map/pallas_call | solution.py:129
  77.6 3.7 %all-to-all-start = ((bf16[8,64,640]{2,1,0:T(8,128)(2,1)}), bf16[8,64,640]{2,1,0:T(8,128)(2,1)S(1)}, u32[]{:S(2)}, u32[]{:S(2)}) async-start(bf16[8,64,640]{2,1,0:T(8,128)(2,1)} %shard_map.86), calls=%async_computation | async-start | bytes 1310720 | tf_op jit(solution)/shard_map/all_to_all | solution.py:348
  81.3 5.1 %collective-permute-done.17.refs_1_ = bf16[320,640]{1,0:T(8,128)(2,1)S(1)} collective-permute-done((bf16[320,640]{1,0:T(8,128)(2,1)S(1)}, bf16[320,640]{1,0:T(8,128)(2,1)S(1)}, u32[]{:S(2)}, u32[]{:S(2)}) %collective-permute-start.17) | collective-permute-done | bytes 409632 | tf_op jit(solution)/shard_map/ppermute | solution.py:107
  86.5 2.5 %collective-permute-done.18.refs_2_ = bf16[320,640]{1,0:T(8,128)(2,1)S(1)} collective-permute-done((bf16[320,640]{1,0:T(8,128)(2,1)S(1)}, bf16[320,640]{1,0:T(8,128)(2,1)S(1)}, u32[]{:S(2)}, u32[]{:S(2)}) %collective-permute-start.18) | collective-permute-done | bytes 409632 | tf_op jit(solution)/shard_map/ppermute | solution.py:107
  91.0 7.0 %collective-permute-done.19.refs_3_ = bf16[320,640]{1,0:T(8,128)(2,1)S(1)} collective-permute-done((bf16[320,640]{1,0:T(8,128)(2,1)S(1)}, bf16[320,640]{1,0:T(8,128)(2,1)S(1)}, u32[]{:S(2)}, u32[]{:S(2)}) %collective-permute-start.19) | collective-permute-done | bytes 409632 | tf_op jit(solution)/shard_map/ppermute | solution.py:107
  98.0 1.0 shard_map.87
  99.7 1.3 %collective-permute-start.22 = (bf16[64,640]{1,0:T(8,128)(2,1)S(1)}, bf16[64,640]{1,0:T(8,128)(2,1)S(1)}, u32[]{:S(2)}, u32[]{:S(2)}) collective-permute-start(bf16[64,640]{1,0:T(8,128)(2,1)S(1)} %get-tuple-element.42), channel_id=1, source_target_pairs={{0,3},{1,2},{2,1},{3,0},{4,7},{5,6},{6,5},{7,4},{8,11},{9,10},{10,... | collective-permute-start | bytes 245768 | tf_op jit(solution)/shard_map/ppermute | solution.py:107
  101.1 3.4 %collective-permute-done.21.two_ref = bf16[64,640]{1,0:T(8,128)(2,1)S(1)} collective-permute-done((bf16[64,640]{1,0:T(8,128)(2,1)S(1)}, bf16[64,640]{1,0:T(8,128)(2,1)S(1)}, u32[]{:S(2)}, u32[]{:S(2)}) %collective-permute-start.21) | collective-permute-done | bytes 81952 | tf_op jit(solution)/shard_map/ppermute | solution.py:107
  105.5 11.2 %all_to_all.10 = bf16[8,16,640]{2,1,0:T(8,128)(2,1)S(1)} all-to-all(bf16[8,16,640]{2,1,0:T(8,128)(2,1)S(1)} %bitcast.24), channel_id=1, replica_groups=mesh['dp'=8,'fsdp'=4] {'dp'}, dimensions={0} | all-to-all | bytes 327680 | tf_op jit(solution)/shard_map/all_to_all | solution.py:373
  (63 shorter events, 15.1 us)
Async XLA Ops:
  0.0 5.9 %copy-start.3 = (bf16[3,160,320]{2,1,0:T(8,128)(2,1)S(1)}, bf16[3,160,320]{2,1,0:T(8,128)(2,1)}, u32[]{:S(2)}) copy-start(bf16[3,160,320]{2,1,0:T(8,128)(2,1)} %param.9) | copy-start | bytes 921604
  0.0 10.1 %copy-start.7 = (s32[1,128]{1,0:T(1,128)S(1)}, s32[1,128]{1,0:T(1,128)}, u32[]{:S(2)}) copy-start(s32[1,128]{1,0:T(1,128)} %param.13) | copy-start | bytes 1540
  0.0 10.1 %copy-start = (bf16[128,1280]{1,0:T(8,128)(2,1)S(1)}, bf16[128,1280]{1,0:T(8,128)(2,1)}, u32[]{:S(2)}) copy-start(bf16[128,1280]{1,0:T(8,128)(2,1)} %tokens_ref.1) | copy-start | bytes 983044
  1.2 35.9 %copy-start.5 = (s32[32,1]{0,1:T(1,128)S(1)}, s32[32,1]{0,1:T(1,128)}, u32[]{:S(2)}) copy-start(s32[32,1]{0,1:T(1,128)} %param.15) | copy-start | bytes 388
  1.2 50.0 %copy-start.2 = (f32[2,1280]{1,0:T(2,128)S(1)}, f32[2,1280]{1,0:T(2,128)}, u32[]{:S(2)}) copy-start(f32[2,1280]{1,0:T(2,128)} %gains_ref.3) | copy-start | bytes 30724
  1.2 23.6 %collective-permute-start.6 = (bf16[4,160,320]{2,1,0:T(8,128)(2,1)S(1)}, bf16[4,160,320]{2,1,0:T(8,128)(2,1)S(1)}, u32[]{:S(2)}, u32[]{:S(2)}) collective-permute-start(bf16[4,160,320]{2,1,0:T(8,128)(2,1)S(1)} %pad_maximum_fusion.refs_4_.refs_0_), channel_id=1, source_target_pairs={{0,4},{4,0},{8,12},{12,8},{16,20},{20,16},{24,28},{28,24},{1,5},{5... | collective-permute-start | bytes 1228808 | tf_op jit(solution)/shard_map/ppermute | solution.py:107
  4.3 20.5 %collective-permute-start.5 = (bf16[4,160,320]{2,1,0:T(8,128)(2,1)S(1)}, bf16[4,160,320]{2,1,0:T(8,128)(2,1)S(1)}, u32[]{:S(2)}, u32[]{:S(2)}) collective-permute-start(bf16[4,160,320]{2,1,0:T(8,128)(2,1)S(1)} %pad_maximum_fusion.refs_4_.refs_0_), channel_id=1, source_target_pairs={{0,8},{4,12},{8,0},{12,4},{16,24},{20,28},{24,16},{28,20},{1,9},{5... | collective-permute-start | bytes 1228808 | tf_op jit(solution)/shard_map/ppermute | solution.py:107
  7.5 13.8 %collective-permute-start = (bf16[2,160,320]{2,1,0:T(8,128)(2,1)S(1)}, bf16[2,160,320]{2,1,0:T(8,128)(2,1)S(1)}, u32[]{:S(2)}, u32[]{:S(2)}) collective-permute-start(bf16[2,160,320]{2,1,0:T(8,128)(2,1)S(1)} %get-tuple-element.45), channel_id=1, source_target_pairs={{0,16},{4,20},{8,24},{12,28},{16,0},{20,4},{24,8},{28,12},{1,17},{... | collective-permute-start | bytes 614408 | tf_op jit(solution)/shard_map/ppermute | solution.py:107
  10.1 25.4 %collective-permute-start.4 = (bf16[144,1280]{1,0:T(8,128)(2,1)S(1)}, bf16[144,1280]{1,0:T(8,128)(2,1)S(1)}, u32[]{:S(2)}, u32[]{:S(2)}) collective-permute-start(bf16[144,1280]{1,0:T(8,128)(2,1)S(1)} %fusion.2.refs_0_), channel_id=1, source_target_pairs={{0,2},{1,3},{2,0},{3,1},{4,6},{5,7},{6,4},{7,5},{8,10},{9,11},{10,... | collective-permute-start | bytes 1105928 | tf_op jit(solution)/shard_map/ppermute | solution.py:107
  21.3 13.7 %collective-permute-start.1 = (bf16[2,160,320]{2,1,0:T(8,128)(2,1)}, bf16[2,160,320]{2,1,0:T(8,128)(2,1)S(1)}, u32[]{:S(2)}, u32[]{:S(2)}) collective-permute-start(bf16[2,160,320]{2,1,0:T(8,128)(2,1)} %get-tuple-element.24), channel_id=1, source_target_pairs={{0,16},{4,20},{8,24},{12,28},{16,0},{20,4},{24,8},{28,12},{1,17},{... | collective-permute-start | bytes 614408 | tf_op jit(solution)/shard_map/ppermute | solution.py:107
  24.7 11.9 %collective-permute-start.8 = (bf16[2,160,320]{2,1,0:T(8,128)(2,1)S(1)}, bf16[2,160,320]{2,1,0:T(8,128)(2,1)S(1)}, u32[]{:S(2)}, u32[]{:S(2)}) collective-permute-start(bf16[2,160,320]{2,1,0:T(8,128)(2,1)S(1)} %collective-permute-done.refs_6_), channel_id=1, source_target_pairs={{0,8},{4,12},{8,0},{12,4},{16,24},{20,28},{24,16},{28,20},{1,9},{5... | collective-permute-start | bytes 614408 | tf_op jit(solution)/shard_map/ppermute | solution.py:107
  24.8 11.8 %collective-permute-start.7 = (bf16[2,160,320]{2,1,0:T(8,128)(2,1)S(1)}, bf16[2,160,320]{2,1,0:T(8,128)(2,1)S(1)}, u32[]{:S(2)}, u32[]{:S(2)}) collective-permute-start(bf16[2,160,320]{2,1,0:T(8,128)(2,1)S(1)} %collective-permute-done.refs_6_), channel_id=1, source_target_pairs={{0,4},{4,0},{8,12},{12,8},{16,20},{20,16},{24,28},{28,24},{1,5},{5... | collective-permute-start | bytes 614408 | tf_op jit(solution)/shard_map/ppermute | solution.py:107
  25.3 21.8 %collective-permute-start.11 = (bf16[4,160,320]{2,1,0:T(8,128)(2,1)S(1)}, bf16[4,160,320]{2,1,0:T(8,128)(2,1)S(1)}, u32[]{:S(2)}, u32[]{:S(2)}) collective-permute-start(bf16[4,160,320]{2,1,0:T(8,128)(2,1)S(1)} %collective-permute-done.6.refs_8_.refs_4_), channel_id=1, source_target_pairs={{0,8},{4,12},{8,0},{12,4},{16,24},{20,28},{24,16},{28,20},{1,9},{5... | collective-permute-start | bytes 1228808 | tf_op jit(solution)/shard_map/ppermute | solution.py:107
  35.0 6.2 %collective-permute-start.2 = (bf16[2,160,320]{2,1,0:T(8,128)(2,1)S(1)}, bf16[2,160,320]{2,1,0:T(8,128)(2,1)S(1)}, u32[]{:S(2)}, u32[]{:S(2)}) collective-permute-start(bf16[2,160,320]{2,1,0:T(8,128)(2,1)S(1)} %collective-permute-done.1.refs_2_), channel_id=1, source_target_pairs={{0,4},{4,0},{8,12},{12,8},{16,20},{20,16},{24,28},{28,24},{1,5},{5... | collective-permute-start | bytes 614408 | tf_op jit(solution)/shard_map/ppermute | solution.py:107
  36.6 14.7 %collective-permute-start.10 = (bf16[144,1280]{1,0:T(8,128)(2,1)S(1)}, bf16[144,1280]{1,0:T(8,128)(2,1)S(1)}, u32[]{:S(2)}, u32[]{:S(2)}) collective-permute-start(bf16[144,1280]{1,0:T(8,128)(2,1)S(1)} %collective-permute-done.4.refs_1_), channel_id=1, source_target_pairs={{0,1},{1,0},{2,3},{3,2},{4,5},{5,4},{6,7},{7,6},{8,9},{9,8},{10,11... | collective-permute-start | bytes 1105928 | tf_op jit(solution)/shard_map/ppermute | solution.py:107
  36.6 14.7 %collective-permute-start.9 = (bf16[144,1280]{1,0:T(8,128)(2,1)S(1)}, bf16[144,1280]{1,0:T(8,128)(2,1)S(1)}, u32[]{:S(2)}, u32[]{:S(2)}) collective-permute-start(bf16[144,1280]{1,0:T(8,128)(2,1)S(1)} %fusion.2.refs_0_), channel_id=1, source_target_pairs={{0,1},{1,0},{2,3},{3,2},{4,5},{5,4},{6,7},{7,6},{8,9},{9,8},{10,11... | collective-permute-start | bytes 1105928 | tf_op jit(solution)/shard_map/ppermute | solution.py:107
  37.1 13.6 %collective-permute-start.13 = (bf16[2,160,320]{2,1,0:T(8,128)(2,1)S(1)}, bf16[2,160,320]{2,1,0:T(8,128)(2,1)S(1)}, u32[]{:S(2)}, u32[]{:S(2)}) collective-permute-start(bf16[2,160,320]{2,1,0:T(8,128)(2,1)S(1)} %collective-permute-done.1.refs_2_), channel_id=1, source_target_pairs={{0,8},{4,12},{8,0},{12,4},{16,24},{20,28},{24,16},{28,20},{1,9},{5... | collective-permute-start | bytes 614408 | tf_op jit(solution)/shard_map/ppermute | solution.py:107
  41.2 10.0 %collective-permute-start.3 = (bf16[176,640]{1,0:T(8,128)(2,1)S(1)}, bf16[176,640]{1,0:T(8,128)(2,1)S(1)}, u32[]{:S(2)}, u32[]{:S(2)}) collective-permute-start(bf16[176,640]{1,0:T(8,128)(2,1)S(1)} %fusion.4), channel_id=1, source_target_pairs={{0,4},{4,0},{8,12},{12,8},{16,20},{20,16},{24,28},{28,24},{1,5},{5... | collective-permute-start | bytes 675848 | tf_op jit(solution)/shard_map/ppermute | solution.py:107
  47.1 7.7 %collective-permute-start.12 = (bf16[2,160,320]{2,1,0:T(8,128)(2,1)S(1)}, bf16[2,160,320]{2,1,0:T(8,128)(2,1)S(1)}, u32[]{:S(2)}, u32[]{:S(2)}) collective-permute-start(bf16[2,160,320]{2,1,0:T(8,128)(2,1)S(1)} %collective-permute-done.8.refs_7_), channel_id=1, source_target_pairs={{0,4},{4,0},{8,12},{12,8},{16,20},{20,16},{24,28},{28,24},{1,5},{5... | collective-permute-start | bytes 614408 | tf_op jit(solution)/shard_map/ppermute | solution.py:107
  50.7 7.8 %collective-permute-start.14 = (bf16[2,160,320]{2,1,0:T(8,128)(2,1)S(1)}, bf16[2,160,320]{2,1,0:T(8,128)(2,1)S(1)}, u32[]{:S(2)}, u32[]{:S(2)}) collective-permute-start(bf16[2,160,320]{2,1,0:T(8,128)(2,1)S(1)} %collective-permute-done.13.refs_3_), channel_id=1, source_target_pairs={{0,4},{4,0},{8,12},{12,8},{16,20},{20,16},{24,28},{28,24},{1,5},{5... | collective-permute-start | bytes 614408 | tf_op jit(solution)/shard_map/ppermute | solution.py:107
  51.2 14.3 %copy-start.4 = (bf16[176,640]{1,0:T(8,128)(2,1)}, bf16[176,640]{1,0:T(8,128)(2,1)S(1)}, u32[]{:S(2)}) copy-start(bf16[176,640]{1,0:T(8,128)(2,1)S(1)} %collective-permute-done.3) | copy-start | bytes 675844
  61.1 2.2 %collective-permute-start.15 = (bf16[256,1280]{1,0:T(8,128)(2,1)S(1)}, bf16[256,1280]{1,0:T(8,128)(2,1)S(1)}, u32[]{:S(2)}, u32[]{:S(2)}) collective-permute-start(bf16[256,1280]{1,0:T(8,128)(2,1)S(1)} %get-tuple-element.36), channel_id=1, source_target_pairs={{0,1},{1,0},{2,3},{3,2},{4,5},{5,4},{6,7},{7,6},{8,9},{9,8},{10,11... | collective-permute-start | bytes 1966088 | tf_op jit(solution)/shard_map/ppermute | solution.py:107
  63.3 6.6 %copy-start.8 = (s32[1,128]{1,0:T(1,128)S(1)}, s32[1,128]{1,0:T(1,128)}, u32[]{:S(2)}) copy-start(s32[1,128]{1,0:T(1,128)} %param.14) | copy-start | bytes 1540
  64.1 10.1 %collective-permute-start.16 = (bf16[128,1280]{1,0:T(8,128)(2,1)}, bf16[128,1280]{1,0:T(8,128)(2,1)}, u32[]{:S(2)}, u32[]{:S(2)}) collective-permute-start(bf16[128,1280]{1,0:T(8,128)(2,1)} %shard_map.85), channel_id=1, source_target_pairs={{0,2},{1,3},{2,0},{3,1},{4,6},{5,7},{6,4},{7,5},{8,10},{9,11},{10,... | collective-permute-start | bytes 983048 | tf_op jit(solution)/shard_map/ppermute | solution.py:107
  65.6 20.8 %collective-permute-start.17 = (bf16[320,640]{1,0:T(8,128)(2,1)S(1)}, bf16[320,640]{1,0:T(8,128)(2,1)S(1)}, u32[]{:S(2)}, u32[]{:S(2)}) collective-permute-start(bf16[320,640]{1,0:T(8,128)(2,1)S(1)} %pad_maximum_fusion.1.refs_0_), channel_id=1, source_target_pairs={{0,8},{4,12},{8,0},{12,4},{16,24},{20,28},{24,16},{28,20},{1,9},{5... | collective-permute-start | bytes 1228808 | tf_op jit(solution)/shard_map/ppermute | solution.py:107
  68.3 20.7 %collective-permute-start.18 = (bf16[320,640]{1,0:T(8,128)(2,1)S(1)}, bf16[320,640]{1,0:T(8,128)(2,1)S(1)}, u32[]{:S(2)}, u32[]{:S(2)}) collective-permute-start(bf16[320,640]{1,0:T(8,128)(2,1)S(1)} %pad_maximum_fusion.1.refs_0_), channel_id=1, source_target_pairs={{0,16},{4,20},{8,24},{12,28},{16,0},{20,4},{24,8},{28,12},{1,17},{... | collective-permute-start | bytes 1228808 | tf_op jit(solution)/shard_map/ppermute | solution.py:107
  77.6 3.7 %copy-start.6 = (s32[32,1]{0,1:T(1,128)S(1)}, s32[32,1]{0,1:T(1,128)}, u32[]{:S(2)}) copy-start(s32[32,1]{0,1:T(1,128)} %param.15) | copy-start | bytes 388
  77.6 20.4 %all-to-all-start = ((bf16[8,64,640]{2,1,0:T(8,128)(2,1)}), bf16[8,64,640]{2,1,0:T(8,128)(2,1)S(1)}, u32[]{:S(2)}, u32[]{:S(2)}) async-start(bf16[8,64,640]{2,1,0:T(8,128)(2,1)} %shard_map.86), calls=%async_computation | async-start | bytes 1310720 | tf_op jit(solution)/shard_map/all_to_all | solution.py:348
  89.0 9.0 %collective-permute-start.19 = (bf16[320,640]{1,0:T(8,128)(2,1)S(1)}, bf16[320,640]{1,0:T(8,128)(2,1)S(1)}, u32[]{:S(2)}, u32[]{:S(2)}) collective-permute-start(bf16[320,640]{1,0:T(8,128)(2,1)S(1)} %collective-permute-done.18.refs_2_), channel_id=1, source_target_pairs={{0,8},{4,12},{8,0},{12,4},{16,24},{20,28},{24,16},{28,20},{1,9},{5... | collective-permute-start | bytes 1228808 | tf_op jit(solution)/shard_map/ppermute | solution.py:107
  99.0 2.0 %collective-permute-start.20 = (bf16[64,640]{1,0:T(8,128)(2,1)S(1)}, bf16[64,640]{1,0:T(8,128)(2,1)S(1)}, u32[]{:S(2)}, u32[]{:S(2)}) collective-permute-start(bf16[64,640]{1,0:T(8,128)(2,1)S(1)} %get-tuple-element.40), channel_id=1, source_target_pairs={{0,1},{1,0},{2,3},{3,2},{4,5},{5,4},{6,7},{7,6},{8,9},{9,8},{10,11... | collective-permute-start | bytes 245768 | tf_op jit(solution)/shard_map/ppermute | solution.py:107
  99.1 5.3 %collective-permute-start.21 = (bf16[64,640]{1,0:T(8,128)(2,1)S(1)}, bf16[64,640]{1,0:T(8,128)(2,1)S(1)}, u32[]{:S(2)}, u32[]{:S(2)}) collective-permute-start(bf16[64,640]{1,0:T(8,128)(2,1)S(1)} %get-tuple-element.41), channel_id=1, source_target_pairs={{0,2},{1,3},{2,0},{3,1},{4,6},{5,7},{6,4},{7,5},{8,10},{9,11},{10,... | collective-permute-start | bytes 245768 | tf_op jit(solution)/shard_map/ppermute | solution.py:107
  99.7 5.6 %collective-permute-start.22 = (bf16[64,640]{1,0:T(8,128)(2,1)S(1)}, bf16[64,640]{1,0:T(8,128)(2,1)S(1)}, u32[]{:S(2)}, u32[]{:S(2)}) collective-permute-start(bf16[64,640]{1,0:T(8,128)(2,1)S(1)} %get-tuple-element.42), channel_id=1, source_target_pairs={{0,3},{1,2},{2,1},{3,0},{4,7},{5,6},{6,5},{7,4},{8,11},{9,10},{10,... | collective-permute-start | bytes 245768 | tf_op jit(solution)/shard_map/ppermute | solution.py:107
  (1 other events, 0.8 us)

commit v10 on v9

--- a/solution.py
+++ b/solution.py
@@ -176,7 +176,7 @@
 
 def value_kernel(me_ref, rows_ref, weights_ref, totals_ref, *refs):
     blocks = refs[0:8]
-    keep_ref, send_ref, v_whole, out_whole = refs[8:]
+    attended_ref, send_ref, v_whole, out_whole = refs[8:]
     lay_out(me_ref[0], blocks, 2, v_whole)
     lay_out(me_ref[0], blocks, 3, out_whole)
     values = dot(rows_ref[...], v_whole[...]).astype(jnp.bfloat16)
@@ -186,8 +186,14 @@
         pieces.append(found / totals_ref[head])
     attended = jnp.concatenate(pieces, axis=1).astype(jnp.bfloat16)
     half = attended.shape[0] // 2
+    attended_ref[...] = attended[:half, :]
     send_ref[...] = dot_turned(attended[half:, :], out_whole[...]).astype(jnp.bfloat16)
-    keep_ref[...] = dot_turned(attended[:half, :], out_whole[...])
+
+
+def keep_kernel(me_ref, attended_ref, *refs):
+    blocks, (keep_ref, out_whole) = refs[0:8], refs[8:]
+    lay_out(me_ref[0], blocks, 3, out_whole)
+    keep_ref[...] = dot_turned(attended_ref[...], out_whole[...])
 
 
 def pass_kernel(keep_ref, got_ref, out_ref):
@@ -197,9 +203,9 @@
 
 def layer_kernel(tokens_ref, keep_ref, core_ref, chip_ref, gains_ref, order_ref, *refs):
     (slices,) = refs
-    rows, width = tokens_ref.shape
+    rows, width = tokens_ref.shape[0] - 16, tokens_ref.shape[1]
     summed = (
-        tokens_ref[...].astype(jnp.float32)
+        tokens_ref[0:rows, :].astype(jnp.float32)
         + keep_ref[0:rows, :]
         + core_ref[0:rows, :].astype(jnp.float32)
         + chip_ref[...].astype(jnp.float32)
@@ -270,29 +276,33 @@
     cols = qkv_weight.shape[2]
     group = n_fsdp * rows
 
-    heads = jnp.concatenate([qkv_weight, out_weight.T[None]], axis=0)
-    near, beside = swap(heads, "dp", 2), swap(heads, "dp", 1)
-    first, second = heads[0:2], heads[2:4]
-    first_far = swap(first, "dp", 4)
-    first_far_y = swap(after(first_far, (near, beside)), "dp", 1)
+    marks = jnp.pad(segments.astype(bf16), ((0, 15), (0, width - rows)))
+    marked = jnp.concatenate([tokens, marks], axis=0)
+    first = qkv_weight[0:2]
+    out_turned = after(out_weight, first).T[None]
+    heads = jnp.concatenate([qkv_weight, out_turned], axis=0)
+    beside = swap(heads, "dp", 1)
+    first_far, first_near = swap(first, "dp", 4), swap(first, "dp", 2)
+    second = jnp.concatenate([qkv_weight[2:3], out_turned], axis=0)
+    first_far_y = swap(first_far, "dp", 1)
     first_last = swap(first_far, "dp", 2)
     corner = swap(beside, "dp", 2)
     second_far = swap(after(second, first_far), "dp", 4)
 
-    marks = jnp.pad(segments.astype(bf16), ((0, 15), (0, width - rows)))
-    marked = after(jnp.concatenate([tokens, marks], axis=0), first)
+    marked = after(marked, heads)
     along_x = swap(marked, "fsdp", 2)
     group_rows = [marked, along_x]
-    group_rows += [swap(after(part, (first_far_y, first_last, second_far)), "fsdp", 1) for part in (marked, along_x)]
+    group_rows += [swap(after(part, (first_near, beside, first_far_y, first_last, second_far)), "fsdp", 1) for part in (marked, along_x)]
     (normed,) = call(norm_kernel, [shape((group, width), bf16)], [ln_gains, *group_rows])
 
+    second_near = swap(after(second, first_last), "dp", 2)
     second_far_y = swap(second_far, "dp", 1)
     second_last = swap(second_far, "dp", 2)
     blocks = [
         [heads, near, far, last, beside, corner, far_y, swap(after(last, corner), "dp", 1)]
-        for far, last, far_y in (
-            (first_far, first_last, first_far_y),
-            (second_far, second_last, second_far_y),
+        for near, far, last, far_y in (
+            (first_near, first_far, first_last, first_far_y),
+            (second_near, second_far, second_last, second_far_y),
         )
     ]
 
@@ -326,21 +336,29 @@
         smem=1,
         exps=found * group * group,
     )
-    keep, send = call(
+    attended, send = call(
         value_kernel,
-        [shape((2 * rows, width), f32), shape((2 * rows, width), bf16)],
+        [shape((2 * rows, cols), bf16), shape((2 * rows, width), bf16)],
         [me_cell, normed, weights, totals, *blocks[1]],
         [pltpu.VMEM((width, cols), bf16)] * 2,
         flops=4 * group * width * cols + 2 * group * group * cols,
         smem=1,
     )
     from_core = swap(send, "fsdp", 1)
+    (keep,) = call(
+        keep_kernel,
+        [shape((2 * rows, width), f32)],
+        [me_cell, attended, *blocks[1]],
+        [pltpu.VMEM((width, cols), bf16)],
+        flops=4 * rows * width * cols,
+        smem=1,
+    )
     (onward,) = call(pass_kernel, [shape((rows, width), bf16)], [keep, from_core])
     from_chip = swap(onward, "fsdp", 2)
     (slices,) = call(
         layer_kernel,
         [shape((8, rows // 2, width // 2), bf16)],
-        [tokens, keep, from_core, from_chip, ln_gains, order],
+        [marked, keep, from_core, from_chip, ln_gains, order],
         flops=2 * rows * rows * width,
     )
     merge_blocks = [pair, merge_near, merge_far, swap(after(merge_far, (slices, merge_near)), "dp", 2)]

time: 118 us -> 120 us (1.017)
  waiting for transfers between devices: 53.6 us -> 61.4 us
  other arithmetic: 7.19 us -> 2.49 us
  starting transfers between devices: 31.1 us -> 27.1 us
  blocking collectives: 11.2 us -> 12.6 us
  Pallas kernels: 11.1 us -> 12.4 us
    ppermute x23 -> x24, waiting for transfers between devices: 53.6 us -> 61.4 us  [swap(): lax.ppermute(value, axis, [(i, i ^ k) for i in range(lax.axis_size(axis))])]
    ppermute x23 -> x24, starting transfers between devices: 27.4 us -> 23.6 us  [swap(): lax.ppermute(value, axis, [(i, i ^ k) for i in range(lax.axis_size(axis))])]
    slice x0 -> x3, local copies, waits for them, and re-layouts: none -> 1.73 us  [the longest x1 1.73 us: by_permutes(): first = qkv_weight[0:2]]
    slice x1 -> x0, other arithmetic: 1.64 us -> none  [by_permutes(): first, second = (heads[0:2], heads[2:4])]
    all_to_all x1, blocking collectives: 11.2 us -> 12.6 us  [by_permutes(): lax.all_to_all(packed.reshape(n_dp, 2 * capacity, half), 'dp', split_axis...]
    pallas_call x7 -> x8, Pallas kernels: 11.1 us -> 12.4 us  [call(): pl.pallas_call(kernel, out_shape=tuple(outs), in_specs=specs, out_specs=t...]
  transfers between devices with their start and end apart: 24 -> 25, of which waited for: 15 -> 16; matrix products, arithmetic and copies ran while one was open for 6% -> 2% of each run, Pallas kernels for 6% -> 6%
where the time goes in v10:
time: 120 us
  waiting for transfers between devices  61.4 us (51%)
  starting transfers between devices  27.1 us (23%)
  blocking collectives  12.6 us (10%)
  Pallas kernels  12.4 us (10%)
  local copies, waits for them, and re-layouts  3.3 us (3%)
  other arithmetic  2.49 us (2%)
    ppermute x24, waiting for transfers between devices, swap(): lax.ppermute(value, axis, [(i, i ^ k) for i in range(lax.axis_size(axis))])  61.4 us
    ppermute x24, starting transfers between devices, swap(): lax.ppermute(value, axis, [(i, i ^ k) for i in range(lax.axis_size(axis))])  23.6 us
    all_to_all x1, blocking collectives, by_permutes(): lax.all_to_all(packed.reshape(n_dp, 2 * capacity, half), 'dp', split_axis...  12.6 us
    pallas_call x8, Pallas kernels, call(): pl.pallas_call(kernel, out_shape=tuple(outs), in_specs=specs, out_specs=t...  12.4 us
    all_to_all x1, starting transfers between devices, by_permutes(): lax.all_to_all(slices, ('dp', 'fsdp'), split_axis=0, concat_axis=0, tiled...  3.54 us
  transfers between devices with their start and end apart: 25, of which 16 were waited for; matrix products, arithmetic and copies ran while one was open for 2% of the time, Pallas kernels for 6%

profile of v10, /device:TPU:0, one launch (start us, length us, event | category | flops | bytes accessed | tf_op | source)
XLA Modules:
  0.0 119.5 jit_solution(7097351045244662644)
XLA Ops:
  0.0 1.7 %slice.21 = bf16[2,160,320]{2,1,0:T(8,128)(2,1)} slice(bf16[3,160,320]{2,1,0:T(8,128)(2,1)} %param.9), slice={[0:2], [0:160], [0:320]} | slice | bytes 409600 | tf_op jit(solution)/shard_map/slice | solution.py:281
  1.7 1.2 pad_maximum_fusion.refs_4_.refs_0_
  2.9 3.0 %collective-permute-start.6 = (bf16[4,160,320]{2,1,0:T(8,128)(2,1)S(1)}, bf16[4,160,320]{2,1,0:T(8,128)(2,1)S(1)}, u32[]{:S(2)}, u32[]{:S(2)}) collective-permute-start(bf16[4,160,320]{2,1,0:T(8,128)(2,1)S(1)} %pad_maximum_fusion.refs_4_.refs_0_), channel_id=1, source_target_pairs={{0,4},{4,0},{8,12},{12,8},{16,20},{20,16},{24,28},{28,24},{1,5},{5... | collective-permute-start | bytes 1228808 | tf_op jit(solution)/shard_map/ppermute | solution.py:107
  6.0 2.6 %collective-permute-start = (bf16[2,160,320]{2,1,0:T(8,128)(2,1)}, bf16[2,160,320]{2,1,0:T(8,128)(2,1)S(1)}, u32[]{:S(2)}, u32[]{:S(2)}) collective-permute-start(bf16[2,160,320]{2,1,0:T(8,128)(2,1)} %slice.21), channel_id=1, source_target_pairs={{0,16},{4,20},{8,24},{12,28},{16,0},{20,4},{24,8},{28,12},{1,17},{... | collective-permute-start | bytes 614408 | tf_op jit(solution)/shard_map/ppermute | solution.py:107
  8.6 1.6 %collective-permute-start.5 = (bf16[2,160,320]{2,1,0:T(8,128)(2,1)}, bf16[2,160,320]{2,1,0:T(8,128)(2,1)S(1)}, u32[]{:S(2)}, u32[]{:S(2)}) collective-permute-start(bf16[2,160,320]{2,1,0:T(8,128)(2,1)} %slice.21), channel_id=1, source_target_pairs={{0,8},{4,12},{8,0},{12,4},{16,24},{20,28},{24,16},{28,20},{1,9},{5... | collective-permute-start | bytes 614408 | tf_op jit(solution)/shard_map/ppermute | solution.py:107
  10.2 1.6 %collective-permute-start.4 = (bf16[144,1280]{1,0:T(8,128)(2,1)S(1)}, bf16[144,1280]{1,0:T(8,128)(2,1)S(1)}, u32[]{:S(2)}, u32[]{:S(2)}) collective-permute-start(bf16[144,1280]{1,0:T(8,128)(2,1)S(1)} %fusion.2.refs_0_.tokens_ref), channel_id=1, source_target_pairs={{0,2},{1,3},{2,0},{3,1},{4,6},{5,7},{6,4},{7,5},{8,10},{9,11},{10,... | collective-permute-start | bytes 1105928 | tf_op jit(solution)/shard_map/ppermute | solution.py:107
  11.8 8.1 %collective-permute-done.refs_6_ = bf16[2,160,320]{2,1,0:T(8,128)(2,1)S(1)} collective-permute-done((bf16[2,160,320]{2,1,0:T(8,128)(2,1)}, bf16[2,160,320]{2,1,0:T(8,128)(2,1)S(1)}, u32[]{:S(2)}, u32[]{:S(2)}) %collective-permute-start) | collective-permute-done | bytes 204832 | tf_op jit(solution)/shard_map/ppermute | solution.py:107
  19.9 3.9 %collective-permute-start.8 = (bf16[2,160,320]{2,1,0:T(8,128)(2,1)S(1)}, bf16[2,160,320]{2,1,0:T(8,128)(2,1)S(1)}, u32[]{:S(2)}, u32[]{:S(2)}) collective-permute-start(bf16[2,160,320]{2,1,0:T(8,128)(2,1)S(1)} %collective-permute-done.refs_6_), channel_id=1, source_target_pairs={{0,8},{4,12},{8,0},{12,4},{16,24},{20,28},{24,16},{28,20},{1,9},{5... | collective-permute-start | bytes 614408 | tf_op jit(solution)/shard_map/ppermute | solution.py:107
  24.4 8.5 %collective-permute-done.1.refs_2_ = bf16[2,160,320]{2,1,0:T(8,128)(2,1)S(1)} collective-permute-done((bf16[2,160,320]{2,1,0:T(8,128)(2,1)S(1)}, bf16[2,160,320]{2,1,0:T(8,128)(2,1)S(1)}, u32[]{:S(2)}, u32[]{:S(2)}) %collective-permute-start.1) | collective-permute-done | bytes 204832 | tf_op jit(solution)/shard_map/ppermute | solution.py:107
  32.9 1.0 collective-permute-done.8.refs_7_
  35.0 7.3 %collective-permute-done.2.refs_6_ = bf16[2,160,320]{2,1,0:T(8,128)(2,1)S(1)} collective-permute-done((bf16[2,160,320]{2,1,0:T(8,128)(2,1)S(1)}, bf16[2,160,320]{2,1,0:T(8,128)(2,1)S(1)}, u32[]{:S(2)}, u32[]{:S(2)}) %collective-permute-start.2) | collective-permute-done | bytes 204832 | tf_op jit(solution)/shard_map/ppermute | solution.py:107
  42.8 1.7 %collective-permute-done.11.refs_9_.refs_5_ = bf16[4,160,320]{2,1,0:T(8,128)(2,1)S(1)} collective-permute-done((bf16[4,160,320]{2,1,0:T(8,128)(2,1)S(1)}, bf16[4,160,320]{2,1,0:T(8,128)(2,1)S(1)}, u32[]{:S(2)}, u32[]{:S(2)}) %collective-permute-start.11) | collective-permute-done | bytes 409632 | tf_op jit(solution)/shard_map/ppermute | solution.py:107
  44.9 3.8 %collective-permute-done.14.refs_3_ = bf16[2,160,320]{2,1,0:T(8,128)(2,1)S(1)} collective-permute-done((bf16[2,160,320]{2,1,0:T(8,128)(2,1)S(1)}, bf16[2,160,320]{2,1,0:T(8,128)(2,1)S(1)}, u32[]{:S(2)}, u32[]{:S(2)}) %collective-permute-start.14) | collective-permute-done | bytes 204832 | tf_op jit(solution)/shard_map/ppermute | solution.py:107
  49.3 0.9 shard_map.82.rows_ref
  50.8 5.3 %collective-permute-done.12.refs_11_ = bf16[2,160,320]{2,1,0:T(8,128)(2,1)S(1)} collective-permute-done((bf16[2,160,320]{2,1,0:T(8,128)(2,1)S(1)}, bf16[2,160,320]{2,1,0:T(8,128)(2,1)S(1)}, u32[]{:S(2)}, u32[]{:S(2)}) %collective-permute-start.12) | collective-permute-done | bytes 204832 | tf_op jit(solution)/shard_map/ppermute | solution.py:107
  56.0 3.0 %shard_map.83 = (bf16[4,512,512]{2,1,0:T(8,128)(2,1)S(1)}, f32[4,512,1]{2,1,0:T(8,128)S(1)}) custom-call(s32[1]{0:T(128)} %bitcast.7.me_ref, bf16[512,1280]{1,0:T(8,128)(2,1)S(1)} %shard_map.82.rows_ref, bf16[144,1280]{1,0:T(8,128)(2,1)S(1)} %fusion.2.refs_0_.tokens_ref, bf16[144,1280]{1,0:T(8,128)(2,1)S(1)} %collective-permute-done.4.refs_1_, ...), custom_call_target="tpu_custom_call" | custom-call | flops 1006632960 | bytes 7143428 | tf_op jit(solution)/shard_map/pallas_call | solution.py:129
  59.4 2.2 %shard_map.84 = (bf16[256,320]{1,0:T(8,128)(2,1)S(1)}, bf16[256,1280]{1,0:T(8,128)(2,1)S(1)}) custom-call(s32[1]{0:T(128)} %bitcast.7.me_ref, bf16[512,1280]{1,0:T(8,128)(2,1)S(1)} %shard_map.82.rows_ref, bf16[4,512,512]{2,1,0:T(8,128)(2,1)S(1)} %get-tuple-element.33.weights_ref, f32[4,512,1]{2,1,0:T(8,128)S(1)} %get-tuple-element.34.totals_ref, ...), custom_call_target="tpu_custom_call" | custom-call | flops 1006632960 | bytes 6488068 | tf_op jit(solution)/shard_map/pallas_call | solution.py:129
  62.3 1.4 %collective-permute-done.16.got_ref.core_ref = bf16[256,1280]{1,0:T(8,128)(2,1)S(1)} collective-permute-done((bf16[256,1280]{1,0:T(8,128)(2,1)S(1)}, bf16[256,1280]{1,0:T(8,128)(2,1)S(1)}, u32[]{:S(2)}, u32[]{:S(2)}) %collective-permute-start.16) | collective-permute-done | bytes 655392 | tf_op jit(solution)/shard_map/ppermute | solution.py:107
  63.8 0.8 shard_map.86
  64.6 1.5 %collective-permute-start.17 = (bf16[128,1280]{1,0:T(8,128)(2,1)}, bf16[128,1280]{1,0:T(8,128)(2,1)}, u32[]{:S(2)}, u32[]{:S(2)}) collective-permute-start(bf16[128,1280]{1,0:T(8,128)(2,1)} %shard_map.86), channel_id=1, source_target_pairs={{0,2},{1,3},{2,0},{3,1},{4,6},{5,7},{6,4},{7,5},{8,10},{9,11},{10,... | collective-permute-start | bytes 983048 | tf_op jit(solution)/shard_map/ppermute | solution.py:107
  66.2 4.0 %collective-permute-start.19 = (bf16[320,640]{1,0:T(8,128)(2,1)S(1)}, bf16[320,640]{1,0:T(8,128)(2,1)}, u32[]{:S(2)}, u32[]{:S(2)}) collective-permute-start(bf16[320,640]{1,0:T(8,128)(2,1)S(1)} %pad_maximum_fusion.1.refs_0_), channel_id=1, source_target_pairs={{0,16},{4,20},{8,24},{12,28},{16,0},{20,4},{24,8},{28,12},{1,17},{... | collective-permute-start | bytes 1228808 | tf_op jit(solution)/shard_map/ppermute | solution.py:107
  71.9 2.8 %collective-permute-done.17.chip_ref = bf16[128,1280]{1,0:T(8,128)(2,1)} collective-permute-done((bf16[128,1280]{1,0:T(8,128)(2,1)}, bf16[128,1280]{1,0:T(8,128)(2,1)}, u32[]{:S(2)}, u32[]{:S(2)}) %collective-permute-start.17) | collective-permute-done | bytes 327712 | tf_op jit(solution)/shard_map/ppermute | solution.py:107
  74.6 2.6 %shard_map.87 = bf16[8,64,640]{2,1,0:T(8,128)(2,1)} custom-call(bf16[144,1280]{1,0:T(8,128)(2,1)S(1)} %fusion.2.refs_0_.tokens_ref, f32[256,1280]{1,0:T(8,128)S(1)} %shard_map.85.keep_ref, bf16[256,1280]{1,0:T(8,128)(2,1)S(1)} %collective-permute-done.16.got_ref.core_ref, bf16[128,1280]{1,0:T(8,128)(2,1)} %collective-permute-done.17.chip_ref, ...), custom_call_target="tpu_custom_call" | custom-call | flops 41943040 | bytes 3328512 | tf_op jit(solution)/shard_map/pallas_call | solution.py:129
  77.3 3.5 %all-to-all-start = ((bf16[8,64,640]{2,1,0:T(8,128)(2,1)}), bf16[8,64,640]{2,1,0:T(8,128)(2,1)S(1)}, u32[]{:S(2)}, u32[]{:S(2)}) async-start(bf16[8,64,640]{2,1,0:T(8,128)(2,1)} %shard_map.87), calls=%async_computation | async-start | bytes 1310720 | tf_op jit(solution)/shard_map/all_to_all | solution.py:366
  80.8 5.1 %collective-permute-done.18.refs_1_ = bf16[320,640]{1,0:T(8,128)(2,1)S(1)} collective-permute-done((bf16[320,640]{1,0:T(8,128)(2,1)S(1)}, bf16[320,640]{1,0:T(8,128)(2,1)S(1)}, u32[]{:S(2)}, u32[]{:S(2)}) %collective-permute-start.18) | collective-permute-done | bytes 409632 | tf_op jit(solution)/shard_map/ppermute | solution.py:107
  86.0 2.4 %collective-permute-done.19.refs_2_ = bf16[320,640]{1,0:T(8,128)(2,1)} collective-permute-done((bf16[320,640]{1,0:T(8,128)(2,1)S(1)}, bf16[320,640]{1,0:T(8,128)(2,1)}, u32[]{:S(2)}, u32[]{:S(2)}) %collective-permute-start.19) | collective-permute-done | bytes 409632 | tf_op jit(solution)/shard_map/ppermute | solution.py:107
  88.9 8.9 %collective-permute-done.20.refs_3_ = bf16[320,640]{1,0:T(8,128)(2,1)S(1)} collective-permute-done((bf16[320,640]{1,0:T(8,128)(2,1)}, bf16[320,640]{1,0:T(8,128)(2,1)S(1)}, u32[]{:S(2)}, u32[]{:S(2)}) %collective-permute-start.20) | collective-permute-done | bytes 409632 | tf_op jit(solution)/shard_map/ppermute | solution.py:107
  97.7 2.0 %shard_map.88 = (f32[64,640]{1,0:T(8,128)S(1)}, bf16[64,640]{1,0:T(8,128)(2,1)S(1)}, bf16[64,640]{1,0:T(8,128)(2,1)S(1)}, bf16[64,640]{1,0:T(8,128)(2,1)S(1)}) custom-call(s32[1]{0:T(128)} %bitcast.7.me_ref, s32[1]{0:T(128)} %bitcast.8.at_ref, bf16[8,64,640]{2,1,0:T(8,128)(2,1)S(1)} %all-to-all-done.inputs, bf16[320,640]{1,0:T(8,128)(2,1)S(1)} %pad_maximum_fusion.1.refs_0_, ...), custom_call_target="tpu_custom_call" | custom-call | flops 419430400 | bytes 2703368 | tf_op jit(solution)/shard_map/pallas_call | solution.py:129
  100.5 1.3 %collective-permute-start.23 = (bf16[64,640]{1,0:T(8,128)(2,1)S(1)}, bf16[64,640]{1,0:T(8,128)(2,1)S(1)}, u32[]{:S(2)}, u32[]{:S(2)}) collective-permute-start(bf16[64,640]{1,0:T(8,128)(2,1)S(1)} %get-tuple-element.44), channel_id=1, source_target_pairs={{0,3},{1,2},{2,1},{3,0},{4,7},{5,6},{6,5},{7,4},{8,11},{9,10},{10,... | collective-permute-start | bytes 245768 | tf_op jit(solution)/shard_map/ppermute | solution.py:107
  101.8 3.4 %collective-permute-done.22.two_ref = bf16[64,640]{1,0:T(8,128)(2,1)S(1)} collective-permute-done((bf16[64,640]{1,0:T(8,128)(2,1)S(1)}, bf16[64,640]{1,0:T(8,128)(2,1)S(1)}, u32[]{:S(2)}, u32[]{:S(2)}) %collective-permute-start.22) | collective-permute-done | bytes 81952 | tf_op jit(solution)/shard_map/ppermute | solution.py:107
  105.2 0.8 collective-permute-done.23.three_ref
  106.2 12.6 %all_to_all.10 = bf16[8,16,640]{2,1,0:T(8,128)(2,1)S(1)} all-to-all(bf16[8,16,640]{2,1,0:T(8,128)(2,1)S(1)} %bitcast.24), channel_id=1, replica_groups=mesh['dp'=8,'fsdp'=4] {'dp'}, dimensions={0} | all-to-all | bytes 327680 | tf_op jit(solution)/shard_map/all_to_all | solution.py:391
  (67 shorter events, 8.8 us)
Async XLA Ops:
  0.0 11.8 %slice-start = ((bf16[3,160,320]{2,1,0:T(8,128)(2,1)}), bf16[1,160,320]{2,1,0:T(8,128)(2,1)S(1)}, s32[]{:S(2)}) async-start(bf16[3,160,320]{2,1,0:T(8,128)(2,1)} %param.9), calls=%async_computation.2 | async-start | bytes 245760 | tf_op jit(solution)/shard_map/slice | solution.py:286
  0.0 11.8 %copy-start.1 = (bf16[320,160]{0,1:T(8,128)(2,1)S(1)}, bf16[320,160]{0,1:T(8,128)(2,1)}, u32[]{:S(2)}) copy-start(bf16[320,160]{0,1:T(8,128)(2,1)} %param.10) | copy-start | bytes 307204
  0.0 10.2 %copy-start.6 = (s32[1,128]{1,0:T(1,128)S(1)}, s32[1,128]{1,0:T(1,128)}, u32[]{:S(2)}) copy-start(s32[1,128]{1,0:T(1,128)} %param.13) | copy-start | bytes 1540
  0.0 10.2 %copy-start.3 = (bf16[128,1280]{1,0:T(8,128)(2,1)S(1)}, bf16[128,1280]{1,0:T(8,128)(2,1)}, u32[]{:S(2)}) copy-start(bf16[128,1280]{1,0:T(8,128)(2,1)} %param.8) | copy-start | bytes 983044
  1.7 22.6 %copy-start.2 = (bf16[160,1280]{1,0:T(8,128)(2,1)S(1)}, bf16[160,1280]{1,0:T(8,128)(2,1)}, u32[]{:S(2)}) copy-start(bf16[160,1280]{1,0:T(8,128)(2,1)} %param.11) | copy-start | bytes 1228804
  2.9 32.0 %copy-start.4 = (s32[32,1]{0,1:T(1,128)S(1)}, s32[32,1]{0,1:T(1,128)}, u32[]{:S(2)}) copy-start(s32[32,1]{0,1:T(1,128)} %param.15) | copy-start | bytes 388
  2.9 21.4 %collective-permute-start.6 = (bf16[4,160,320]{2,1,0:T(8,128)(2,1)S(1)}, bf16[4,160,320]{2,1,0:T(8,128)(2,1)S(1)}, u32[]{:S(2)}, u32[]{:S(2)}) collective-permute-start(bf16[4,160,320]{2,1,0:T(8,128)(2,1)S(1)} %pad_maximum_fusion.refs_4_.refs_0_), channel_id=1, source_target_pairs={{0,4},{4,0},{8,12},{12,8},{16,20},{20,16},{24,28},{28,24},{1,5},{5... | collective-permute-start | bytes 1228808 | tf_op jit(solution)/shard_map/ppermute | solution.py:107
  6.0 13.9 %collective-permute-start = (bf16[2,160,320]{2,1,0:T(8,128)(2,1)}, bf16[2,160,320]{2,1,0:T(8,128)(2,1)S(1)}, u32[]{:S(2)}, u32[]{:S(2)}) collective-permute-start(bf16[2,160,320]{2,1,0:T(8,128)(2,1)} %slice.21), channel_id=1, source_target_pairs={{0,16},{4,20},{8,24},{12,28},{16,0},{20,4},{24,8},{28,12},{1,17},{... | collective-permute-start | bytes 614408 | tf_op jit(solution)/shard_map/ppermute | solution.py:107
  8.6 15.3 %collective-permute-start.5 = (bf16[2,160,320]{2,1,0:T(8,128)(2,1)}, bf16[2,160,320]{2,1,0:T(8,128)(2,1)S(1)}, u32[]{:S(2)}, u32[]{:S(2)}) collective-permute-start(bf16[2,160,320]{2,1,0:T(8,128)(2,1)} %slice.21), channel_id=1, source_target_pairs={{0,8},{4,12},{8,0},{12,4},{16,24},{20,28},{24,16},{28,20},{1,9},{5... | collective-permute-start | bytes 614408 | tf_op jit(solution)/shard_map/ppermute | solution.py:107
  10.2 39.1 %copy-start = (f32[2,1280]{1,0:T(2,128)S(1)}, f32[2,1280]{1,0:T(2,128)}, u32[]{:S(2)}) copy-start(f32[2,1280]{1,0:T(2,128)} %gains_ref.3) | copy-start | bytes 30724
  10.2 14.2 %collective-permute-start.4 = (bf16[144,1280]{1,0:T(8,128)(2,1)S(1)}, bf16[144,1280]{1,0:T(8,128)(2,1)S(1)}, u32[]{:S(2)}, u32[]{:S(2)}) collective-permute-start(bf16[144,1280]{1,0:T(8,128)(2,1)S(1)} %fusion.2.refs_0_.tokens_ref), channel_id=1, source_target_pairs={{0,2},{1,3},{2,0},{3,1},{4,6},{5,7},{6,4},{7,5},{8,10},{9,11},{10,... | collective-permute-start | bytes 1105928 | tf_op jit(solution)/shard_map/ppermute | solution.py:107
  19.9 13.0 %collective-permute-start.1 = (bf16[2,160,320]{2,1,0:T(8,128)(2,1)S(1)}, bf16[2,160,320]{2,1,0:T(8,128)(2,1)S(1)}, u32[]{:S(2)}, u32[]{:S(2)}) collective-permute-start(bf16[2,160,320]{2,1,0:T(8,128)(2,1)S(1)} %pad_maximum_fusion.2), channel_id=1, source_target_pairs={{0,16},{4,20},{8,24},{12,28},{16,0},{20,4},{24,8},{28,12},{1,17},{... | collective-permute-start | bytes 614408 | tf_op jit(solution)/shard_map/ppermute | solution.py:107
  19.9 14.0 %collective-permute-start.8 = (bf16[2,160,320]{2,1,0:T(8,128)(2,1)S(1)}, bf16[2,160,320]{2,1,0:T(8,128)(2,1)S(1)}, u32[]{:S(2)}, u32[]{:S(2)}) collective-permute-start(bf16[2,160,320]{2,1,0:T(8,128)(2,1)S(1)} %collective-permute-done.refs_6_), channel_id=1, source_target_pairs={{0,8},{4,12},{8,0},{12,4},{16,24},{20,28},{24,16},{28,20},{1,9},{5... | collective-permute-start | bytes 614408 | tf_op jit(solution)/shard_map/ppermute | solution.py:107
  23.8 10.1 %collective-permute-start.7 = (bf16[2,160,320]{2,1,0:T(8,128)(2,1)S(1)}, bf16[2,160,320]{2,1,0:T(8,128)(2,1)S(1)}, u32[]{:S(2)}, u32[]{:S(2)}) collective-permute-start(bf16[2,160,320]{2,1,0:T(8,128)(2,1)S(1)} %collective-permute-done.refs_6_), channel_id=1, source_target_pairs={{0,4},{4,0},{8,12},{12,8},{16,20},{20,16},{24,28},{28,24},{1,5},{5... | collective-permute-start | bytes 614408 | tf_op jit(solution)/shard_map/ppermute | solution.py:107
  24.3 20.1 %collective-permute-start.11 = (bf16[4,160,320]{2,1,0:T(8,128)(2,1)S(1)}, bf16[4,160,320]{2,1,0:T(8,128)(2,1)S(1)}, u32[]{:S(2)}, u32[]{:S(2)}) collective-permute-start(bf16[4,160,320]{2,1,0:T(8,128)(2,1)S(1)} %collective-permute-done.6.refs_8_.refs_4_), channel_id=1, source_target_pairs={{0,8},{4,12},{8,0},{12,4},{16,24},{20,28},{24,16},{28,20},{1,9},{5... | collective-permute-start | bytes 1228808 | tf_op jit(solution)/shard_map/ppermute | solution.py:107
  33.9 14.9 %collective-permute-start.10 = (bf16[144,1280]{1,0:T(8,128)(2,1)S(1)}, bf16[144,1280]{1,0:T(8,128)(2,1)S(1)}, u32[]{:S(2)}, u32[]{:S(2)}) collective-permute-start(bf16[144,1280]{1,0:T(8,128)(2,1)S(1)} %collective-permute-done.4.refs_1_), channel_id=1, source_target_pairs={{0,1},{1,0},{2,3},{3,2},{4,5},{5,4},{6,7},{7,6},{8,9},{9,8},{10,11... | collective-permute-start | bytes 1105928 | tf_op jit(solution)/shard_map/ppermute | solution.py:107
  33.9 15.4 %collective-permute-start.9 = (bf16[144,1280]{1,0:T(8,128)(2,1)S(1)}, bf16[144,1280]{1,0:T(8,128)(2,1)S(1)}, u32[]{:S(2)}, u32[]{:S(2)}) collective-permute-start(bf16[144,1280]{1,0:T(8,128)(2,1)S(1)} %fusion.2.refs_0_.tokens_ref), channel_id=1, source_target_pairs={{0,1},{1,0},{2,3},{3,2},{4,5},{5,4},{6,7},{7,6},{8,9},{9,8},{10,11... | collective-permute-start | bytes 1105928 | tf_op jit(solution)/shard_map/ppermute | solution.py:107
  34.4 7.9 %collective-permute-start.2 = (bf16[2,160,320]{2,1,0:T(8,128)(2,1)S(1)}, bf16[2,160,320]{2,1,0:T(8,128)(2,1)S(1)}, u32[]{:S(2)}, u32[]{:S(2)}) collective-permute-start(bf16[2,160,320]{2,1,0:T(8,128)(2,1)S(1)} %collective-permute-done.1.refs_2_), channel_id=1, source_target_pairs={{0,4},{4,0},{8,12},{12,8},{16,20},{20,16},{24,28},{28,24},{1,5},{5... | collective-permute-start | bytes 614408 | tf_op jit(solution)/shard_map/ppermute | solution.py:107
  34.9 13.9 %collective-permute-start.14 = (bf16[2,160,320]{2,1,0:T(8,128)(2,1)S(1)}, bf16[2,160,320]{2,1,0:T(8,128)(2,1)S(1)}, u32[]{:S(2)}, u32[]{:S(2)}) collective-permute-start(bf16[2,160,320]{2,1,0:T(8,128)(2,1)S(1)} %collective-permute-done.1.refs_2_), channel_id=1, source_target_pairs={{0,8},{4,12},{8,0},{12,4},{16,24},{20,28},{24,16},{28,20},{1,9},{5... | collective-permute-start | bytes 614408 | tf_op jit(solution)/shard_map/ppermute | solution.py:107
  42.3 8.5 %collective-permute-start.3 = (bf16[176,640]{1,0:T(8,128)(2,1)S(1)}, bf16[176,640]{1,0:T(8,128)(2,1)S(1)}, u32[]{:S(2)}, u32[]{:S(2)}) collective-permute-start(bf16[176,640]{1,0:T(8,128)(2,1)S(1)} %fusion.3), channel_id=1, source_target_pairs={{0,4},{4,0},{8,12},{12,8},{16,20},{20,16},{24,28},{28,24},{1,5},{5... | collective-permute-start | bytes 675848 | tf_op jit(solution)/shard_map/ppermute | solution.py:107
  44.4 11.6 %collective-permute-start.12 = (bf16[2,160,320]{2,1,0:T(8,128)(2,1)S(1)}, bf16[2,160,320]{2,1,0:T(8,128)(2,1)S(1)}, u32[]{:S(2)}, u32[]{:S(2)}) collective-permute-start(bf16[2,160,320]{2,1,0:T(8,128)(2,1)S(1)} %collective-permute-done.8.refs_7_), channel_id=1, source_target_pairs={{0,4},{4,0},{8,12},{12,8},{16,20},{20,16},{24,28},{28,24},{1,5},{5... | collective-permute-start | bytes 614408 | tf_op jit(solution)/shard_map/ppermute | solution.py:107
  48.8 10.3 %collective-permute-start.13 = (bf16[2,160,320]{2,1,0:T(8,128)(2,1)S(1)}, bf16[2,160,320]{2,1,0:T(8,128)(2,1)S(1)}, u32[]{:S(2)}, u32[]{:S(2)}) collective-permute-start(bf16[2,160,320]{2,1,0:T(8,128)(2,1)S(1)} %pad_maximum_fusion.2), channel_id=1, source_target_pairs={{0,8},{4,12},{8,0},{12,4},{16,24},{20,28},{24,16},{28,20},{1,9},{5... | collective-permute-start | bytes 614408 | tf_op jit(solution)/shard_map/ppermute | solution.py:107
  48.8 10.6 %collective-permute-start.15 = (bf16[2,160,320]{2,1,0:T(8,128)(2,1)S(1)}, bf16[2,160,320]{2,1,0:T(8,128)(2,1)S(1)}, u32[]{:S(2)}, u32[]{:S(2)}) collective-permute-start(bf16[2,160,320]{2,1,0:T(8,128)(2,1)S(1)} %collective-permute-done.14.refs_3_), channel_id=1, source_target_pairs={{0,4},{4,0},{8,12},{12,8},{16,20},{20,16},{24,28},{28,24},{1,5},{5... | collective-permute-start | bytes 614408 | tf_op jit(solution)/shard_map/ppermute | solution.py:107
  61.6 2.2 %collective-permute-start.16 = (bf16[256,1280]{1,0:T(8,128)(2,1)S(1)}, bf16[256,1280]{1,0:T(8,128)(2,1)S(1)}, u32[]{:S(2)}, u32[]{:S(2)}) collective-permute-start(bf16[256,1280]{1,0:T(8,128)(2,1)S(1)} %get-tuple-element.38), channel_id=1, source_target_pairs={{0,1},{1,0},{2,3},{3,2},{4,5},{5,4},{6,7},{7,6},{8,9},{9,8},{10,11... | collective-permute-start | bytes 1966088 | tf_op jit(solution)/shard_map/ppermute | solution.py:107
  64.6 10.1 %collective-permute-start.17 = (bf16[128,1280]{1,0:T(8,128)(2,1)}, bf16[128,1280]{1,0:T(8,128)(2,1)}, u32[]{:S(2)}, u32[]{:S(2)}) collective-permute-start(bf16[128,1280]{1,0:T(8,128)(2,1)} %shard_map.86), channel_id=1, source_target_pairs={{0,2},{1,3},{2,0},{3,1},{4,6},{5,7},{6,4},{7,5},{8,10},{9,11},{10,... | collective-permute-start | bytes 983048 | tf_op jit(solution)/shard_map/ppermute | solution.py:107
  66.1 19.8 %collective-permute-start.18 = (bf16[320,640]{1,0:T(8,128)(2,1)S(1)}, bf16[320,640]{1,0:T(8,128)(2,1)S(1)}, u32[]{:S(2)}, u32[]{:S(2)}) collective-permute-start(bf16[320,640]{1,0:T(8,128)(2,1)S(1)} %pad_maximum_fusion.1.refs_0_), channel_id=1, source_target_pairs={{0,8},{4,12},{8,0},{12,4},{16,24},{20,28},{24,16},{28,20},{1,9},{5... | collective-permute-start | bytes 1228808 | tf_op jit(solution)/shard_map/ppermute | solution.py:107
  66.2 22.1 %collective-permute-start.19 = (bf16[320,640]{1,0:T(8,128)(2,1)S(1)}, bf16[320,640]{1,0:T(8,128)(2,1)}, u32[]{:S(2)}, u32[]{:S(2)}) collective-permute-start(bf16[320,640]{1,0:T(8,128)(2,1)S(1)} %pad_maximum_fusion.1.refs_0_), channel_id=1, source_target_pairs={{0,16},{4,20},{8,24},{12,28},{16,0},{20,4},{24,8},{28,12},{1,17},{... | collective-permute-start | bytes 1228808 | tf_op jit(solution)/shard_map/ppermute | solution.py:107
  77.3 20.5 %all-to-all-start = ((bf16[8,64,640]{2,1,0:T(8,128)(2,1)}), bf16[8,64,640]{2,1,0:T(8,128)(2,1)S(1)}, u32[]{:S(2)}, u32[]{:S(2)}) async-start(bf16[8,64,640]{2,1,0:T(8,128)(2,1)} %shard_map.87), calls=%async_computation | async-start | bytes 1310720 | tf_op jit(solution)/shard_map/all_to_all | solution.py:366
  88.3 9.4 %collective-permute-start.20 = (bf16[320,640]{1,0:T(8,128)(2,1)}, bf16[320,640]{1,0:T(8,128)(2,1)S(1)}, u32[]{:S(2)}, u32[]{:S(2)}) collective-permute-start(bf16[320,640]{1,0:T(8,128)(2,1)} %collective-permute-done.19.refs_2_), channel_id=1, source_target_pairs={{0,8},{4,12},{8,0},{12,4},{16,24},{20,28},{24,16},{28,20},{1,9},{5... | collective-permute-start | bytes 1228808 | tf_op jit(solution)/shard_map/ppermute | solution.py:107
  99.8 2.0 %collective-permute-start.21 = (bf16[64,640]{1,0:T(8,128)(2,1)S(1)}, bf16[64,640]{1,0:T(8,128)(2,1)S(1)}, u32[]{:S(2)}, u32[]{:S(2)}) collective-permute-start(bf16[64,640]{1,0:T(8,128)(2,1)S(1)} %get-tuple-element.42), channel_id=1, source_target_pairs={{0,1},{1,0},{2,3},{3,2},{4,5},{5,4},{6,7},{7,6},{8,9},{9,8},{10,11... | collective-permute-start | bytes 245768 | tf_op jit(solution)/shard_map/ppermute | solution.py:107
  99.9 5.3 %collective-permute-start.22 = (bf16[64,640]{1,0:T(8,128)(2,1)S(1)}, bf16[64,640]{1,0:T(8,128)(2,1)S(1)}, u32[]{:S(2)}, u32[]{:S(2)}) collective-permute-start(bf16[64,640]{1,0:T(8,128)(2,1)S(1)} %get-tuple-element.43), channel_id=1, source_target_pairs={{0,2},{1,3},{2,0},{3,1},{4,6},{5,7},{6,4},{7,5},{8,10},{9,11},{10,... | collective-permute-start | bytes 245768 | tf_op jit(solution)/shard_map/ppermute | solution.py:107
  100.5 5.6 %collective-permute-start.23 = (bf16[64,640]{1,0:T(8,128)(2,1)S(1)}, bf16[64,640]{1,0:T(8,128)(2,1)S(1)}, u32[]{:S(2)}, u32[]{:S(2)}) collective-permute-start(bf16[64,640]{1,0:T(8,128)(2,1)S(1)} %get-tuple-element.44), channel_id=1, source_target_pairs={{0,3},{1,2},{2,1},{3,0},{4,7},{5,6},{6,5},{7,4},{8,11},{9,10},{10,... | collective-permute-start | bytes 245768 | tf_op jit(solution)/shard_map/ppermute | solution.py:107
  (2 other events, 17.8 us)

commit v11 on v6

--- a/solution.py
+++ b/solution.py
@@ -150,16 +150,16 @@
     step = blocks[0].shape[1]
     for number, block in zip(ORDER, blocks):
         start = pl.multiple_of((me ^ number) * step, 32)
-        whole[pl.ds(start, step), :] = block[part]
+        whole[pl.ds(start, step), :] = block[part if part < block.shape[0] else 0]
 
 
 def attention_kernel(me_ref, rows_ref, *refs):
-    marks, blocks = refs[0:4], refs[4:12]
-    keep_ref, send_ref, q_whole, k_whole, v_whole, out_whole = refs[12:]
+    marks, blocks, out_blocks = refs[0:4], refs[4:12], refs[12:20]
+    attended_ref, send_ref, q_whole, k_whole, v_whole, out_whole = refs[20:]
     lay_out(me_ref[0], blocks, 0, q_whole)
     lay_out(me_ref[0], blocks, 1, k_whole)
     lay_out(me_ref[0], blocks, 2, v_whole)
-    lay_out(me_ref[0], blocks, 3, out_whole)
+    lay_out(me_ref[0], out_blocks, 3, out_whole)
     queries = dot(rows_ref[...], q_whole[...]).astype(jnp.bfloat16)
     keys = dot(rows_ref[...], k_whole[...]).astype(jnp.bfloat16)
     values = dot(rows_ref[...], v_whole[...]).astype(jnp.bfloat16)
@@ -178,8 +178,14 @@
         pieces.append(dot(weights.astype(jnp.bfloat16), values[:, cols]) / totals)
     attended = jnp.concatenate(pieces, axis=1).astype(jnp.bfloat16)
     half = attended.shape[0] // 2
+    attended_ref[...] = attended[:half, :]
     send_ref[...] = dot_turned(attended[half:, :], out_whole[...]).astype(jnp.bfloat16)
-    keep_ref[...] = dot_turned(attended[:half, :], out_whole[...])
+
+
+def keep_kernel(me_ref, attended_ref, *refs):
+    blocks, (keep_ref, out_whole) = refs[0:8], refs[8:]
+    lay_out(me_ref[0], blocks, 3, out_whole)
+    keep_ref[...] = dot_turned(attended_ref[...], out_whole[...])
 
 
 def pass_kernel(keep_ref, got_ref, out_ref):
@@ -189,9 +195,9 @@
 
 def layer_kernel(tokens_ref, keep_ref, core_ref, chip_ref, gains_ref, order_ref, *refs):
     (slices,) = refs
-    rows, width = tokens_ref.shape
+    rows, width = tokens_ref.shape[0] - 16, tokens_ref.shape[1]
     summed = (
-        tokens_ref[...].astype(jnp.float32)
+        tokens_ref[0:rows, :].astype(jnp.float32)
         + keep_ref[0:rows, :]
         + core_ref[0:rows, :].astype(jnp.float32)
         + chip_ref[...].astype(jnp.float32)
@@ -215,7 +221,7 @@
 
 
 def merge_kernel(me_ref, at_ref, inputs, *refs):
-    pieces, (keep_ref, *sends), total = refs[0:8], refs[8:12], refs[12]
+    blocks, (keep_ref, *sends), total = refs[0:4], refs[4:8], refs[8]
     count, width = inputs.shape[1] // 2, inputs.shape[2] // 2
     z, y = me_ref[0] // 2, lax.rem(me_ref[0], 2)
     for number in range(4):
@@ -223,7 +229,8 @@
         at = pl.multiple_of(lax.rem(position, 2) * count, 32)
         rows = inputs[:, pl.ds(at, count), :].reshape(8 * count, 2 * width)
         rows = jnp.where(position < 2, rows[:, :width], rows[:, width:])
-        own, other = pieces[2 * number][...], pieces[2 * number + 1][...]
+        step = blocks[number].shape[0] // 2
+        own, other = blocks[number][:step, :], blocks[number][step:, :]
         block = jnp.concatenate(
             [jnp.where(y == 0, own, other), jnp.where(y == 0, other, own)], axis=0
         )
@@ -261,33 +268,39 @@
     cols = qkv_weight.shape[2]
     group = n_fsdp * rows
 
-    heads = jnp.concatenate([qkv_weight, out_weight.T[None]], axis=0)
-    along_z, along_y = [swap(heads, "dp", 2)], [swap(heads, "dp", 1)]
-    along_z += [swap(after(heads, (along_z[0], along_y[0])), "dp", 4)]
-    along_y += [swap(along_z[0], "dp", 1)]
+    far = swap(qkv_weight, "dp", 4)
+    out_turned = out_weight.T[None]
+    heads = jnp.concatenate([qkv_weight, out_turned], axis=0)
+    near, beside = swap(heads, "dp", 2), swap(heads, "dp", 1)
+    far_y, last = swap(far, "dp", 1), swap(after(far, beside), "dp", 2)
+    last_y = swap(last, "dp", 1)
+    corner = swap(after(beside, last), "dp", 2)
     half = merge_weight.shape[1] // 2
     low, high = merge_weight[:, :half], merge_weight[:, half:]
     lower = y == 0
-    mine = jnp.where(lower, low, high)
-    theirs = swap(after(jnp.where(lower, high, low), along_z[0]), "dp", 1)
-    along_z += [swap(after(along_z[1], (along_y[1], theirs)), "dp", 2)]
-    along_y += [swap(block, "dp", 1) for block in along_z[1:]]
+    mine = owners[:, 0]
+    note = jnp.pad(owners.astype(bf16).T, ((0, 15), (0, half - count)))
+    given = jnp.concatenate([jnp.where(lower, high, low), note], axis=0)
+    theirs = swap(after(given, heads), "dp", 1)
+    other = theirs[-16, :count].astype(jnp.int32)
+    out_far = swap(after(out_turned, (far, near)), "dp", 4)
+    out_far_y, out_last = swap(out_far, "dp", 1), swap(after(out_far, last), "dp", 2)
+    blocks = [heads, near, far, last, beside, corner, far_y, last_y]
+    out_blocks = [heads, near, out_far, out_last, beside, corner, out_far_y]
+    out_blocks += [swap(out_last, "dp", 1)]
 
     marks = jnp.pad(segments.astype(bf16), ((0, 15), (0, width - rows)))
-    marked = after(jnp.concatenate([tokens, marks], axis=0), along_z[0])
+    marked = after(jnp.concatenate([tokens, marks], axis=0), heads)
     along_x = swap(marked, "fsdp", 2)
-    group_rows = [marked, along_x, swap(marked, "fsdp", 1), swap(along_x, "fsdp", 1)]
+    group_rows = [marked, along_x]
+    group_rows += [swap(after(part, (far_y, last, theirs, out_far)), "fsdp", 1) for part in (marked, along_x)]
     (normed,) = call(norm_kernel, [shape((group, width), bf16)], [ln_gains, *group_rows])
 
-    far = swap(after(mine, (along_z[2], *group_rows[2:])), "dp", 4)
-    held, held_other = after((mine, theirs), far)
-    merge_pieces = [mine, theirs, swap(held, "dp", 2), swap(held_other, "dp", 2)]
-    merge_pieces += [far, swap(held_other, "dp", 4)]
-    merge_pieces += [swap(piece, "dp", 2) for piece in merge_pieces[4:6]]
+    pair = jnp.concatenate([jnp.where(lower, low, high), theirs[:-16]], axis=0)
+    held = after(pair, (last, out_last))
+    merge_near, merge_far = swap(held, "dp", 2), swap(held, "dp", 4)
 
     capacity = max(2, (2 * count + n_dp - 1) // n_dp)
-    mine = owners[:, 0]
-    other = swap(owners, "dp", 1)[:, 0]
     slots = []
     for number, targets in enumerate((mine, other)):
         start, rank = slot_numbers(targets, 2 * capacity)
@@ -295,31 +308,33 @@
     slots = jnp.concatenate(slots).reshape(1, 2 * count)
     order = merge_rows.reshape(count, 4).T.reshape(rows, 1)
 
-    keep, send = call(
+    attended, send = call(
         attention_kernel,
-        [shape((2 * rows, width), f32), shape((2 * rows, width), bf16)],
-        [
-            after(me_cell, far),
-            normed,
-            *group_rows,
-            heads,
-            *along_z,
-            *along_y,
-        ],
+        [shape((2 * rows, cols), bf16), shape((2 * rows, width), bf16)],
+        [after(me_cell, pair), normed, *group_rows, *blocks, *out_blocks],
         [pltpu.VMEM((width, cols), bf16)] * 4,
         flops=8 * group * width * cols + 4 * group * group * cols,
         smem=1,
         exps=cols // HD * group * group,
     )
     from_core = swap(send, "fsdp", 1)
+    (keep,) = call(
+        keep_kernel,
+        [shape((2 * rows, width), f32)],
+        [me_cell, attended, *out_blocks],
+        [pltpu.VMEM((width, cols), bf16)],
+        flops=4 * rows * width * cols,
+        smem=1,
+    )
     (onward,) = call(pass_kernel, [shape((rows, width), bf16)], [keep, from_core])
     from_chip = swap(onward, "fsdp", 2)
     (slices,) = call(
         layer_kernel,
         [shape((8, rows // 2, width // 2), bf16)],
-        [tokens, keep, from_core, after(from_chip, merge_pieces[5:7]), ln_gains, order],
+        [marked, keep, from_core, from_chip, ln_gains, order],
         flops=2 * rows * rows * width,
     )
+    merge_blocks = [pair, merge_near, merge_far, swap(after(merge_far, (slices, merge_near)), "dp", 2)]
     both = 2 * n_fsdp
     inputs = lax.all_to_all(
         slices,
@@ -334,7 +349,7 @@
     shares = call(
         merge_kernel,
         [shape((2 * count, half), f32)] + [shape((2 * count, half), bf16)] * 3,
-        [me_cell, at_cell, inputs, *merge_pieces],
+        [me_cell, at_cell, inputs, *merge_blocks],
         [pltpu.VMEM((8, count, half), f32)],
         flops=2 * 8 * count * width * half,
         smem=2,

time: 132 us -> 124 us (0.939)
  waiting for transfers between devices: 76.3 us -> 63.5 us
  blocking collectives: 10.4 us -> 13.5 us
  other arithmetic: 3.31 us -> 4.79 us
    ppermute x23, waiting for transfers between devices: 76.3 us -> 63.5 us  [swap(): lax.ppermute(value, axis, [(i, i ^ k) for i in range(lax.axis_size(axis))])]
    all_to_all x1, blocking collectives: 10.4 us -> 13.5 us  [by_permutes(): lax.all_to_all(packed.reshape(n_dp, 2 * capacity, half), 'dp', split_axis...]
    concatenate x2 -> x4, other arithmetic: 1.21 us -> 2.98 us  [the longest x1 1.17 us: by_permutes(): heads = jnp.concatenate([qkv_weight, out_turned], axis=0)]
    pallas_call x6 -> x7, Pallas kernels: 10.2 us -> 10.3 us  [call(): pl.pallas_call(kernel, out_shape=tuple(outs), in_specs=specs, out_specs=t...]
  transfers between devices with their start and end apart: 24 -> 24, of which waited for: 13 -> 14; matrix products, arithmetic and copies ran while one was open for 2% -> 5% of each run, Pallas kernels for 2% -> 3%
where the time goes in v11:
time: 124 us; the launch traced here: 123 us
  waiting for transfers between devices  63.5 us (51%)
  starting transfers between devices  27.8 us (22%)
  blocking collectives  13.5 us (11%)
  Pallas kernels  10.3 us (8%)
  other arithmetic  4.79 us (4%)
  local copies, waits for them, and re-layouts  3.52 us (3%)
    ppermute x23, waiting for transfers between devices, swap(): lax.ppermute(value, axis, [(i, i ^ k) for i in range(lax.axis_size(axis))])  63.5 us
    ppermute x23, starting transfers between devices, swap(): lax.ppermute(value, axis, [(i, i ^ k) for i in range(lax.axis_size(axis))])  24.2 us
    all_to_all x1, blocking collectives, by_permutes(): lax.all_to_all(packed.reshape(n_dp, 2 * capacity, half), 'dp', split_axis...  13.5 us
    pallas_call x7, Pallas kernels, call(): pl.pallas_call(kernel, out_shape=tuple(outs), in_specs=specs, out_specs=t...  10.3 us
    all_to_all x1, starting transfers between devices, by_permutes(): lax.all_to_all(slices, ('dp', 'fsdp'), split_axis=0, concat_axis=0, tiled...  3.54 us
    unnamed x15, local copies, waits for them, and re-layouts  2.53 us
  transfers between devices with their start and end apart: 24, of which 14 were waited for; matrix products, arithmetic and copies ran while one was open for 5% of the time, Pallas kernels for 3%

profile of v11, /device:TPU:0, one launch (start us, length us, event | category | flops | bytes accessed | tf_op | source)
XLA Modules:
  0.0 123.5 jit_solution(3244678205575507218)
XLA Ops:
  0.0 4.0 %collective-permute-start.2 = (bf16[3,160,320]{2,1,0:T(8,128)(2,1)}, bf16[3,160,320]{2,1,0:T(8,128)(2,1)S(1)}, u32[]{:S(2)}, u32[]{:S(2)}) collective-permute-start(bf16[3,160,320]{2,1,0:T(8,128)(2,1)} %param.9), channel_id=1, source_target_pairs={{0,16},{4,20},{8,24},{12,28},{16,0},{20,4},{24,8},{28,12},{1,17},{... | collective-permute-start | bytes 921608 | tf_op jit(solution)/shard_map/ppermute | solution.py:107
  4.0 1.2 pad_maximum_fusion.refs_4_.refs_12_.refs_0_
  5.2 1.6 %collective-permute-start.4 = (bf16[4,160,320]{2,1,0:T(8,128)(2,1)S(1)}, bf16[4,160,320]{2,1,0:T(8,128)(2,1)S(1)}, u32[]{:S(2)}, u32[]{:S(2)}) collective-permute-start(bf16[4,160,320]{2,1,0:T(8,128)(2,1)S(1)} %pad_maximum_fusion.refs_4_.refs_12_.refs_0_), channel_id=1, source_target_pairs={{0,4},{4,0},{8,12},{12,8},{16,20},{20,16},{24,28},{28,24},{1,5},{5... | collective-permute-start | bytes 1228808 | tf_op jit(solution)/shard_map/ppermute | solution.py:107
  6.8 1.6 %collective-permute-start.6 = (bf16[4,160,320]{2,1,0:T(8,128)(2,1)S(1)}, bf16[4,160,320]{2,1,0:T(8,128)(2,1)S(1)}, u32[]{:S(2)}, u32[]{:S(2)}) collective-permute-start(bf16[4,160,320]{2,1,0:T(8,128)(2,1)S(1)} %pad_maximum_fusion.refs_4_.refs_12_.refs_0_), channel_id=1, source_target_pairs={{0,8},{4,12},{8,0},{12,4},{16,24},{20,28},{24,16},{28,20},{1,9},{5... | collective-permute-start | bytes 1228808 | tf_op jit(solution)/shard_map/ppermute | solution.py:107
  9.0 1.0 fusion.2.refs_0_.tokens_ref
  10.0 1.6 %collective-permute-start.1 = (bf16[144,1280]{1,0:T(8,128)(2,1)S(1)}, bf16[144,1280]{1,0:T(8,128)(2,1)S(1)}, u32[]{:S(2)}, u32[]{:S(2)}) collective-permute-start(bf16[144,1280]{1,0:T(8,128)(2,1)S(1)} %fusion.2.refs_0_.tokens_ref), channel_id=1, source_target_pairs={{0,2},{1,3},{2,0},{3,1},{4,6},{5,7},{6,4},{7,5},{8,10},{9,11},{10,... | collective-permute-start | bytes 1105928 | tf_op jit(solution)/shard_map/ppermute | solution.py:107
  11.7 9.2 %collective-permute-done.2.refs_6_ = bf16[3,160,320]{2,1,0:T(8,128)(2,1)S(1)} collective-permute-done((bf16[3,160,320]{2,1,0:T(8,128)(2,1)}, bf16[3,160,320]{2,1,0:T(8,128)(2,1)S(1)}, u32[]{:S(2)}, u32[]{:S(2)}) %collective-permute-start.2) | collective-permute-done | bytes 307232 | tf_op jit(solution)/shard_map/ppermute | solution.py:107
  20.8 1.6 %collective-permute-start.3 = (bf16[3,160,320]{2,1,0:T(8,128)(2,1)S(1)}, bf16[3,160,320]{2,1,0:T(8,128)(2,1)S(1)}, u32[]{:S(2)}, u32[]{:S(2)}) collective-permute-start(bf16[3,160,320]{2,1,0:T(8,128)(2,1)S(1)} %collective-permute-done.2.refs_6_), channel_id=1, source_target_pairs={{0,4},{4,0},{8,12},{12,8},{16,20},{20,16},{24,28},{28,24},{1,5},{5... | collective-permute-start | bytes 921608 | tf_op jit(solution)/shard_map/ppermute | solution.py:107
  23.7 4.0 %collective-permute-done.6.refs_5_.refs_13_.refs_1_ = bf16[4,160,320]{2,1,0:T(8,128)(2,1)S(1)} collective-permute-done((bf16[4,160,320]{2,1,0:T(8,128)(2,1)S(1)}, bf16[4,160,320]{2,1,0:T(8,128)(2,1)S(1)}, u32[]{:S(2)}, u32[]{:S(2)}) %collective-permute-start.6) | collective-permute-done | bytes 409632 | tf_op jit(solution)/shard_map/ppermute | solution.py:107
  27.7 7.7 %collective-permute-done = bf16[176,640]{1,0:T(8,128)(2,1)S(1)} collective-permute-done((bf16[176,640]{1,0:T(8,128)(2,1)S(1)}, bf16[176,640]{1,0:T(8,128)(2,1)S(1)}, u32[]{:S(2)}, u32[]{:S(2)}) %collective-permute-start) | collective-permute-done | bytes 225312 | tf_op jit(solution)/shard_map/ppermute | solution.py:107
  35.4 1.1 collective-permute-done.5.refs_7_
  36.5 1.1 collective-permute-start.10
  37.8 1.0 collective-permute-start.11
  39.3 13.4 %collective-permute-done.12.refs_15_.refs_3_ = bf16[1,160,320]{2,1,0:T(8,128)(2,1)S(1)} collective-permute-done((bf16[1,160,320]{2,1,0:T(8,128)(2,1)S(1)}, bf16[1,160,320]{2,1,0:T(8,128)(2,1)S(1)}, u32[]{:S(2)}, u32[]{:S(2)}) %collective-permute-start.12) | collective-permute-done | bytes 102432 | tf_op jit(solution)/shard_map/ppermute | solution.py:107
  53.3 1.5 %collective-permute-start.14 = (bf16[1,160,320]{2,1,0:T(8,128)(2,1)S(1)}, bf16[1,160,320]{2,1,0:T(8,128)(2,1)S(1)}, u32[]{:S(2)}, u32[]{:S(2)}) collective-permute-start(bf16[1,160,320]{2,1,0:T(8,128)(2,1)S(1)} %collective-permute-done.12.refs_15_.refs_3_), channel_id=1, source_target_pairs={{0,4},{4,0},{8,12},{12,8},{16,20},{20,16},{24,28},{28,24},{1,5},{5... | collective-permute-start | bytes 307208 | tf_op jit(solution)/shard_map/ppermute | solution.py:107
  56.4 2.5 %collective-permute-done.13.refs_18_.refs_6_ = bf16[1,160,320]{2,1,0:T(8,128)(2,1)S(1)} collective-permute-done((bf16[1,160,320]{2,1,0:T(8,128)(2,1)S(1)}, bf16[1,160,320]{2,1,0:T(8,128)(2,1)S(1)}, u32[]{:S(2)}, u32[]{:S(2)}) %collective-permute-start.13) | collective-permute-done | bytes 102432 | tf_op jit(solution)/shard_map/ppermute | solution.py:107
  59.0 1.4 %collective-permute-done.14.refs_19_.refs_7_ = bf16[1,160,320]{2,1,0:T(8,128)(2,1)S(1)} collective-permute-done((bf16[1,160,320]{2,1,0:T(8,128)(2,1)S(1)}, bf16[1,160,320]{2,1,0:T(8,128)(2,1)S(1)}, u32[]{:S(2)}, u32[]{:S(2)}) %collective-permute-start.14) | collective-permute-done | bytes 102432 | tf_op jit(solution)/shard_map/ppermute | solution.py:107
  60.3 4.8 %shard_map.83 = (bf16[256,320]{1,0:T(8,128)(2,1)S(1)}, bf16[256,1280]{1,0:T(8,128)(2,1)S(1)}) custom-call(s32[1]{0:T(128)} %bitcast.7.me_ref, bf16[512,1280]{1,0:T(8,128)(2,1)S(1)} %shard_map.82.rows_ref, bf16[144,1280]{1,0:T(8,128)(2,1)S(1)} %fusion.2.refs_0_.tokens_ref, bf16[144,1280]{1,0:T(8,128)(2,1)S(1)} %collective-permute-done.1.refs_1_, ...), custom_call_target="tpu_custom_call" | custom-call | flops 2013265920 | bytes 8519684 | tf_op jit(solution)/shard_map/pallas_call | solution.py:129
  65.9 1.4 %collective-permute-done.15.got_ref.core_ref = bf16[256,1280]{1,0:T(8,128)(2,1)S(1)} collective-permute-done((bf16[256,1280]{1,0:T(8,128)(2,1)S(1)}, bf16[256,1280]{1,0:T(8,128)(2,1)S(1)}, u32[]{:S(2)}, u32[]{:S(2)}) %collective-permute-start.15) | collective-permute-done | bytes 655392 | tf_op jit(solution)/shard_map/ppermute | solution.py:107
  68.2 1.5 %collective-permute-start.16 = (bf16[128,1280]{1,0:T(8,128)(2,1)S(1)}, bf16[128,1280]{1,0:T(8,128)(2,1)S(1)}, u32[]{:S(2)}, u32[]{:S(2)}) collective-permute-start(bf16[128,1280]{1,0:T(8,128)(2,1)S(1)} %shard_map.85), channel_id=1, source_target_pairs={{0,2},{1,3},{2,0},{3,1},{4,6},{5,7},{6,4},{7,5},{8,10},{9,11},{10,... | collective-permute-start | bytes 983048 | tf_op jit(solution)/shard_map/ppermute | solution.py:107
  70.7 2.8 %collective-permute-start.18 = (bf16[320,640]{1,0:T(8,128)(2,1)}, bf16[320,640]{1,0:T(8,128)(2,1)S(1)}, u32[]{:S(2)}, u32[]{:S(2)}) collective-permute-start(bf16[320,640]{1,0:T(8,128)(2,1)} %pad_maximum_fusion.1.refs_0_), channel_id=1, source_target_pairs={{0,16},{4,20},{8,24},{12,28},{16,0},{20,4},{24,8},{28,12},{1,17},{... | collective-permute-start | bytes 1228808 | tf_op jit(solution)/shard_map/ppermute | solution.py:107
  75.2 2.8 %collective-permute-done.16.chip_ref = bf16[128,1280]{1,0:T(8,128)(2,1)S(1)} collective-permute-done((bf16[128,1280]{1,0:T(8,128)(2,1)S(1)}, bf16[128,1280]{1,0:T(8,128)(2,1)S(1)}, u32[]{:S(2)}, u32[]{:S(2)}) %collective-permute-start.16) | collective-permute-done | bytes 327712 | tf_op jit(solution)/shard_map/ppermute | solution.py:107
  78.0 1.1 copy-done.1
  79.1 1.7 %shard_map.86 = bf16[8,64,640]{2,1,0:T(8,128)(2,1)} custom-call(bf16[144,1280]{1,0:T(8,128)(2,1)S(1)} %fusion.2.refs_0_.tokens_ref, f32[256,1280]{1,0:T(8,128)S(1)} %shard_map.84.keep_ref, bf16[256,1280]{1,0:T(8,128)(2,1)S(1)} %copy-done.1, bf16[128,1280]{1,0:T(8,128)(2,1)S(1)} %collective-permute-done.16.chip_ref, f32[2,1280]{1,0:T(2,128)S(1)} %copy-done.2, ...), custom_call_target="tpu_custom_call" | custom-call | flops 41943040 | bytes 3328512 | tf_op jit(solution)/shard_map/pallas_call | solution.py:129
  80.7 3.5 %all-to-all-start = ((bf16[8,64,640]{2,1,0:T(8,128)(2,1)}), bf16[8,64,640]{2,1,0:T(8,128)(2,1)S(1)}, u32[]{:S(2)}, u32[]{:S(2)}) async-start(bf16[8,64,640]{2,1,0:T(8,128)(2,1)} %shard_map.86), calls=%async_computation | async-start | bytes 1310720 | tf_op jit(solution)/shard_map/all_to_all | solution.py:339
  84.3 5.6 %collective-permute-done.17.refs_1_ = bf16[320,640]{1,0:T(8,128)(2,1)S(1)} collective-permute-done((bf16[320,640]{1,0:T(8,128)(2,1)}, bf16[320,640]{1,0:T(8,128)(2,1)S(1)}, u32[]{:S(2)}, u32[]{:S(2)}) %collective-permute-start.17) | collective-permute-done | bytes 409632 | tf_op jit(solution)/shard_map/ppermute | solution.py:107
  89.9 1.9 %collective-permute-done.18.refs_2_ = bf16[320,640]{1,0:T(8,128)(2,1)S(1)} collective-permute-done((bf16[320,640]{1,0:T(8,128)(2,1)}, bf16[320,640]{1,0:T(8,128)(2,1)S(1)}, u32[]{:S(2)}, u32[]{:S(2)}) %collective-permute-start.18) | collective-permute-done | bytes 409632 | tf_op jit(solution)/shard_map/ppermute | solution.py:107
  92.4 8.4 %collective-permute-done.19.refs_3_ = bf16[320,640]{1,0:T(8,128)(2,1)S(1)} collective-permute-done((bf16[320,640]{1,0:T(8,128)(2,1)S(1)}, bf16[320,640]{1,0:T(8,128)(2,1)S(1)}, u32[]{:S(2)}, u32[]{:S(2)}) %collective-permute-start.19) | collective-permute-done | bytes 409632 | tf_op jit(solution)/shard_map/ppermute | solution.py:107
  100.8 2.1 %shard_map.87 = (f32[64,640]{1,0:T(8,128)S(1)}, bf16[64,640]{1,0:T(8,128)(2,1)S(1)}, bf16[64,640]{1,0:T(8,128)(2,1)S(1)}, bf16[64,640]{1,0:T(8,128)(2,1)S(1)}) custom-call(s32[1]{0:T(128)} %bitcast.7.me_ref, s32[1]{0:T(128)} %bitcast.8.at_ref, bf16[8,64,640]{2,1,0:T(8,128)(2,1)S(1)} %all-to-all-done.inputs, bf16[320,640]{1,0:T(8,128)(2,1)} %pad_maximum_fusion.1.refs_0_, ...), custom_call_target="tpu_custom_call" | custom-call | flops 419430400 | bytes 2703368 | tf_op jit(solution)/shard_map/pallas_call | solution.py:129
  103.6 1.3 %collective-permute-start.22 = (bf16[64,640]{1,0:T(8,128)(2,1)S(1)}, bf16[64,640]{1,0:T(8,128)(2,1)S(1)}, u32[]{:S(2)}, u32[]{:S(2)}) collective-permute-start(bf16[64,640]{1,0:T(8,128)(2,1)S(1)} %get-tuple-element.38), channel_id=1, source_target_pairs={{0,3},{1,2},{2,1},{3,0},{4,7},{5,6},{6,5},{7,4},{8,11},{9,10},{10,... | collective-permute-start | bytes 245768 | tf_op jit(solution)/shard_map/ppermute | solution.py:107
  104.9 3.4 %collective-permute-done.21.two_ref = bf16[64,640]{1,0:T(8,128)(2,1)S(1)} collective-permute-done((bf16[64,640]{1,0:T(8,128)(2,1)S(1)}, bf16[64,640]{1,0:T(8,128)(2,1)S(1)}, u32[]{:S(2)}, u32[]{:S(2)}) %collective-permute-start.21) | collective-permute-done | bytes 81952 | tf_op jit(solution)/shard_map/ppermute | solution.py:107
  109.3 13.5 %all_to_all.10 = bf16[8,16,640]{2,1,0:T(8,128)(2,1)S(1)} all-to-all(bf16[8,16,640]{2,1,0:T(8,128)(2,1)S(1)} %bitcast.24), channel_id=1, replica_groups=mesh['dp'=8,'fsdp'=4] {'dp'}, dimensions={0} | all-to-all | bytes 327680 | tf_op jit(solution)/shard_map/all_to_all | solution.py:364
  (58 shorter events, 12.3 us)
Async XLA Ops:
  0.0 11.6 %copy-start.3 = (bf16[160,1280]{1,0:T(8,128)(2,1)S(1)}, bf16[160,1280]{1,0:T(8,128)(2,1)}, u32[]{:S(2)}) copy-start(bf16[160,1280]{1,0:T(8,128)(2,1)} %param.11) | copy-start | bytes 1228804
  0.0 11.7 %copy-start.5 = (s32[32,1]{0,1:T(1,128)S(1)}, s32[32,1]{0,1:T(1,128)}, u32[]{:S(2)}) copy-start(s32[32,1]{0,1:T(1,128)} %param.15) | copy-start | bytes 388
  0.0 20.8 %collective-permute-start.2 = (bf16[3,160,320]{2,1,0:T(8,128)(2,1)}, bf16[3,160,320]{2,1,0:T(8,128)(2,1)S(1)}, u32[]{:S(2)}, u32[]{:S(2)}) collective-permute-start(bf16[3,160,320]{2,1,0:T(8,128)(2,1)} %param.9), channel_id=1, source_target_pairs={{0,16},{4,20},{8,24},{12,28},{16,0},{20,4},{24,8},{28,12},{1,17},{... | collective-permute-start | bytes 921608 | tf_op jit(solution)/shard_map/ppermute | solution.py:107
  4.0 23.7 %copy-start.4 = (bf16[320,160]{0,1:T(8,128)(2,1)S(1)}, bf16[320,160]{0,1:T(8,128)(2,1)}, u32[]{:S(2)}) copy-start(bf16[320,160]{0,1:T(8,128)(2,1)} %param.10) | copy-start | bytes 307204
  5.2 17.2 %collective-permute-start.4 = (bf16[4,160,320]{2,1,0:T(8,128)(2,1)S(1)}, bf16[4,160,320]{2,1,0:T(8,128)(2,1)S(1)}, u32[]{:S(2)}, u32[]{:S(2)}) collective-permute-start(bf16[4,160,320]{2,1,0:T(8,128)(2,1)S(1)} %pad_maximum_fusion.refs_4_.refs_12_.refs_0_), channel_id=1, source_target_pairs={{0,4},{4,0},{8,12},{12,8},{16,20},{20,16},{24,28},{28,24},{1,5},{5... | collective-permute-start | bytes 1228808 | tf_op jit(solution)/shard_map/ppermute | solution.py:107
  6.8 20.9 %collective-permute-start.6 = (bf16[4,160,320]{2,1,0:T(8,128)(2,1)S(1)}, bf16[4,160,320]{2,1,0:T(8,128)(2,1)S(1)}, u32[]{:S(2)}, u32[]{:S(2)}) collective-permute-start(bf16[4,160,320]{2,1,0:T(8,128)(2,1)S(1)} %pad_maximum_fusion.refs_4_.refs_12_.refs_0_), channel_id=1, source_target_pairs={{0,8},{4,12},{8,0},{12,4},{16,24},{20,28},{24,16},{28,20},{1,9},{5... | collective-permute-start | bytes 1228808 | tf_op jit(solution)/shard_map/ppermute | solution.py:107
  10.0 45.5 %copy-start.2 = (f32[2,1280]{1,0:T(2,128)S(1)}, f32[2,1280]{1,0:T(2,128)}, u32[]{:S(2)}) copy-start(f32[2,1280]{1,0:T(2,128)} %gains_ref.3) | copy-start | bytes 30724
  10.0 27.6 %collective-permute-start.1 = (bf16[144,1280]{1,0:T(8,128)(2,1)S(1)}, bf16[144,1280]{1,0:T(8,128)(2,1)S(1)}, u32[]{:S(2)}, u32[]{:S(2)}) collective-permute-start(bf16[144,1280]{1,0:T(8,128)(2,1)S(1)} %fusion.2.refs_0_.tokens_ref), channel_id=1, source_target_pairs={{0,2},{1,3},{2,0},{3,1},{4,6},{5,7},{6,4},{7,5},{8,10},{9,11},{10,... | collective-permute-start | bytes 1105928 | tf_op jit(solution)/shard_map/ppermute | solution.py:107
  20.8 14.5 %collective-permute-start.3 = (bf16[3,160,320]{2,1,0:T(8,128)(2,1)S(1)}, bf16[3,160,320]{2,1,0:T(8,128)(2,1)S(1)}, u32[]{:S(2)}, u32[]{:S(2)}) collective-permute-start(bf16[3,160,320]{2,1,0:T(8,128)(2,1)S(1)} %collective-permute-done.2.refs_6_), channel_id=1, source_target_pairs={{0,4},{4,0},{8,12},{12,8},{16,20},{20,16},{24,28},{28,24},{1,5},{5... | collective-permute-start | bytes 921608 | tf_op jit(solution)/shard_map/ppermute | solution.py:107
  22.4 14.0 %collective-permute-start.5 = (bf16[3,160,320]{2,1,0:T(8,128)(2,1)S(1)}, bf16[3,160,320]{2,1,0:T(8,128)(2,1)S(1)}, u32[]{:S(2)}, u32[]{:S(2)}) collective-permute-start(bf16[3,160,320]{2,1,0:T(8,128)(2,1)S(1)} %collective-permute-done.2.refs_6_), channel_id=1, source_target_pairs={{0,8},{4,12},{8,0},{12,4},{16,24},{20,28},{24,16},{28,20},{1,9},{5... | collective-permute-start | bytes 921608 | tf_op jit(solution)/shard_map/ppermute | solution.py:107
  23.2 12.2 %collective-permute-start = (bf16[176,640]{1,0:T(8,128)(2,1)S(1)}, bf16[176,640]{1,0:T(8,128)(2,1)S(1)}, u32[]{:S(2)}, u32[]{:S(2)}) collective-permute-start(bf16[176,640]{1,0:T(8,128)(2,1)S(1)} %fusion.3), channel_id=1, source_target_pairs={{0,4},{4,0},{8,12},{12,8},{16,20},{20,16},{24,28},{28,24},{1,5},{5... | collective-permute-start | bytes 675848 | tf_op jit(solution)/shard_map/ppermute | solution.py:107
  27.7 7.7 %collective-permute-start.7 = (bf16[1,160,320]{2,1,0:T(8,128)(2,1)S(1)}, bf16[1,160,320]{2,1,0:T(8,128)(2,1)S(1)}, u32[]{:S(2)}, u32[]{:S(2)}) collective-permute-start(bf16[1,160,320]{2,1,0:T(8,128)(2,1)S(1)} %bitcast.27), channel_id=1, source_target_pairs={{0,16},{4,20},{8,24},{12,28},{16,0},{20,4},{24,8},{28,12},{1,17},{... | collective-permute-start | bytes 307208 | tf_op jit(solution)/shard_map/ppermute | solution.py:107
  36.5 16.8 %collective-permute-start.8 = (bf16[144,1280]{1,0:T(8,128)(2,1)S(1)}, bf16[144,1280]{1,0:T(8,128)(2,1)S(1)}, u32[]{:S(2)}, u32[]{:S(2)}) collective-permute-start(bf16[144,1280]{1,0:T(8,128)(2,1)S(1)} %fusion.2.refs_0_.tokens_ref), channel_id=1, source_target_pairs={{0,1},{1,0},{2,3},{3,2},{4,5},{5,4},{6,7},{7,6},{8,9},{9,8},{10,11... | collective-permute-start | bytes 1105928 | tf_op jit(solution)/shard_map/ppermute | solution.py:107
  36.5 23.9 %collective-permute-start.10 = (bf16[4,160,320]{2,1,0:T(8,128)(2,1)S(1)}, bf16[4,160,320]{2,1,0:T(8,128)(2,1)S(1)}, u32[]{:S(2)}, u32[]{:S(2)}) collective-permute-start(bf16[4,160,320]{2,1,0:T(8,128)(2,1)S(1)} %collective-permute-done.4.refs_8_.refs_16_.refs_4_), channel_id=1, source_target_pairs={{0,8},{4,12},{8,0},{12,4},{16,24},{20,28},{24,16},{28,20},{1,9},{5... | collective-permute-start | bytes 1228808 | tf_op jit(solution)/shard_map/ppermute | solution.py:107
  37.6 18.0 %collective-permute-start.9 = (bf16[144,1280]{1,0:T(8,128)(2,1)S(1)}, bf16[144,1280]{1,0:T(8,128)(2,1)S(1)}, u32[]{:S(2)}, u32[]{:S(2)}) collective-permute-start(bf16[144,1280]{1,0:T(8,128)(2,1)S(1)} %collective-permute-done.1.refs_1_), channel_id=1, source_target_pairs={{0,1},{1,0},{2,3},{3,2},{4,5},{5,4},{6,7},{7,6},{8,9},{9,8},{10,11... | collective-permute-start | bytes 1105928 | tf_op jit(solution)/shard_map/ppermute | solution.py:107
  37.8 22.6 %collective-permute-start.11 = (bf16[3,160,320]{2,1,0:T(8,128)(2,1)S(1)}, bf16[3,160,320]{2,1,0:T(8,128)(2,1)S(1)}, u32[]{:S(2)}, u32[]{:S(2)}) collective-permute-start(bf16[3,160,320]{2,1,0:T(8,128)(2,1)S(1)} %collective-permute-done.5.refs_7_), channel_id=1, source_target_pairs={{0,4},{4,0},{8,12},{12,8},{16,20},{20,16},{24,28},{28,24},{1,5},{5... | collective-permute-start | bytes 921608 | tf_op jit(solution)/shard_map/ppermute | solution.py:107
  38.8 13.9 %collective-permute-start.12 = (bf16[1,160,320]{2,1,0:T(8,128)(2,1)S(1)}, bf16[1,160,320]{2,1,0:T(8,128)(2,1)S(1)}, u32[]{:S(2)}, u32[]{:S(2)}) collective-permute-start(bf16[1,160,320]{2,1,0:T(8,128)(2,1)S(1)} %collective-permute-done.7.refs_14_.refs_2_), channel_id=1, source_target_pairs={{0,8},{4,12},{8,0},{12,4},{16,24},{20,28},{24,16},{28,20},{1,9},{5... | collective-permute-start | bytes 307208 | tf_op jit(solution)/shard_map/ppermute | solution.py:107
  52.7 6.2 %collective-permute-start.13 = (bf16[1,160,320]{2,1,0:T(8,128)(2,1)S(1)}, bf16[1,160,320]{2,1,0:T(8,128)(2,1)S(1)}, u32[]{:S(2)}, u32[]{:S(2)}) collective-permute-start(bf16[1,160,320]{2,1,0:T(8,128)(2,1)S(1)} %collective-permute-done.7.refs_14_.refs_2_), channel_id=1, source_target_pairs={{0,4},{4,0},{8,12},{12,8},{16,20},{20,16},{24,28},{28,24},{1,5},{5... | collective-permute-start | bytes 307208 | tf_op jit(solution)/shard_map/ppermute | solution.py:107
  53.3 7.0 %collective-permute-start.14 = (bf16[1,160,320]{2,1,0:T(8,128)(2,1)S(1)}, bf16[1,160,320]{2,1,0:T(8,128)(2,1)S(1)}, u32[]{:S(2)}, u32[]{:S(2)}) collective-permute-start(bf16[1,160,320]{2,1,0:T(8,128)(2,1)S(1)} %collective-permute-done.12.refs_15_.refs_3_), channel_id=1, source_target_pairs={{0,4},{4,0},{8,12},{12,8},{16,20},{20,16},{24,28},{28,24},{1,5},{5... | collective-permute-start | bytes 307208 | tf_op jit(solution)/shard_map/ppermute | solution.py:107
  65.1 2.2 %collective-permute-start.15 = (bf16[256,1280]{1,0:T(8,128)(2,1)S(1)}, bf16[256,1280]{1,0:T(8,128)(2,1)S(1)}, u32[]{:S(2)}, u32[]{:S(2)}) collective-permute-start(bf16[256,1280]{1,0:T(8,128)(2,1)S(1)} %get-tuple-element.32), channel_id=1, source_target_pairs={{0,1},{1,0},{2,3},{3,2},{4,5},{5,4},{6,7},{7,6},{8,9},{9,8},{10,11... | collective-permute-start | bytes 1966088 | tf_op jit(solution)/shard_map/ppermute | solution.py:107
  65.8 8.2 %copy-start.6 = (s32[1,128]{1,0:T(1,128)S(1)}, s32[1,128]{1,0:T(1,128)}, u32[]{:S(2)}) copy-start(s32[1,128]{1,0:T(1,128)} %param.14) | copy-start | bytes 1540
  67.4 0.9 copy-start
  68.2 9.8 %collective-permute-start.16 = (bf16[128,1280]{1,0:T(8,128)(2,1)S(1)}, bf16[128,1280]{1,0:T(8,128)(2,1)S(1)}, u32[]{:S(2)}, u32[]{:S(2)}) collective-permute-start(bf16[128,1280]{1,0:T(8,128)(2,1)S(1)} %shard_map.85), channel_id=1, source_target_pairs={{0,2},{1,3},{2,0},{3,1},{4,6},{5,7},{6,4},{7,5},{8,10},{9,11},{10,... | collective-permute-start | bytes 983048 | tf_op jit(solution)/shard_map/ppermute | solution.py:107
  69.8 20.1 %collective-permute-start.17 = (bf16[320,640]{1,0:T(8,128)(2,1)}, bf16[320,640]{1,0:T(8,128)(2,1)S(1)}, u32[]{:S(2)}, u32[]{:S(2)}) collective-permute-start(bf16[320,640]{1,0:T(8,128)(2,1)} %pad_maximum_fusion.1.refs_0_), channel_id=1, source_target_pairs={{0,8},{4,12},{8,0},{12,4},{16,24},{20,28},{24,16},{28,20},{1,9},{5... | collective-permute-start | bytes 1228808 | tf_op jit(solution)/shard_map/ppermute | solution.py:107
  70.7 21.1 %collective-permute-start.18 = (bf16[320,640]{1,0:T(8,128)(2,1)}, bf16[320,640]{1,0:T(8,128)(2,1)S(1)}, u32[]{:S(2)}, u32[]{:S(2)}) collective-permute-start(bf16[320,640]{1,0:T(8,128)(2,1)} %pad_maximum_fusion.1.refs_0_), channel_id=1, source_target_pairs={{0,16},{4,20},{8,24},{12,28},{16,0},{20,4},{24,8},{28,12},{1,17},{... | collective-permute-start | bytes 1228808 | tf_op jit(solution)/shard_map/ppermute | solution.py:107
  78.0 1.1 copy-start.1
  80.7 20.1 %all-to-all-start = ((bf16[8,64,640]{2,1,0:T(8,128)(2,1)}), bf16[8,64,640]{2,1,0:T(8,128)(2,1)S(1)}, u32[]{:S(2)}, u32[]{:S(2)}) async-start(bf16[8,64,640]{2,1,0:T(8,128)(2,1)} %shard_map.86), calls=%async_computation | async-start | bytes 1310720 | tf_op jit(solution)/shard_map/all_to_all | solution.py:339
  91.8 9.0 %collective-permute-start.19 = (bf16[320,640]{1,0:T(8,128)(2,1)S(1)}, bf16[320,640]{1,0:T(8,128)(2,1)S(1)}, u32[]{:S(2)}, u32[]{:S(2)}) collective-permute-start(bf16[320,640]{1,0:T(8,128)(2,1)S(1)} %collective-permute-done.18.refs_2_), channel_id=1, source_target_pairs={{0,8},{4,12},{8,0},{12,4},{16,24},{20,28},{24,16},{28,20},{1,9},{5... | collective-permute-start | bytes 1228808 | tf_op jit(solution)/shard_map/ppermute | solution.py:107
  102.9 2.0 %collective-permute-start.20 = (bf16[64,640]{1,0:T(8,128)(2,1)S(1)}, bf16[64,640]{1,0:T(8,128)(2,1)S(1)}, u32[]{:S(2)}, u32[]{:S(2)}) collective-permute-start(bf16[64,640]{1,0:T(8,128)(2,1)S(1)} %get-tuple-element.36), channel_id=1, source_target_pairs={{0,1},{1,0},{2,3},{3,2},{4,5},{5,4},{6,7},{7,6},{8,9},{9,8},{10,11... | collective-permute-start | bytes 245768 | tf_op jit(solution)/shard_map/ppermute | solution.py:107
  102.9 5.3 %collective-permute-start.21 = (bf16[64,640]{1,0:T(8,128)(2,1)S(1)}, bf16[64,640]{1,0:T(8,128)(2,1)S(1)}, u32[]{:S(2)}, u32[]{:S(2)}) collective-permute-start(bf16[64,640]{1,0:T(8,128)(2,1)S(1)} %get-tuple-element.37), channel_id=1, source_target_pairs={{0,2},{1,3},{2,0},{3,1},{4,6},{5,7},{6,4},{7,5},{8,10},{9,11},{10,... | collective-permute-start | bytes 245768 | tf_op jit(solution)/shard_map/ppermute | solution.py:107
  103.6 5.6 %collective-permute-start.22 = (bf16[64,640]{1,0:T(8,128)(2,1)S(1)}, bf16[64,640]{1,0:T(8,128)(2,1)S(1)}, u32[]{:S(2)}, u32[]{:S(2)}) collective-permute-start(bf16[64,640]{1,0:T(8,128)(2,1)S(1)} %get-tuple-element.38), channel_id=1, source_target_pairs={{0,3},{1,2},{2,1},{3,0},{4,7},{5,6},{6,5},{7,4},{8,11},{9,10},{10,... | collective-permute-start | bytes 245768 | tf_op jit(solution)/shard_map/ppermute | solution.py:107

commit v12 on v9

--- a/solution.py
+++ b/solution.py
@@ -122,8 +122,8 @@
     return lax.dot_general(a, b, (((1,), (1,)), ((), ())), preferred_element_type=jnp.float32)
 
 
-def call(kernel, outs, operands, scratch=(), flops=0, smem=0, exps=0):
-    moved = sum(math.prod(x.shape) * x.dtype.itemsize for x in (*operands, *outs))
+def call(kernel, outs, operands, scratch=(), flops=0, smem=0, exps=0, moved=None):
+    moved = moved or sum(math.prod(x.shape) * x.dtype.itemsize for x in (*operands, *outs))
     specs = [pl.BlockSpec(memory_space=pltpu.SMEM)] * smem
     specs += [pl.BlockSpec(memory_space=pltpu.VMEM)] * (len(operands) - smem)
     return pl.pallas_call(
@@ -176,7 +176,7 @@
 
 def value_kernel(me_ref, rows_ref, weights_ref, totals_ref, *refs):
     blocks = refs[0:8]
-    keep_ref, send_ref, v_whole, out_whole = refs[8:]
+    keep_ref, send_near, send_far, v_whole, out_whole = refs[8:]
     lay_out(me_ref[0], blocks, 2, v_whole)
     lay_out(me_ref[0], blocks, 3, out_whole)
     values = dot(rows_ref[...], v_whole[...]).astype(jnp.bfloat16)
@@ -186,23 +186,28 @@
         pieces.append(found / totals_ref[head])
     attended = jnp.concatenate(pieces, axis=1).astype(jnp.bfloat16)
     half = attended.shape[0] // 2
-    send_ref[...] = dot_turned(attended[half:, :], out_whole[...]).astype(jnp.bfloat16)
+    sent = dot_turned(attended[half:, :], out_whole[...]).astype(jnp.bfloat16)
+    send_near[...], send_far[...] = sent[: half // 2, :], sent[half // 2 :, :]
     keep_ref[...] = dot_turned(attended[:half, :], out_whole[...])
 
 
-def pass_kernel(keep_ref, got_ref, out_ref):
-    rows = out_ref.shape[0]
-    out_ref[...] = (keep_ref[rows:, :] + got_ref[rows:, :].astype(jnp.float32)).astype(jnp.bfloat16)
-
-
-def layer_kernel(tokens_ref, keep_ref, core_ref, chip_ref, gains_ref, order_ref, *refs):
-    (slices,) = refs
-    rows, width = tokens_ref.shape
+def pass_kernel(keep_ref, got_ref, *outs):
+    rows, parts = got_ref.shape[0], len(outs)
+    step = rows // parts
+    for n, out_ref in enumerate(outs):
+        kept = keep_ref[rows + n * step : rows + (n + 1) * step, :]
+        got = got_ref[n * step : (n + 1) * step, :].astype(jnp.float32)
+        out_ref[...] = (kept + got).astype(jnp.bfloat16)
+
+
+def layer_kernel(tokens_ref, keep_ref, core_ref, gains_ref, order_ref, *refs):
+    chips, slices = refs[:-1], refs[-1]
+    rows, width = tokens_ref.shape[0] - 16, tokens_ref.shape[1]
     summed = (
-        tokens_ref[...].astype(jnp.float32)
+        tokens_ref[0:rows, :].astype(jnp.float32)
         + keep_ref[0:rows, :]
         + core_ref[0:rows, :].astype(jnp.float32)
-        + chip_ref[...].astype(jnp.float32)
+        + jnp.concatenate([ref[...] for ref in chips], axis=0).astype(jnp.float32)
     )
     merge_in = normalize(summed.astype(jnp.bfloat16), gains_ref[1:2, :])
     places = lax.broadcasted_iota(jnp.int32, (rows, rows), 1)
@@ -274,7 +279,15 @@
     near, beside = swap(heads, "dp", 2), swap(heads, "dp", 1)
     first, second = heads[0:2], heads[2:4]
     first_far = swap(first, "dp", 4)
-    first_far_y = swap(after(first_far, (near, beside)), "dp", 1)
+    half = merge_weight.shape[1] // 2
+    low, high = merge_weight[:, :half], merge_weight[:, half:]
+    lower = y == 0
+    mine = owners[:, 0]
+    note = jnp.pad(owners.astype(bf16).T, ((0, 15), (0, half - count)))
+    given = jnp.concatenate([jnp.where(lower, high, low), note], axis=0)
+    theirs = swap(after(given, first), "dp", 1)
+    other = theirs[-16, :count].astype(jnp.int32)
+    first_far_y = swap(after(first_far, (near, beside, theirs)), "dp", 1)
     first_last = swap(first_far, "dp", 2)
     corner = swap(beside, "dp", 2)
     second_far = swap(after(second, first_far), "dp", 4)
@@ -296,14 +309,6 @@
         )
     ]
 
-    half = merge_weight.shape[1] // 2
-    low, high = merge_weight[:, :half], merge_weight[:, half:]
-    lower = y == 0
-    mine = owners[:, 0]
-    note = jnp.pad(owners.astype(bf16).T, ((0, 15), (0, half - count)))
-    given = jnp.concatenate([jnp.where(lower, high, low), note], axis=0)
-    theirs = swap(after(given, second_far_y), "dp", 1)
-    other = theirs[-16, :count].astype(jnp.int32)
     pair = jnp.concatenate([jnp.where(lower, low, high), theirs[:-16]], axis=0)
     held = after(pair, (second_last, second_far_y, blocks[0][7]))
     merge_near, merge_far = swap(held, "dp", 2), swap(held, "dp", 4)
@@ -326,22 +331,25 @@
         smem=1,
         exps=found * group * group,
     )
-    keep, send = call(
+    keep, *send = call(
         value_kernel,
-        [shape((2 * rows, width), f32), shape((2 * rows, width), bf16)],
+        [shape((2 * rows, width), f32)] + [shape((rows, width), bf16)] * 2,
         [me_cell, normed, weights, totals, *blocks[1]],
         [pltpu.VMEM((width, cols), bf16)] * 2,
         flops=4 * group * width * cols + 2 * group * group * cols,
         smem=1,
     )
-    from_core = swap(send, "fsdp", 1)
-    (onward,) = call(pass_kernel, [shape((rows, width), bf16)], [keep, from_core])
-    from_chip = swap(onward, "fsdp", 2)
+    from_core = [swap(part, "fsdp", 1) for part in send]
+    parts = 2
+    onward = call(
+        pass_kernel, [shape((rows // parts, width), bf16)] * parts, [keep, from_core[1]], moved=1
+    )
+    from_chip = [swap(part, "fsdp", 2) for part in onward]
     (slices,) = call(
         layer_kernel,
         [shape((8, rows // 2, width // 2), bf16)],
-        [tokens, keep, from_core, from_chip, ln_gains, order],
-        flops=2 * rows * rows * width,
+        [marked, keep, from_core[0], ln_gains, order, *from_chip],
+        moved=1,
     )
     merge_blocks = [pair, merge_near, merge_far, swap(after(merge_far, (slices, merge_near)), "dp", 2)]
     both = 2 * n_fsdp

time: 118 us -> 120 us (1.017)
  starting transfers between devices: 31.1 us -> 33.6 us
  other arithmetic: 7.19 us -> 5.58 us
  local copies, waits for them, and re-layouts: 3.01 us -> 1.62 us
  blocking collectives: 11.2 us -> 12.4 us
    ppermute x23 -> x25, starting transfers between devices: 27.4 us -> 30 us  [swap(): lax.ppermute(value, axis, [(i, i ^ k) for i in range(lax.axis_size(axis))])]
    concatenate x1 -> x2, other arithmetic: 1.2 us -> 2.96 us  [by_permutes(): heads = jnp.concatenate([qkv_weight, out_weight.T[None]], axis=0)]
    slice x1 -> x0, other arithmetic: 1.64 us -> none  [by_permutes(): first, second = (heads[0:2], heads[2:4])]
    all_to_all x1, blocking collectives: 11.2 us -> 12.4 us  [by_permutes(): lax.all_to_all(packed.reshape(n_dp, 2 * capacity, half), 'dp', split_axis...]
    ppermute x23 -> x25, waiting for transfers between devices: 53.6 us -> 54.5 us  [swap(): lax.ppermute(value, axis, [(i, i ^ k) for i in range(lax.axis_size(axis))])]
  transfers between devices with their start and end apart: 24 -> 26, of which waited for: 15 -> 14; matrix products, arithmetic and copies ran while one was open for 6% -> 4% of each run, Pallas kernels for 6% -> 6%
where the time goes in v12:
time: 120 us; the launch traced here: 119 us
  waiting for transfers between devices  54.5 us (45%)
  starting transfers between devices  33.6 us (28%)
  blocking collectives  12.4 us (10%)
  Pallas kernels  11.4 us (10%)
  other arithmetic  5.58 us (5%)
  local copies, waits for them, and re-layouts  1.62 us (1%)
    ppermute x25, waiting for transfers between devices, swap(): lax.ppermute(value, axis, [(i, i ^ k) for i in range(lax.axis_size(axis))])  54.5 us
    ppermute x25, starting transfers between devices, swap(): lax.ppermute(value, axis, [(i, i ^ k) for i in range(lax.axis_size(axis))])  30 us
    all_to_all x1, blocking collectives, by_permutes(): lax.all_to_all(packed.reshape(n_dp, 2 * capacity, half), 'dp', split_axis...  12.4 us
    pallas_call x7, Pallas kernels, call(): pl.pallas_call(kernel, out_shape=tuple(outs), in_specs=specs, out_specs=t...  11.4 us
    all_to_all x1, starting transfers between devices, by_permutes(): lax.all_to_all(slices, ('dp', 'fsdp'), split_axis=0, concat_axis=0, tiled...  3.54 us
    concatenate x2, other arithmetic, by_permutes(): heads = jnp.concatenate([qkv_weight, out_weight.T[None]], axis=0)  2.96 us
  transfers between devices with their start and end apart: 26, of which 14 were waited for; matrix products, arithmetic and copies ran while one was open for 4% of the time, Pallas kernels for 6%

profile of v12, /device:TPU:0, one launch (start us, length us, event | category | flops | bytes accessed | tf_op | source)
XLA Modules:
  0.0 119.4 jit_solution(8687951317318505985)
XLA Ops:
  0.0 1.2 %pad_maximum_fusion.refs_4_.refs_0_ = bf16[4,160,320]{2,1,0:T(8,128)(2,1)S(1)} fusion(bf16[1,160,320]{2,1,0:T(8,128)(2,1)} %bitcast.26, bf16[3,160,320]{2,1,0:T(8,128)(2,1)} %param.9), kind=kLoop, calls=%fused_computation.3 | loop fusion | flops 204800 | bytes 819200 | tf_op jit(solution)/shard_map/concatenate | solution.py:278
  1.3 3.0 %collective-permute-start.4 = (bf16[4,160,320]{2,1,0:T(8,128)(2,1)S(1)}, bf16[4,160,320]{2,1,0:T(8,128)(2,1)S(1)}, u32[]{:S(2)}, u32[]{:S(2)}) collective-permute-start(bf16[4,160,320]{2,1,0:T(8,128)(2,1)S(1)} %pad_maximum_fusion.refs_4_.refs_0_), channel_id=1, source_target_pairs={{0,4},{4,0},{8,12},{12,8},{16,20},{20,16},{24,28},{28,24},{1,5},{5... | collective-permute-start | bytes 1228808 | tf_op jit(solution)/shard_map/ppermute | solution.py:107
  4.3 1.6 %collective-permute-start.3 = (bf16[4,160,320]{2,1,0:T(8,128)(2,1)S(1)}, bf16[4,160,320]{2,1,0:T(8,128)(2,1)S(1)}, u32[]{:S(2)}, u32[]{:S(2)}) collective-permute-start(bf16[4,160,320]{2,1,0:T(8,128)(2,1)S(1)} %pad_maximum_fusion.refs_4_.refs_0_), channel_id=1, source_target_pairs={{0,8},{4,12},{8,0},{12,4},{16,24},{20,28},{24,16},{28,20},{1,9},{5... | collective-permute-start | bytes 1228808 | tf_op jit(solution)/shard_map/ppermute | solution.py:107
  5.9 1.8 %fusion.3 = (bf16[2,160,320]{2,1,0:T(8,128)(2,1)}, bf16[2,160,320]{2,1,0:T(8,128)(2,1)}) fusion(bf16[3,160,320]{2,1,0:T(8,128)(2,1)S(1)} %copy-done.1, bf16[1,160,320]{2,1,0:T(8,128)(2,1)} %bitcast.27), kind=kLoop, calls=%fused_computation.9 | loop fusion | flops 102400 | bytes 1126400 | tf_op jit(solution)/shard_map/concatenate | solution.py:278
  7.6 2.6 %collective-permute-start.2 = (bf16[2,160,320]{2,1,0:T(8,128)(2,1)}, bf16[2,160,320]{2,1,0:T(8,128)(2,1)S(1)}, u32[]{:S(2)}, u32[]{:S(2)}) collective-permute-start(bf16[2,160,320]{2,1,0:T(8,128)(2,1)} %get-tuple-element.52), channel_id=1, source_target_pairs={{0,16},{4,20},{8,24},{12,28},{16,0},{20,4},{24,8},{28,12},{1,17},{... | collective-permute-start | bytes 614408 | tf_op jit(solution)/shard_map/ppermute | solution.py:107
  10.9 1.6 %collective-permute-start.1 = (bf16[144,1280]{1,0:T(8,128)(2,1)S(1)}, bf16[144,1280]{1,0:T(8,128)(2,1)S(1)}, u32[]{:S(2)}, u32[]{:S(2)}) collective-permute-start(bf16[144,1280]{1,0:T(8,128)(2,1)S(1)} %fusion.2.refs_0_.tokens_ref), channel_id=1, source_target_pairs={{0,2},{1,3},{2,0},{3,1},{4,6},{5,7},{6,4},{7,5},{8,10},{9,11},{10,... | collective-permute-start | bytes 1105928 | tf_op jit(solution)/shard_map/ppermute | solution.py:107
  12.5 3.8 %collective-permute-done.4.refs_8_.refs_4_ = bf16[4,160,320]{2,1,0:T(8,128)(2,1)S(1)} collective-permute-done((bf16[4,160,320]{2,1,0:T(8,128)(2,1)S(1)}, bf16[4,160,320]{2,1,0:T(8,128)(2,1)S(1)}, u32[]{:S(2)}, u32[]{:S(2)}) %collective-permute-start.4) | collective-permute-done | bytes 409632 | tf_op jit(solution)/shard_map/ppermute | solution.py:107
  16.3 2.1 %collective-permute-start.10 = (bf16[4,160,320]{2,1,0:T(8,128)(2,1)S(1)}, bf16[4,160,320]{2,1,0:T(8,128)(2,1)S(1)}, u32[]{:S(2)}, u32[]{:S(2)}) collective-permute-start(bf16[4,160,320]{2,1,0:T(8,128)(2,1)S(1)} %collective-permute-done.4.refs_8_.refs_4_), channel_id=1, source_target_pairs={{0,8},{4,12},{8,0},{12,4},{16,24},{20,28},{24,16},{28,20},{1,9},{5... | collective-permute-start | bytes 1228808 | tf_op jit(solution)/shard_map/ppermute | solution.py:107
  18.5 4.4 %collective-permute-done.2.refs_6_ = bf16[2,160,320]{2,1,0:T(8,128)(2,1)S(1)} collective-permute-done((bf16[2,160,320]{2,1,0:T(8,128)(2,1)}, bf16[2,160,320]{2,1,0:T(8,128)(2,1)S(1)}, u32[]{:S(2)}, u32[]{:S(2)}) %collective-permute-start.2) | collective-permute-done | bytes 204832 | tf_op jit(solution)/shard_map/ppermute | solution.py:107
  22.9 3.3 %collective-permute-start.7 = (bf16[2,160,320]{2,1,0:T(8,128)(2,1)S(1)}, bf16[2,160,320]{2,1,0:T(8,128)(2,1)S(1)}, u32[]{:S(2)}, u32[]{:S(2)}) collective-permute-start(bf16[2,160,320]{2,1,0:T(8,128)(2,1)S(1)} %copy-done.4), channel_id=1, source_target_pairs={{0,16},{4,20},{8,24},{12,28},{16,0},{20,4},{24,8},{28,12},{1,17},{... | collective-permute-start | bytes 614408 | tf_op jit(solution)/shard_map/ppermute | solution.py:107
  26.9 11.7 %collective-permute-done.7.refs_2_ = bf16[2,160,320]{2,1,0:T(8,128)(2,1)S(1)} collective-permute-done((bf16[2,160,320]{2,1,0:T(8,128)(2,1)S(1)}, bf16[2,160,320]{2,1,0:T(8,128)(2,1)S(1)}, u32[]{:S(2)}, u32[]{:S(2)}) %collective-permute-start.7) | collective-permute-done | bytes 204832 | tf_op jit(solution)/shard_map/ppermute | solution.py:107
  38.6 4.7 %collective-permute-done.6.refs_7_ = bf16[2,160,320]{2,1,0:T(8,128)(2,1)S(1)} collective-permute-done((bf16[2,160,320]{2,1,0:T(8,128)(2,1)S(1)}, bf16[2,160,320]{2,1,0:T(8,128)(2,1)S(1)}, u32[]{:S(2)}, u32[]{:S(2)}) %collective-permute-start.6) | collective-permute-done | bytes 204832 | tf_op jit(solution)/shard_map/ppermute | solution.py:107
  43.8 1.6 %collective-permute-start.12 = (bf16[2,160,320]{2,1,0:T(8,128)(2,1)S(1)}, bf16[2,160,320]{2,1,0:T(8,128)(2,1)S(1)}, u32[]{:S(2)}, u32[]{:S(2)}) collective-permute-start(bf16[2,160,320]{2,1,0:T(8,128)(2,1)S(1)} %collective-permute-done.7.refs_2_), channel_id=1, source_target_pairs={{0,8},{4,12},{8,0},{12,4},{16,24},{20,28},{24,16},{28,20},{1,9},{5... | collective-permute-start | bytes 614408 | tf_op jit(solution)/shard_map/ppermute | solution.py:107
  45.9 1.5 %collective-permute-start.13 = (bf16[2,160,320]{2,1,0:T(8,128)(2,1)S(1)}, bf16[2,160,320]{2,1,0:T(8,128)(2,1)S(1)}, u32[]{:S(2)}, u32[]{:S(2)}) collective-permute-start(bf16[2,160,320]{2,1,0:T(8,128)(2,1)S(1)} %collective-permute-done.7.refs_2_), channel_id=1, source_target_pairs={{0,4},{4,0},{8,12},{12,8},{16,20},{20,16},{24,28},{28,24},{1,5},{5... | collective-permute-start | bytes 614408 | tf_op jit(solution)/shard_map/ppermute | solution.py:107
  47.4 4.3 %collective-permute-done.12.refs_3_ = bf16[2,160,320]{2,1,0:T(8,128)(2,1)S(1)} collective-permute-done((bf16[2,160,320]{2,1,0:T(8,128)(2,1)S(1)}, bf16[2,160,320]{2,1,0:T(8,128)(2,1)S(1)}, u32[]{:S(2)}, u32[]{:S(2)}) %collective-permute-start.12) | collective-permute-done | bytes 204832 | tf_op jit(solution)/shard_map/ppermute | solution.py:107
  52.9 1.3 %collective-permute-done.11.refs_11_ = bf16[2,160,320]{2,1,0:T(8,128)(2,1)S(1)} collective-permute-done((bf16[2,160,320]{2,1,0:T(8,128)(2,1)S(1)}, bf16[2,160,320]{2,1,0:T(8,128)(2,1)S(1)}, u32[]{:S(2)}, u32[]{:S(2)}) %collective-permute-start.11) | collective-permute-done | bytes 204832 | tf_op jit(solution)/shard_map/ppermute | solution.py:107
  54.3 3.0 %shard_map.83 = (bf16[4,512,512]{2,1,0:T(8,128)(2,1)S(1)}, f32[4,512,1]{2,1,0:T(8,128)S(1)}) custom-call(s32[1]{0:T(128)} %bitcast.5.me_ref, bf16[512,1280]{1,0:T(8,128)(2,1)S(1)} %shard_map.82.rows_ref, bf16[144,1280]{1,0:T(8,128)(2,1)S(1)} %fusion.2.refs_0_.tokens_ref, bf16[144,1280]{1,0:T(8,128)(2,1)S(1)} %collective-permute-done.1.refs_1_, ...), custom_call_target="tpu_custom_call" | custom-call | flops 1006632960 | bytes 7348228 | tf_op jit(solution)/shard_map/pallas_call | solution.py:129
  57.3 2.2 %collective-permute-done.13.refs_6_ = bf16[2,160,320]{2,1,0:T(8,128)(2,1)S(1)} collective-permute-done((bf16[2,160,320]{2,1,0:T(8,128)(2,1)S(1)}, bf16[2,160,320]{2,1,0:T(8,128)(2,1)S(1)}, u32[]{:S(2)}, u32[]{:S(2)}) %collective-permute-start.13) | collective-permute-done | bytes 204832 | tf_op jit(solution)/shard_map/ppermute | solution.py:107
  59.5 4.0 %collective-permute-done.14.refs_7_ = bf16[2,160,320]{2,1,0:T(8,128)(2,1)S(1)} collective-permute-done((bf16[2,160,320]{2,1,0:T(8,128)(2,1)S(1)}, bf16[2,160,320]{2,1,0:T(8,128)(2,1)S(1)}, u32[]{:S(2)}, u32[]{:S(2)}) %collective-permute-start.14) | collective-permute-done | bytes 204832 | tf_op jit(solution)/shard_map/ppermute | solution.py:107
  63.5 3.0 %shard_map.84 = (f32[256,1280]{1,0:T(8,128)S(1)}, bf16[128,1280]{1,0:T(8,128)(2,1)}, bf16[128,1280]{1,0:T(8,128)(2,1)S(1)}) custom-call(s32[1]{0:T(128)} %bitcast.5.me_ref, bf16[512,1280]{1,0:T(8,128)(2,1)S(1)} %shard_map.82.rows_ref, bf16[4,512,512]{2,1,0:T(8,128)(2,1)S(1)} %get-tuple-element.35.weights_ref, f32[4,512,1]{2,1,0:T(8,128)S(1)} %get-tuple-element.36.totals_ref, ...), custom_call_target="tpu_custom_call" | custom-call | flops 1006632960 | bytes 7839748 | tf_op jit(solution)/shard_map/pallas_call | solution.py:129
  67.6 2.6 %collective-permute-start.20 = (bf16[320,640]{1,0:T(8,128)(2,1)S(1)}, bf16[320,640]{1,0:T(8,128)(2,1)S(1)}, u32[]{:S(2)}, u32[]{:S(2)}) collective-permute-start(bf16[320,640]{1,0:T(8,128)(2,1)S(1)} %pad_maximum_fusion.1.refs_0_), channel_id=1, source_target_pairs={{0,16},{4,20},{8,24},{12,28},{16,0},{20,4},{24,8},{28,12},{1,17},{... | collective-permute-start | bytes 1228808 | tf_op jit(solution)/shard_map/ppermute | solution.py:107
  70.9 1.5 %collective-permute-start.17 = (bf16[64,1280]{1,0:T(8,128)(2,1)}, bf16[64,1280]{1,0:T(8,128)(2,1)S(1)}, u32[]{:S(2)}, u32[]{:S(2)}) collective-permute-start(bf16[64,1280]{1,0:T(8,128)(2,1)} %get-tuple-element.41), channel_id=1, source_target_pairs={{0,2},{1,3},{2,0},{3,1},{4,6},{5,7},{6,4},{7,5},{8,10},{9,11},{10,... | collective-permute-start | bytes 491528 | tf_op jit(solution)/shard_map/ppermute | solution.py:107
  74.8 3.5 %collective-permute-done.17.refs_0_ = bf16[64,1280]{1,0:T(8,128)(2,1)S(1)} collective-permute-done((bf16[64,1280]{1,0:T(8,128)(2,1)}, bf16[64,1280]{1,0:T(8,128)(2,1)S(1)}, u32[]{:S(2)}, u32[]{:S(2)}) %collective-permute-start.17) | collective-permute-done | bytes 163872 | tf_op jit(solution)/shard_map/ppermute | solution.py:107
  78.3 2.0 %collective-permute-done.18.refs_1_ = bf16[64,1280]{1,0:T(8,128)(2,1)} collective-permute-done((bf16[64,1280]{1,0:T(8,128)(2,1)}, bf16[64,1280]{1,0:T(8,128)(2,1)}, u32[]{:S(2)}, u32[]{:S(2)}) %collective-permute-start.18) | collective-permute-done | bytes 163872 | tf_op jit(solution)/shard_map/ppermute | solution.py:107
  80.3 2.6 %shard_map.86 = bf16[8,64,640]{2,1,0:T(8,128)(2,1)} custom-call(bf16[144,1280]{1,0:T(8,128)(2,1)S(1)} %fusion.2.refs_0_.tokens_ref, f32[256,1280]{1,0:T(8,128)S(1)} %get-tuple-element.38.keep_ref, bf16[128,1280]{1,0:T(8,128)(2,1)S(1)} %collective-permute-done.15.core_ref, f32[2,1280]{1,0:T(2,128)S(1)} %copy-done, s32[128,1]{1,0:T(8,128)S(1)} %reshape.41.order_ref, ...), custom_call_target="tpu_custom_call" | custom-call | bytes 1 | tf_op jit(solution)/shard_map/pallas_call | solution.py:129
  82.9 3.5 %all-to-all-start = ((bf16[8,64,640]{2,1,0:T(8,128)(2,1)}), bf16[8,64,640]{2,1,0:T(8,128)(2,1)S(1)}, u32[]{:S(2)}, u32[]{:S(2)}) async-start(bf16[8,64,640]{2,1,0:T(8,128)(2,1)} %shard_map.86), calls=%async_computation | async-start | bytes 1310720 | tf_op jit(solution)/shard_map/all_to_all | solution.py:356
  87.3 2.6 %collective-permute-start.21 = (bf16[320,640]{1,0:T(8,128)(2,1)S(1)}, bf16[320,640]{1,0:T(8,128)(2,1)S(1)}, u32[]{:S(2)}, u32[]{:S(2)}) collective-permute-start(bf16[320,640]{1,0:T(8,128)(2,1)S(1)} %collective-permute-done.20.refs_2_), channel_id=1, source_target_pairs={{0,8},{4,12},{8,0},{12,4},{16,24},{20,28},{24,16},{28,20},{1,9},{5... | collective-permute-start | bytes 1228808 | tf_op jit(solution)/shard_map/ppermute | solution.py:107
  91.4 7.3 %collective-permute-done.21.refs_3_ = bf16[320,640]{1,0:T(8,128)(2,1)S(1)} collective-permute-done((bf16[320,640]{1,0:T(8,128)(2,1)S(1)}, bf16[320,640]{1,0:T(8,128)(2,1)S(1)}, u32[]{:S(2)}, u32[]{:S(2)}) %collective-permute-start.21) | collective-permute-done | bytes 409632 | tf_op jit(solution)/shard_map/ppermute | solution.py:107
  99.8 1.6 %collective-permute-start.23 = (bf16[64,640]{1,0:T(8,128)(2,1)S(1)}, bf16[64,640]{1,0:T(8,128)(2,1)S(1)}, u32[]{:S(2)}, u32[]{:S(2)}) collective-permute-start(bf16[64,640]{1,0:T(8,128)(2,1)S(1)} %get-tuple-element.47), channel_id=1, source_target_pairs={{0,2},{1,3},{2,0},{3,1},{4,6},{5,7},{6,4},{7,5},{8,10},{9,11},{10,... | collective-permute-start | bytes 245768 | tf_op jit(solution)/shard_map/ppermute | solution.py:107
  101.7 3.2 %collective-permute-done.23.two_ref = bf16[64,640]{1,0:T(8,128)(2,1)S(1)} collective-permute-done((bf16[64,640]{1,0:T(8,128)(2,1)S(1)}, bf16[64,640]{1,0:T(8,128)(2,1)S(1)}, u32[]{:S(2)}, u32[]{:S(2)}) %collective-permute-start.23) | collective-permute-done | bytes 81952 | tf_op jit(solution)/shard_map/ppermute | solution.py:107
  105.0 1.1 collective-permute-done.24.three_ref
  106.3 12.4 %all_to_all.10 = bf16[8,16,640]{2,1,0:T(8,128)(2,1)S(1)} all-to-all(bf16[8,16,640]{2,1,0:T(8,128)(2,1)S(1)} %bitcast.24), channel_id=1, replica_groups=mesh['dp'=8,'fsdp'=4] {'dp'}, dimensions={0} | all-to-all | bytes 327680 | tf_op jit(solution)/shard_map/all_to_all | solution.py:381
  (67 shorter events, 12.6 us)
Async XLA Ops:
  0.0 10.2 %copy-start.6 = (s32[32,1]{0,1:T(1,128)S(1)}, s32[32,1]{0,1:T(1,128)}, u32[]{:S(2)}) copy-start(s32[32,1]{0,1:T(1,128)} %param.15) | copy-start | bytes 388
  0.0 10.2 %copy-start.2 = (bf16[160,1280]{1,0:T(8,128)(2,1)S(1)}, bf16[160,1280]{1,0:T(8,128)(2,1)}, u32[]{:S(2)}) copy-start(bf16[160,1280]{1,0:T(8,128)(2,1)} %param.11) | copy-start | bytes 1228804
  1.2 9.7 %copy-start.7 = (s32[1,128]{1,0:T(1,128)S(1)}, s32[1,128]{1,0:T(1,128)}, u32[]{:S(2)}) copy-start(s32[1,128]{1,0:T(1,128)} %param.13) | copy-start | bytes 1540
  1.2 50.8 %copy-start = (f32[2,1280]{1,0:T(2,128)S(1)}, f32[2,1280]{1,0:T(2,128)}, u32[]{:S(2)}) copy-start(f32[2,1280]{1,0:T(2,128)} %gains_ref.3) | copy-start | bytes 30724
  1.3 15.1 %collective-permute-start.4 = (bf16[4,160,320]{2,1,0:T(8,128)(2,1)S(1)}, bf16[4,160,320]{2,1,0:T(8,128)(2,1)S(1)}, u32[]{:S(2)}, u32[]{:S(2)}) collective-permute-start(bf16[4,160,320]{2,1,0:T(8,128)(2,1)S(1)} %pad_maximum_fusion.refs_4_.refs_0_), channel_id=1, source_target_pairs={{0,4},{4,0},{8,12},{12,8},{16,20},{20,16},{24,28},{28,24},{1,5},{5... | collective-permute-start | bytes 1228808 | tf_op jit(solution)/shard_map/ppermute | solution.py:107
  4.3 22.1 %collective-permute-start.3 = (bf16[4,160,320]{2,1,0:T(8,128)(2,1)S(1)}, bf16[4,160,320]{2,1,0:T(8,128)(2,1)S(1)}, u32[]{:S(2)}, u32[]{:S(2)}) collective-permute-start(bf16[4,160,320]{2,1,0:T(8,128)(2,1)S(1)} %pad_maximum_fusion.refs_4_.refs_0_), channel_id=1, source_target_pairs={{0,8},{4,12},{8,0},{12,4},{16,24},{20,28},{24,16},{28,20},{1,9},{5... | collective-permute-start | bytes 1228808 | tf_op jit(solution)/shard_map/ppermute | solution.py:107
  7.6 15.3 %collective-permute-start.2 = (bf16[2,160,320]{2,1,0:T(8,128)(2,1)}, bf16[2,160,320]{2,1,0:T(8,128)(2,1)S(1)}, u32[]{:S(2)}, u32[]{:S(2)}) collective-permute-start(bf16[2,160,320]{2,1,0:T(8,128)(2,1)} %get-tuple-element.52), channel_id=1, source_target_pairs={{0,16},{4,20},{8,24},{12,28},{16,0},{20,4},{24,8},{28,12},{1,17},{... | collective-permute-start | bytes 614408 | tf_op jit(solution)/shard_map/ppermute | solution.py:107
  10.2 12.7 %copy-start.4 = (bf16[2,160,320]{2,1,0:T(8,128)(2,1)S(1)}, bf16[2,160,320]{2,1,0:T(8,128)(2,1)}, u32[]{:S(2)}) copy-start(bf16[2,160,320]{2,1,0:T(8,128)(2,1)} %get-tuple-element.30) | copy-start | bytes 614404
  10.3 15.9 %collective-permute-start = (bf16[176,640]{1,0:T(8,128)(2,1)S(1)}, bf16[176,640]{1,0:T(8,128)(2,1)S(1)}, u32[]{:S(2)}, u32[]{:S(2)}) collective-permute-start(bf16[176,640]{1,0:T(8,128)(2,1)S(1)} %fusion.4), channel_id=1, source_target_pairs={{0,4},{4,0},{8,12},{12,8},{16,20},{20,16},{24,28},{28,24},{1,5},{5... | collective-permute-start | bytes 675848 | tf_op jit(solution)/shard_map/ppermute | solution.py:107
  10.9 16.0 %collective-permute-start.1 = (bf16[144,1280]{1,0:T(8,128)(2,1)S(1)}, bf16[144,1280]{1,0:T(8,128)(2,1)S(1)}, u32[]{:S(2)}, u32[]{:S(2)}) collective-permute-start(bf16[144,1280]{1,0:T(8,128)(2,1)S(1)} %fusion.2.refs_0_.tokens_ref), channel_id=1, source_target_pairs={{0,2},{1,3},{2,0},{3,1},{4,6},{5,7},{6,4},{7,5},{8,10},{9,11},{10,... | collective-permute-start | bytes 1105928 | tf_op jit(solution)/shard_map/ppermute | solution.py:107
  16.3 29.1 %collective-permute-start.10 = (bf16[4,160,320]{2,1,0:T(8,128)(2,1)S(1)}, bf16[4,160,320]{2,1,0:T(8,128)(2,1)S(1)}, u32[]{:S(2)}, u32[]{:S(2)}) collective-permute-start(bf16[4,160,320]{2,1,0:T(8,128)(2,1)S(1)} %collective-permute-done.4.refs_8_.refs_4_), channel_id=1, source_target_pairs={{0,8},{4,12},{8,0},{12,4},{16,24},{20,28},{24,16},{28,20},{1,9},{5... | collective-permute-start | bytes 1228808 | tf_op jit(solution)/shard_map/ppermute | solution.py:107
  22.9 15.7 %collective-permute-start.7 = (bf16[2,160,320]{2,1,0:T(8,128)(2,1)S(1)}, bf16[2,160,320]{2,1,0:T(8,128)(2,1)S(1)}, u32[]{:S(2)}, u32[]{:S(2)}) collective-permute-start(bf16[2,160,320]{2,1,0:T(8,128)(2,1)S(1)} %copy-done.4), channel_id=1, source_target_pairs={{0,16},{4,20},{8,24},{12,28},{16,0},{20,4},{24,8},{28,12},{1,17},{... | collective-permute-start | bytes 614408 | tf_op jit(solution)/shard_map/ppermute | solution.py:107
  26.2 40.8 %copy-start.5 = (bf16[176,640]{1,0:T(8,128)(2,1)}, bf16[176,640]{1,0:T(8,128)(2,1)S(1)}, u32[]{:S(2)}) copy-start(bf16[176,640]{1,0:T(8,128)(2,1)S(1)} %collective-permute-done) | copy-start | bytes 675844
  26.2 17.1 %collective-permute-start.6 = (bf16[2,160,320]{2,1,0:T(8,128)(2,1)S(1)}, bf16[2,160,320]{2,1,0:T(8,128)(2,1)S(1)}, u32[]{:S(2)}, u32[]{:S(2)}) collective-permute-start(bf16[2,160,320]{2,1,0:T(8,128)(2,1)S(1)} %collective-permute-done.2.refs_6_), channel_id=1, source_target_pairs={{0,8},{4,12},{8,0},{12,4},{16,24},{20,28},{24,16},{28,20},{1,9},{5... | collective-permute-start | bytes 614408 | tf_op jit(solution)/shard_map/ppermute | solution.py:107
  26.4 16.9 %collective-permute-start.5 = (bf16[2,160,320]{2,1,0:T(8,128)(2,1)S(1)}, bf16[2,160,320]{2,1,0:T(8,128)(2,1)S(1)}, u32[]{:S(2)}, u32[]{:S(2)}) collective-permute-start(bf16[2,160,320]{2,1,0:T(8,128)(2,1)S(1)} %collective-permute-done.2.refs_6_), channel_id=1, source_target_pairs={{0,4},{4,0},{8,12},{12,8},{16,20},{20,16},{24,28},{28,24},{1,5},{5... | collective-permute-start | bytes 614408 | tf_op jit(solution)/shard_map/ppermute | solution.py:107
  43.3 8.7 %collective-permute-start.9 = (bf16[144,1280]{1,0:T(8,128)(2,1)S(1)}, bf16[144,1280]{1,0:T(8,128)(2,1)S(1)}, u32[]{:S(2)}, u32[]{:S(2)}) collective-permute-start(bf16[144,1280]{1,0:T(8,128)(2,1)S(1)} %collective-permute-done.1.refs_1_), channel_id=1, source_target_pairs={{0,1},{1,0},{2,3},{3,2},{4,5},{5,4},{6,7},{7,6},{8,9},{9,8},{10,11... | collective-permute-start | bytes 1105928 | tf_op jit(solution)/shard_map/ppermute | solution.py:107
  43.3 8.7 %collective-permute-start.8 = (bf16[144,1280]{1,0:T(8,128)(2,1)S(1)}, bf16[144,1280]{1,0:T(8,128)(2,1)S(1)}, u32[]{:S(2)}, u32[]{:S(2)}) collective-permute-start(bf16[144,1280]{1,0:T(8,128)(2,1)S(1)} %fusion.2.refs_0_.tokens_ref), channel_id=1, source_target_pairs={{0,1},{1,0},{2,3},{3,2},{4,5},{5,4},{6,7},{7,6},{8,9},{9,8},{10,11... | collective-permute-start | bytes 1105928 | tf_op jit(solution)/shard_map/ppermute | solution.py:107
  43.8 7.9 %collective-permute-start.12 = (bf16[2,160,320]{2,1,0:T(8,128)(2,1)S(1)}, bf16[2,160,320]{2,1,0:T(8,128)(2,1)S(1)}, u32[]{:S(2)}, u32[]{:S(2)}) collective-permute-start(bf16[2,160,320]{2,1,0:T(8,128)(2,1)S(1)} %collective-permute-done.7.refs_2_), channel_id=1, source_target_pairs={{0,8},{4,12},{8,0},{12,4},{16,24},{20,28},{24,16},{28,20},{1,9},{5... | collective-permute-start | bytes 614408 | tf_op jit(solution)/shard_map/ppermute | solution.py:107
  45.4 8.9 %collective-permute-start.11 = (bf16[2,160,320]{2,1,0:T(8,128)(2,1)S(1)}, bf16[2,160,320]{2,1,0:T(8,128)(2,1)S(1)}, u32[]{:S(2)}, u32[]{:S(2)}) collective-permute-start(bf16[2,160,320]{2,1,0:T(8,128)(2,1)S(1)} %collective-permute-done.6.refs_7_), channel_id=1, source_target_pairs={{0,4},{4,0},{8,12},{12,8},{16,20},{20,16},{24,28},{28,24},{1,5},{5... | collective-permute-start | bytes 614408 | tf_op jit(solution)/shard_map/ppermute | solution.py:107
  45.9 13.6 %collective-permute-start.13 = (bf16[2,160,320]{2,1,0:T(8,128)(2,1)S(1)}, bf16[2,160,320]{2,1,0:T(8,128)(2,1)S(1)}, u32[]{:S(2)}, u32[]{:S(2)}) collective-permute-start(bf16[2,160,320]{2,1,0:T(8,128)(2,1)S(1)} %collective-permute-done.7.refs_2_), channel_id=1, source_target_pairs={{0,4},{4,0},{8,12},{12,8},{16,20},{20,16},{24,28},{28,24},{1,5},{5... | collective-permute-start | bytes 614408 | tf_op jit(solution)/shard_map/ppermute | solution.py:107
  51.7 11.8 %collective-permute-start.14 = (bf16[2,160,320]{2,1,0:T(8,128)(2,1)S(1)}, bf16[2,160,320]{2,1,0:T(8,128)(2,1)S(1)}, u32[]{:S(2)}, u32[]{:S(2)}) collective-permute-start(bf16[2,160,320]{2,1,0:T(8,128)(2,1)S(1)} %collective-permute-done.12.refs_3_), channel_id=1, source_target_pairs={{0,4},{4,0},{8,12},{12,8},{16,20},{20,16},{24,28},{28,24},{1,5},{5... | collective-permute-start | bytes 614408 | tf_op jit(solution)/shard_map/ppermute | solution.py:107
  66.5 3.7 %collective-permute-start.16 = (bf16[128,1280]{1,0:T(8,128)(2,1)S(1)}, bf16[128,1280]{1,0:T(8,128)(2,1)S(1)}, u32[]{:S(2)}, u32[]{:S(2)}) collective-permute-start(bf16[128,1280]{1,0:T(8,128)(2,1)S(1)} %get-tuple-element.40), channel_id=1, source_target_pairs={{0,1},{1,0},{2,3},{3,2},{4,5},{5,4},{6,7},{7,6},{8,9},{9,8},{10,11... | collective-permute-start | bytes 983048 | tf_op jit(solution)/shard_map/ppermute | solution.py:107
  66.5 8.3 %collective-permute-start.15 = (bf16[128,1280]{1,0:T(8,128)(2,1)}, bf16[128,1280]{1,0:T(8,128)(2,1)S(1)}, u32[]{:S(2)}, u32[]{:S(2)}) collective-permute-start(bf16[128,1280]{1,0:T(8,128)(2,1)} %get-tuple-element.39), channel_id=1, source_target_pairs={{0,1},{1,0},{2,3},{3,2},{4,5},{5,4},{6,7},{7,6},{8,9},{9,8},{10,11... | collective-permute-start | bytes 983048 | tf_op jit(solution)/shard_map/ppermute | solution.py:107
  67.1 20.2 %collective-permute-start.19 = (bf16[320,640]{1,0:T(8,128)(2,1)S(1)}, bf16[320,640]{1,0:T(8,128)(2,1)S(1)}, u32[]{:S(2)}, u32[]{:S(2)}) collective-permute-start(bf16[320,640]{1,0:T(8,128)(2,1)S(1)} %pad_maximum_fusion.1.refs_0_), channel_id=1, source_target_pairs={{0,8},{4,12},{8,0},{12,4},{16,24},{20,28},{24,16},{28,20},{1,9},{5... | collective-permute-start | bytes 1228808 | tf_op jit(solution)/shard_map/ppermute | solution.py:107
  67.6 19.7 %collective-permute-start.20 = (bf16[320,640]{1,0:T(8,128)(2,1)S(1)}, bf16[320,640]{1,0:T(8,128)(2,1)S(1)}, u32[]{:S(2)}, u32[]{:S(2)}) collective-permute-start(bf16[320,640]{1,0:T(8,128)(2,1)S(1)} %pad_maximum_fusion.1.refs_0_), channel_id=1, source_target_pairs={{0,16},{4,20},{8,24},{12,28},{16,0},{20,4},{24,8},{28,12},{1,17},{... | collective-permute-start | bytes 1228808 | tf_op jit(solution)/shard_map/ppermute | solution.py:107
  70.9 7.3 %collective-permute-start.17 = (bf16[64,1280]{1,0:T(8,128)(2,1)}, bf16[64,1280]{1,0:T(8,128)(2,1)S(1)}, u32[]{:S(2)}, u32[]{:S(2)}) collective-permute-start(bf16[64,1280]{1,0:T(8,128)(2,1)} %get-tuple-element.41), channel_id=1, source_target_pairs={{0,2},{1,3},{2,0},{3,1},{4,6},{5,7},{6,4},{7,5},{8,10},{9,11},{10,... | collective-permute-start | bytes 491528 | tf_op jit(solution)/shard_map/ppermute | solution.py:107
  72.5 7.9 %collective-permute-start.18 = (bf16[64,1280]{1,0:T(8,128)(2,1)}, bf16[64,1280]{1,0:T(8,128)(2,1)}, u32[]{:S(2)}, u32[]{:S(2)}) collective-permute-start(bf16[64,1280]{1,0:T(8,128)(2,1)} %get-tuple-element.42), channel_id=1, source_target_pairs={{0,2},{1,3},{2,0},{3,1},{4,6},{5,7},{6,4},{7,5},{8,10},{9,11},{10,... | collective-permute-start | bytes 491528 | tf_op jit(solution)/shard_map/ppermute | solution.py:107
  82.9 15.8 %all-to-all-start = ((bf16[8,64,640]{2,1,0:T(8,128)(2,1)}), bf16[8,64,640]{2,1,0:T(8,128)(2,1)S(1)}, u32[]{:S(2)}, u32[]{:S(2)}) async-start(bf16[8,64,640]{2,1,0:T(8,128)(2,1)} %shard_map.86), calls=%async_computation | async-start | bytes 1310720 | tf_op jit(solution)/shard_map/all_to_all | solution.py:356
  87.3 11.4 %collective-permute-start.21 = (bf16[320,640]{1,0:T(8,128)(2,1)S(1)}, bf16[320,640]{1,0:T(8,128)(2,1)S(1)}, u32[]{:S(2)}, u32[]{:S(2)}) collective-permute-start(bf16[320,640]{1,0:T(8,128)(2,1)S(1)} %collective-permute-done.20.refs_2_), channel_id=1, source_target_pairs={{0,8},{4,12},{8,0},{12,4},{16,24},{20,28},{24,16},{28,20},{1,9},{5... | collective-permute-start | bytes 1228808 | tf_op jit(solution)/shard_map/ppermute | solution.py:107
  99.7 2.0 %collective-permute-start.22 = (bf16[64,640]{1,0:T(8,128)(2,1)S(1)}, bf16[64,640]{1,0:T(8,128)(2,1)S(1)}, u32[]{:S(2)}, u32[]{:S(2)}) collective-permute-start(bf16[64,640]{1,0:T(8,128)(2,1)S(1)} %get-tuple-element.46), channel_id=1, source_target_pairs={{0,1},{1,0},{2,3},{3,2},{4,5},{5,4},{6,7},{7,6},{8,9},{9,8},{10,11... | collective-permute-start | bytes 245768 | tf_op jit(solution)/shard_map/ppermute | solution.py:107
  99.8 5.2 %collective-permute-start.23 = (bf16[64,640]{1,0:T(8,128)(2,1)S(1)}, bf16[64,640]{1,0:T(8,128)(2,1)S(1)}, u32[]{:S(2)}, u32[]{:S(2)}) collective-permute-start(bf16[64,640]{1,0:T(8,128)(2,1)S(1)} %get-tuple-element.47), channel_id=1, source_target_pairs={{0,2},{1,3},{2,0},{3,1},{4,6},{5,7},{6,4},{7,5},{8,10},{9,11},{10,... | collective-permute-start | bytes 245768 | tf_op jit(solution)/shard_map/ppermute | solution.py:107
  101.3 4.7 %collective-permute-start.24 = (bf16[64,640]{1,0:T(8,128)(2,1)S(1)}, bf16[64,640]{1,0:T(8,128)(2,1)S(1)}, u32[]{:S(2)}, u32[]{:S(2)}) collective-permute-start(bf16[64,640]{1,0:T(8,128)(2,1)S(1)} %get-tuple-element.48), channel_id=1, source_target_pairs={{0,3},{1,2},{2,1},{3,0},{4,7},{5,6},{6,5},{7,4},{8,11},{9,10},{10,... | collective-permute-start | bytes 245768 | tf_op jit(solution)/shard_map/ppermute | solution.py:107
  (3 other events, 22.1 us)

commit v13 on v12

--- a/solution.py
+++ b/solution.py
@@ -279,17 +279,9 @@
     near, beside = swap(heads, "dp", 2), swap(heads, "dp", 1)
     first, second = heads[0:2], heads[2:4]
     first_far = swap(first, "dp", 4)
-    half = merge_weight.shape[1] // 2
-    low, high = merge_weight[:, :half], merge_weight[:, half:]
-    lower = y == 0
-    mine = owners[:, 0]
-    note = jnp.pad(owners.astype(bf16).T, ((0, 15), (0, half - count)))
-    given = jnp.concatenate([jnp.where(lower, high, low), note], axis=0)
-    theirs = swap(after(given, first), "dp", 1)
-    other = theirs[-16, :count].astype(jnp.int32)
-    first_far_y = swap(after(first_far, (near, beside, theirs)), "dp", 1)
+    first_far_y = swap(after(first_far, (near, beside)), "dp", 1)
     first_last = swap(first_far, "dp", 2)
-    corner = swap(beside, "dp", 2)
+    corner = swap(after(beside, first_last), "dp", 2)
     second_far = swap(after(second, first_far), "dp", 4)
 
     marks = jnp.pad(segments.astype(bf16), ((0, 15), (0, width - rows)))
@@ -309,6 +301,14 @@
         )
     ]
 
+    half = merge_weight.shape[1] // 2
+    low, high = merge_weight[:, :half], merge_weight[:, half:]
+    lower = y == 0
+    mine = owners[:, 0]
+    note = jnp.pad(owners.astype(bf16).T, ((0, 15), (0, half - count)))
+    given = jnp.concatenate([jnp.where(lower, high, low), note], axis=0)
+    theirs = swap(after(given, second_far_y), "dp", 1)
+    other = theirs[-16, :count].astype(jnp.int32)
     pair = jnp.concatenate([jnp.where(lower, low, high), theirs[:-16]], axis=0)
     held = after(pair, (second_last, second_far_y, blocks[0][7]))
     merge_near, merge_far = swap(held, "dp", 2), swap(held, "dp", 4)

time: 120 us -> 115 us (0.958)
  starting transfers between devices: 33.6 us -> 28 us
  waiting for transfers between devices: 54.5 us -> 57.3 us
  other arithmetic: 5.58 us -> 3.94 us
    ppermute x25, starting transfers between devices: 30 us -> 24.5 us  [swap(): lax.ppermute(value, axis, [(i, i ^ k) for i in range(lax.axis_size(axis))])]
    concatenate x2 -> x1, other arithmetic: 2.96 us -> 0.09 us  [by_permutes(): heads = jnp.concatenate([qkv_weight, out_weight.T[None]], axis=0)]
    ppermute x25, waiting for transfers between devices: 54.5 us -> 57.3 us  [swap(): lax.ppermute(value, axis, [(i, i ^ k) for i in range(lax.axis_size(axis))])]
    slice x0 -> x1, other arithmetic: none -> 1.23 us  [by_permutes(): first, second = (heads[0:2], heads[2:4])]
  transfers between devices with their start and end apart: 26 -> 26, of which waited for: 14 -> 15; matrix products, arithmetic and copies ran while one was open for 4% -> 3% of each run, Pallas kernels for 6% -> 6%
where the time goes in v13:
time: 115 us; the launch traced here: 114 us
  waiting for transfers between devices  57.3 us (50%)
  starting transfers between devices  28 us (24%)
  blocking collectives  11.8 us (10%)
  Pallas kernels  11.5 us (10%)
  other arithmetic  3.94 us (3%)
  local copies, waits for them, and re-layouts  1.62 us (1%)
    ppermute x25, waiting for transfers between devices, swap(): lax.ppermute(value, axis, [(i, i ^ k) for i in range(lax.axis_size(axis))])  57.3 us
    ppermute x25, starting transfers between devices, swap(): lax.ppermute(value, axis, [(i, i ^ k) for i in range(lax.axis_size(axis))])  24.5 us
    all_to_all x1, blocking collectives, by_permutes(): lax.all_to_all(packed.reshape(n_dp, 2 * capacity, half), 'dp', split_axis...  11.8 us
    pallas_call x7, Pallas kernels, call(): pl.pallas_call(kernel, out_shape=tuple(outs), in_specs=specs, out_specs=t...  11.5 us
    all_to_all x1, starting transfers between devices, by_permutes(): lax.all_to_all(slices, ('dp', 'fsdp'), split_axis=0, concat_axis=0, tiled...  3.54 us
  transfers between devices with their start and end apart: 26, of which 15 were waited for; matrix products, arithmetic and copies ran while one was open for 3% of the time, Pallas kernels for 6%

profile of v13, /device:TPU:0, one launch (start us, length us, event | category | flops | bytes accessed | tf_op | source)
XLA Modules:
  0.0 114.3 jit_solution(9365759735531932135)
XLA Ops:
  0.0 1.2 %fusion.8 = (bf16[2,160,320]{2,1,0:T(8,128)(2,1)S(1)}, bf16[2,160,320]{2,1,0:T(8,128)(2,1)S(1)}) fusion(bf16[3,160,320]{2,1,0:T(8,128)(2,1)} %param.9, bf16[1,160,320]{2,1,0:T(8,128)(2,1)} %bitcast.26), kind=kLoop, calls=%fused_computation.24 | loop fusion | flops 102400 | bytes 1146880 | tf_op jit(solution)/shard_map/slice | solution.py:280
  1.3 4.1 %collective-permute-start = (bf16[2,160,320]{2,1,0:T(8,128)(2,1)S(1)}, bf16[2,160,320]{2,1,0:T(8,128)(2,1)S(1)}, u32[]{:S(2)}, u32[]{:S(2)}) collective-permute-start(bf16[2,160,320]{2,1,0:T(8,128)(2,1)S(1)} %get-tuple-element.53), channel_id=1, source_target_pairs={{0,16},{4,20},{8,24},{12,28},{16,0},{20,4},{24,8},{28,12},{1,17},{... | collective-permute-start | bytes 614408 | tf_op jit(solution)/shard_map/ppermute | solution.py:107
  5.5 1.6 %collective-permute-start.6 = (bf16[4,160,320]{2,1,0:T(8,128)(2,1)S(1)}, bf16[4,160,320]{2,1,0:T(8,128)(2,1)S(1)}, u32[]{:S(2)}, u32[]{:S(2)}) collective-permute-start(bf16[4,160,320]{2,1,0:T(8,128)(2,1)S(1)} %pad_maximum_fusion.refs_4_.refs_0_), channel_id=1, source_target_pairs={{0,4},{4,0},{8,12},{12,8},{16,20},{20,16},{24,28},{28,24},{1,5},{5... | collective-permute-start | bytes 1228808 | tf_op jit(solution)/shard_map/ppermute | solution.py:107
  7.1 1.6 %collective-permute-start.5 = (bf16[4,160,320]{2,1,0:T(8,128)(2,1)S(1)}, bf16[4,160,320]{2,1,0:T(8,128)(2,1)S(1)}, u32[]{:S(2)}, u32[]{:S(2)}) collective-permute-start(bf16[4,160,320]{2,1,0:T(8,128)(2,1)S(1)} %pad_maximum_fusion.refs_4_.refs_0_), channel_id=1, source_target_pairs={{0,8},{4,12},{8,0},{12,4},{16,24},{20,28},{24,16},{28,20},{1,9},{5... | collective-permute-start | bytes 1228808 | tf_op jit(solution)/shard_map/ppermute | solution.py:107
  8.7 8.1 %collective-permute-done.refs_6_ = bf16[2,160,320]{2,1,0:T(8,128)(2,1)S(1)} collective-permute-done((bf16[2,160,320]{2,1,0:T(8,128)(2,1)S(1)}, bf16[2,160,320]{2,1,0:T(8,128)(2,1)S(1)}, u32[]{:S(2)}, u32[]{:S(2)}) %collective-permute-start) | collective-permute-done | bytes 204832 | tf_op jit(solution)/shard_map/ppermute | solution.py:107
  17.4 1.6 %collective-permute-start.4 = (bf16[144,1280]{1,0:T(8,128)(2,1)S(1)}, bf16[144,1280]{1,0:T(8,128)(2,1)S(1)}, u32[]{:S(2)}, u32[]{:S(2)}) collective-permute-start(bf16[144,1280]{1,0:T(8,128)(2,1)S(1)} %fusion.2.refs_0_.tokens_ref), channel_id=1, source_target_pairs={{0,2},{1,3},{2,0},{3,1},{4,6},{5,7},{6,4},{7,5},{8,10},{9,11},{10,... | collective-permute-start | bytes 1105928 | tf_op jit(solution)/shard_map/ppermute | solution.py:107
  19.0 3.4 %collective-permute-start.1 = (bf16[2,160,320]{2,1,0:T(8,128)(2,1)S(1)}, bf16[2,160,320]{2,1,0:T(8,128)(2,1)S(1)}, u32[]{:S(2)}, u32[]{:S(2)}) collective-permute-start(bf16[2,160,320]{2,1,0:T(8,128)(2,1)S(1)} %get-tuple-element.28), channel_id=1, source_target_pairs={{0,16},{4,20},{8,24},{12,28},{16,0},{20,4},{24,8},{28,12},{1,17},{... | collective-permute-start | bytes 614408 | tf_op jit(solution)/shard_map/ppermute | solution.py:107
  22.4 8.2 %collective-permute-done.5.refs_5_.refs_1_ = bf16[4,160,320]{2,1,0:T(8,128)(2,1)S(1)} collective-permute-done((bf16[4,160,320]{2,1,0:T(8,128)(2,1)S(1)}, bf16[4,160,320]{2,1,0:T(8,128)(2,1)S(1)}, u32[]{:S(2)}, u32[]{:S(2)}) %collective-permute-start.5) | collective-permute-done | bytes 409632 | tf_op jit(solution)/shard_map/ppermute | solution.py:107
  31.2 2.9 %collective-permute-done.8.refs_7_ = bf16[2,160,320]{2,1,0:T(8,128)(2,1)S(1)} collective-permute-done((bf16[2,160,320]{2,1,0:T(8,128)(2,1)S(1)}, bf16[2,160,320]{2,1,0:T(8,128)(2,1)S(1)}, u32[]{:S(2)}, u32[]{:S(2)}) %collective-permute-start.8) | collective-permute-done | bytes 204832 | tf_op jit(solution)/shard_map/ppermute | solution.py:107
  34.8 3.6 %collective-permute-done.7.refs_10_ = bf16[2,160,320]{2,1,0:T(8,128)(2,1)S(1)} collective-permute-done((bf16[2,160,320]{2,1,0:T(8,128)(2,1)S(1)}, bf16[2,160,320]{2,1,0:T(8,128)(2,1)S(1)}, u32[]{:S(2)}, u32[]{:S(2)}) %collective-permute-start.7) | collective-permute-done | bytes 204832 | tf_op jit(solution)/shard_map/ppermute | solution.py:107
  39.0 3.1 %collective-permute-done.2.refs_6_ = bf16[2,160,320]{2,1,0:T(8,128)(2,1)S(1)} collective-permute-done((bf16[2,160,320]{2,1,0:T(8,128)(2,1)S(1)}, bf16[2,160,320]{2,1,0:T(8,128)(2,1)S(1)}, u32[]{:S(2)}, u32[]{:S(2)}) %collective-permute-start.2) | collective-permute-done | bytes 204832 | tf_op jit(solution)/shard_map/ppermute | solution.py:107
  42.6 5.6 %collective-permute-done.11.refs_9_.refs_5_ = bf16[4,160,320]{2,1,0:T(8,128)(2,1)S(1)} collective-permute-done((bf16[4,160,320]{2,1,0:T(8,128)(2,1)S(1)}, bf16[4,160,320]{2,1,0:T(8,128)(2,1)S(1)}, u32[]{:S(2)}, u32[]{:S(2)}) %collective-permute-start.11) | collective-permute-done | bytes 409632 | tf_op jit(solution)/shard_map/ppermute | solution.py:107
  48.8 2.1 %collective-permute-done.13.refs_3_ = bf16[2,160,320]{2,1,0:T(8,128)(2,1)S(1)} collective-permute-done((bf16[2,160,320]{2,1,0:T(8,128)(2,1)S(1)}, bf16[2,160,320]{2,1,0:T(8,128)(2,1)S(1)}, u32[]{:S(2)}, u32[]{:S(2)}) %collective-permute-start.13) | collective-permute-done | bytes 204832 | tf_op jit(solution)/shard_map/ppermute | solution.py:107
  51.4 0.9 shard_map.82.rows_ref
  52.3 3.8 %collective-permute-done.12.refs_11_ = bf16[2,160,320]{2,1,0:T(8,128)(2,1)S(1)} collective-permute-done((bf16[2,160,320]{2,1,0:T(8,128)(2,1)S(1)}, bf16[2,160,320]{2,1,0:T(8,128)(2,1)S(1)}, u32[]{:S(2)}, u32[]{:S(2)}) %collective-permute-start.12) | collective-permute-done | bytes 204832 | tf_op jit(solution)/shard_map/ppermute | solution.py:107
  56.1 3.0 %shard_map.83 = (bf16[4,512,512]{2,1,0:T(8,128)(2,1)S(1)}, f32[4,512,1]{2,1,0:T(8,128)S(1)}) custom-call(s32[1]{0:T(128)} %bitcast.7.me_ref, bf16[512,1280]{1,0:T(8,128)(2,1)S(1)} %shard_map.82.rows_ref, bf16[144,1280]{1,0:T(8,128)(2,1)S(1)} %fusion.2.refs_0_.tokens_ref, bf16[144,1280]{1,0:T(8,128)(2,1)S(1)} %collective-permute-done.4.refs_1_, ...), custom_call_target="tpu_custom_call" | custom-call | flops 1006632960 | bytes 7348228 | tf_op jit(solution)/shard_map/pallas_call | solution.py:129
  59.2 3.0 %shard_map.84 = (f32[256,1280]{1,0:T(8,128)S(1)}, bf16[128,1280]{1,0:T(8,128)(2,1)}, bf16[128,1280]{1,0:T(8,128)(2,1)S(1)}) custom-call(s32[1]{0:T(128)} %bitcast.7.me_ref, bf16[512,1280]{1,0:T(8,128)(2,1)S(1)} %shard_map.82.rows_ref, bf16[4,512,512]{2,1,0:T(8,128)(2,1)S(1)} %get-tuple-element.37.weights_ref, f32[4,512,1]{2,1,0:T(8,128)S(1)} %get-tuple-element.38.totals_ref, ...), custom_call_target="tpu_custom_call" | custom-call | flops 1006632960 | bytes 7839748 | tf_op jit(solution)/shard_map/pallas_call | solution.py:129
  63.4 2.6 %collective-permute-start.20 = (bf16[320,640]{1,0:T(8,128)(2,1)S(1)}, bf16[320,640]{1,0:T(8,128)(2,1)S(1)}, u32[]{:S(2)}, u32[]{:S(2)}) collective-permute-start(bf16[320,640]{1,0:T(8,128)(2,1)S(1)} %pad_maximum_fusion.1.refs_0_), channel_id=1, source_target_pairs={{0,16},{4,20},{8,24},{12,28},{16,0},{20,4},{24,8},{28,12},{1,17},{... | collective-permute-start | bytes 1228808 | tf_op jit(solution)/shard_map/ppermute | solution.py:107
  65.9 0.8 shard_map.85
  66.7 1.5 %collective-permute-start.17 = (bf16[64,1280]{1,0:T(8,128)(2,1)}, bf16[64,1280]{1,0:T(8,128)(2,1)S(1)}, u32[]{:S(2)}, u32[]{:S(2)}) collective-permute-start(bf16[64,1280]{1,0:T(8,128)(2,1)} %get-tuple-element.43), channel_id=1, source_target_pairs={{0,2},{1,3},{2,0},{3,1},{4,6},{5,7},{6,4},{7,5},{8,10},{9,11},{10,... | collective-permute-start | bytes 491528 | tf_op jit(solution)/shard_map/ppermute | solution.py:107
  69.3 0.7 reduce.3
  70.5 3.5 %collective-permute-done.17.refs_0_ = bf16[64,1280]{1,0:T(8,128)(2,1)S(1)} collective-permute-done((bf16[64,1280]{1,0:T(8,128)(2,1)}, bf16[64,1280]{1,0:T(8,128)(2,1)S(1)}, u32[]{:S(2)}, u32[]{:S(2)}) %collective-permute-start.17) | collective-permute-done | bytes 163872 | tf_op jit(solution)/shard_map/ppermute | solution.py:107
  74.1 2.0 %collective-permute-done.18.refs_1_ = bf16[64,1280]{1,0:T(8,128)(2,1)} collective-permute-done((bf16[64,1280]{1,0:T(8,128)(2,1)}, bf16[64,1280]{1,0:T(8,128)(2,1)}, u32[]{:S(2)}, u32[]{:S(2)}) %collective-permute-start.18) | collective-permute-done | bytes 163872 | tf_op jit(solution)/shard_map/ppermute | solution.py:107
  76.1 2.6 %shard_map.86 = bf16[8,64,640]{2,1,0:T(8,128)(2,1)} custom-call(bf16[144,1280]{1,0:T(8,128)(2,1)S(1)} %fusion.2.refs_0_.tokens_ref, f32[256,1280]{1,0:T(8,128)S(1)} %get-tuple-element.40.keep_ref, bf16[128,1280]{1,0:T(8,128)(2,1)S(1)} %collective-permute-done.15.core_ref, f32[2,1280]{1,0:T(2,128)S(1)} %copy-done, s32[128,1]{1,0:T(8,128)S(1)} %reshape.41.order_ref, ...), custom_call_target="tpu_custom_call" | custom-call | bytes 1 | tf_op jit(solution)/shard_map/pallas_call | solution.py:129
  78.6 3.5 %all-to-all-start = ((bf16[8,64,640]{2,1,0:T(8,128)(2,1)}), bf16[8,64,640]{2,1,0:T(8,128)(2,1)S(1)}, u32[]{:S(2)}, u32[]{:S(2)}) async-start(bf16[8,64,640]{2,1,0:T(8,128)(2,1)} %shard_map.86), calls=%async_computation | async-start | bytes 1310720 | tf_op jit(solution)/shard_map/all_to_all | solution.py:356
  82.9 1.3 %collective-permute-done.20.refs_2_ = bf16[320,640]{1,0:T(8,128)(2,1)S(1)} collective-permute-done((bf16[320,640]{1,0:T(8,128)(2,1)S(1)}, bf16[320,640]{1,0:T(8,128)(2,1)S(1)}, u32[]{:S(2)}, u32[]{:S(2)}) %collective-permute-start.20) | collective-permute-done | bytes 409632 | tf_op jit(solution)/shard_map/ppermute | solution.py:107
  86.2 7.8 %collective-permute-done.21.refs_3_ = bf16[320,640]{1,0:T(8,128)(2,1)S(1)} collective-permute-done((bf16[320,640]{1,0:T(8,128)(2,1)S(1)}, bf16[320,640]{1,0:T(8,128)(2,1)S(1)}, u32[]{:S(2)}, u32[]{:S(2)}) %collective-permute-start.21) | collective-permute-done | bytes 409632 | tf_op jit(solution)/shard_map/ppermute | solution.py:107
  94.1 1.1 shard_map.87
  95.2 1.7 %collective-permute-start.23 = (bf16[64,640]{1,0:T(8,128)(2,1)S(1)}, bf16[64,640]{1,0:T(8,128)(2,1)S(1)}, u32[]{:S(2)}, u32[]{:S(2)}) collective-permute-start(bf16[64,640]{1,0:T(8,128)(2,1)S(1)} %get-tuple-element.49), channel_id=1, source_target_pairs={{0,2},{1,3},{2,0},{3,1},{4,6},{5,7},{6,4},{7,5},{8,10},{9,11},{10,... | collective-permute-start | bytes 245768 | tf_op jit(solution)/shard_map/ppermute | solution.py:107
  97.1 3.0 %collective-permute-done.23.two_ref = bf16[64,640]{1,0:T(8,128)(2,1)S(1)} collective-permute-done((bf16[64,640]{1,0:T(8,128)(2,1)S(1)}, bf16[64,640]{1,0:T(8,128)(2,1)S(1)}, u32[]{:S(2)}, u32[]{:S(2)}) %collective-permute-start.23) | collective-permute-done | bytes 81952 | tf_op jit(solution)/shard_map/ppermute | solution.py:107
  100.2 1.4 %collective-permute-done.24.three_ref = bf16[64,640]{1,0:T(8,128)(2,1)S(1)} collective-permute-done((bf16[64,640]{1,0:T(8,128)(2,1)S(1)}, bf16[64,640]{1,0:T(8,128)(2,1)S(1)}, u32[]{:S(2)}, u32[]{:S(2)}) %collective-permute-start.24) | collective-permute-done | bytes 81952 | tf_op jit(solution)/shard_map/ppermute | solution.py:107
  101.8 11.8 %all_to_all.10 = bf16[8,16,640]{2,1,0:T(8,128)(2,1)S(1)} all-to-all(bf16[8,16,640]{2,1,0:T(8,128)(2,1)S(1)} %bitcast.24), channel_id=1, replica_groups=mesh['dp'=8,'fsdp'=4] {'dp'}, dimensions={0} | all-to-all | bytes 327680 | tf_op jit(solution)/shard_map/all_to_all | solution.py:381
  (67 shorter events, 11.0 us)
Async XLA Ops:
  0.0 8.6 %copy-start.7 = (s32[1,128]{1,0:T(1,128)S(1)}, s32[1,128]{1,0:T(1,128)}, u32[]{:S(2)}) copy-start(s32[1,128]{1,0:T(1,128)} %param.13) | copy-start | bytes 1540
  0.0 17.4 %copy-start.4 = (bf16[128,1280]{1,0:T(8,128)(2,1)S(1)}, bf16[128,1280]{1,0:T(8,128)(2,1)}, u32[]{:S(2)}) copy-start(bf16[128,1280]{1,0:T(8,128)(2,1)} %param.8) | copy-start | bytes 983044
  0.0 34.1 %copy-start.3 = (bf16[160,1280]{1,0:T(8,128)(2,1)S(1)}, bf16[160,1280]{1,0:T(8,128)(2,1)}, u32[]{:S(2)}) copy-start(bf16[160,1280]{1,0:T(8,128)(2,1)} %param.11) | copy-start | bytes 1228804
  1.2 37.7 %copy-start.6 = (s32[32,1]{0,1:T(1,128)S(1)}, s32[32,1]{0,1:T(1,128)}, u32[]{:S(2)}) copy-start(s32[32,1]{0,1:T(1,128)} %param.15) | copy-start | bytes 388
  1.3 50.2 %copy-start = (f32[2,1280]{1,0:T(2,128)S(1)}, f32[2,1280]{1,0:T(2,128)}, u32[]{:S(2)}) copy-start(f32[2,1280]{1,0:T(2,128)} %gains_ref.3) | copy-start | bytes 30724
  1.3 15.4 %collective-permute-start = (bf16[2,160,320]{2,1,0:T(8,128)(2,1)S(1)}, bf16[2,160,320]{2,1,0:T(8,128)(2,1)S(1)}, u32[]{:S(2)}, u32[]{:S(2)}) collective-permute-start(bf16[2,160,320]{2,1,0:T(8,128)(2,1)S(1)} %get-tuple-element.53), channel_id=1, source_target_pairs={{0,16},{4,20},{8,24},{12,28},{16,0},{20,4},{24,8},{28,12},{1,17},{... | collective-permute-start | bytes 614408 | tf_op jit(solution)/shard_map/ppermute | solution.py:107
  5.5 16.9 %collective-permute-start.6 = (bf16[4,160,320]{2,1,0:T(8,128)(2,1)S(1)}, bf16[4,160,320]{2,1,0:T(8,128)(2,1)S(1)}, u32[]{:S(2)}, u32[]{:S(2)}) collective-permute-start(bf16[4,160,320]{2,1,0:T(8,128)(2,1)S(1)} %pad_maximum_fusion.refs_4_.refs_0_), channel_id=1, source_target_pairs={{0,4},{4,0},{8,12},{12,8},{16,20},{20,16},{24,28},{28,24},{1,5},{5... | collective-permute-start | bytes 1228808 | tf_op jit(solution)/shard_map/ppermute | solution.py:107
  7.1 23.5 %collective-permute-start.5 = (bf16[4,160,320]{2,1,0:T(8,128)(2,1)S(1)}, bf16[4,160,320]{2,1,0:T(8,128)(2,1)S(1)}, u32[]{:S(2)}, u32[]{:S(2)}) collective-permute-start(bf16[4,160,320]{2,1,0:T(8,128)(2,1)S(1)} %pad_maximum_fusion.refs_4_.refs_0_), channel_id=1, source_target_pairs={{0,8},{4,12},{8,0},{12,4},{16,24},{20,28},{24,16},{28,20},{1,9},{5... | collective-permute-start | bytes 1228808 | tf_op jit(solution)/shard_map/ppermute | solution.py:107
  16.7 17.4 %collective-permute-start.8 = (bf16[2,160,320]{2,1,0:T(8,128)(2,1)S(1)}, bf16[2,160,320]{2,1,0:T(8,128)(2,1)S(1)}, u32[]{:S(2)}, u32[]{:S(2)}) collective-permute-start(bf16[2,160,320]{2,1,0:T(8,128)(2,1)S(1)} %collective-permute-done.refs_6_), channel_id=1, source_target_pairs={{0,8},{4,12},{8,0},{12,4},{16,24},{20,28},{24,16},{28,20},{1,9},{5... | collective-permute-start | bytes 614408 | tf_op jit(solution)/shard_map/ppermute | solution.py:107
  17.4 17.4 %collective-permute-start.4 = (bf16[144,1280]{1,0:T(8,128)(2,1)S(1)}, bf16[144,1280]{1,0:T(8,128)(2,1)S(1)}, u32[]{:S(2)}, u32[]{:S(2)}) collective-permute-start(bf16[144,1280]{1,0:T(8,128)(2,1)S(1)} %fusion.2.refs_0_.tokens_ref), channel_id=1, source_target_pairs={{0,2},{1,3},{2,0},{3,1},{4,6},{5,7},{6,4},{7,5},{8,10},{9,11},{10,... | collective-permute-start | bytes 1105928 | tf_op jit(solution)/shard_map/ppermute | solution.py:107
  19.0 15.2 %collective-permute-start.1 = (bf16[2,160,320]{2,1,0:T(8,128)(2,1)S(1)}, bf16[2,160,320]{2,1,0:T(8,128)(2,1)S(1)}, u32[]{:S(2)}, u32[]{:S(2)}) collective-permute-start(bf16[2,160,320]{2,1,0:T(8,128)(2,1)S(1)} %get-tuple-element.28), channel_id=1, source_target_pairs={{0,16},{4,20},{8,24},{12,28},{16,0},{20,4},{24,8},{28,12},{1,17},{... | collective-permute-start | bytes 614408 | tf_op jit(solution)/shard_map/ppermute | solution.py:107
  30.6 7.8 %collective-permute-start.7 = (bf16[2,160,320]{2,1,0:T(8,128)(2,1)S(1)}, bf16[2,160,320]{2,1,0:T(8,128)(2,1)S(1)}, u32[]{:S(2)}, u32[]{:S(2)}) collective-permute-start(bf16[2,160,320]{2,1,0:T(8,128)(2,1)S(1)} %collective-permute-done.refs_6_), channel_id=1, source_target_pairs={{0,4},{4,0},{8,12},{12,8},{16,20},{20,16},{24,28},{28,24},{1,5},{5... | collective-permute-start | bytes 614408 | tf_op jit(solution)/shard_map/ppermute | solution.py:107
  34.1 14.1 %collective-permute-start.11 = (bf16[4,160,320]{2,1,0:T(8,128)(2,1)S(1)}, bf16[4,160,320]{2,1,0:T(8,128)(2,1)S(1)}, u32[]{:S(2)}, u32[]{:S(2)}) collective-permute-start(bf16[4,160,320]{2,1,0:T(8,128)(2,1)S(1)} %collective-permute-done.6.refs_8_.refs_4_), channel_id=1, source_target_pairs={{0,8},{4,12},{8,0},{12,4},{16,24},{20,28},{24,16},{28,20},{1,9},{5... | collective-permute-start | bytes 1228808 | tf_op jit(solution)/shard_map/ppermute | solution.py:107
  34.2 7.9 %collective-permute-start.2 = (bf16[2,160,320]{2,1,0:T(8,128)(2,1)S(1)}, bf16[2,160,320]{2,1,0:T(8,128)(2,1)S(1)}, u32[]{:S(2)}, u32[]{:S(2)}) collective-permute-start(bf16[2,160,320]{2,1,0:T(8,128)(2,1)S(1)} %collective-permute-done.1.refs_2_), channel_id=1, source_target_pairs={{0,4},{4,0},{8,12},{12,8},{16,20},{20,16},{24,28},{28,24},{1,5},{5... | collective-permute-start | bytes 614408 | tf_op jit(solution)/shard_map/ppermute | solution.py:107
  38.4 13.0 %collective-permute-start.10 = (bf16[144,1280]{1,0:T(8,128)(2,1)S(1)}, bf16[144,1280]{1,0:T(8,128)(2,1)S(1)}, u32[]{:S(2)}, u32[]{:S(2)}) collective-permute-start(bf16[144,1280]{1,0:T(8,128)(2,1)S(1)} %collective-permute-done.4.refs_1_), channel_id=1, source_target_pairs={{0,1},{1,0},{2,3},{3,2},{4,5},{5,4},{6,7},{7,6},{8,9},{9,8},{10,11... | collective-permute-start | bytes 1105928 | tf_op jit(solution)/shard_map/ppermute | solution.py:107
  38.4 13.0 %collective-permute-start.9 = (bf16[144,1280]{1,0:T(8,128)(2,1)S(1)}, bf16[144,1280]{1,0:T(8,128)(2,1)S(1)}, u32[]{:S(2)}, u32[]{:S(2)}) collective-permute-start(bf16[144,1280]{1,0:T(8,128)(2,1)S(1)} %fusion.2.refs_0_.tokens_ref), channel_id=1, source_target_pairs={{0,1},{1,0},{2,3},{3,2},{4,5},{5,4},{6,7},{7,6},{8,9},{9,8},{10,11... | collective-permute-start | bytes 1105928 | tf_op jit(solution)/shard_map/ppermute | solution.py:107
  38.9 11.9 %collective-permute-start.13 = (bf16[2,160,320]{2,1,0:T(8,128)(2,1)S(1)}, bf16[2,160,320]{2,1,0:T(8,128)(2,1)S(1)}, u32[]{:S(2)}, u32[]{:S(2)}) collective-permute-start(bf16[2,160,320]{2,1,0:T(8,128)(2,1)S(1)} %collective-permute-done.1.refs_2_), channel_id=1, source_target_pairs={{0,8},{4,12},{8,0},{12,4},{16,24},{20,28},{24,16},{28,20},{1,9},{5... | collective-permute-start | bytes 614408 | tf_op jit(solution)/shard_map/ppermute | solution.py:107
  42.1 9.3 %collective-permute-start.3 = (bf16[176,640]{1,0:T(8,128)(2,1)S(1)}, bf16[176,640]{1,0:T(8,128)(2,1)S(1)}, u32[]{:S(2)}, u32[]{:S(2)}) collective-permute-start(bf16[176,640]{1,0:T(8,128)(2,1)S(1)} %fusion.4), channel_id=1, source_target_pairs={{0,4},{4,0},{8,12},{12,8},{16,20},{20,16},{24,28},{28,24},{1,5},{5... | collective-permute-start | bytes 675848 | tf_op jit(solution)/shard_map/ppermute | solution.py:107
  48.2 7.9 %collective-permute-start.12 = (bf16[2,160,320]{2,1,0:T(8,128)(2,1)S(1)}, bf16[2,160,320]{2,1,0:T(8,128)(2,1)S(1)}, u32[]{:S(2)}, u32[]{:S(2)}) collective-permute-start(bf16[2,160,320]{2,1,0:T(8,128)(2,1)S(1)} %collective-permute-done.8.refs_7_), channel_id=1, source_target_pairs={{0,4},{4,0},{8,12},{12,8},{16,20},{20,16},{24,28},{28,24},{1,5},{5... | collective-permute-start | bytes 614408 | tf_op jit(solution)/shard_map/ppermute | solution.py:107
  50.9 8.3 %collective-permute-start.14 = (bf16[2,160,320]{2,1,0:T(8,128)(2,1)S(1)}, bf16[2,160,320]{2,1,0:T(8,128)(2,1)S(1)}, u32[]{:S(2)}, u32[]{:S(2)}) collective-permute-start(bf16[2,160,320]{2,1,0:T(8,128)(2,1)S(1)} %collective-permute-done.13.refs_3_), channel_id=1, source_target_pairs={{0,4},{4,0},{8,12},{12,8},{16,20},{20,16},{24,28},{28,24},{1,5},{5... | collective-permute-start | bytes 614408 | tf_op jit(solution)/shard_map/ppermute | solution.py:107
  51.4 11.2 %copy-start.5 = (bf16[176,640]{1,0:T(8,128)(2,1)}, bf16[176,640]{1,0:T(8,128)(2,1)S(1)}, u32[]{:S(2)}) copy-start(bf16[176,640]{1,0:T(8,128)(2,1)S(1)} %collective-permute-done.3) | copy-start | bytes 675844
  62.2 3.8 %collective-permute-start.16 = (bf16[128,1280]{1,0:T(8,128)(2,1)S(1)}, bf16[128,1280]{1,0:T(8,128)(2,1)S(1)}, u32[]{:S(2)}, u32[]{:S(2)}) collective-permute-start(bf16[128,1280]{1,0:T(8,128)(2,1)S(1)} %get-tuple-element.42), channel_id=1, source_target_pairs={{0,1},{1,0},{2,3},{3,2},{4,5},{5,4},{6,7},{7,6},{8,9},{9,8},{10,11... | collective-permute-start | bytes 983048 | tf_op jit(solution)/shard_map/ppermute | solution.py:107
  62.2 8.4 %collective-permute-start.15 = (bf16[128,1280]{1,0:T(8,128)(2,1)}, bf16[128,1280]{1,0:T(8,128)(2,1)S(1)}, u32[]{:S(2)}, u32[]{:S(2)}) collective-permute-start(bf16[128,1280]{1,0:T(8,128)(2,1)} %get-tuple-element.41), channel_id=1, source_target_pairs={{0,1},{1,0},{2,3},{3,2},{4,5},{5,4},{6,7},{7,6},{8,9},{9,8},{10,11... | collective-permute-start | bytes 983048 | tf_op jit(solution)/shard_map/ppermute | solution.py:107
  62.7 20.2 %collective-permute-start.19 = (bf16[320,640]{1,0:T(8,128)(2,1)S(1)}, bf16[320,640]{1,0:T(8,128)(2,1)S(1)}, u32[]{:S(2)}, u32[]{:S(2)}) collective-permute-start(bf16[320,640]{1,0:T(8,128)(2,1)S(1)} %pad_maximum_fusion.1.refs_0_), channel_id=1, source_target_pairs={{0,8},{4,12},{8,0},{12,4},{16,24},{20,28},{24,16},{28,20},{1,9},{5... | collective-permute-start | bytes 1228808 | tf_op jit(solution)/shard_map/ppermute | solution.py:107
  63.4 20.8 %collective-permute-start.20 = (bf16[320,640]{1,0:T(8,128)(2,1)S(1)}, bf16[320,640]{1,0:T(8,128)(2,1)S(1)}, u32[]{:S(2)}, u32[]{:S(2)}) collective-permute-start(bf16[320,640]{1,0:T(8,128)(2,1)S(1)} %pad_maximum_fusion.1.refs_0_), channel_id=1, source_target_pairs={{0,16},{4,20},{8,24},{12,28},{16,0},{20,4},{24,8},{28,12},{1,17},{... | collective-permute-start | bytes 1228808 | tf_op jit(solution)/shard_map/ppermute | solution.py:107
  66.7 7.3 %collective-permute-start.17 = (bf16[64,1280]{1,0:T(8,128)(2,1)}, bf16[64,1280]{1,0:T(8,128)(2,1)S(1)}, u32[]{:S(2)}, u32[]{:S(2)}) collective-permute-start(bf16[64,1280]{1,0:T(8,128)(2,1)} %get-tuple-element.43), channel_id=1, source_target_pairs={{0,2},{1,3},{2,0},{3,1},{4,6},{5,7},{6,4},{7,5},{8,10},{9,11},{10,... | collective-permute-start | bytes 491528 | tf_op jit(solution)/shard_map/ppermute | solution.py:107
  68.2 7.9 %collective-permute-start.18 = (bf16[64,1280]{1,0:T(8,128)(2,1)}, bf16[64,1280]{1,0:T(8,128)(2,1)}, u32[]{:S(2)}, u32[]{:S(2)}) collective-permute-start(bf16[64,1280]{1,0:T(8,128)(2,1)} %get-tuple-element.44), channel_id=1, source_target_pairs={{0,2},{1,3},{2,0},{3,1},{4,6},{5,7},{6,4},{7,5},{8,10},{9,11},{10,... | collective-permute-start | bytes 491528 | tf_op jit(solution)/shard_map/ppermute | solution.py:107
  78.6 15.4 %all-to-all-start = ((bf16[8,64,640]{2,1,0:T(8,128)(2,1)}), bf16[8,64,640]{2,1,0:T(8,128)(2,1)S(1)}, u32[]{:S(2)}, u32[]{:S(2)}) async-start(bf16[8,64,640]{2,1,0:T(8,128)(2,1)} %shard_map.86), calls=%async_computation | async-start | bytes 1310720 | tf_op jit(solution)/shard_map/all_to_all | solution.py:356
  84.2 9.9 %collective-permute-start.21 = (bf16[320,640]{1,0:T(8,128)(2,1)S(1)}, bf16[320,640]{1,0:T(8,128)(2,1)S(1)}, u32[]{:S(2)}, u32[]{:S(2)}) collective-permute-start(bf16[320,640]{1,0:T(8,128)(2,1)S(1)} %collective-permute-done.20.refs_2_), channel_id=1, source_target_pairs={{0,8},{4,12},{8,0},{12,4},{16,24},{20,28},{24,16},{28,20},{1,9},{5... | collective-permute-start | bytes 1228808 | tf_op jit(solution)/shard_map/ppermute | solution.py:107
  95.1 2.0 %collective-permute-start.22 = (bf16[64,640]{1,0:T(8,128)(2,1)S(1)}, bf16[64,640]{1,0:T(8,128)(2,1)S(1)}, u32[]{:S(2)}, u32[]{:S(2)}) collective-permute-start(bf16[64,640]{1,0:T(8,128)(2,1)S(1)} %get-tuple-element.48), channel_id=1, source_target_pairs={{0,1},{1,0},{2,3},{3,2},{4,5},{5,4},{6,7},{7,6},{8,9},{9,8},{10,11... | collective-permute-start | bytes 245768 | tf_op jit(solution)/shard_map/ppermute | solution.py:107
  95.2 5.0 %collective-permute-start.23 = (bf16[64,640]{1,0:T(8,128)(2,1)S(1)}, bf16[64,640]{1,0:T(8,128)(2,1)S(1)}, u32[]{:S(2)}, u32[]{:S(2)}) collective-permute-start(bf16[64,640]{1,0:T(8,128)(2,1)S(1)} %get-tuple-element.49), channel_id=1, source_target_pairs={{0,2},{1,3},{2,0},{3,1},{4,6},{5,7},{6,4},{7,5},{8,10},{9,11},{10,... | collective-permute-start | bytes 245768 | tf_op jit(solution)/shard_map/ppermute | solution.py:107
  96.9 4.7 %collective-permute-start.24 = (bf16[64,640]{1,0:T(8,128)(2,1)S(1)}, bf16[64,640]{1,0:T(8,128)(2,1)S(1)}, u32[]{:S(2)}, u32[]{:S(2)}) collective-permute-start(bf16[64,640]{1,0:T(8,128)(2,1)S(1)} %get-tuple-element.50), channel_id=1, source_target_pairs={{0,3},{1,2},{2,1},{3,0},{4,7},{5,6},{6,5},{7,4},{8,11},{9,10},{10,... | collective-permute-start | bytes 245768 | tf_op jit(solution)/shard_map/ppermute | solution.py:107
  (3 other events, 17.4 us)

commit v14 on v13

--- a/solution.py
+++ b/solution.py
@@ -281,7 +281,7 @@
     first_far = swap(first, "dp", 4)
     first_far_y = swap(after(first_far, (near, beside)), "dp", 1)
     first_last = swap(first_far, "dp", 2)
-    corner = swap(after(beside, first_last), "dp", 2)
+    corner = swap(after(beside[0:2], first_last), "dp", 2)
     second_far = swap(after(second, first_far), "dp", 4)
 
     marks = jnp.pad(segments.astype(bf16), ((0, 15), (0, width - rows)))
@@ -293,11 +293,12 @@
 
     second_far_y = swap(second_far, "dp", 1)
     second_last = swap(second_far, "dp", 2)
+    other_corner = swap(beside[2:4], "dp", 2)
     blocks = [
-        [heads, near, far, last, beside, corner, far_y, swap(after(last, corner), "dp", 1)]
-        for far, last, far_y in (
-            (first_far, first_last, first_far_y),
-            (second_far, second_last, second_far_y),
+        [heads, near, far, last, beside, part, far_y, swap(after(last, corner), "dp", 1)]
+        for far, last, far_y, part in (
+            (first_far, first_last, first_far_y, corner),
+            (second_far, second_last, second_far_y, other_corner),
         )
     ]
 

time: 115 us -> 113 us (0.983)
  waiting for transfers between devices: 57.3 us -> 53.2 us
  starting transfers between devices: 28 us -> 30.4 us
  other arithmetic: 3.94 us -> 5.38 us
  blocking collectives: 11.8 us -> 10.5 us
    ppermute x25 -> x26, waiting for transfers between devices: 57.3 us -> 53.2 us  [swap(): lax.ppermute(value, axis, [(i, i ^ k) for i in range(lax.axis_size(axis))])]
    ppermute x25 -> x26, starting transfers between devices: 24.5 us -> 26.8 us  [swap(): lax.ppermute(value, axis, [(i, i ^ k) for i in range(lax.axis_size(axis))])]
    all_to_all x1, blocking collectives: 11.8 us -> 10.5 us  [by_permutes(): lax.all_to_all(packed.reshape(n_dp, 2 * capacity, half), 'dp', split_axis...]
  transfers between devices with their start and end apart: 26 -> 27, of which waited for: 15 -> 14; matrix products, arithmetic and copies ran while one was open for 3% -> 4% of each run, Pallas kernels for 6% -> 6%
where the time goes in v14:
time: 113 us
  waiting for transfers between devices  53.2 us (47%)
  starting transfers between devices  30.4 us (27%)
  Pallas kernels  11.5 us (10%)
  blocking collectives  10.5 us (9%)
  other arithmetic  5.38 us (5%)
  local copies, waits for them, and re-layouts  1.59 us (1%)
    ppermute x26, waiting for transfers between devices, swap(): lax.ppermute(value, axis, [(i, i ^ k) for i in range(lax.axis_size(axis))])  53.2 us
    ppermute x26, starting transfers between devices, swap(): lax.ppermute(value, axis, [(i, i ^ k) for i in range(lax.axis_size(axis))])  26.8 us
    pallas_call x7, Pallas kernels, call(): pl.pallas_call(kernel, out_shape=tuple(outs), in_specs=specs, out_specs=t...  11.5 us
    all_to_all x1, blocking collectives, by_permutes(): lax.all_to_all(packed.reshape(n_dp, 2 * capacity, half), 'dp', split_axis...  10.5 us
    all_to_all x1, starting transfers between devices, by_permutes(): lax.all_to_all(slices, ('dp', 'fsdp'), split_axis=0, concat_axis=0, tiled...  3.54 us
  transfers between devices with their start and end apart: 27, of which 14 were waited for; matrix products, arithmetic and copies ran while one was open for 4% of the time, Pallas kernels for 6%

profile of v14, /device:TPU:0, one launch (start us, length us, event | category | flops | bytes accessed | tf_op | source)
XLA Modules:
  0.0 112.7 jit_solution(1051432024161616993)
XLA Ops:
  0.0 1.2 %pad_maximum_fusion.refs_4_.refs_0_ = bf16[4,160,320]{2,1,0:T(8,128)(2,1)S(1)} fusion(bf16[1,160,320]{2,1,0:T(8,128)(2,1)} %bitcast.26, bf16[3,160,320]{2,1,0:T(8,128)(2,1)} %param.9), kind=kLoop, calls=%fused_computation.3 | loop fusion | flops 204800 | bytes 819200 | tf_op jit(solution)/shard_map/concatenate | solution.py:278
  1.2 3.0 %collective-permute-start.6 = (bf16[4,160,320]{2,1,0:T(8,128)(2,1)S(1)}, bf16[4,160,320]{2,1,0:T(8,128)(2,1)S(1)}, u32[]{:S(2)}, u32[]{:S(2)}) collective-permute-start(bf16[4,160,320]{2,1,0:T(8,128)(2,1)S(1)} %pad_maximum_fusion.refs_4_.refs_0_), channel_id=1, source_target_pairs={{0,4},{4,0},{8,12},{12,8},{16,20},{20,16},{24,28},{28,24},{1,5},{5... | collective-permute-start | bytes 1228808 | tf_op jit(solution)/shard_map/ppermute | solution.py:107
  4.3 1.6 %collective-permute-start.5 = (bf16[4,160,320]{2,1,0:T(8,128)(2,1)S(1)}, bf16[4,160,320]{2,1,0:T(8,128)(2,1)S(1)}, u32[]{:S(2)}, u32[]{:S(2)}) collective-permute-start(bf16[4,160,320]{2,1,0:T(8,128)(2,1)S(1)} %pad_maximum_fusion.refs_4_.refs_0_), channel_id=1, source_target_pairs={{0,8},{4,12},{8,0},{12,4},{16,24},{20,28},{24,16},{28,20},{1,9},{5... | collective-permute-start | bytes 1228808 | tf_op jit(solution)/shard_map/ppermute | solution.py:107
  5.9 1.6 %fusion.9 = (bf16[2,160,320]{2,1,0:T(8,128)(2,1)}, bf16[2,160,320]{2,1,0:T(8,128)(2,1)S(1)}) fusion(bf16[3,160,320]{2,1,0:T(8,128)(2,1)S(1)} %copy-done.1, bf16[1,160,320]{2,1,0:T(8,128)(2,1)} %bitcast.27), kind=kLoop, calls=%fused_computation.25 | loop fusion | flops 102400 | bytes 1126400 | tf_op jit(solution)/shard_map/slice | solution.py:280
  7.5 2.6 %collective-permute-start = (bf16[2,160,320]{2,1,0:T(8,128)(2,1)}, bf16[2,160,320]{2,1,0:T(8,128)(2,1)S(1)}, u32[]{:S(2)}, u32[]{:S(2)}) collective-permute-start(bf16[2,160,320]{2,1,0:T(8,128)(2,1)} %get-tuple-element.55), channel_id=1, source_target_pairs={{0,16},{4,20},{8,24},{12,28},{16,0},{20,4},{24,8},{28,12},{1,17},{... | collective-permute-start | bytes 614408 | tf_op jit(solution)/shard_map/ppermute | solution.py:107
  10.2 1.6 %collective-permute-start.4 = (bf16[144,1280]{1,0:T(8,128)(2,1)S(1)}, bf16[144,1280]{1,0:T(8,128)(2,1)S(1)}, u32[]{:S(2)}, u32[]{:S(2)}) collective-permute-start(bf16[144,1280]{1,0:T(8,128)(2,1)S(1)} %fusion.2.refs_0_.tokens_ref), channel_id=1, source_target_pairs={{0,2},{1,3},{2,0},{3,1},{4,6},{5,7},{6,4},{7,5},{8,10},{9,11},{10,... | collective-permute-start | bytes 1105928 | tf_op jit(solution)/shard_map/ppermute | solution.py:107
  11.8 9.7 %collective-permute-done.refs_6_ = bf16[2,160,320]{2,1,0:T(8,128)(2,1)S(1)} collective-permute-done((bf16[2,160,320]{2,1,0:T(8,128)(2,1)}, bf16[2,160,320]{2,1,0:T(8,128)(2,1)S(1)}, u32[]{:S(2)}, u32[]{:S(2)}) %collective-permute-start) | collective-permute-done | bytes 204832 | tf_op jit(solution)/shard_map/ppermute | solution.py:107
  21.4 3.3 %collective-permute-start.1 = (bf16[2,160,320]{2,1,0:T(8,128)(2,1)S(1)}, bf16[2,160,320]{2,1,0:T(8,128)(2,1)S(1)}, u32[]{:S(2)}, u32[]{:S(2)}) collective-permute-start(bf16[2,160,320]{2,1,0:T(8,128)(2,1)S(1)} %get-tuple-element.28), channel_id=1, source_target_pairs={{0,16},{4,20},{8,24},{12,28},{16,0},{20,4},{24,8},{28,12},{1,17},{... | collective-permute-start | bytes 614408 | tf_op jit(solution)/shard_map/ppermute | solution.py:107
  25.4 9.4 %collective-permute-done.1.refs_2_ = bf16[2,160,320]{2,1,0:T(8,128)(2,1)S(1)} collective-permute-done((bf16[2,160,320]{2,1,0:T(8,128)(2,1)S(1)}, bf16[2,160,320]{2,1,0:T(8,128)(2,1)S(1)}, u32[]{:S(2)}, u32[]{:S(2)}) %collective-permute-start.1) | collective-permute-done | bytes 204832 | tf_op jit(solution)/shard_map/ppermute | solution.py:107
  35.4 1.2 %collective-permute-start.11 = (bf16[2,160,320]{2,1,0:T(8,128)(2,1)S(1)}, bf16[2,160,320]{2,1,0:T(8,128)(2,1)S(1)}, u32[]{:S(2)}, u32[]{:S(2)}) collective-permute-start(bf16[2,160,320]{2,1,0:T(8,128)(2,1)S(1)} %get-tuple-element.35), channel_id=1, source_target_pairs={{0,8},{4,12},{8,0},{12,4},{16,24},{20,28},{24,16},{28,20},{1,9},{5... | collective-permute-start | bytes 614408 | tf_op jit(solution)/shard_map/ppermute | solution.py:107
  37.1 5.0 %collective-permute-done.2.refs_6_ = bf16[2,160,320]{2,1,0:T(8,128)(2,1)S(1)} collective-permute-done((bf16[2,160,320]{2,1,0:T(8,128)(2,1)S(1)}, bf16[2,160,320]{2,1,0:T(8,128)(2,1)S(1)}, u32[]{:S(2)}, u32[]{:S(2)}) %collective-permute-start.2) | collective-permute-done | bytes 204832 | tf_op jit(solution)/shard_map/ppermute | solution.py:107
  43.0 1.7 %collective-permute-start.12 = (bf16[2,160,320]{2,1,0:T(8,128)(2,1)S(1)}, bf16[2,160,320]{2,1,0:T(8,128)(2,1)S(1)}, u32[]{:S(2)}, u32[]{:S(2)}) collective-permute-start(bf16[2,160,320]{2,1,0:T(8,128)(2,1)S(1)} %collective-permute-done.8.refs_7_), channel_id=1, source_target_pairs={{0,4},{4,0},{8,12},{12,8},{16,20},{20,16},{24,28},{28,24},{1,5},{5... | collective-permute-start | bytes 614408 | tf_op jit(solution)/shard_map/ppermute | solution.py:107
  44.7 6.2 %collective-permute-done.13.refs_3_ = bf16[2,160,320]{2,1,0:T(8,128)(2,1)S(1)} collective-permute-done((bf16[2,160,320]{2,1,0:T(8,128)(2,1)S(1)}, bf16[2,160,320]{2,1,0:T(8,128)(2,1)S(1)}, u32[]{:S(2)}, u32[]{:S(2)}) %collective-permute-start.13) | collective-permute-done | bytes 204832 | tf_op jit(solution)/shard_map/ppermute | solution.py:107
  51.0 1.6 %collective-permute-start.15 = (bf16[2,160,320]{2,1,0:T(8,128)(2,1)S(1)}, bf16[2,160,320]{2,1,0:T(8,128)(2,1)S(1)}, u32[]{:S(2)}, u32[]{:S(2)}) collective-permute-start(bf16[2,160,320]{2,1,0:T(8,128)(2,1)S(1)} %collective-permute-done.13.refs_3_), channel_id=1, source_target_pairs={{0,4},{4,0},{8,12},{12,8},{16,20},{20,16},{24,28},{28,24},{1,5},{5... | collective-permute-start | bytes 614408 | tf_op jit(solution)/shard_map/ppermute | solution.py:107
  52.6 0.9 shard_map.82.rows_ref
  53.7 3.0 %shard_map.83 = (bf16[4,512,512]{2,1,0:T(8,128)(2,1)S(1)}, f32[4,512,1]{2,1,0:T(8,128)S(1)}) custom-call(s32[1]{0:T(128)} %bitcast.7.me_ref, bf16[512,1280]{1,0:T(8,128)(2,1)S(1)} %shard_map.82.rows_ref, bf16[144,1280]{1,0:T(8,128)(2,1)S(1)} %fusion.2.refs_0_.tokens_ref, bf16[144,1280]{1,0:T(8,128)(2,1)S(1)} %collective-permute-done.4.refs_1_, ...), custom_call_target="tpu_custom_call" | custom-call | flops 1006632960 | bytes 7143428 | tf_op jit(solution)/shard_map/pallas_call | solution.py:129
  57.2 3.0 %shard_map.84 = (f32[256,1280]{1,0:T(8,128)S(1)}, bf16[128,1280]{1,0:T(8,128)(2,1)}, bf16[128,1280]{1,0:T(8,128)(2,1)S(1)}) custom-call(s32[1]{0:T(128)} %bitcast.7.me_ref, bf16[512,1280]{1,0:T(8,128)(2,1)S(1)} %shard_map.82.rows_ref, bf16[4,512,512]{2,1,0:T(8,128)(2,1)S(1)} %get-tuple-element.37.weights_ref, f32[4,512,1]{2,1,0:T(8,128)S(1)} %get-tuple-element.38.totals_ref, ...), custom_call_target="tpu_custom_call" | custom-call | flops 1006632960 | bytes 7634948 | tf_op jit(solution)/shard_map/pallas_call | solution.py:129
  60.8 2.0 %collective-permute-start.20 = (bf16[320,640]{1,0:T(8,128)(2,1)S(1)}, bf16[320,640]{1,0:T(8,128)(2,1)S(1)}, u32[]{:S(2)}, u32[]{:S(2)}) collective-permute-start(bf16[320,640]{1,0:T(8,128)(2,1)S(1)} %pad_maximum_fusion.1.refs_0_), channel_id=1, source_target_pairs={{0,8},{4,12},{8,0},{12,4},{16,24},{20,28},{24,16},{28,20},{1,9},{5... | collective-permute-start | bytes 1228808 | tf_op jit(solution)/shard_map/ppermute | solution.py:107
  62.8 1.6 %collective-permute-start.21 = (bf16[320,640]{1,0:T(8,128)(2,1)S(1)}, bf16[320,640]{1,0:T(8,128)(2,1)S(1)}, u32[]{:S(2)}, u32[]{:S(2)}) collective-permute-start(bf16[320,640]{1,0:T(8,128)(2,1)S(1)} %pad_maximum_fusion.1.refs_0_), channel_id=1, source_target_pairs={{0,16},{4,20},{8,24},{12,28},{16,0},{20,4},{24,8},{28,12},{1,17},{... | collective-permute-start | bytes 1228808 | tf_op jit(solution)/shard_map/ppermute | solution.py:107
  64.4 0.8 shard_map.85
  65.2 1.5 %collective-permute-start.18 = (bf16[64,1280]{1,0:T(8,128)(2,1)}, bf16[64,1280]{1,0:T(8,128)(2,1)S(1)}, u32[]{:S(2)}, u32[]{:S(2)}) collective-permute-start(bf16[64,1280]{1,0:T(8,128)(2,1)} %get-tuple-element.43), channel_id=1, source_target_pairs={{0,2},{1,3},{2,0},{3,1},{4,6},{5,7},{6,4},{7,5},{8,10},{9,11},{10,... | collective-permute-start | bytes 491528 | tf_op jit(solution)/shard_map/ppermute | solution.py:107
  68.8 3.7 %collective-permute-done.18.refs_0_ = bf16[64,1280]{1,0:T(8,128)(2,1)S(1)} collective-permute-done((bf16[64,1280]{1,0:T(8,128)(2,1)}, bf16[64,1280]{1,0:T(8,128)(2,1)S(1)}, u32[]{:S(2)}, u32[]{:S(2)}) %collective-permute-start.18) | collective-permute-done | bytes 163872 | tf_op jit(solution)/shard_map/ppermute | solution.py:107
  72.5 2.0 %collective-permute-done.19.refs_1_ = bf16[64,1280]{1,0:T(8,128)(2,1)} collective-permute-done((bf16[64,1280]{1,0:T(8,128)(2,1)}, bf16[64,1280]{1,0:T(8,128)(2,1)}, u32[]{:S(2)}, u32[]{:S(2)}) %collective-permute-start.19) | collective-permute-done | bytes 163872 | tf_op jit(solution)/shard_map/ppermute | solution.py:107
  74.6 2.6 %shard_map.86 = bf16[8,64,640]{2,1,0:T(8,128)(2,1)} custom-call(bf16[144,1280]{1,0:T(8,128)(2,1)S(1)} %fusion.2.refs_0_.tokens_ref, f32[256,1280]{1,0:T(8,128)S(1)} %get-tuple-element.40.keep_ref, bf16[128,1280]{1,0:T(8,128)(2,1)S(1)} %collective-permute-done.16.core_ref, f32[2,1280]{1,0:T(2,128)S(1)} %copy-done, s32[128,1]{1,0:T(8,128)S(1)} %reshape.41.order_ref, ...), custom_call_target="tpu_custom_call" | custom-call | bytes 1 | tf_op jit(solution)/shard_map/pallas_call | solution.py:129
  77.1 3.5 %all-to-all-start = ((bf16[8,64,640]{2,1,0:T(8,128)(2,1)}), bf16[8,64,640]{2,1,0:T(8,128)(2,1)S(1)}, u32[]{:S(2)}, u32[]{:S(2)}) async-start(bf16[8,64,640]{2,1,0:T(8,128)(2,1)} %shard_map.86), calls=%async_computation | async-start | bytes 1310720 | tf_op jit(solution)/shard_map/all_to_all | solution.py:357
  80.7 2.9 %collective-permute-done.21.refs_2_ = bf16[320,640]{1,0:T(8,128)(2,1)S(1)} collective-permute-done((bf16[320,640]{1,0:T(8,128)(2,1)S(1)}, bf16[320,640]{1,0:T(8,128)(2,1)S(1)}, u32[]{:S(2)}, u32[]{:S(2)}) %collective-permute-start.21) | collective-permute-done | bytes 409632 | tf_op jit(solution)/shard_map/ppermute | solution.py:107
  85.2 8.7 %collective-permute-done.22.refs_3_ = bf16[320,640]{1,0:T(8,128)(2,1)S(1)} collective-permute-done((bf16[320,640]{1,0:T(8,128)(2,1)S(1)}, bf16[320,640]{1,0:T(8,128)(2,1)S(1)}, u32[]{:S(2)}, u32[]{:S(2)}) %collective-permute-start.22) | collective-permute-done | bytes 409632 | tf_op jit(solution)/shard_map/ppermute | solution.py:107
  93.9 1.1 shard_map.87
  95.0 1.6 %collective-permute-start.24 = (bf16[64,640]{1,0:T(8,128)(2,1)S(1)}, bf16[64,640]{1,0:T(8,128)(2,1)S(1)}, u32[]{:S(2)}, u32[]{:S(2)}) collective-permute-start(bf16[64,640]{1,0:T(8,128)(2,1)S(1)} %get-tuple-element.49), channel_id=1, source_target_pairs={{0,2},{1,3},{2,0},{3,1},{4,6},{5,7},{6,4},{7,5},{8,10},{9,11},{10,... | collective-permute-start | bytes 245768 | tf_op jit(solution)/shard_map/ppermute | solution.py:107
  97.0 3.2 %collective-permute-done.24.two_ref = bf16[64,640]{1,0:T(8,128)(2,1)S(1)} collective-permute-done((bf16[64,640]{1,0:T(8,128)(2,1)S(1)}, bf16[64,640]{1,0:T(8,128)(2,1)S(1)}, u32[]{:S(2)}, u32[]{:S(2)}) %collective-permute-start.24) | collective-permute-done | bytes 81952 | tf_op jit(solution)/shard_map/ppermute | solution.py:107
  100.2 1.1 collective-permute-done.25.three_ref
  101.5 10.5 %all_to_all.10 = bf16[8,16,640]{2,1,0:T(8,128)(2,1)S(1)} all-to-all(bf16[8,16,640]{2,1,0:T(8,128)(2,1)S(1)} %bitcast.24), channel_id=1, replica_groups=mesh['dp'=8,'fsdp'=4] {'dp'}, dimensions={0} | all-to-all | bytes 327680 | tf_op jit(solution)/shard_map/all_to_all | solution.py:382
  (68 shorter events, 9.0 us)
Async XLA Ops:
  0.0 10.1 %copy-start.6 = (s32[1,128]{1,0:T(1,128)S(1)}, s32[1,128]{1,0:T(1,128)}, u32[]{:S(2)}) copy-start(s32[1,128]{1,0:T(1,128)} %param.13) | copy-start | bytes 1540
  0.0 10.1 %copy-start.3 = (bf16[128,1280]{1,0:T(8,128)(2,1)S(1)}, bf16[128,1280]{1,0:T(8,128)(2,1)}, u32[]{:S(2)}) copy-start(bf16[128,1280]{1,0:T(8,128)(2,1)} %param.8) | copy-start | bytes 983044
  0.0 11.7 %copy-start.2 = (bf16[160,1280]{1,0:T(8,128)(2,1)S(1)}, bf16[160,1280]{1,0:T(8,128)(2,1)}, u32[]{:S(2)}) copy-start(bf16[160,1280]{1,0:T(8,128)(2,1)} %param.11) | copy-start | bytes 1228804
  1.2 23.5 %copy-start.5 = (s32[32,1]{0,1:T(1,128)S(1)}, s32[32,1]{0,1:T(1,128)}, u32[]{:S(2)}) copy-start(s32[32,1]{0,1:T(1,128)} %param.15) | copy-start | bytes 388
  1.2 23.7 %collective-permute-start.6 = (bf16[4,160,320]{2,1,0:T(8,128)(2,1)S(1)}, bf16[4,160,320]{2,1,0:T(8,128)(2,1)S(1)}, u32[]{:S(2)}, u32[]{:S(2)}) collective-permute-start(bf16[4,160,320]{2,1,0:T(8,128)(2,1)S(1)} %pad_maximum_fusion.refs_4_.refs_0_), channel_id=1, source_target_pairs={{0,4},{4,0},{8,12},{12,8},{16,20},{20,16},{24,28},{28,24},{1,5},{5... | collective-permute-start | bytes 1228808 | tf_op jit(solution)/shard_map/ppermute | solution.py:107
  4.3 20.6 %collective-permute-start.5 = (bf16[4,160,320]{2,1,0:T(8,128)(2,1)S(1)}, bf16[4,160,320]{2,1,0:T(8,128)(2,1)S(1)}, u32[]{:S(2)}, u32[]{:S(2)}) collective-permute-start(bf16[4,160,320]{2,1,0:T(8,128)(2,1)S(1)} %pad_maximum_fusion.refs_4_.refs_0_), channel_id=1, source_target_pairs={{0,8},{4,12},{8,0},{12,4},{16,24},{20,28},{24,16},{28,20},{1,9},{5... | collective-permute-start | bytes 1228808 | tf_op jit(solution)/shard_map/ppermute | solution.py:107
  7.5 13.9 %collective-permute-start = (bf16[2,160,320]{2,1,0:T(8,128)(2,1)}, bf16[2,160,320]{2,1,0:T(8,128)(2,1)S(1)}, u32[]{:S(2)}, u32[]{:S(2)}) collective-permute-start(bf16[2,160,320]{2,1,0:T(8,128)(2,1)} %get-tuple-element.55), channel_id=1, source_target_pairs={{0,16},{4,20},{8,24},{12,28},{16,0},{20,4},{24,8},{28,12},{1,17},{... | collective-permute-start | bytes 614408 | tf_op jit(solution)/shard_map/ppermute | solution.py:107
  10.1 42.5 %copy-start = (f32[2,1280]{1,0:T(2,128)S(1)}, f32[2,1280]{1,0:T(2,128)}, u32[]{:S(2)}) copy-start(f32[2,1280]{1,0:T(2,128)} %gains_ref.3) | copy-start | bytes 30724
  10.2 26.4 %collective-permute-start.4 = (bf16[144,1280]{1,0:T(8,128)(2,1)S(1)}, bf16[144,1280]{1,0:T(8,128)(2,1)S(1)}, u32[]{:S(2)}, u32[]{:S(2)}) collective-permute-start(bf16[144,1280]{1,0:T(8,128)(2,1)S(1)} %fusion.2.refs_0_.tokens_ref), channel_id=1, source_target_pairs={{0,2},{1,3},{2,0},{3,1},{4,6},{5,7},{6,4},{7,5},{8,10},{9,11},{10,... | collective-permute-start | bytes 1105928 | tf_op jit(solution)/shard_map/ppermute | solution.py:107
  21.4 13.4 %collective-permute-start.1 = (bf16[2,160,320]{2,1,0:T(8,128)(2,1)S(1)}, bf16[2,160,320]{2,1,0:T(8,128)(2,1)S(1)}, u32[]{:S(2)}, u32[]{:S(2)}) collective-permute-start(bf16[2,160,320]{2,1,0:T(8,128)(2,1)S(1)} %get-tuple-element.28), channel_id=1, source_target_pairs={{0,16},{4,20},{8,24},{12,28},{16,0},{20,4},{24,8},{28,12},{1,17},{... | collective-permute-start | bytes 614408 | tf_op jit(solution)/shard_map/ppermute | solution.py:107
  24.7 10.6 %collective-permute-start.8 = (bf16[2,160,320]{2,1,0:T(8,128)(2,1)S(1)}, bf16[2,160,320]{2,1,0:T(8,128)(2,1)S(1)}, u32[]{:S(2)}, u32[]{:S(2)}) collective-permute-start(bf16[2,160,320]{2,1,0:T(8,128)(2,1)S(1)} %collective-permute-done.refs_6_), channel_id=1, source_target_pairs={{0,8},{4,12},{8,0},{12,4},{16,24},{20,28},{24,16},{28,20},{1,9},{5... | collective-permute-start | bytes 614408 | tf_op jit(solution)/shard_map/ppermute | solution.py:107
  24.9 11.6 %collective-permute-start.7 = (bf16[2,160,320]{2,1,0:T(8,128)(2,1)S(1)}, bf16[2,160,320]{2,1,0:T(8,128)(2,1)S(1)}, u32[]{:S(2)}, u32[]{:S(2)}) collective-permute-start(bf16[2,160,320]{2,1,0:T(8,128)(2,1)S(1)} %collective-permute-done.refs_6_), channel_id=1, source_target_pairs={{0,4},{4,0},{8,12},{12,8},{16,20},{20,16},{24,28},{28,24},{1,5},{5... | collective-permute-start | bytes 614408 | tf_op jit(solution)/shard_map/ppermute | solution.py:107
  34.8 7.3 %collective-permute-start.2 = (bf16[2,160,320]{2,1,0:T(8,128)(2,1)S(1)}, bf16[2,160,320]{2,1,0:T(8,128)(2,1)S(1)}, u32[]{:S(2)}, u32[]{:S(2)}) collective-permute-start(bf16[2,160,320]{2,1,0:T(8,128)(2,1)S(1)} %collective-permute-done.1.refs_2_), channel_id=1, source_target_pairs={{0,4},{4,0},{8,12},{12,8},{16,20},{20,16},{24,28},{28,24},{1,5},{5... | collective-permute-start | bytes 614408 | tf_op jit(solution)/shard_map/ppermute | solution.py:107
  35.4 7.6 %collective-permute-start.11 = (bf16[2,160,320]{2,1,0:T(8,128)(2,1)S(1)}, bf16[2,160,320]{2,1,0:T(8,128)(2,1)S(1)}, u32[]{:S(2)}, u32[]{:S(2)}) collective-permute-start(bf16[2,160,320]{2,1,0:T(8,128)(2,1)S(1)} %get-tuple-element.35), channel_id=1, source_target_pairs={{0,8},{4,12},{8,0},{12,4},{16,24},{20,28},{24,16},{28,20},{1,9},{5... | collective-permute-start | bytes 614408 | tf_op jit(solution)/shard_map/ppermute | solution.py:107
  36.5 16.1 %collective-permute-start.10 = (bf16[144,1280]{1,0:T(8,128)(2,1)S(1)}, bf16[144,1280]{1,0:T(8,128)(2,1)S(1)}, u32[]{:S(2)}, u32[]{:S(2)}) collective-permute-start(bf16[144,1280]{1,0:T(8,128)(2,1)S(1)} %collective-permute-done.4.refs_1_), channel_id=1, source_target_pairs={{0,1},{1,0},{2,3},{3,2},{4,5},{5,4},{6,7},{7,6},{8,9},{9,8},{10,11... | collective-permute-start | bytes 1105928 | tf_op jit(solution)/shard_map/ppermute | solution.py:107
  36.6 16.1 %collective-permute-start.9 = (bf16[144,1280]{1,0:T(8,128)(2,1)S(1)}, bf16[144,1280]{1,0:T(8,128)(2,1)S(1)}, u32[]{:S(2)}, u32[]{:S(2)}) collective-permute-start(bf16[144,1280]{1,0:T(8,128)(2,1)S(1)} %fusion.2.refs_0_.tokens_ref), channel_id=1, source_target_pairs={{0,1},{1,0},{2,3},{3,2},{4,5},{5,4},{6,7},{7,6},{8,9},{9,8},{10,11... | collective-permute-start | bytes 1105928 | tf_op jit(solution)/shard_map/ppermute | solution.py:107
  42.1 8.9 %collective-permute-start.3 = (bf16[176,640]{1,0:T(8,128)(2,1)S(1)}, bf16[176,640]{1,0:T(8,128)(2,1)S(1)}, u32[]{:S(2)}, u32[]{:S(2)}) collective-permute-start(bf16[176,640]{1,0:T(8,128)(2,1)S(1)} %fusion.4), channel_id=1, source_target_pairs={{0,4},{4,0},{8,12},{12,8},{16,20},{20,16},{24,28},{28,24},{1,5},{5... | collective-permute-start | bytes 675848 | tf_op jit(solution)/shard_map/ppermute | solution.py:107
  42.6 8.4 %collective-permute-start.13 = (bf16[2,160,320]{2,1,0:T(8,128)(2,1)S(1)}, bf16[2,160,320]{2,1,0:T(8,128)(2,1)S(1)}, u32[]{:S(2)}, u32[]{:S(2)}) collective-permute-start(bf16[2,160,320]{2,1,0:T(8,128)(2,1)S(1)} %collective-permute-done.1.refs_2_), channel_id=1, source_target_pairs={{0,8},{4,12},{8,0},{12,4},{16,24},{20,28},{24,16},{28,20},{1,9},{5... | collective-permute-start | bytes 614408 | tf_op jit(solution)/shard_map/ppermute | solution.py:107
  43.0 10.7 %collective-permute-start.12 = (bf16[2,160,320]{2,1,0:T(8,128)(2,1)S(1)}, bf16[2,160,320]{2,1,0:T(8,128)(2,1)S(1)}, u32[]{:S(2)}, u32[]{:S(2)}) collective-permute-start(bf16[2,160,320]{2,1,0:T(8,128)(2,1)S(1)} %collective-permute-done.8.refs_7_), channel_id=1, source_target_pairs={{0,4},{4,0},{8,12},{12,8},{16,20},{20,16},{24,28},{28,24},{1,5},{5... | collective-permute-start | bytes 614408 | tf_op jit(solution)/shard_map/ppermute | solution.py:107
  51.0 6.2 %collective-permute-start.14 = (bf16[2,160,320]{2,1,0:T(8,128)(2,1)S(1)}, bf16[2,160,320]{2,1,0:T(8,128)(2,1)S(1)}, u32[]{:S(2)}, u32[]{:S(2)}) collective-permute-start(bf16[2,160,320]{2,1,0:T(8,128)(2,1)S(1)} %get-tuple-element.51), channel_id=1, source_target_pairs={{0,8},{4,12},{8,0},{12,4},{16,24},{20,28},{24,16},{28,20},{1,9},{5... | collective-permute-start | bytes 614408 | tf_op jit(solution)/shard_map/ppermute | solution.py:107
  51.0 6.3 %collective-permute-start.15 = (bf16[2,160,320]{2,1,0:T(8,128)(2,1)S(1)}, bf16[2,160,320]{2,1,0:T(8,128)(2,1)S(1)}, u32[]{:S(2)}, u32[]{:S(2)}) collective-permute-start(bf16[2,160,320]{2,1,0:T(8,128)(2,1)S(1)} %collective-permute-done.13.refs_3_), channel_id=1, source_target_pairs={{0,4},{4,0},{8,12},{12,8},{16,20},{20,16},{24,28},{28,24},{1,5},{5... | collective-permute-start | bytes 614408 | tf_op jit(solution)/shard_map/ppermute | solution.py:107
  60.2 4.2 %collective-permute-start.17 = (bf16[128,1280]{1,0:T(8,128)(2,1)S(1)}, bf16[128,1280]{1,0:T(8,128)(2,1)S(1)}, u32[]{:S(2)}, u32[]{:S(2)}) collective-permute-start(bf16[128,1280]{1,0:T(8,128)(2,1)S(1)} %get-tuple-element.42), channel_id=1, source_target_pairs={{0,1},{1,0},{2,3},{3,2},{4,5},{5,4},{6,7},{7,6},{8,9},{9,8},{10,11... | collective-permute-start | bytes 983048 | tf_op jit(solution)/shard_map/ppermute | solution.py:107
  60.2 8.6 %collective-permute-start.16 = (bf16[128,1280]{1,0:T(8,128)(2,1)}, bf16[128,1280]{1,0:T(8,128)(2,1)S(1)}, u32[]{:S(2)}, u32[]{:S(2)}) collective-permute-start(bf16[128,1280]{1,0:T(8,128)(2,1)} %get-tuple-element.41), channel_id=1, source_target_pairs={{0,1},{1,0},{2,3},{3,2},{4,5},{5,4},{6,7},{7,6},{8,9},{9,8},{10,11... | collective-permute-start | bytes 983048 | tf_op jit(solution)/shard_map/ppermute | solution.py:107
  60.8 19.9 %collective-permute-start.20 = (bf16[320,640]{1,0:T(8,128)(2,1)S(1)}, bf16[320,640]{1,0:T(8,128)(2,1)S(1)}, u32[]{:S(2)}, u32[]{:S(2)}) collective-permute-start(bf16[320,640]{1,0:T(8,128)(2,1)S(1)} %pad_maximum_fusion.1.refs_0_), channel_id=1, source_target_pairs={{0,8},{4,12},{8,0},{12,4},{16,24},{20,28},{24,16},{28,20},{1,9},{5... | collective-permute-start | bytes 1228808 | tf_op jit(solution)/shard_map/ppermute | solution.py:107
  62.8 20.8 %collective-permute-start.21 = (bf16[320,640]{1,0:T(8,128)(2,1)S(1)}, bf16[320,640]{1,0:T(8,128)(2,1)S(1)}, u32[]{:S(2)}, u32[]{:S(2)}) collective-permute-start(bf16[320,640]{1,0:T(8,128)(2,1)S(1)} %pad_maximum_fusion.1.refs_0_), channel_id=1, source_target_pairs={{0,16},{4,20},{8,24},{12,28},{16,0},{20,4},{24,8},{28,12},{1,17},{... | collective-permute-start | bytes 1228808 | tf_op jit(solution)/shard_map/ppermute | solution.py:107
  65.2 7.3 %collective-permute-start.18 = (bf16[64,1280]{1,0:T(8,128)(2,1)}, bf16[64,1280]{1,0:T(8,128)(2,1)S(1)}, u32[]{:S(2)}, u32[]{:S(2)}) collective-permute-start(bf16[64,1280]{1,0:T(8,128)(2,1)} %get-tuple-element.43), channel_id=1, source_target_pairs={{0,2},{1,3},{2,0},{3,1},{4,6},{5,7},{6,4},{7,5},{8,10},{9,11},{10,... | collective-permute-start | bytes 491528 | tf_op jit(solution)/shard_map/ppermute | solution.py:107
  66.7 7.9 %collective-permute-start.19 = (bf16[64,1280]{1,0:T(8,128)(2,1)}, bf16[64,1280]{1,0:T(8,128)(2,1)}, u32[]{:S(2)}, u32[]{:S(2)}) collective-permute-start(bf16[64,1280]{1,0:T(8,128)(2,1)} %get-tuple-element.44), channel_id=1, source_target_pairs={{0,2},{1,3},{2,0},{3,1},{4,6},{5,7},{6,4},{7,5},{8,10},{9,11},{10,... | collective-permute-start | bytes 491528 | tf_op jit(solution)/shard_map/ppermute | solution.py:107
  77.1 16.8 %all-to-all-start = ((bf16[8,64,640]{2,1,0:T(8,128)(2,1)}), bf16[8,64,640]{2,1,0:T(8,128)(2,1)S(1)}, u32[]{:S(2)}, u32[]{:S(2)}) async-start(bf16[8,64,640]{2,1,0:T(8,128)(2,1)} %shard_map.86), calls=%async_computation | async-start | bytes 1310720 | tf_op jit(solution)/shard_map/all_to_all | solution.py:357
  83.6 10.3 %collective-permute-start.22 = (bf16[320,640]{1,0:T(8,128)(2,1)S(1)}, bf16[320,640]{1,0:T(8,128)(2,1)S(1)}, u32[]{:S(2)}, u32[]{:S(2)}) collective-permute-start(bf16[320,640]{1,0:T(8,128)(2,1)S(1)} %collective-permute-done.21.refs_2_), channel_id=1, source_target_pairs={{0,8},{4,12},{8,0},{12,4},{16,24},{20,28},{24,16},{28,20},{1,9},{5... | collective-permute-start | bytes 1228808 | tf_op jit(solution)/shard_map/ppermute | solution.py:107
  94.9 2.0 %collective-permute-start.23 = (bf16[64,640]{1,0:T(8,128)(2,1)S(1)}, bf16[64,640]{1,0:T(8,128)(2,1)S(1)}, u32[]{:S(2)}, u32[]{:S(2)}) collective-permute-start(bf16[64,640]{1,0:T(8,128)(2,1)S(1)} %get-tuple-element.48), channel_id=1, source_target_pairs={{0,1},{1,0},{2,3},{3,2},{4,5},{5,4},{6,7},{7,6},{8,9},{9,8},{10,11... | collective-permute-start | bytes 245768 | tf_op jit(solution)/shard_map/ppermute | solution.py:107
  95.0 5.2 %collective-permute-start.24 = (bf16[64,640]{1,0:T(8,128)(2,1)S(1)}, bf16[64,640]{1,0:T(8,128)(2,1)S(1)}, u32[]{:S(2)}, u32[]{:S(2)}) collective-permute-start(bf16[64,640]{1,0:T(8,128)(2,1)S(1)} %get-tuple-element.49), channel_id=1, source_target_pairs={{0,2},{1,3},{2,0},{3,1},{4,6},{5,7},{6,4},{7,5},{8,10},{9,11},{10,... | collective-permute-start | bytes 245768 | tf_op jit(solution)/shard_map/ppermute | solution.py:107
  96.6 4.7 %collective-permute-start.25 = (bf16[64,640]{1,0:T(8,128)(2,1)S(1)}, bf16[64,640]{1,0:T(8,128)(2,1)S(1)}, u32[]{:S(2)}, u32[]{:S(2)}) collective-permute-start(bf16[64,640]{1,0:T(8,128)(2,1)S(1)} %get-tuple-element.50), channel_id=1, source_target_pairs={{0,3},{1,2},{2,1},{3,0},{4,7},{5,6},{6,5},{7,4},{8,11},{9,10},{10,... | collective-permute-start | bytes 245768 | tf_op jit(solution)/shard_map/ppermute | solution.py:107
  (3 other events, 22.6 us)

commit v15 on v14

--- a/solution.py
+++ b/solution.py
@@ -277,11 +277,12 @@
 
     heads = jnp.concatenate([qkv_weight, out_weight.T[None]], axis=0)
     near, beside = swap(heads, "dp", 2), swap(heads, "dp", 1)
-    first, second = heads[0:2], heads[2:4]
+    first = qkv_weight[0:2]
+    second = jnp.concatenate([qkv_weight[2:3], out_weight.T[None]], axis=0)
     first_far = swap(first, "dp", 4)
-    first_far_y = swap(after(first_far, (near, beside)), "dp", 1)
+    first_far_y = swap(after(first_far, beside), "dp", 1)
     first_last = swap(first_far, "dp", 2)
-    corner = swap(after(beside[0:2], first_last), "dp", 2)
+    corner = swap(after(beside[0:2], (first_last, near)), "dp", 2)
     second_far = swap(after(second, first_far), "dp", 4)
 
     marks = jnp.pad(segments.astype(bf16), ((0, 15), (0, width - rows)))
@@ -293,7 +294,7 @@
 
     second_far_y = swap(second_far, "dp", 1)
     second_last = swap(second_far, "dp", 2)
-    other_corner = swap(beside[2:4], "dp", 2)
+    other_corner = swap(after(beside[2:4], first_last), "dp", 2)
     blocks = [
         [heads, near, far, last, beside, part, far_y, swap(after(last, corner), "dp", 1)]
         for far, last, far_y, part in (

time: 113 us -> 113 us (level)
  local copies, waits for them, and re-layouts: 1.59 us -> 3.27 us
  other arithmetic: 5.38 us -> 3.89 us
    slice x1 -> x4, local copies, waits for them, and re-layouts: 0.05 us -> 1.71 us  [the longest x1 1.66 us: by_permutes(): first = qkv_weight[0:2]]
    slice x1 -> x0, other arithmetic: 1.64 us -> none  [by_permutes(): first, second = (heads[0:2], heads[2:4])]
  transfers between devices with their start and end apart: 27 -> 27, of which waited for: 14 -> 14; matrix products, arithmetic and copies ran while one was open for 4% -> 5% of each run, Pallas kernels for 6% -> 6%
where the time goes in v15:
time: 113 us
  waiting for transfers between devices  52.9 us (47%)
  starting transfers between devices  30.4 us (27%)
  Pallas kernels  11.5 us (10%)
  blocking collectives  10.5 us (9%)
  other arithmetic  3.89 us (3%)
  local copies, waits for them, and re-layouts  3.27 us (3%)
    ppermute x26, waiting for transfers between devices, swap(): lax.ppermute(value, axis, [(i, i ^ k) for i in range(lax.axis_size(axis))])  52.9 us
    ppermute x26, starting transfers between devices, swap(): lax.ppermute(value, axis, [(i, i ^ k) for i in range(lax.axis_size(axis))])  26.9 us
    pallas_call x7, Pallas kernels, call(): pl.pallas_call(kernel, out_shape=tuple(outs), in_specs=specs, out_specs=t...  11.5 us
    all_to_all x1, blocking collectives, by_permutes(): lax.all_to_all(packed.reshape(n_dp, 2 * capacity, half), 'dp', split_axis...  10.5 us
    all_to_all x1, starting transfers between devices, by_permutes(): lax.all_to_all(slices, ('dp', 'fsdp'), split_axis=0, concat_axis=0, tiled...  3.54 us
  transfers between devices with their start and end apart: 27, of which 14 were waited for; matrix products, arithmetic and copies ran while one was open for 5% of the time, Pallas kernels for 6%

profile of v15, /device:TPU:0, one launch (start us, length us, event | category | flops | bytes accessed | tf_op | source)
XLA Modules:
  0.0 112.6 jit_solution(8582561920385951162)
XLA Ops:
  0.0 1.2 %pad_maximum_fusion.refs_4_.refs_0_ = bf16[4,160,320]{2,1,0:T(8,128)(2,1)S(1)} fusion(bf16[1,160,320]{2,1,0:T(8,128)(2,1)} %bitcast.26, bf16[3,160,320]{2,1,0:T(8,128)(2,1)} %param.9), kind=kLoop, calls=%fused_computation.2 | loop fusion | flops 204800 | bytes 819200 | tf_op jit(solution)/shard_map/concatenate | solution.py:278
  1.2 3.0 %collective-permute-start.5 = (bf16[4,160,320]{2,1,0:T(8,128)(2,1)S(1)}, bf16[4,160,320]{2,1,0:T(8,128)(2,1)S(1)}, u32[]{:S(2)}, u32[]{:S(2)}) collective-permute-start(bf16[4,160,320]{2,1,0:T(8,128)(2,1)S(1)} %pad_maximum_fusion.refs_4_.refs_0_), channel_id=1, source_target_pairs={{0,4},{4,0},{8,12},{12,8},{16,20},{20,16},{24,28},{28,24},{1,5},{5... | collective-permute-start | bytes 1228808 | tf_op jit(solution)/shard_map/ppermute | solution.py:107
  4.3 1.6 %collective-permute-start.10 = (bf16[4,160,320]{2,1,0:T(8,128)(2,1)S(1)}, bf16[4,160,320]{2,1,0:T(8,128)(2,1)S(1)}, u32[]{:S(2)}, u32[]{:S(2)}) collective-permute-start(bf16[4,160,320]{2,1,0:T(8,128)(2,1)S(1)} %pad_maximum_fusion.refs_4_.refs_0_), channel_id=1, source_target_pairs={{0,8},{4,12},{8,0},{12,4},{16,24},{20,28},{24,16},{28,20},{1,9},{5... | collective-permute-start | bytes 1228808 | tf_op jit(solution)/shard_map/ppermute | solution.py:107
  5.9 1.7 %slice.27 = bf16[2,160,320]{2,1,0:T(8,128)(2,1)} slice(bf16[3,160,320]{2,1,0:T(8,128)(2,1)} %param.9), slice={[0:2], [0:160], [0:320]} | slice | bytes 409600 | tf_op jit(solution)/shard_map/slice | solution.py:280
  7.5 2.6 %collective-permute-start = (bf16[2,160,320]{2,1,0:T(8,128)(2,1)}, bf16[2,160,320]{2,1,0:T(8,128)(2,1)S(1)}, u32[]{:S(2)}, u32[]{:S(2)}) collective-permute-start(bf16[2,160,320]{2,1,0:T(8,128)(2,1)} %slice.27), channel_id=1, source_target_pairs={{0,16},{4,20},{8,24},{12,28},{16,0},{20,4},{24,8},{28,12},{1,17},{... | collective-permute-start | bytes 614408 | tf_op jit(solution)/shard_map/ppermute | solution.py:107
  10.2 1.6 %collective-permute-start.4 = (bf16[144,1280]{1,0:T(8,128)(2,1)S(1)}, bf16[144,1280]{1,0:T(8,128)(2,1)S(1)}, u32[]{:S(2)}, u32[]{:S(2)}) collective-permute-start(bf16[144,1280]{1,0:T(8,128)(2,1)S(1)} %fusion.2.refs_0_.tokens_ref), channel_id=1, source_target_pairs={{0,2},{1,3},{2,0},{3,1},{4,6},{5,7},{6,4},{7,5},{8,10},{9,11},{10,... | collective-permute-start | bytes 1105928 | tf_op jit(solution)/shard_map/ppermute | solution.py:107
  11.9 9.6 %collective-permute-done.refs_6_ = bf16[2,160,320]{2,1,0:T(8,128)(2,1)S(1)} collective-permute-done((bf16[2,160,320]{2,1,0:T(8,128)(2,1)}, bf16[2,160,320]{2,1,0:T(8,128)(2,1)S(1)}, u32[]{:S(2)}, u32[]{:S(2)}) %collective-permute-start) | collective-permute-done | bytes 204832 | tf_op jit(solution)/shard_map/ppermute | solution.py:107
  21.4 3.3 %collective-permute-start.1 = (bf16[2,160,320]{2,1,0:T(8,128)(2,1)S(1)}, bf16[2,160,320]{2,1,0:T(8,128)(2,1)S(1)}, u32[]{:S(2)}, u32[]{:S(2)}) collective-permute-start(bf16[2,160,320]{2,1,0:T(8,128)(2,1)S(1)} %pad_maximum_fusion.2), channel_id=1, source_target_pairs={{0,16},{4,20},{8,24},{12,28},{16,0},{20,4},{24,8},{28,12},{1,17},{... | collective-permute-start | bytes 614408 | tf_op jit(solution)/shard_map/ppermute | solution.py:107
  25.4 9.4 %collective-permute-done.1.refs_2_ = bf16[2,160,320]{2,1,0:T(8,128)(2,1)S(1)} collective-permute-done((bf16[2,160,320]{2,1,0:T(8,128)(2,1)S(1)}, bf16[2,160,320]{2,1,0:T(8,128)(2,1)S(1)}, u32[]{:S(2)}, u32[]{:S(2)}) %collective-permute-start.1) | collective-permute-done | bytes 204832 | tf_op jit(solution)/shard_map/ppermute | solution.py:107
  35.4 1.2 %collective-permute-start.11 = (bf16[2,160,320]{2,1,0:T(8,128)(2,1)S(1)}, bf16[2,160,320]{2,1,0:T(8,128)(2,1)S(1)}, u32[]{:S(2)}, u32[]{:S(2)}) collective-permute-start(bf16[2,160,320]{2,1,0:T(8,128)(2,1)S(1)} %get-tuple-element.36), channel_id=1, source_target_pairs={{0,8},{4,12},{8,0},{12,4},{16,24},{20,28},{24,16},{28,20},{1,9},{5... | collective-permute-start | bytes 614408 | tf_op jit(solution)/shard_map/ppermute | solution.py:107
  37.1 5.0 %collective-permute-done.2.refs_6_ = bf16[2,160,320]{2,1,0:T(8,128)(2,1)S(1)} collective-permute-done((bf16[2,160,320]{2,1,0:T(8,128)(2,1)S(1)}, bf16[2,160,320]{2,1,0:T(8,128)(2,1)S(1)}, u32[]{:S(2)}, u32[]{:S(2)}) %collective-permute-start.2) | collective-permute-done | bytes 204832 | tf_op jit(solution)/shard_map/ppermute | solution.py:107
  43.0 1.8 %collective-permute-start.12 = (bf16[2,160,320]{2,1,0:T(8,128)(2,1)S(1)}, bf16[2,160,320]{2,1,0:T(8,128)(2,1)S(1)}, u32[]{:S(2)}, u32[]{:S(2)}) collective-permute-start(bf16[2,160,320]{2,1,0:T(8,128)(2,1)S(1)} %collective-permute-done.7.refs_7_), channel_id=1, source_target_pairs={{0,4},{4,0},{8,12},{12,8},{16,20},{20,16},{24,28},{28,24},{1,5},{5... | collective-permute-start | bytes 614408 | tf_op jit(solution)/shard_map/ppermute | solution.py:107
  44.8 6.2 %collective-permute-done.13.refs_3_ = bf16[2,160,320]{2,1,0:T(8,128)(2,1)S(1)} collective-permute-done((bf16[2,160,320]{2,1,0:T(8,128)(2,1)S(1)}, bf16[2,160,320]{2,1,0:T(8,128)(2,1)S(1)}, u32[]{:S(2)}, u32[]{:S(2)}) %collective-permute-start.13) | collective-permute-done | bytes 204832 | tf_op jit(solution)/shard_map/ppermute | solution.py:107
  50.9 1.7 %collective-permute-start.15 = (bf16[2,160,320]{2,1,0:T(8,128)(2,1)S(1)}, bf16[2,160,320]{2,1,0:T(8,128)(2,1)S(1)}, u32[]{:S(2)}, u32[]{:S(2)}) collective-permute-start(bf16[2,160,320]{2,1,0:T(8,128)(2,1)S(1)} %collective-permute-done.13.refs_3_), channel_id=1, source_target_pairs={{0,4},{4,0},{8,12},{12,8},{16,20},{20,16},{24,28},{28,24},{1,5},{5... | collective-permute-start | bytes 614408 | tf_op jit(solution)/shard_map/ppermute | solution.py:107
  52.6 0.9 shard_map.82.rows_ref
  53.7 3.0 %shard_map.83 = (bf16[4,512,512]{2,1,0:T(8,128)(2,1)S(1)}, f32[4,512,1]{2,1,0:T(8,128)S(1)}) custom-call(s32[1]{0:T(128)} %bitcast.7.me_ref, bf16[512,1280]{1,0:T(8,128)(2,1)S(1)} %shard_map.82.rows_ref, bf16[144,1280]{1,0:T(8,128)(2,1)S(1)} %fusion.2.refs_0_.tokens_ref, bf16[144,1280]{1,0:T(8,128)(2,1)S(1)} %collective-permute-done.4.refs_1_, ...), custom_call_target="tpu_custom_call" | custom-call | flops 1006632960 | bytes 7143428 | tf_op jit(solution)/shard_map/pallas_call | solution.py:129
  57.2 3.0 %shard_map.84 = (f32[256,1280]{1,0:T(8,128)S(1)}, bf16[128,1280]{1,0:T(8,128)(2,1)}, bf16[128,1280]{1,0:T(8,128)(2,1)S(1)}) custom-call(s32[1]{0:T(128)} %bitcast.7.me_ref, bf16[512,1280]{1,0:T(8,128)(2,1)S(1)} %shard_map.82.rows_ref, bf16[4,512,512]{2,1,0:T(8,128)(2,1)S(1)} %get-tuple-element.38.weights_ref, f32[4,512,1]{2,1,0:T(8,128)S(1)} %get-tuple-element.39.totals_ref, ...), custom_call_target="tpu_custom_call" | custom-call | flops 1006632960 | bytes 7634948 | tf_op jit(solution)/shard_map/pallas_call | solution.py:129
  60.8 2.0 %collective-permute-start.20 = (bf16[320,640]{1,0:T(8,128)(2,1)S(1)}, bf16[320,640]{1,0:T(8,128)(2,1)S(1)}, u32[]{:S(2)}, u32[]{:S(2)}) collective-permute-start(bf16[320,640]{1,0:T(8,128)(2,1)S(1)} %pad_maximum_fusion.1.refs_0_), channel_id=1, source_target_pairs={{0,8},{4,12},{8,0},{12,4},{16,24},{20,28},{24,16},{28,20},{1,9},{5... | collective-permute-start | bytes 1228808 | tf_op jit(solution)/shard_map/ppermute | solution.py:107
  62.8 1.6 %collective-permute-start.21 = (bf16[320,640]{1,0:T(8,128)(2,1)S(1)}, bf16[320,640]{1,0:T(8,128)(2,1)S(1)}, u32[]{:S(2)}, u32[]{:S(2)}) collective-permute-start(bf16[320,640]{1,0:T(8,128)(2,1)S(1)} %pad_maximum_fusion.1.refs_0_), channel_id=1, source_target_pairs={{0,16},{4,20},{8,24},{12,28},{16,0},{20,4},{24,8},{28,12},{1,17},{... | collective-permute-start | bytes 1228808 | tf_op jit(solution)/shard_map/ppermute | solution.py:107
  64.4 0.8 shard_map.85
  65.2 1.5 %collective-permute-start.18 = (bf16[64,1280]{1,0:T(8,128)(2,1)}, bf16[64,1280]{1,0:T(8,128)(2,1)S(1)}, u32[]{:S(2)}, u32[]{:S(2)}) collective-permute-start(bf16[64,1280]{1,0:T(8,128)(2,1)} %get-tuple-element.45), channel_id=1, source_target_pairs={{0,2},{1,3},{2,0},{3,1},{4,6},{5,7},{6,4},{7,5},{8,10},{9,11},{10,... | collective-permute-start | bytes 491528 | tf_op jit(solution)/shard_map/ppermute | solution.py:107
  68.9 3.6 %collective-permute-done.18.refs_0_ = bf16[64,1280]{1,0:T(8,128)(2,1)S(1)} collective-permute-done((bf16[64,1280]{1,0:T(8,128)(2,1)}, bf16[64,1280]{1,0:T(8,128)(2,1)S(1)}, u32[]{:S(2)}, u32[]{:S(2)}) %collective-permute-start.18) | collective-permute-done | bytes 163872 | tf_op jit(solution)/shard_map/ppermute | solution.py:107
  72.5 2.0 %collective-permute-done.19.refs_1_ = bf16[64,1280]{1,0:T(8,128)(2,1)} collective-permute-done((bf16[64,1280]{1,0:T(8,128)(2,1)}, bf16[64,1280]{1,0:T(8,128)(2,1)}, u32[]{:S(2)}, u32[]{:S(2)}) %collective-permute-start.19) | collective-permute-done | bytes 163872 | tf_op jit(solution)/shard_map/ppermute | solution.py:107
  74.5 2.6 %shard_map.86 = bf16[8,64,640]{2,1,0:T(8,128)(2,1)} custom-call(bf16[144,1280]{1,0:T(8,128)(2,1)S(1)} %fusion.2.refs_0_.tokens_ref, f32[256,1280]{1,0:T(8,128)S(1)} %get-tuple-element.42.keep_ref, bf16[128,1280]{1,0:T(8,128)(2,1)S(1)} %collective-permute-done.16.core_ref, f32[2,1280]{1,0:T(2,128)S(1)} %copy-done, s32[128,1]{1,0:T(8,128)S(1)} %reshape.41.order_ref, ...), custom_call_target="tpu_custom_call" | custom-call | bytes 1 | tf_op jit(solution)/shard_map/pallas_call | solution.py:129
  77.1 3.5 %all-to-all-start = ((bf16[8,64,640]{2,1,0:T(8,128)(2,1)}), bf16[8,64,640]{2,1,0:T(8,128)(2,1)S(1)}, u32[]{:S(2)}, u32[]{:S(2)}) async-start(bf16[8,64,640]{2,1,0:T(8,128)(2,1)} %shard_map.86), calls=%async_computation | async-start | bytes 1310720 | tf_op jit(solution)/shard_map/all_to_all | solution.py:358
  80.7 2.9 %collective-permute-done.21.refs_2_ = bf16[320,640]{1,0:T(8,128)(2,1)S(1)} collective-permute-done((bf16[320,640]{1,0:T(8,128)(2,1)S(1)}, bf16[320,640]{1,0:T(8,128)(2,1)S(1)}, u32[]{:S(2)}, u32[]{:S(2)}) %collective-permute-start.21) | collective-permute-done | bytes 409632 | tf_op jit(solution)/shard_map/ppermute | solution.py:107
  85.2 8.7 %collective-permute-done.22.refs_3_ = bf16[320,640]{1,0:T(8,128)(2,1)S(1)} collective-permute-done((bf16[320,640]{1,0:T(8,128)(2,1)S(1)}, bf16[320,640]{1,0:T(8,128)(2,1)S(1)}, u32[]{:S(2)}, u32[]{:S(2)}) %collective-permute-start.22) | collective-permute-done | bytes 409632 | tf_op jit(solution)/shard_map/ppermute | solution.py:107
  93.8 1.1 shard_map.87
  95.0 1.6 %collective-permute-start.24 = (bf16[64,640]{1,0:T(8,128)(2,1)S(1)}, bf16[64,640]{1,0:T(8,128)(2,1)S(1)}, u32[]{:S(2)}, u32[]{:S(2)}) collective-permute-start(bf16[64,640]{1,0:T(8,128)(2,1)S(1)} %get-tuple-element.51), channel_id=1, source_target_pairs={{0,2},{1,3},{2,0},{3,1},{4,6},{5,7},{6,4},{7,5},{8,10},{9,11},{10,... | collective-permute-start | bytes 245768 | tf_op jit(solution)/shard_map/ppermute | solution.py:107
  96.9 3.2 %collective-permute-done.24.two_ref = bf16[64,640]{1,0:T(8,128)(2,1)S(1)} collective-permute-done((bf16[64,640]{1,0:T(8,128)(2,1)S(1)}, bf16[64,640]{1,0:T(8,128)(2,1)S(1)}, u32[]{:S(2)}, u32[]{:S(2)}) %collective-permute-start.24) | collective-permute-done | bytes 81952 | tf_op jit(solution)/shard_map/ppermute | solution.py:107
  100.2 1.1 collective-permute-done.25.three_ref
  101.5 10.5 %all_to_all.10 = bf16[8,16,640]{2,1,0:T(8,128)(2,1)S(1)} all-to-all(bf16[8,16,640]{2,1,0:T(8,128)(2,1)S(1)} %bitcast.24), channel_id=1, replica_groups=mesh['dp'=8,'fsdp'=4] {'dp'}, dimensions={0} | all-to-all | bytes 327680 | tf_op jit(solution)/shard_map/all_to_all | solution.py:383
  (71 shorter events, 9.2 us)
Async XLA Ops:
  0.0 11.7 %copy-start.1 = (bf16[320,160]{0,1:T(8,128)(2,1)S(1)}, bf16[320,160]{0,1:T(8,128)(2,1)}, u32[]{:S(2)}) copy-start(bf16[320,160]{0,1:T(8,128)(2,1)} %param.10) | copy-start | bytes 307204
  0.0 11.7 %slice-start = ((bf16[3,160,320]{2,1,0:T(8,128)(2,1)}), bf16[1,160,320]{2,1,0:T(8,128)(2,1)S(1)}, s32[]{:S(2)}) async-start(bf16[3,160,320]{2,1,0:T(8,128)(2,1)} %param.9), calls=%async_computation.2 | async-start | bytes 245760 | tf_op jit(solution)/shard_map/slice | solution.py:281
  0.0 11.8 %copy-start.2 = (bf16[160,1280]{1,0:T(8,128)(2,1)S(1)}, bf16[160,1280]{1,0:T(8,128)(2,1)}, u32[]{:S(2)}) copy-start(bf16[160,1280]{1,0:T(8,128)(2,1)} %param.11) | copy-start | bytes 1228804
  1.2 23.5 %copy-start.5 = (s32[32,1]{0,1:T(1,128)S(1)}, s32[32,1]{0,1:T(1,128)}, u32[]{:S(2)}) copy-start(s32[32,1]{0,1:T(1,128)} %param.15) | copy-start | bytes 388
  1.2 23.7 %collective-permute-start.5 = (bf16[4,160,320]{2,1,0:T(8,128)(2,1)S(1)}, bf16[4,160,320]{2,1,0:T(8,128)(2,1)S(1)}, u32[]{:S(2)}, u32[]{:S(2)}) collective-permute-start(bf16[4,160,320]{2,1,0:T(8,128)(2,1)S(1)} %pad_maximum_fusion.refs_4_.refs_0_), channel_id=1, source_target_pairs={{0,4},{4,0},{8,12},{12,8},{16,20},{20,16},{24,28},{28,24},{1,5},{5... | collective-permute-start | bytes 1228808 | tf_op jit(solution)/shard_map/ppermute | solution.py:107
  4.3 31.1 %collective-permute-start.10 = (bf16[4,160,320]{2,1,0:T(8,128)(2,1)S(1)}, bf16[4,160,320]{2,1,0:T(8,128)(2,1)S(1)}, u32[]{:S(2)}, u32[]{:S(2)}) collective-permute-start(bf16[4,160,320]{2,1,0:T(8,128)(2,1)S(1)} %pad_maximum_fusion.refs_4_.refs_0_), channel_id=1, source_target_pairs={{0,8},{4,12},{8,0},{12,4},{16,24},{20,28},{24,16},{28,20},{1,9},{5... | collective-permute-start | bytes 1228808 | tf_op jit(solution)/shard_map/ppermute | solution.py:107
  7.5 13.9 %collective-permute-start = (bf16[2,160,320]{2,1,0:T(8,128)(2,1)}, bf16[2,160,320]{2,1,0:T(8,128)(2,1)S(1)}, u32[]{:S(2)}, u32[]{:S(2)}) collective-permute-start(bf16[2,160,320]{2,1,0:T(8,128)(2,1)} %slice.27), channel_id=1, source_target_pairs={{0,16},{4,20},{8,24},{12,28},{16,0},{20,4},{24,8},{28,12},{1,17},{... | collective-permute-start | bytes 614408 | tf_op jit(solution)/shard_map/ppermute | solution.py:107
  10.2 26.4 %collective-permute-start.4 = (bf16[144,1280]{1,0:T(8,128)(2,1)S(1)}, bf16[144,1280]{1,0:T(8,128)(2,1)S(1)}, u32[]{:S(2)}, u32[]{:S(2)}) collective-permute-start(bf16[144,1280]{1,0:T(8,128)(2,1)S(1)} %fusion.2.refs_0_.tokens_ref), channel_id=1, source_target_pairs={{0,2},{1,3},{2,0},{3,1},{4,6},{5,7},{6,4},{7,5},{8,10},{9,11},{10,... | collective-permute-start | bytes 1105928 | tf_op jit(solution)/shard_map/ppermute | solution.py:107
  11.7 40.9 %copy-start = (f32[2,1280]{1,0:T(2,128)S(1)}, f32[2,1280]{1,0:T(2,128)}, u32[]{:S(2)}) copy-start(f32[2,1280]{1,0:T(2,128)} %gains_ref.3) | copy-start | bytes 30724
  21.4 13.4 %collective-permute-start.1 = (bf16[2,160,320]{2,1,0:T(8,128)(2,1)S(1)}, bf16[2,160,320]{2,1,0:T(8,128)(2,1)S(1)}, u32[]{:S(2)}, u32[]{:S(2)}) collective-permute-start(bf16[2,160,320]{2,1,0:T(8,128)(2,1)S(1)} %pad_maximum_fusion.2), channel_id=1, source_target_pairs={{0,16},{4,20},{8,24},{12,28},{16,0},{20,4},{24,8},{28,12},{1,17},{... | collective-permute-start | bytes 614408 | tf_op jit(solution)/shard_map/ppermute | solution.py:107
  24.7 10.6 %collective-permute-start.7 = (bf16[2,160,320]{2,1,0:T(8,128)(2,1)S(1)}, bf16[2,160,320]{2,1,0:T(8,128)(2,1)S(1)}, u32[]{:S(2)}, u32[]{:S(2)}) collective-permute-start(bf16[2,160,320]{2,1,0:T(8,128)(2,1)S(1)} %collective-permute-done.refs_6_), channel_id=1, source_target_pairs={{0,8},{4,12},{8,0},{12,4},{16,24},{20,28},{24,16},{28,20},{1,9},{5... | collective-permute-start | bytes 614408 | tf_op jit(solution)/shard_map/ppermute | solution.py:107
  24.9 11.6 %collective-permute-start.6 = (bf16[2,160,320]{2,1,0:T(8,128)(2,1)S(1)}, bf16[2,160,320]{2,1,0:T(8,128)(2,1)S(1)}, u32[]{:S(2)}, u32[]{:S(2)}) collective-permute-start(bf16[2,160,320]{2,1,0:T(8,128)(2,1)S(1)} %collective-permute-done.refs_6_), channel_id=1, source_target_pairs={{0,4},{4,0},{8,12},{12,8},{16,20},{20,16},{24,28},{28,24},{1,5},{5... | collective-permute-start | bytes 614408 | tf_op jit(solution)/shard_map/ppermute | solution.py:107
  34.8 7.3 %collective-permute-start.2 = (bf16[2,160,320]{2,1,0:T(8,128)(2,1)S(1)}, bf16[2,160,320]{2,1,0:T(8,128)(2,1)S(1)}, u32[]{:S(2)}, u32[]{:S(2)}) collective-permute-start(bf16[2,160,320]{2,1,0:T(8,128)(2,1)S(1)} %collective-permute-done.1.refs_2_), channel_id=1, source_target_pairs={{0,4},{4,0},{8,12},{12,8},{16,20},{20,16},{24,28},{28,24},{1,5},{5... | collective-permute-start | bytes 614408 | tf_op jit(solution)/shard_map/ppermute | solution.py:107
  35.4 7.6 %collective-permute-start.11 = (bf16[2,160,320]{2,1,0:T(8,128)(2,1)S(1)}, bf16[2,160,320]{2,1,0:T(8,128)(2,1)S(1)}, u32[]{:S(2)}, u32[]{:S(2)}) collective-permute-start(bf16[2,160,320]{2,1,0:T(8,128)(2,1)S(1)} %get-tuple-element.36), channel_id=1, source_target_pairs={{0,8},{4,12},{8,0},{12,4},{16,24},{20,28},{24,16},{28,20},{1,9},{5... | collective-permute-start | bytes 614408 | tf_op jit(solution)/shard_map/ppermute | solution.py:107
  36.5 16.1 %collective-permute-start.9 = (bf16[144,1280]{1,0:T(8,128)(2,1)S(1)}, bf16[144,1280]{1,0:T(8,128)(2,1)S(1)}, u32[]{:S(2)}, u32[]{:S(2)}) collective-permute-start(bf16[144,1280]{1,0:T(8,128)(2,1)S(1)} %collective-permute-done.4.refs_1_), channel_id=1, source_target_pairs={{0,1},{1,0},{2,3},{3,2},{4,5},{5,4},{6,7},{7,6},{8,9},{9,8},{10,11... | collective-permute-start | bytes 1105928 | tf_op jit(solution)/shard_map/ppermute | solution.py:107
  36.6 16.0 %collective-permute-start.8 = (bf16[144,1280]{1,0:T(8,128)(2,1)S(1)}, bf16[144,1280]{1,0:T(8,128)(2,1)S(1)}, u32[]{:S(2)}, u32[]{:S(2)}) collective-permute-start(bf16[144,1280]{1,0:T(8,128)(2,1)S(1)} %fusion.2.refs_0_.tokens_ref), channel_id=1, source_target_pairs={{0,1},{1,0},{2,3},{3,2},{4,5},{5,4},{6,7},{7,6},{8,9},{9,8},{10,11... | collective-permute-start | bytes 1105928 | tf_op jit(solution)/shard_map/ppermute | solution.py:107
  42.1 8.8 %collective-permute-start.3 = (bf16[176,640]{1,0:T(8,128)(2,1)S(1)}, bf16[176,640]{1,0:T(8,128)(2,1)S(1)}, u32[]{:S(2)}, u32[]{:S(2)}) collective-permute-start(bf16[176,640]{1,0:T(8,128)(2,1)S(1)} %fusion.3), channel_id=1, source_target_pairs={{0,4},{4,0},{8,12},{12,8},{16,20},{20,16},{24,28},{28,24},{1,5},{5... | collective-permute-start | bytes 675848 | tf_op jit(solution)/shard_map/ppermute | solution.py:107
  42.6 8.3 %collective-permute-start.13 = (bf16[2,160,320]{2,1,0:T(8,128)(2,1)S(1)}, bf16[2,160,320]{2,1,0:T(8,128)(2,1)S(1)}, u32[]{:S(2)}, u32[]{:S(2)}) collective-permute-start(bf16[2,160,320]{2,1,0:T(8,128)(2,1)S(1)} %collective-permute-done.1.refs_2_), channel_id=1, source_target_pairs={{0,8},{4,12},{8,0},{12,4},{16,24},{20,28},{24,16},{28,20},{1,9},{5... | collective-permute-start | bytes 614408 | tf_op jit(solution)/shard_map/ppermute | solution.py:107
  43.0 10.7 %collective-permute-start.12 = (bf16[2,160,320]{2,1,0:T(8,128)(2,1)S(1)}, bf16[2,160,320]{2,1,0:T(8,128)(2,1)S(1)}, u32[]{:S(2)}, u32[]{:S(2)}) collective-permute-start(bf16[2,160,320]{2,1,0:T(8,128)(2,1)S(1)} %collective-permute-done.7.refs_7_), channel_id=1, source_target_pairs={{0,4},{4,0},{8,12},{12,8},{16,20},{20,16},{24,28},{28,24},{1,5},{5... | collective-permute-start | bytes 614408 | tf_op jit(solution)/shard_map/ppermute | solution.py:107
  50.9 6.2 %collective-permute-start.14 = (bf16[2,160,320]{2,1,0:T(8,128)(2,1)S(1)}, bf16[2,160,320]{2,1,0:T(8,128)(2,1)S(1)}, u32[]{:S(2)}, u32[]{:S(2)}) collective-permute-start(bf16[2,160,320]{2,1,0:T(8,128)(2,1)S(1)} %get-tuple-element.40), channel_id=1, source_target_pairs={{0,8},{4,12},{8,0},{12,4},{16,24},{20,28},{24,16},{28,20},{1,9},{5... | collective-permute-start | bytes 614408 | tf_op jit(solution)/shard_map/ppermute | solution.py:107
  50.9 6.3 %collective-permute-start.15 = (bf16[2,160,320]{2,1,0:T(8,128)(2,1)S(1)}, bf16[2,160,320]{2,1,0:T(8,128)(2,1)S(1)}, u32[]{:S(2)}, u32[]{:S(2)}) collective-permute-start(bf16[2,160,320]{2,1,0:T(8,128)(2,1)S(1)} %collective-permute-done.13.refs_3_), channel_id=1, source_target_pairs={{0,4},{4,0},{8,12},{12,8},{16,20},{20,16},{24,28},{28,24},{1,5},{5... | collective-permute-start | bytes 614408 | tf_op jit(solution)/shard_map/ppermute | solution.py:107
  60.2 4.2 %collective-permute-start.17 = (bf16[128,1280]{1,0:T(8,128)(2,1)S(1)}, bf16[128,1280]{1,0:T(8,128)(2,1)S(1)}, u32[]{:S(2)}, u32[]{:S(2)}) collective-permute-start(bf16[128,1280]{1,0:T(8,128)(2,1)S(1)} %get-tuple-element.44), channel_id=1, source_target_pairs={{0,1},{1,0},{2,3},{3,2},{4,5},{5,4},{6,7},{7,6},{8,9},{9,8},{10,11... | collective-permute-start | bytes 983048 | tf_op jit(solution)/shard_map/ppermute | solution.py:107
  60.2 8.7 %collective-permute-start.16 = (bf16[128,1280]{1,0:T(8,128)(2,1)}, bf16[128,1280]{1,0:T(8,128)(2,1)S(1)}, u32[]{:S(2)}, u32[]{:S(2)}) collective-permute-start(bf16[128,1280]{1,0:T(8,128)(2,1)} %get-tuple-element.43), channel_id=1, source_target_pairs={{0,1},{1,0},{2,3},{3,2},{4,5},{5,4},{6,7},{7,6},{8,9},{9,8},{10,11... | collective-permute-start | bytes 983048 | tf_op jit(solution)/shard_map/ppermute | solution.py:107
  60.8 19.9 %collective-permute-start.20 = (bf16[320,640]{1,0:T(8,128)(2,1)S(1)}, bf16[320,640]{1,0:T(8,128)(2,1)S(1)}, u32[]{:S(2)}, u32[]{:S(2)}) collective-permute-start(bf16[320,640]{1,0:T(8,128)(2,1)S(1)} %pad_maximum_fusion.1.refs_0_), channel_id=1, source_target_pairs={{0,8},{4,12},{8,0},{12,4},{16,24},{20,28},{24,16},{28,20},{1,9},{5... | collective-permute-start | bytes 1228808 | tf_op jit(solution)/shard_map/ppermute | solution.py:107
  62.8 20.8 %collective-permute-start.21 = (bf16[320,640]{1,0:T(8,128)(2,1)S(1)}, bf16[320,640]{1,0:T(8,128)(2,1)S(1)}, u32[]{:S(2)}, u32[]{:S(2)}) collective-permute-start(bf16[320,640]{1,0:T(8,128)(2,1)S(1)} %pad_maximum_fusion.1.refs_0_), channel_id=1, source_target_pairs={{0,16},{4,20},{8,24},{12,28},{16,0},{20,4},{24,8},{28,12},{1,17},{... | collective-permute-start | bytes 1228808 | tf_op jit(solution)/shard_map/ppermute | solution.py:107
  65.2 7.3 %collective-permute-start.18 = (bf16[64,1280]{1,0:T(8,128)(2,1)}, bf16[64,1280]{1,0:T(8,128)(2,1)S(1)}, u32[]{:S(2)}, u32[]{:S(2)}) collective-permute-start(bf16[64,1280]{1,0:T(8,128)(2,1)} %get-tuple-element.45), channel_id=1, source_target_pairs={{0,2},{1,3},{2,0},{3,1},{4,6},{5,7},{6,4},{7,5},{8,10},{9,11},{10,... | collective-permute-start | bytes 491528 | tf_op jit(solution)/shard_map/ppermute | solution.py:107
  66.7 7.9 %collective-permute-start.19 = (bf16[64,1280]{1,0:T(8,128)(2,1)}, bf16[64,1280]{1,0:T(8,128)(2,1)}, u32[]{:S(2)}, u32[]{:S(2)}) collective-permute-start(bf16[64,1280]{1,0:T(8,128)(2,1)} %get-tuple-element.46), channel_id=1, source_target_pairs={{0,2},{1,3},{2,0},{3,1},{4,6},{5,7},{6,4},{7,5},{8,10},{9,11},{10,... | collective-permute-start | bytes 491528 | tf_op jit(solution)/shard_map/ppermute | solution.py:107
  77.1 16.7 %all-to-all-start = ((bf16[8,64,640]{2,1,0:T(8,128)(2,1)}), bf16[8,64,640]{2,1,0:T(8,128)(2,1)S(1)}, u32[]{:S(2)}, u32[]{:S(2)}) async-start(bf16[8,64,640]{2,1,0:T(8,128)(2,1)} %shard_map.86), calls=%async_computation | async-start | bytes 1310720 | tf_op jit(solution)/shard_map/all_to_all | solution.py:358
  83.6 10.3 %collective-permute-start.22 = (bf16[320,640]{1,0:T(8,128)(2,1)S(1)}, bf16[320,640]{1,0:T(8,128)(2,1)S(1)}, u32[]{:S(2)}, u32[]{:S(2)}) collective-permute-start(bf16[320,640]{1,0:T(8,128)(2,1)S(1)} %collective-permute-done.21.refs_2_), channel_id=1, source_target_pairs={{0,8},{4,12},{8,0},{12,4},{16,24},{20,28},{24,16},{28,20},{1,9},{5... | collective-permute-start | bytes 1228808 | tf_op jit(solution)/shard_map/ppermute | solution.py:107
  94.9 2.0 %collective-permute-start.23 = (bf16[64,640]{1,0:T(8,128)(2,1)S(1)}, bf16[64,640]{1,0:T(8,128)(2,1)S(1)}, u32[]{:S(2)}, u32[]{:S(2)}) collective-permute-start(bf16[64,640]{1,0:T(8,128)(2,1)S(1)} %get-tuple-element.50), channel_id=1, source_target_pairs={{0,1},{1,0},{2,3},{3,2},{4,5},{5,4},{6,7},{7,6},{8,9},{9,8},{10,11... | collective-permute-start | bytes 245768 | tf_op jit(solution)/shard_map/ppermute | solution.py:107
  95.0 5.2 %collective-permute-start.24 = (bf16[64,640]{1,0:T(8,128)(2,1)S(1)}, bf16[64,640]{1,0:T(8,128)(2,1)S(1)}, u32[]{:S(2)}, u32[]{:S(2)}) collective-permute-start(bf16[64,640]{1,0:T(8,128)(2,1)S(1)} %get-tuple-element.51), channel_id=1, source_target_pairs={{0,2},{1,3},{2,0},{3,1},{4,6},{5,7},{6,4},{7,5},{8,10},{9,11},{10,... | collective-permute-start | bytes 245768 | tf_op jit(solution)/shard_map/ppermute | solution.py:107
  96.5 4.7 %collective-permute-start.25 = (bf16[64,640]{1,0:T(8,128)(2,1)S(1)}, bf16[64,640]{1,0:T(8,128)(2,1)S(1)}, u32[]{:S(2)}, u32[]{:S(2)}) collective-permute-start(bf16[64,640]{1,0:T(8,128)(2,1)S(1)} %get-tuple-element.52), channel_id=1, source_target_pairs={{0,3},{1,2},{2,1},{3,0},{4,7},{5,6},{6,5},{7,4},{8,11},{9,10},{10,... | collective-permute-start | bytes 245768 | tf_op jit(solution)/shard_map/ppermute | solution.py:107
  (4 other events, 37.0 us)

commit v16 on v15

--- a/solution.py
+++ b/solution.py
@@ -164,12 +164,12 @@
     in_row = [t[rows : rows + 16, 0:rows].astype(jnp.float32)[0:1, :] for t in marks]
     in_col = [jnp.broadcast_to(s, (rows, rows)).T[:, 0:1] for s in in_row]
     allowed = jnp.concatenate(in_col, axis=0) == jnp.concatenate(in_row, axis=1)
-    factor = 1.0 / math.sqrt(HD)
+    factor = math.log2(math.e) / math.sqrt(HD)
     for head in range(queries.shape[1] // HD):
         cols = slice(head * HD, (head + 1) * HD)
         scores = dot_turned(queries[:, cols], keys[:, cols]) * factor
         masked = jnp.where(allowed, scores, -jnp.inf)
-        weights = jnp.exp(masked - jnp.max(masked, axis=1, keepdims=True))
+        weights = jnp.exp2(masked - jnp.max(masked, axis=1, keepdims=True))
         weights_ref[head] = weights.astype(jnp.bfloat16)
         totals_ref[head] = jnp.sum(weights, axis=1, keepdims=True)
 

time: 113 us -> 113 us (level)
  no operation moved by 1% of the time
where the time goes in v16:
time: 113 us
  waiting for transfers between devices  53.2 us (47%)
  starting transfers between devices  30.3 us (27%)
  Pallas kernels  11.3 us (10%)
  blocking collectives  10.5 us (9%)
  other arithmetic  3.89 us (3%)
  local copies, waits for them, and re-layouts  3.27 us (3%)
    ppermute x26, waiting for transfers between devices, swap(): lax.ppermute(value, axis, [(i, i ^ k) for i in range(lax.axis_size(axis))])  53.2 us
    ppermute x26, starting transfers between devices, swap(): lax.ppermute(value, axis, [(i, i ^ k) for i in range(lax.axis_size(axis))])  26.7 us
    pallas_call x7, Pallas kernels, call(): pl.pallas_call(kernel, out_shape=tuple(outs), in_specs=specs, out_specs=t...  11.3 us
    all_to_all x1, blocking collectives, by_permutes(): lax.all_to_all(packed.reshape(n_dp, 2 * capacity, half), 'dp', split_axis...  10.5 us
    all_to_all x1, starting transfers between devices, by_permutes(): lax.all_to_all(slices, ('dp', 'fsdp'), split_axis=0, concat_axis=0, tiled...  3.54 us
  transfers between devices with their start and end apart: 27, of which 14 were waited for; matrix products, arithmetic and copies ran while one was open for 5% of the time, Pallas kernels for 6%

profile of v16, /device:TPU:0, one launch (start us, length us, event | category | flops | bytes accessed | tf_op | source)
XLA Modules:
  0.0 112.6 jit_solution(8207680617378368511)
XLA Ops:
  0.0 1.2 %pad_maximum_fusion.refs_4_.refs_0_ = bf16[4,160,320]{2,1,0:T(8,128)(2,1)S(1)} fusion(bf16[1,160,320]{2,1,0:T(8,128)(2,1)} %bitcast.26, bf16[3,160,320]{2,1,0:T(8,128)(2,1)} %param.9), kind=kLoop, calls=%fused_computation.2 | loop fusion | flops 204800 | bytes 819200 | tf_op jit(solution)/shard_map/concatenate | solution.py:278
  1.2 3.0 %collective-permute-start.5 = (bf16[4,160,320]{2,1,0:T(8,128)(2,1)S(1)}, bf16[4,160,320]{2,1,0:T(8,128)(2,1)S(1)}, u32[]{:S(2)}, u32[]{:S(2)}) collective-permute-start(bf16[4,160,320]{2,1,0:T(8,128)(2,1)S(1)} %pad_maximum_fusion.refs_4_.refs_0_), channel_id=1, source_target_pairs={{0,4},{4,0},{8,12},{12,8},{16,20},{20,16},{24,28},{28,24},{1,5},{5... | collective-permute-start | bytes 1228808 | tf_op jit(solution)/shard_map/ppermute | solution.py:107
  4.3 1.6 %collective-permute-start.10 = (bf16[4,160,320]{2,1,0:T(8,128)(2,1)S(1)}, bf16[4,160,320]{2,1,0:T(8,128)(2,1)S(1)}, u32[]{:S(2)}, u32[]{:S(2)}) collective-permute-start(bf16[4,160,320]{2,1,0:T(8,128)(2,1)S(1)} %pad_maximum_fusion.refs_4_.refs_0_), channel_id=1, source_target_pairs={{0,8},{4,12},{8,0},{12,4},{16,24},{20,28},{24,16},{28,20},{1,9},{5... | collective-permute-start | bytes 1228808 | tf_op jit(solution)/shard_map/ppermute | solution.py:107
  5.9 1.7 %slice.27 = bf16[2,160,320]{2,1,0:T(8,128)(2,1)} slice(bf16[3,160,320]{2,1,0:T(8,128)(2,1)} %param.9), slice={[0:2], [0:160], [0:320]} | slice | bytes 409600 | tf_op jit(solution)/shard_map/slice | solution.py:280
  7.5 2.6 %collective-permute-start = (bf16[2,160,320]{2,1,0:T(8,128)(2,1)}, bf16[2,160,320]{2,1,0:T(8,128)(2,1)S(1)}, u32[]{:S(2)}, u32[]{:S(2)}) collective-permute-start(bf16[2,160,320]{2,1,0:T(8,128)(2,1)} %slice.27), channel_id=1, source_target_pairs={{0,16},{4,20},{8,24},{12,28},{16,0},{20,4},{24,8},{28,12},{1,17},{... | collective-permute-start | bytes 614408 | tf_op jit(solution)/shard_map/ppermute | solution.py:107
  10.2 1.6 %collective-permute-start.4 = (bf16[144,1280]{1,0:T(8,128)(2,1)S(1)}, bf16[144,1280]{1,0:T(8,128)(2,1)S(1)}, u32[]{:S(2)}, u32[]{:S(2)}) collective-permute-start(bf16[144,1280]{1,0:T(8,128)(2,1)S(1)} %fusion.2.refs_0_.tokens_ref), channel_id=1, source_target_pairs={{0,2},{1,3},{2,0},{3,1},{4,6},{5,7},{6,4},{7,5},{8,10},{9,11},{10,... | collective-permute-start | bytes 1105928 | tf_op jit(solution)/shard_map/ppermute | solution.py:107
  11.9 9.6 %collective-permute-done.refs_6_ = bf16[2,160,320]{2,1,0:T(8,128)(2,1)S(1)} collective-permute-done((bf16[2,160,320]{2,1,0:T(8,128)(2,1)}, bf16[2,160,320]{2,1,0:T(8,128)(2,1)S(1)}, u32[]{:S(2)}, u32[]{:S(2)}) %collective-permute-start) | collective-permute-done | bytes 204832 | tf_op jit(solution)/shard_map/ppermute | solution.py:107
  21.4 3.3 %collective-permute-start.1 = (bf16[2,160,320]{2,1,0:T(8,128)(2,1)S(1)}, bf16[2,160,320]{2,1,0:T(8,128)(2,1)S(1)}, u32[]{:S(2)}, u32[]{:S(2)}) collective-permute-start(bf16[2,160,320]{2,1,0:T(8,128)(2,1)S(1)} %pad_maximum_fusion.2), channel_id=1, source_target_pairs={{0,16},{4,20},{8,24},{12,28},{16,0},{20,4},{24,8},{28,12},{1,17},{... | collective-permute-start | bytes 614408 | tf_op jit(solution)/shard_map/ppermute | solution.py:107
  25.4 9.4 %collective-permute-done.1.refs_2_ = bf16[2,160,320]{2,1,0:T(8,128)(2,1)S(1)} collective-permute-done((bf16[2,160,320]{2,1,0:T(8,128)(2,1)S(1)}, bf16[2,160,320]{2,1,0:T(8,128)(2,1)S(1)}, u32[]{:S(2)}, u32[]{:S(2)}) %collective-permute-start.1) | collective-permute-done | bytes 204832 | tf_op jit(solution)/shard_map/ppermute | solution.py:107
  35.4 1.2 %collective-permute-start.11 = (bf16[2,160,320]{2,1,0:T(8,128)(2,1)S(1)}, bf16[2,160,320]{2,1,0:T(8,128)(2,1)S(1)}, u32[]{:S(2)}, u32[]{:S(2)}) collective-permute-start(bf16[2,160,320]{2,1,0:T(8,128)(2,1)S(1)} %get-tuple-element.36), channel_id=1, source_target_pairs={{0,8},{4,12},{8,0},{12,4},{16,24},{20,28},{24,16},{28,20},{1,9},{5... | collective-permute-start | bytes 614408 | tf_op jit(solution)/shard_map/ppermute | solution.py:107
  37.1 5.0 %collective-permute-done.2.refs_6_ = bf16[2,160,320]{2,1,0:T(8,128)(2,1)S(1)} collective-permute-done((bf16[2,160,320]{2,1,0:T(8,128)(2,1)S(1)}, bf16[2,160,320]{2,1,0:T(8,128)(2,1)S(1)}, u32[]{:S(2)}, u32[]{:S(2)}) %collective-permute-start.2) | collective-permute-done | bytes 204832 | tf_op jit(solution)/shard_map/ppermute | solution.py:107
  43.0 1.8 %collective-permute-start.12 = (bf16[2,160,320]{2,1,0:T(8,128)(2,1)S(1)}, bf16[2,160,320]{2,1,0:T(8,128)(2,1)S(1)}, u32[]{:S(2)}, u32[]{:S(2)}) collective-permute-start(bf16[2,160,320]{2,1,0:T(8,128)(2,1)S(1)} %collective-permute-done.7.refs_7_), channel_id=1, source_target_pairs={{0,4},{4,0},{8,12},{12,8},{16,20},{20,16},{24,28},{28,24},{1,5},{5... | collective-permute-start | bytes 614408 | tf_op jit(solution)/shard_map/ppermute | solution.py:107
  44.8 6.2 %collective-permute-done.13.refs_3_ = bf16[2,160,320]{2,1,0:T(8,128)(2,1)S(1)} collective-permute-done((bf16[2,160,320]{2,1,0:T(8,128)(2,1)S(1)}, bf16[2,160,320]{2,1,0:T(8,128)(2,1)S(1)}, u32[]{:S(2)}, u32[]{:S(2)}) %collective-permute-start.13) | collective-permute-done | bytes 204832 | tf_op jit(solution)/shard_map/ppermute | solution.py:107
  50.9 1.7 %collective-permute-start.15 = (bf16[2,160,320]{2,1,0:T(8,128)(2,1)S(1)}, bf16[2,160,320]{2,1,0:T(8,128)(2,1)S(1)}, u32[]{:S(2)}, u32[]{:S(2)}) collective-permute-start(bf16[2,160,320]{2,1,0:T(8,128)(2,1)S(1)} %collective-permute-done.13.refs_3_), channel_id=1, source_target_pairs={{0,4},{4,0},{8,12},{12,8},{16,20},{20,16},{24,28},{28,24},{1,5},{5... | collective-permute-start | bytes 614408 | tf_op jit(solution)/shard_map/ppermute | solution.py:107
  52.6 0.9 shard_map.82.rows_ref
  53.7 2.9 %shard_map.83 = (bf16[4,512,512]{2,1,0:T(8,128)(2,1)S(1)}, f32[4,512,1]{2,1,0:T(8,128)S(1)}) custom-call(s32[1]{0:T(128)} %bitcast.7.me_ref, bf16[512,1280]{1,0:T(8,128)(2,1)S(1)} %shard_map.82.rows_ref, bf16[144,1280]{1,0:T(8,128)(2,1)S(1)} %fusion.2.refs_0_.tokens_ref, bf16[144,1280]{1,0:T(8,128)(2,1)S(1)} %collective-permute-done.4.refs_1_, ...), custom_call_target="tpu_custom_call" | custom-call | flops 1006632960 | bytes 7143428 | tf_op jit(solution)/shard_map/pallas_call | solution.py:129
  57.2 3.0 %shard_map.84 = (f32[256,1280]{1,0:T(8,128)S(1)}, bf16[128,1280]{1,0:T(8,128)(2,1)}, bf16[128,1280]{1,0:T(8,128)(2,1)S(1)}) custom-call(s32[1]{0:T(128)} %bitcast.7.me_ref, bf16[512,1280]{1,0:T(8,128)(2,1)S(1)} %shard_map.82.rows_ref, bf16[4,512,512]{2,1,0:T(8,128)(2,1)S(1)} %get-tuple-element.38.weights_ref, f32[4,512,1]{2,1,0:T(8,128)S(1)} %get-tuple-element.39.totals_ref, ...), custom_call_target="tpu_custom_call" | custom-call | flops 1006632960 | bytes 7634948 | tf_op jit(solution)/shard_map/pallas_call | solution.py:129
  60.8 2.0 %collective-permute-start.20 = (bf16[320,640]{1,0:T(8,128)(2,1)S(1)}, bf16[320,640]{1,0:T(8,128)(2,1)S(1)}, u32[]{:S(2)}, u32[]{:S(2)}) collective-permute-start(bf16[320,640]{1,0:T(8,128)(2,1)S(1)} %pad_maximum_fusion.1.refs_0_), channel_id=1, source_target_pairs={{0,8},{4,12},{8,0},{12,4},{16,24},{20,28},{24,16},{28,20},{1,9},{5... | collective-permute-start | bytes 1228808 | tf_op jit(solution)/shard_map/ppermute | solution.py:107
  62.8 1.5 %collective-permute-start.21 = (bf16[320,640]{1,0:T(8,128)(2,1)S(1)}, bf16[320,640]{1,0:T(8,128)(2,1)S(1)}, u32[]{:S(2)}, u32[]{:S(2)}) collective-permute-start(bf16[320,640]{1,0:T(8,128)(2,1)S(1)} %pad_maximum_fusion.1.refs_0_), channel_id=1, source_target_pairs={{0,16},{4,20},{8,24},{12,28},{16,0},{20,4},{24,8},{28,12},{1,17},{... | collective-permute-start | bytes 1228808 | tf_op jit(solution)/shard_map/ppermute | solution.py:107
  64.2 0.8 shard_map.85
  65.0 1.5 %collective-permute-start.18 = (bf16[64,1280]{1,0:T(8,128)(2,1)}, bf16[64,1280]{1,0:T(8,128)(2,1)S(1)}, u32[]{:S(2)}, u32[]{:S(2)}) collective-permute-start(bf16[64,1280]{1,0:T(8,128)(2,1)} %get-tuple-element.45), channel_id=1, source_target_pairs={{0,2},{1,3},{2,0},{3,1},{4,6},{5,7},{6,4},{7,5},{8,10},{9,11},{10,... | collective-permute-start | bytes 491528 | tf_op jit(solution)/shard_map/ppermute | solution.py:107
  68.7 3.6 %collective-permute-done.18.refs_0_ = bf16[64,1280]{1,0:T(8,128)(2,1)S(1)} collective-permute-done((bf16[64,1280]{1,0:T(8,128)(2,1)}, bf16[64,1280]{1,0:T(8,128)(2,1)S(1)}, u32[]{:S(2)}, u32[]{:S(2)}) %collective-permute-start.18) | collective-permute-done | bytes 163872 | tf_op jit(solution)/shard_map/ppermute | solution.py:107
  72.4 2.0 %collective-permute-done.19.refs_1_ = bf16[64,1280]{1,0:T(8,128)(2,1)} collective-permute-done((bf16[64,1280]{1,0:T(8,128)(2,1)}, bf16[64,1280]{1,0:T(8,128)(2,1)}, u32[]{:S(2)}, u32[]{:S(2)}) %collective-permute-start.19) | collective-permute-done | bytes 163872 | tf_op jit(solution)/shard_map/ppermute | solution.py:107
  74.4 2.6 %shard_map.86 = bf16[8,64,640]{2,1,0:T(8,128)(2,1)} custom-call(bf16[144,1280]{1,0:T(8,128)(2,1)S(1)} %fusion.2.refs_0_.tokens_ref, f32[256,1280]{1,0:T(8,128)S(1)} %get-tuple-element.42.keep_ref, bf16[128,1280]{1,0:T(8,128)(2,1)S(1)} %collective-permute-done.16.core_ref, f32[2,1280]{1,0:T(2,128)S(1)} %copy-done, s32[128,1]{1,0:T(8,128)S(1)} %reshape.41.order_ref, ...), custom_call_target="tpu_custom_call" | custom-call | bytes 1 | tf_op jit(solution)/shard_map/pallas_call | solution.py:129
  77.0 3.5 %all-to-all-start = ((bf16[8,64,640]{2,1,0:T(8,128)(2,1)}), bf16[8,64,640]{2,1,0:T(8,128)(2,1)S(1)}, u32[]{:S(2)}, u32[]{:S(2)}) async-start(bf16[8,64,640]{2,1,0:T(8,128)(2,1)} %shard_map.86), calls=%async_computation | async-start | bytes 1310720 | tf_op jit(solution)/shard_map/all_to_all | solution.py:358
  80.5 3.0 %collective-permute-done.21.refs_2_ = bf16[320,640]{1,0:T(8,128)(2,1)S(1)} collective-permute-done((bf16[320,640]{1,0:T(8,128)(2,1)S(1)}, bf16[320,640]{1,0:T(8,128)(2,1)S(1)}, u32[]{:S(2)}, u32[]{:S(2)}) %collective-permute-start.21) | collective-permute-done | bytes 409632 | tf_op jit(solution)/shard_map/ppermute | solution.py:107
  85.2 8.7 %collective-permute-done.22.refs_3_ = bf16[320,640]{1,0:T(8,128)(2,1)S(1)} collective-permute-done((bf16[320,640]{1,0:T(8,128)(2,1)S(1)}, bf16[320,640]{1,0:T(8,128)(2,1)S(1)}, u32[]{:S(2)}, u32[]{:S(2)}) %collective-permute-start.22) | collective-permute-done | bytes 409632 | tf_op jit(solution)/shard_map/ppermute | solution.py:107
  93.8 1.1 shard_map.87
  95.0 1.6 %collective-permute-start.24 = (bf16[64,640]{1,0:T(8,128)(2,1)S(1)}, bf16[64,640]{1,0:T(8,128)(2,1)S(1)}, u32[]{:S(2)}, u32[]{:S(2)}) collective-permute-start(bf16[64,640]{1,0:T(8,128)(2,1)S(1)} %get-tuple-element.51), channel_id=1, source_target_pairs={{0,2},{1,3},{2,0},{3,1},{4,6},{5,7},{6,4},{7,5},{8,10},{9,11},{10,... | collective-permute-start | bytes 245768 | tf_op jit(solution)/shard_map/ppermute | solution.py:107
  96.9 3.2 %collective-permute-done.24.two_ref = bf16[64,640]{1,0:T(8,128)(2,1)S(1)} collective-permute-done((bf16[64,640]{1,0:T(8,128)(2,1)S(1)}, bf16[64,640]{1,0:T(8,128)(2,1)S(1)}, u32[]{:S(2)}, u32[]{:S(2)}) %collective-permute-start.24) | collective-permute-done | bytes 81952 | tf_op jit(solution)/shard_map/ppermute | solution.py:107
  100.2 1.1 collective-permute-done.25.three_ref
  101.5 10.5 %all_to_all.10 = bf16[8,16,640]{2,1,0:T(8,128)(2,1)S(1)} all-to-all(bf16[8,16,640]{2,1,0:T(8,128)(2,1)S(1)} %bitcast.24), channel_id=1, replica_groups=mesh['dp'=8,'fsdp'=4] {'dp'}, dimensions={0} | all-to-all | bytes 327680 | tf_op jit(solution)/shard_map/all_to_all | solution.py:383
  (71 shorter events, 9.4 us)
Async XLA Ops:
  0.0 11.7 %copy-start.1 = (bf16[320,160]{0,1:T(8,128)(2,1)S(1)}, bf16[320,160]{0,1:T(8,128)(2,1)}, u32[]{:S(2)}) copy-start(bf16[320,160]{0,1:T(8,128)(2,1)} %param.10) | copy-start | bytes 307204
  0.0 11.7 %slice-start = ((bf16[3,160,320]{2,1,0:T(8,128)(2,1)}), bf16[1,160,320]{2,1,0:T(8,128)(2,1)S(1)}, s32[]{:S(2)}) async-start(bf16[3,160,320]{2,1,0:T(8,128)(2,1)} %param.9), calls=%async_computation.2 | async-start | bytes 245760 | tf_op jit(solution)/shard_map/slice | solution.py:281
  0.0 11.8 %copy-start.2 = (bf16[160,1280]{1,0:T(8,128)(2,1)S(1)}, bf16[160,1280]{1,0:T(8,128)(2,1)}, u32[]{:S(2)}) copy-start(bf16[160,1280]{1,0:T(8,128)(2,1)} %param.11) | copy-start | bytes 1228804
  1.2 23.5 %copy-start.5 = (s32[32,1]{0,1:T(1,128)S(1)}, s32[32,1]{0,1:T(1,128)}, u32[]{:S(2)}) copy-start(s32[32,1]{0,1:T(1,128)} %param.15) | copy-start | bytes 388
  1.2 23.7 %collective-permute-start.5 = (bf16[4,160,320]{2,1,0:T(8,128)(2,1)S(1)}, bf16[4,160,320]{2,1,0:T(8,128)(2,1)S(1)}, u32[]{:S(2)}, u32[]{:S(2)}) collective-permute-start(bf16[4,160,320]{2,1,0:T(8,128)(2,1)S(1)} %pad_maximum_fusion.refs_4_.refs_0_), channel_id=1, source_target_pairs={{0,4},{4,0},{8,12},{12,8},{16,20},{20,16},{24,28},{28,24},{1,5},{5... | collective-permute-start | bytes 1228808 | tf_op jit(solution)/shard_map/ppermute | solution.py:107
  4.3 31.1 %collective-permute-start.10 = (bf16[4,160,320]{2,1,0:T(8,128)(2,1)S(1)}, bf16[4,160,320]{2,1,0:T(8,128)(2,1)S(1)}, u32[]{:S(2)}, u32[]{:S(2)}) collective-permute-start(bf16[4,160,320]{2,1,0:T(8,128)(2,1)S(1)} %pad_maximum_fusion.refs_4_.refs_0_), channel_id=1, source_target_pairs={{0,8},{4,12},{8,0},{12,4},{16,24},{20,28},{24,16},{28,20},{1,9},{5... | collective-permute-start | bytes 1228808 | tf_op jit(solution)/shard_map/ppermute | solution.py:107
  7.5 13.9 %collective-permute-start = (bf16[2,160,320]{2,1,0:T(8,128)(2,1)}, bf16[2,160,320]{2,1,0:T(8,128)(2,1)S(1)}, u32[]{:S(2)}, u32[]{:S(2)}) collective-permute-start(bf16[2,160,320]{2,1,0:T(8,128)(2,1)} %slice.27), channel_id=1, source_target_pairs={{0,16},{4,20},{8,24},{12,28},{16,0},{20,4},{24,8},{28,12},{1,17},{... | collective-permute-start | bytes 614408 | tf_op jit(solution)/shard_map/ppermute | solution.py:107
  10.2 26.4 %collective-permute-start.4 = (bf16[144,1280]{1,0:T(8,128)(2,1)S(1)}, bf16[144,1280]{1,0:T(8,128)(2,1)S(1)}, u32[]{:S(2)}, u32[]{:S(2)}) collective-permute-start(bf16[144,1280]{1,0:T(8,128)(2,1)S(1)} %fusion.2.refs_0_.tokens_ref), channel_id=1, source_target_pairs={{0,2},{1,3},{2,0},{3,1},{4,6},{5,7},{6,4},{7,5},{8,10},{9,11},{10,... | collective-permute-start | bytes 1105928 | tf_op jit(solution)/shard_map/ppermute | solution.py:107
  11.7 40.9 %copy-start = (f32[2,1280]{1,0:T(2,128)S(1)}, f32[2,1280]{1,0:T(2,128)}, u32[]{:S(2)}) copy-start(f32[2,1280]{1,0:T(2,128)} %gains_ref.3) | copy-start | bytes 30724
  21.4 13.4 %collective-permute-start.1 = (bf16[2,160,320]{2,1,0:T(8,128)(2,1)S(1)}, bf16[2,160,320]{2,1,0:T(8,128)(2,1)S(1)}, u32[]{:S(2)}, u32[]{:S(2)}) collective-permute-start(bf16[2,160,320]{2,1,0:T(8,128)(2,1)S(1)} %pad_maximum_fusion.2), channel_id=1, source_target_pairs={{0,16},{4,20},{8,24},{12,28},{16,0},{20,4},{24,8},{28,12},{1,17},{... | collective-permute-start | bytes 614408 | tf_op jit(solution)/shard_map/ppermute | solution.py:107
  24.7 10.6 %collective-permute-start.7 = (bf16[2,160,320]{2,1,0:T(8,128)(2,1)S(1)}, bf16[2,160,320]{2,1,0:T(8,128)(2,1)S(1)}, u32[]{:S(2)}, u32[]{:S(2)}) collective-permute-start(bf16[2,160,320]{2,1,0:T(8,128)(2,1)S(1)} %collective-permute-done.refs_6_), channel_id=1, source_target_pairs={{0,8},{4,12},{8,0},{12,4},{16,24},{20,28},{24,16},{28,20},{1,9},{5... | collective-permute-start | bytes 614408 | tf_op jit(solution)/shard_map/ppermute | solution.py:107
  24.9 11.6 %collective-permute-start.6 = (bf16[2,160,320]{2,1,0:T(8,128)(2,1)S(1)}, bf16[2,160,320]{2,1,0:T(8,128)(2,1)S(1)}, u32[]{:S(2)}, u32[]{:S(2)}) collective-permute-start(bf16[2,160,320]{2,1,0:T(8,128)(2,1)S(1)} %collective-permute-done.refs_6_), channel_id=1, source_target_pairs={{0,4},{4,0},{8,12},{12,8},{16,20},{20,16},{24,28},{28,24},{1,5},{5... | collective-permute-start | bytes 614408 | tf_op jit(solution)/shard_map/ppermute | solution.py:107
  34.8 7.3 %collective-permute-start.2 = (bf16[2,160,320]{2,1,0:T(8,128)(2,1)S(1)}, bf16[2,160,320]{2,1,0:T(8,128)(2,1)S(1)}, u32[]{:S(2)}, u32[]{:S(2)}) collective-permute-start(bf16[2,160,320]{2,1,0:T(8,128)(2,1)S(1)} %collective-permute-done.1.refs_2_), channel_id=1, source_target_pairs={{0,4},{4,0},{8,12},{12,8},{16,20},{20,16},{24,28},{28,24},{1,5},{5... | collective-permute-start | bytes 614408 | tf_op jit(solution)/shard_map/ppermute | solution.py:107
  35.4 7.6 %collective-permute-start.11 = (bf16[2,160,320]{2,1,0:T(8,128)(2,1)S(1)}, bf16[2,160,320]{2,1,0:T(8,128)(2,1)S(1)}, u32[]{:S(2)}, u32[]{:S(2)}) collective-permute-start(bf16[2,160,320]{2,1,0:T(8,128)(2,1)S(1)} %get-tuple-element.36), channel_id=1, source_target_pairs={{0,8},{4,12},{8,0},{12,4},{16,24},{20,28},{24,16},{28,20},{1,9},{5... | collective-permute-start | bytes 614408 | tf_op jit(solution)/shard_map/ppermute | solution.py:107
  36.5 16.1 %collective-permute-start.9 = (bf16[144,1280]{1,0:T(8,128)(2,1)S(1)}, bf16[144,1280]{1,0:T(8,128)(2,1)S(1)}, u32[]{:S(2)}, u32[]{:S(2)}) collective-permute-start(bf16[144,1280]{1,0:T(8,128)(2,1)S(1)} %collective-permute-done.4.refs_1_), channel_id=1, source_target_pairs={{0,1},{1,0},{2,3},{3,2},{4,5},{5,4},{6,7},{7,6},{8,9},{9,8},{10,11... | collective-permute-start | bytes 1105928 | tf_op jit(solution)/shard_map/ppermute | solution.py:107
  36.6 16.0 %collective-permute-start.8 = (bf16[144,1280]{1,0:T(8,128)(2,1)S(1)}, bf16[144,1280]{1,0:T(8,128)(2,1)S(1)}, u32[]{:S(2)}, u32[]{:S(2)}) collective-permute-start(bf16[144,1280]{1,0:T(8,128)(2,1)S(1)} %fusion.2.refs_0_.tokens_ref), channel_id=1, source_target_pairs={{0,1},{1,0},{2,3},{3,2},{4,5},{5,4},{6,7},{7,6},{8,9},{9,8},{10,11... | collective-permute-start | bytes 1105928 | tf_op jit(solution)/shard_map/ppermute | solution.py:107
  42.1 8.8 %collective-permute-start.3 = (bf16[176,640]{1,0:T(8,128)(2,1)S(1)}, bf16[176,640]{1,0:T(8,128)(2,1)S(1)}, u32[]{:S(2)}, u32[]{:S(2)}) collective-permute-start(bf16[176,640]{1,0:T(8,128)(2,1)S(1)} %fusion.3), channel_id=1, source_target_pairs={{0,4},{4,0},{8,12},{12,8},{16,20},{20,16},{24,28},{28,24},{1,5},{5... | collective-permute-start | bytes 675848 | tf_op jit(solution)/shard_map/ppermute | solution.py:107
  42.6 8.3 %collective-permute-start.13 = (bf16[2,160,320]{2,1,0:T(8,128)(2,1)S(1)}, bf16[2,160,320]{2,1,0:T(8,128)(2,1)S(1)}, u32[]{:S(2)}, u32[]{:S(2)}) collective-permute-start(bf16[2,160,320]{2,1,0:T(8,128)(2,1)S(1)} %collective-permute-done.1.refs_2_), channel_id=1, source_target_pairs={{0,8},{4,12},{8,0},{12,4},{16,24},{20,28},{24,16},{28,20},{1,9},{5... | collective-permute-start | bytes 614408 | tf_op jit(solution)/shard_map/ppermute | solution.py:107
  43.0 10.7 %collective-permute-start.12 = (bf16[2,160,320]{2,1,0:T(8,128)(2,1)S(1)}, bf16[2,160,320]{2,1,0:T(8,128)(2,1)S(1)}, u32[]{:S(2)}, u32[]{:S(2)}) collective-permute-start(bf16[2,160,320]{2,1,0:T(8,128)(2,1)S(1)} %collective-permute-done.7.refs_7_), channel_id=1, source_target_pairs={{0,4},{4,0},{8,12},{12,8},{16,20},{20,16},{24,28},{28,24},{1,5},{5... | collective-permute-start | bytes 614408 | tf_op jit(solution)/shard_map/ppermute | solution.py:107
  50.9 6.2 %collective-permute-start.14 = (bf16[2,160,320]{2,1,0:T(8,128)(2,1)S(1)}, bf16[2,160,320]{2,1,0:T(8,128)(2,1)S(1)}, u32[]{:S(2)}, u32[]{:S(2)}) collective-permute-start(bf16[2,160,320]{2,1,0:T(8,128)(2,1)S(1)} %get-tuple-element.40), channel_id=1, source_target_pairs={{0,8},{4,12},{8,0},{12,4},{16,24},{20,28},{24,16},{28,20},{1,9},{5... | collective-permute-start | bytes 614408 | tf_op jit(solution)/shard_map/ppermute | solution.py:107
  50.9 6.3 %collective-permute-start.15 = (bf16[2,160,320]{2,1,0:T(8,128)(2,1)S(1)}, bf16[2,160,320]{2,1,0:T(8,128)(2,1)S(1)}, u32[]{:S(2)}, u32[]{:S(2)}) collective-permute-start(bf16[2,160,320]{2,1,0:T(8,128)(2,1)S(1)} %collective-permute-done.13.refs_3_), channel_id=1, source_target_pairs={{0,4},{4,0},{8,12},{12,8},{16,20},{20,16},{24,28},{28,24},{1,5},{5... | collective-permute-start | bytes 614408 | tf_op jit(solution)/shard_map/ppermute | solution.py:107
  60.2 4.1 %collective-permute-start.17 = (bf16[128,1280]{1,0:T(8,128)(2,1)S(1)}, bf16[128,1280]{1,0:T(8,128)(2,1)S(1)}, u32[]{:S(2)}, u32[]{:S(2)}) collective-permute-start(bf16[128,1280]{1,0:T(8,128)(2,1)S(1)} %get-tuple-element.44), channel_id=1, source_target_pairs={{0,1},{1,0},{2,3},{3,2},{4,5},{5,4},{6,7},{7,6},{8,9},{9,8},{10,11... | collective-permute-start | bytes 983048 | tf_op jit(solution)/shard_map/ppermute | solution.py:107
  60.2 8.6 %collective-permute-start.16 = (bf16[128,1280]{1,0:T(8,128)(2,1)}, bf16[128,1280]{1,0:T(8,128)(2,1)S(1)}, u32[]{:S(2)}, u32[]{:S(2)}) collective-permute-start(bf16[128,1280]{1,0:T(8,128)(2,1)} %get-tuple-element.43), channel_id=1, source_target_pairs={{0,1},{1,0},{2,3},{3,2},{4,5},{5,4},{6,7},{7,6},{8,9},{9,8},{10,11... | collective-permute-start | bytes 983048 | tf_op jit(solution)/shard_map/ppermute | solution.py:107
  60.8 19.8 %collective-permute-start.20 = (bf16[320,640]{1,0:T(8,128)(2,1)S(1)}, bf16[320,640]{1,0:T(8,128)(2,1)S(1)}, u32[]{:S(2)}, u32[]{:S(2)}) collective-permute-start(bf16[320,640]{1,0:T(8,128)(2,1)S(1)} %pad_maximum_fusion.1.refs_0_), channel_id=1, source_target_pairs={{0,8},{4,12},{8,0},{12,4},{16,24},{20,28},{24,16},{28,20},{1,9},{5... | collective-permute-start | bytes 1228808 | tf_op jit(solution)/shard_map/ppermute | solution.py:107
  62.8 20.8 %collective-permute-start.21 = (bf16[320,640]{1,0:T(8,128)(2,1)S(1)}, bf16[320,640]{1,0:T(8,128)(2,1)S(1)}, u32[]{:S(2)}, u32[]{:S(2)}) collective-permute-start(bf16[320,640]{1,0:T(8,128)(2,1)S(1)} %pad_maximum_fusion.1.refs_0_), channel_id=1, source_target_pairs={{0,16},{4,20},{8,24},{12,28},{16,0},{20,4},{24,8},{28,12},{1,17},{... | collective-permute-start | bytes 1228808 | tf_op jit(solution)/shard_map/ppermute | solution.py:107
  65.0 7.3 %collective-permute-start.18 = (bf16[64,1280]{1,0:T(8,128)(2,1)}, bf16[64,1280]{1,0:T(8,128)(2,1)S(1)}, u32[]{:S(2)}, u32[]{:S(2)}) collective-permute-start(bf16[64,1280]{1,0:T(8,128)(2,1)} %get-tuple-element.45), channel_id=1, source_target_pairs={{0,2},{1,3},{2,0},{3,1},{4,6},{5,7},{6,4},{7,5},{8,10},{9,11},{10,... | collective-permute-start | bytes 491528 | tf_op jit(solution)/shard_map/ppermute | solution.py:107
  66.5 7.9 %collective-permute-start.19 = (bf16[64,1280]{1,0:T(8,128)(2,1)}, bf16[64,1280]{1,0:T(8,128)(2,1)}, u32[]{:S(2)}, u32[]{:S(2)}) collective-permute-start(bf16[64,1280]{1,0:T(8,128)(2,1)} %get-tuple-element.46), channel_id=1, source_target_pairs={{0,2},{1,3},{2,0},{3,1},{4,6},{5,7},{6,4},{7,5},{8,10},{9,11},{10,... | collective-permute-start | bytes 491528 | tf_op jit(solution)/shard_map/ppermute | solution.py:107
  77.0 16.9 %all-to-all-start = ((bf16[8,64,640]{2,1,0:T(8,128)(2,1)}), bf16[8,64,640]{2,1,0:T(8,128)(2,1)S(1)}, u32[]{:S(2)}, u32[]{:S(2)}) async-start(bf16[8,64,640]{2,1,0:T(8,128)(2,1)} %shard_map.86), calls=%async_computation | async-start | bytes 1310720 | tf_op jit(solution)/shard_map/all_to_all | solution.py:358
  83.6 10.3 %collective-permute-start.22 = (bf16[320,640]{1,0:T(8,128)(2,1)S(1)}, bf16[320,640]{1,0:T(8,128)(2,1)S(1)}, u32[]{:S(2)}, u32[]{:S(2)}) collective-permute-start(bf16[320,640]{1,0:T(8,128)(2,1)S(1)} %collective-permute-done.21.refs_2_), channel_id=1, source_target_pairs={{0,8},{4,12},{8,0},{12,4},{16,24},{20,28},{24,16},{28,20},{1,9},{5... | collective-permute-start | bytes 1228808 | tf_op jit(solution)/shard_map/ppermute | solution.py:107
  94.9 2.0 %collective-permute-start.23 = (bf16[64,640]{1,0:T(8,128)(2,1)S(1)}, bf16[64,640]{1,0:T(8,128)(2,1)S(1)}, u32[]{:S(2)}, u32[]{:S(2)}) collective-permute-start(bf16[64,640]{1,0:T(8,128)(2,1)S(1)} %get-tuple-element.50), channel_id=1, source_target_pairs={{0,1},{1,0},{2,3},{3,2},{4,5},{5,4},{6,7},{7,6},{8,9},{9,8},{10,11... | collective-permute-start | bytes 245768 | tf_op jit(solution)/shard_map/ppermute | solution.py:107
  95.0 5.2 %collective-permute-start.24 = (bf16[64,640]{1,0:T(8,128)(2,1)S(1)}, bf16[64,640]{1,0:T(8,128)(2,1)S(1)}, u32[]{:S(2)}, u32[]{:S(2)}) collective-permute-start(bf16[64,640]{1,0:T(8,128)(2,1)S(1)} %get-tuple-element.51), channel_id=1, source_target_pairs={{0,2},{1,3},{2,0},{3,1},{4,6},{5,7},{6,4},{7,5},{8,10},{9,11},{10,... | collective-permute-start | bytes 245768 | tf_op jit(solution)/shard_map/ppermute | solution.py:107
  96.5 4.7 %collective-permute-start.25 = (bf16[64,640]{1,0:T(8,128)(2,1)S(1)}, bf16[64,640]{1,0:T(8,128)(2,1)S(1)}, u32[]{:S(2)}, u32[]{:S(2)}) collective-permute-start(bf16[64,640]{1,0:T(8,128)(2,1)S(1)} %get-tuple-element.52), channel_id=1, source_target_pairs={{0,3},{1,2},{2,1},{3,0},{4,7},{5,6},{6,5},{7,4},{8,11},{9,10},{10,... | collective-permute-start | bytes 245768 | tf_op jit(solution)/shard_map/ppermute | solution.py:107
  (4 other events, 36.9 us)
